TPU v7x, 768 devices: a whole 4x8x12 slice. The times are simulated.
768 devices in a mesh: sec: 12 (over z), blk: 64 (over x, y, core).
Axes of the slice: x: 4, y: 8, z: 12, core: 2. Of those that a mesh axis runs over, the one named last changes fastest.
Arguments:
- atm_flux: bfloat16 [12, 4096, 16, 128], P('sec', 'blk'), may hold values from 0.19921875 to 2
- remap_weights: bfloat16 [12, 4096, 128, 128], P('sec', 'blk'), may hold values from 0 to 0.3, as said below
- dest_block: int32 [12, 4096, 1], P('sec', 'blk'), may hold values from 0 to 63; in each aligned block of 64 rows (0 to 63, 64 to 127, ..., all dimensions but the last counted through in order) at most 2 rows name the same one
- dest_row: int32 [12, 4096], P('sec', 'blk'), may hold values from 0 to 7
- ocean_state: float32 [2, 80, 96, 8192], P(None, None, 'sec', 'blk'), may hold values from -6 to 6
- land_mask: int32 [96, 8192], P('sec', 'blk'), may hold values 0 or 1
- wet_fraction: float32 [96, 8192], P('sec', 'blk'), may hold values from 0.25 to 1
- mixing: float32 [80, 80], replicated, may hold values from 0 to 0.7, as said below
Outputs:
- ocean_out: float32 [2, 80, 96, 8192], P(None, None, 'sec', 'blk')
- atm_surface: float32 [12, 4096, 2, 128], P('sec', 'blk')
Inputs may be any that keep to these rules, and one draw needn't show every extreme that they name: `dest_block`: the tiles of one device name at most 2 tiles for one ocean block, and in every draw some device names exactly 2 for some block. `remap_weights`: Nonnegative, each row dominated by its diagonal entry. `mixing`: Nonnegative, each row dominated by its diagonal entry.
All inputs are finite; a program needn't handle non-finite values. No bound on the sum of `land_mask` on one device may be relied on, other than what follows from the above.
Results may differ from a plain program's by a relative error of at most 0.0021.
Values may be sent and summed in bfloat16 or wider, within the bound.
No kernel may reach another device: no remote copies, remote signals or barrier semaphores. Data moves between devices by JAX's collectives and lax.ppermute only.
A program may use at most 32 MiB of HBM per device.

v0:
```python
import jax
import jax.numpy as jnp
from jax import lax
from jax.sharding import PartitionSpec as P

diffusion_rate = 0.2
forcing_step = 0.01


def with_halo(shard, sides, width):
    for axis, dim in sides:
        peers, length = (lax.axis_size(axis), shard.shape[dim])
        up = [(i, (i + 1) % peers) for i in range(peers - 1)]
        down = [(j, i) for i, j in up]
        last = lax.slice_in_dim(shard, length - width, length, axis=dim)
        initial = lax.slice_in_dim(shard, 0, width, axis=dim)
        before = lax.ppermute(last, axis, up)
        after = lax.ppermute(initial, axis, down)
        shard = jnp.concatenate([before, shard, after], axis=dim)
    return shard


def advance(padded, mask_padded, drive_sum, drive_rate, mixing):
    center = padded[:, :, 1:-1, 1:-1]
    inside = mask_padded[1:-1, 1:-1]
    laplace = jnp.zeros_like(center)
    for rows_slice, cols_slice in (
        (slice(2, None), slice(1, -1)),
        (slice(None, -2), slice(1, -1)),
        (slice(1, -1), slice(2, None)),
        (slice(1, -1), slice(None, -2)),
    ):
        laplace = laplace + mask_padded[rows_slice, cols_slice] * inside * (
            padded[:, :, rows_slice, cols_slice] - center
        )
    updated = center + diffusion_rate * laplace
    surface = updated[:, 0] + forcing_step * (drive_sum - drive_rate * center[:, 0])
    updated = jnp.concatenate([surface[:, None], updated[:, 1:]], axis=1)
    vertical = jnp.einsum("ij,kjxy->kixy", mixing, updated, precision=lax.Precision.HIGHEST)
    return vertical * inside


def per_device(
    atm_flux, remap_weights, dest_block, dest_row, ocean_state, land_mask, wet_fraction, mixing
):
    block_count = lax.axis_size("blk")
    row_count = land_mask.shape[0]
    tiles = atm_flux.shape[1]
    fields = atm_flux.shape[2]
    width = atm_flux.shape[3]
    tracer_count = ocean_state.shape[0]
    weights = remap_weights[0]
    blocks = dest_block[0, :, 0]
    target_rows = dest_row[0]
    remapped = jnp.einsum(
        "tfa,tao->tfo", atm_flux[0], weights, preferred_element_type=jnp.float32
    ).reshape(tiles, fields * width)
    row_key = blocks * row_count + target_rows
    row_onehot = jnp.arange(block_count * row_count, dtype=jnp.int32)[:, None] == row_key[None, :]
    partial_rows = jnp.dot(
        row_onehot.astype(jnp.float32), remapped, precision=lax.Precision.HIGHEST
    )
    partial_rows = partial_rows.astype(jnp.bfloat16).reshape(block_count, row_count, fields, width)
    received = lax.all_to_all(partial_rows, "blk", split_axis=0, concat_axis=0, tiled=True)
    cell_flux = jnp.sum(received, axis=0, dtype=jnp.float32)
    field_grid = jnp.transpose(cell_flux, (1, 0, 2))
    pairs = fields // 4
    coefficient = field_grid[0::2].reshape(2, pairs, row_count, width)
    target = field_grid[1::2].reshape(2, pairs, row_count, width)
    drive_sum = jnp.sum(coefficient * target, axis=1) / wet_fraction
    drive_rate = jnp.sum(coefficient, axis=1) / wet_fraction
    mask_padded = with_halo(land_mask, (("sec", 0), ("blk", 1)), 2).astype(jnp.float32)
    state = ocean_state
    for step_index in range(2):
        padded = with_halo(state, (("sec", 2), ("blk", 3)), 1)
        state = advance(padded, mask_padded[1:-1, 1:-1], drive_sum, drive_rate, mixing)
    surface = jnp.transpose(state[:, 0], (1, 0, 2)).astype(jnp.bfloat16)
    gathered = lax.all_gather(surface, "blk", axis=0, tiled=True)
    returned = jnp.dot(
        row_onehot.T.astype(jnp.bfloat16),
        gathered.reshape(block_count * row_count, tracer_count * width),
        preferred_element_type=jnp.float32,
    )
    returned = returned.astype(jnp.bfloat16).reshape(tiles, tracer_count, width)
    numerator = jnp.einsum("tik,tck->tci", weights, returned, preferred_element_type=jnp.float32)
    denominator = jnp.sum(weights, axis=2, dtype=jnp.float32)
    atmosphere = (numerator / denominator[:, None, :])[None]
    return (state, atmosphere)


def solution(mesh):
    placed = (
        P("sec", "blk", None, None),
        P("sec", "blk", None, None),
        P("sec", "blk", None),
        P("sec", "blk"),
        P(None, None, "sec", "blk"),
        P("sec", "blk"),
        P("sec", "blk"),
        P(),
    )
    return jax.shard_map(
        per_device,
        mesh=mesh,
        in_specs=placed,
        out_specs=(P(None, None, "sec", "blk"), P("sec", "blk", None, None)),
        check_vma=False,
    )
```

profile of v0, /device:TPU:1, one launch (start us, length us, event | category | flops | bytes accessed | tf_op | source)
XLA Modules:
  0.0 169.8 jit_solution(5587210196973703295)
XLA Ops:
  0.6 0.0 copy-start
  0.6 0.7 fusion.55
  1.4 0.3 copy-done
  1.6 2.2 %fusion.2 = f32[64,16,128]{2,1,0:T(8,128)S(1)} fusion(bf16[1,64,128,128]{3,2,1,0:T(8,128)(2,1)} %param.9, bf16[1,64,16,128]{3,2,1,0:T(8,128)(2,1)S(1)} %copy-done), kind=kOutput, calls=%fused_computation.5 | convolution fusion | flops 33554432 | bytes 2883584 | tf_op jit(solution)/shard_map/tfa,tao->tfo/dot_general | solution.py:55
  3.9 3.2 %fusion.4 = bf16[64,8,16,128]{3,1,2,0:T(8,128)(2,1)} fusion(f32[8,8,16,128]{3,2,1,0:T(8,128)S(1)} %bitcast.56, s32[64]{0:T(128)S(1)} %fusion.55), kind=kOutput, calls=%fused_computation.7 | convolution fusion | flops 806387712 | bytes 2621696 | tf_op jit(solution)/shard_map/dot_general | solution.py:60
  7.0 14.8 %all-to-all-start = ((bf16[64,8,16,128]{3,1,2,0:T(8,128)(2,1)}), bf16[64,8,16,128]{3,1,2,0:T(8,128)(2,1)S(1)}, u32[]{:S(2)}, u32[]{:S(2)}) async-start(bf16[64,8,16,128]{3,1,2,0:T(8,128)(2,1)} %fusion.4), calls=%async_computation | async-start | bytes 4194304 | tf_op jit(solution)/shard_map/all_to_all | solution.py:64
  21.8 0.0 copy-start.4
  21.8 1.4 collective-permute-start
  23.3 1.3 collective-permute-start.1
  24.6 0.1 copy.48
  24.7 0.0 copy-start.2
  24.8 4.3 %collective-permute-start.5 = (f32[2,80,1,128]{3,1,2,0:T(8,128)S(1)}, f32[2,80,1,128]{3,1,2,0:T(8,128)S(1)}, u32[]{:S(2)}, u32[]{:S(2)}) collective-permute-start(f32[2,80,1,128]{3,1,2,0:T(8,128)S(1)} %get-tuple-element.20), channel_id=1, source_target_pairs={{0,64},{64,128},{128,192},{192,256},{256,320},{320,384},{384,448},... | collective-permute-start | bytes 245768 | tf_op jit(solution)/shard_map/ppermute | solution.py:17
  29.1 1.3 collective-permute-start.4
  30.4 0.0 collective-permute-done
  30.4 0.0 collective-permute-done.1
  30.4 0.1 fusion.63
  30.5 4.1 %collective-permute-start.2 = (s32[12,2]{1,0:T(8,128)S(1)}, s32[12,2]{1,0:T(8,128)S(1)}, u32[]{:S(2)}, u32[]{:S(2)}) collective-permute-start(s32[12,2]{1,0:T(8,128)S(1)} %get-tuple-element.26), channel_id=1, source_target_pairs={{0,1},{1,2},{2,3},{3,4},{4,5},{5,6},{6,7},{7,8},{8,9},{9,10},{10,1... | collective-permute-start | bytes 296 | tf_op jit(solution)/shard_map/ppermute | solution.py:17
  34.6 1.9 %collective-permute-start.3 = (s32[12,2]{1,0:T(8,128)S(1)}, s32[12,2]{1,0:T(8,128)S(1)}, u32[]{:S(2)}, u32[]{:S(2)}) collective-permute-start(s32[12,2]{1,0:T(8,128)S(1)} %get-tuple-element.27), channel_id=1, source_target_pairs={{1,0},{2,1},{3,2},{4,3},{5,4},{6,5},{7,6},{8,7},{9,8},{10,9},{11,1... | collective-permute-start | bytes 296 | tf_op jit(solution)/shard_map/ppermute | solution.py:18
  36.5 27.4 %collective-permute-done.2 = s32[12,2]{1,0:T(8,128)S(1)} collective-permute-done((s32[12,2]{1,0:T(8,128)S(1)}, s32[12,2]{1,0:T(8,128)S(1)}, u32[]{:S(2)}, u32[]{:S(2)}) %collective-permute-start.2) | collective-permute-done | bytes 128 | tf_op jit(solution)/shard_map/ppermute | solution.py:17
  63.9 5.3 %collective-permute-done.3 = s32[12,2]{1,0:T(8,128)S(1)} collective-permute-done((s32[12,2]{1,0:T(8,128)S(1)}, s32[12,2]{1,0:T(8,128)S(1)}, u32[]{:S(2)}, u32[]{:S(2)}) %collective-permute-start.3) | collective-permute-done | bytes 128 | tf_op jit(solution)/shard_map/ppermute | solution.py:18
  69.2 0.1 add_convert_fusion
  69.3 0.0 collective-permute-done.5
  69.3 0.1 constant_dynamic-update-slice_fusion.1
  69.4 0.0 collective-permute-done.4
  69.5 1.4 fusion.59
  70.9 1.4 copy.42
  72.3 1.9 %collective-permute-start.6 = (f32[2,80,10,1]{1,0,3,2:T(2,128)S(1)}, f32[2,80,10,1]{1,0,3,2:T(2,128)S(1)}, u32[]{:S(2)}, u32[]{:S(2)}) collective-permute-start(f32[2,80,10,1]{1,0,3,2:T(2,128)S(1)} %copy.42), channel_id=1, source_target_pairs={{1,0},{2,1},{3,2},{4,3},{5,4},{6,5},{7,6},{8,7},{9,8},{10,9},{11,1... | collective-permute-start | bytes 19208 | tf_op jit(solution)/shard_map/ppermute | solution.py:18
  74.2 1.4 copy.45
  75.7 3.6 %collective-permute-start.7 = (f32[2,80,10,1]{1,0,3,2:T(2,128)S(1)}, f32[2,80,10,1]{1,0,3,2:T(2,128)S(1)}, u32[]{:S(2)}, u32[]{:S(2)}) collective-permute-start(f32[2,80,10,1]{1,0,3,2:T(2,128)S(1)} %copy.45), channel_id=1, source_target_pairs={{0,1},{1,2},{2,3},{3,4},{4,5},{5,6},{6,7},{7,8},{8,9},{9,10},{10,1... | collective-permute-start | bytes 19208 | tf_op jit(solution)/shard_map/ppermute | solution.py:17
  79.3 0.1 fusion.62
  79.4 0.0 collective-permute-done.6
  79.4 1.2 copy.43
  80.6 0.0 collective-permute-done.7
  80.7 1.2 copy.46
  81.9 2.5 %fusion.30 = f32[2,80,8,128]{3,1,2,0:T(8,128)S(1)} fusion(f32[2,80,8,128]{3,1,2,0:T(8,128)} %copy-done.2, f32[2,80,10,128]{3,1,2,0:T(8,128)S(1)} %constant_dynamic-update-slice_fusion, f32[2,80,10,1]{3,1,2,0:T(8,128)} %copy.46, f32[2,80,10,1]{3,1,2,0:T(8,128)} %copy.43, f32[2,80,1,128]{3,1,2,0:T(8,128)S(1)} %collective-permute-done.5, ...), kind=kLoop, calls=%fused_computation.42 | loop fusion | flops 2785280 | bytes 2322944 | tf_op jit(solution)/shard_map/add | solution.py:36
  84.4 0.8 copy-done.5
  85.3 0.9 slice.169
  86.2 0.0 all-to-all-done
  86.2 0.3 convert_reduce_fusion.1
  86.5 0.9 slice_add_fusion.1
  87.4 0.8 fusion.6
  88.2 1.3 collective-permute-start.8
  89.5 4.0 %collective-permute-start.9 = (f32[2,80,1,128]{3,1,2,0:T(8,128)S(1)}, f32[2,80,1,128]{3,1,2,0:T(8,128)S(1)}, u32[]{:S(2)}, u32[]{:S(2)}) collective-permute-start(f32[2,80,1,128]{3,1,2,0:T(8,128)S(1)} %get-tuple-element.17), channel_id=1, source_target_pairs={{0,64},{64,128},{128,192},{192,256},{256,320},{320,384},{384,448},... | collective-permute-start | bytes 245768 | tf_op jit(solution)/shard_map/ppermute | solution.py:17
  93.5 0.0 collective-permute-done.8
  93.5 1.7 %collective-permute-done.9 = f32[2,80,1,128]{3,1,2,0:T(8,128)S(1)} collective-permute-done((f32[2,80,1,128]{3,1,2,0:T(8,128)S(1)}, f32[2,80,1,128]{3,1,2,0:T(8,128)S(1)}, u32[]{:S(2)}, u32[]{:S(2)}) %collective-permute-start.9) | collective-permute-done | bytes 81952 | tf_op jit(solution)/shard_map/ppermute | solution.py:17
  95.3 0.1 pad_maximum_fusion
  95.3 0.0 copy-start.1
  95.3 1.4 fusion.58
  96.8 1.4 copy.50
  98.2 1.9 %collective-permute-start.10 = (f32[2,80,10,1]{1,0,3,2:T(2,128)S(1)}, f32[2,80,10,1]{1,0,3,2:T(2,128)S(1)}, u32[]{:S(2)}, u32[]{:S(2)}) collective-permute-start(f32[2,80,10,1]{1,0,3,2:T(2,128)S(1)} %copy.50), channel_id=1, source_target_pairs={{1,0},{2,1},{3,2},{4,3},{5,4},{6,5},{7,6},{8,7},{9,8},{10,9},{11,1... | collective-permute-start | bytes 19208 | tf_op jit(solution)/shard_map/ppermute | solution.py:18
  100.2 1.4 copy.52
  101.6 4.5 %collective-permute-start.11 = (f32[2,80,10,1]{1,0,3,2:T(2,128)S(1)}, f32[2,80,10,1]{1,0,3,2:T(2,128)S(1)}, u32[]{:S(2)}, u32[]{:S(2)}) collective-permute-start(f32[2,80,10,1]{1,0,3,2:T(2,128)S(1)} %copy.52), channel_id=1, source_target_pairs={{0,1},{1,2},{2,3},{3,4},{4,5},{5,6},{6,7},{7,8},{8,9},{9,10},{10,1... | collective-permute-start | bytes 19208 | tf_op jit(solution)/shard_map/ppermute | solution.py:17
  106.1 0.6 convert_reduce_fusion
  106.7 0.0 collective-permute-done.10
  106.8 1.3 copy.51
  108.0 0.0 collective-permute-done.11
  108.0 1.2 copy.53
  109.3 1.9 %fusion.17 = f32[2,80,8,128]{3,1,2,0:T(8,128)S(1)} fusion(f32[2,80,8,128]{3,1,2,0:T(8,128)S(1)} %fusion.6, f32[2,80,10,1]{3,1,2,0:T(8,128)} %copy.53, f32[2,80,1,128]{3,1,2,0:T(8,128)S(1)} %collective-permute-done.8, f32[2,80,1,128]{3,1,2,0:T(8,128)S(1)} %collective-permute-done.9, f32[2,80,10,1]{3,1,2,0:T(8,128)} %copy.51, ...), kind=kLoop, calls=%fused_computation.21 | loop fusion | flops 3440640 | bytes 1503744 | tf_op jit(solution)/shard_map/add | solution.py:36
  111.2 0.8 fusion.5
  112.0 1.0 copy.55
  113.1 54.5 %all_gather.3 = bf16[512,2,128]{2,0,1:T(8,128)(2,1)S(1)} all-gather(bf16[8,2,128]{2,0,1:T(8,128)(2,1)S(1)} %bitcast.61), channel_id=1, replica_groups=mesh['sec'=12,'blk'=64] {'blk'}, dimensions={0}, use_global_device_ids=true | all-gather | bytes 266240 | tf_op jit(solution)/shard_map/all_gather | solution.py:78
  167.5 0.1 copy.54
  167.7 0.2 convolution_convert_fusion.1
  167.9 1.8 %fusion.10 = f32[1,64,2,128]{3,2,1,0:T(2,128)} fusion(bf16[64,2,128]{2,1,0:T(2,128)(2,1)S(1)} %reshape.63, bf16[1,64,128,128]{3,2,1,0:T(8,128)(2,1)S(1)} %copy-done.1, f32[64,128]{1,0:T(8,128)S(1)} %convert_reduce_fusion), kind=kOutput, calls=%fused_computation.13 | convolution fusion | flops 4210688 | bytes 2228224 | tf_op jit(solution)/shard_map/tik,tck->tci/dot_general | solution.py:85
  (28 shorter events, 0.2 us)
Async XLA Ops:
  0.6 1.0 copy-start
  7.0 14.8 %copy-start.8 = (s32[8,128]{1,0:T(8,128)S(1)}, s32[8,128]{1,0:T(8,128)}, u32[]{:S(2)}) copy-start(s32[8,128]{1,0:T(8,128)} %param.13) | copy-start | bytes 12292
  7.0 17.5 %copy-start.3 = (f32[2,80,8,128]{3,2,1,0:T(8,128)S(1)}, f32[2,80,8,128]{3,2,1,0:T(8,128)}, u32[]{:S(2)}) copy-start(f32[2,80,8,128]{3,2,1,0:T(8,128)} %param.12) | copy-start | bytes 1966084
  7.0 79.1 %all-to-all-start = ((bf16[64,8,16,128]{3,1,2,0:T(8,128)(2,1)}), bf16[64,8,16,128]{3,1,2,0:T(8,128)(2,1)S(1)}, u32[]{:S(2)}, u32[]{:S(2)}) async-start(bf16[64,8,16,128]{3,1,2,0:T(8,128)(2,1)} %fusion.4), calls=%async_computation | async-start | bytes 4194304 | tf_op jit(solution)/shard_map/all_to_all | solution.py:64
  21.8 47.5 %copy-start.4 = (f32[2,80,8,128]{3,2,1,0:T(8,128)S(1)}, f32[2,80,8,128]{3,2,1,0:T(8,128)}, u32[]{:S(2)}) copy-start(f32[2,80,8,128]{3,2,1,0:T(8,128)} %param.12) | copy-start | bytes 1966084
  21.8 8.5 %collective-permute-start = (s32[2,128]{1,0:T(2,128)S(1)}, s32[2,128]{1,0:T(2,128)S(1)}, u32[]{:S(2)}, u32[]{:S(2)}) collective-permute-start(s32[2,128]{1,0:T(2,128)S(1)} %get-tuple-element.28), channel_id=1, source_target_pairs={{0,64},{64,128},{128,192},{192,256},{256,320},{320,384},{384,448},... | collective-permute-start | bytes 3080 | tf_op jit(solution)/shard_map/ppermute | solution.py:17
  23.3 7.1 %collective-permute-start.1 = (s32[2,128]{1,0:T(2,128)S(1)}, s32[2,128]{1,0:T(2,128)S(1)}, u32[]{:S(2)}, u32[]{:S(2)}) collective-permute-start(s32[2,128]{1,0:T(2,128)S(1)} %get-tuple-element.29), channel_id=1, source_target_pairs={{64,0},{128,64},{192,128},{256,192},{320,256},{384,320},{448,384},... | collective-permute-start | bytes 3080 | tf_op jit(solution)/shard_map/ppermute | solution.py:18
  24.7 44.7 %copy-start.2 = (f32[2,80,8,128]{3,1,2,0:T(8,128)}, f32[2,80,8,128]{3,1,2,0:T(8,128)S(1)}, u32[]{:S(2)}) copy-start(f32[2,80,8,128]{3,1,2,0:T(8,128)S(1)} %copy.48) | copy-start | bytes 1966084
  24.8 44.5 %collective-permute-start.5 = (f32[2,80,1,128]{3,1,2,0:T(8,128)S(1)}, f32[2,80,1,128]{3,1,2,0:T(8,128)S(1)}, u32[]{:S(2)}, u32[]{:S(2)}) collective-permute-start(f32[2,80,1,128]{3,1,2,0:T(8,128)S(1)} %get-tuple-element.20), channel_id=1, source_target_pairs={{0,64},{64,128},{128,192},{192,256},{256,320},{320,384},{384,448},... | collective-permute-start | bytes 245768 | tf_op jit(solution)/shard_map/ppermute | solution.py:17
  29.1 40.4 %collective-permute-start.4 = (f32[2,80,1,128]{3,1,2,0:T(8,128)S(1)}, f32[2,80,1,128]{3,1,2,0:T(8,128)S(1)}, u32[]{:S(2)}, u32[]{:S(2)}) collective-permute-start(f32[2,80,1,128]{3,1,2,0:T(8,128)S(1)} %get-tuple-element.19), channel_id=1, source_target_pairs={{64,0},{128,64},{192,128},{256,192},{320,256},{384,320},{448,384},... | collective-permute-start | bytes 245768 | tf_op jit(solution)/shard_map/ppermute | solution.py:18
  30.5 33.4 %collective-permute-start.2 = (s32[12,2]{1,0:T(8,128)S(1)}, s32[12,2]{1,0:T(8,128)S(1)}, u32[]{:S(2)}, u32[]{:S(2)}) collective-permute-start(s32[12,2]{1,0:T(8,128)S(1)} %get-tuple-element.26), channel_id=1, source_target_pairs={{0,1},{1,2},{2,3},{3,4},{4,5},{5,6},{6,7},{7,8},{8,9},{9,10},{10,1... | collective-permute-start | bytes 296 | tf_op jit(solution)/shard_map/ppermute | solution.py:17
  34.6 34.6 %collective-permute-start.3 = (s32[12,2]{1,0:T(8,128)S(1)}, s32[12,2]{1,0:T(8,128)S(1)}, u32[]{:S(2)}, u32[]{:S(2)}) collective-permute-start(s32[12,2]{1,0:T(8,128)S(1)} %get-tuple-element.27), channel_id=1, source_target_pairs={{1,0},{2,1},{3,2},{4,3},{5,4},{6,5},{7,6},{8,7},{9,8},{10,9},{11,1... | collective-permute-start | bytes 296 | tf_op jit(solution)/shard_map/ppermute | solution.py:18
  72.3 7.1 %collective-permute-start.6 = (f32[2,80,10,1]{1,0,3,2:T(2,128)S(1)}, f32[2,80,10,1]{1,0,3,2:T(2,128)S(1)}, u32[]{:S(2)}, u32[]{:S(2)}) collective-permute-start(f32[2,80,10,1]{1,0,3,2:T(2,128)S(1)} %copy.42), channel_id=1, source_target_pairs={{1,0},{2,1},{3,2},{4,3},{5,4},{6,5},{7,6},{8,7},{9,8},{10,9},{11,1... | collective-permute-start | bytes 19208 | tf_op jit(solution)/shard_map/ppermute | solution.py:18
  75.7 5.0 %collective-permute-start.7 = (f32[2,80,10,1]{1,0,3,2:T(2,128)S(1)}, f32[2,80,10,1]{1,0,3,2:T(2,128)S(1)}, u32[]{:S(2)}, u32[]{:S(2)}) collective-permute-start(f32[2,80,10,1]{1,0,3,2:T(2,128)S(1)} %copy.45), channel_id=1, source_target_pairs={{0,1},{1,2},{2,3},{3,4},{4,5},{5,6},{6,7},{7,8},{8,9},{9,10},{10,1... | collective-permute-start | bytes 19208 | tf_op jit(solution)/shard_map/ppermute | solution.py:17
  84.4 0.9 copy-start.5
  85.3 1.2 slice-start
  85.3 1.2 copy-start.9
  85.3 2.1 %copy-start.7 = (f32[80,80]{1,0:T(8,128)S(1)}, f32[80,80]{1,0:T(8,128)}, u32[]{:S(2)}) copy-start(f32[80,80]{1,0:T(8,128)} %param.15) | copy-start | bytes 76804
  86.2 1.2 copy-start.6
  88.2 5.3 %collective-permute-start.8 = (f32[2,80,1,128]{3,1,2,0:T(8,128)S(1)}, f32[2,80,1,128]{3,1,2,0:T(8,128)S(1)}, u32[]{:S(2)}, u32[]{:S(2)}) collective-permute-start(f32[2,80,1,128]{3,1,2,0:T(8,128)S(1)} %get-tuple-element.18), channel_id=1, source_target_pairs={{64,0},{128,64},{192,128},{256,192},{320,256},{384,320},{448,384},... | collective-permute-start | bytes 245768 | tf_op jit(solution)/shard_map/ppermute | solution.py:18
  89.5 5.8 %collective-permute-start.9 = (f32[2,80,1,128]{3,1,2,0:T(8,128)S(1)}, f32[2,80,1,128]{3,1,2,0:T(8,128)S(1)}, u32[]{:S(2)}, u32[]{:S(2)}) collective-permute-start(f32[2,80,1,128]{3,1,2,0:T(8,128)S(1)} %get-tuple-element.17), channel_id=1, source_target_pairs={{0,64},{64,128},{128,192},{192,256},{256,320},{320,384},{384,448},... | collective-permute-start | bytes 245768 | tf_op jit(solution)/shard_map/ppermute | solution.py:17
  95.3 10.8 %copy-start.1 = (bf16[1,64,128,128]{3,2,1,0:T(8,128)(2,1)S(1)}, bf16[1,64,128,128]{3,2,1,0:T(8,128)(2,1)}, u32[]{:S(2)}) copy-start(bf16[1,64,128,128]{3,2,1,0:T(8,128)(2,1)} %param.9) | copy-start | bytes 6291460
  98.2 8.5 %collective-permute-start.10 = (f32[2,80,10,1]{1,0,3,2:T(2,128)S(1)}, f32[2,80,10,1]{1,0,3,2:T(2,128)S(1)}, u32[]{:S(2)}, u32[]{:S(2)}) collective-permute-start(f32[2,80,10,1]{1,0,3,2:T(2,128)S(1)} %copy.50), channel_id=1, source_target_pairs={{1,0},{2,1},{3,2},{4,3},{5,4},{6,5},{7,6},{8,7},{9,8},{10,9},{11,1... | collective-permute-start | bytes 19208 | tf_op jit(solution)/shard_map/ppermute | solution.py:18
  101.6 6.4 %collective-permute-start.11 = (f32[2,80,10,1]{1,0,3,2:T(2,128)S(1)}, f32[2,80,10,1]{1,0,3,2:T(2,128)S(1)}, u32[]{:S(2)}, u32[]{:S(2)}) collective-permute-start(f32[2,80,10,1]{1,0,3,2:T(2,128)S(1)} %copy.52), channel_id=1, source_target_pairs={{0,1},{1,2},{2,3},{3,4},{4,5},{5,6},{6,7},{7,8},{8,9},{9,10},{10,1... | collective-permute-start | bytes 19208 | tf_op jit(solution)/shard_map/ppermute | solution.py:17
where the time goes:
time: 171 us; the launch traced here: 170 us
  blocking collectives  54.5 us (32%)
  starting transfers between devices  46.4 us (27%)
  waiting for transfers between devices  34.5 us (20%)
  local copies, waits for them, and re-layouts  17.2 us (10%)
  matrix products  9 us (5%)
  other arithmetic  7.18 us (4%)
    all_gather x1, blocking collectives, per_device(): gathered = lax.all_gather(surface, 'blk', axis=0, tiled=True)  54.5 us
    ppermute x6, waiting for transfers between devices, with_halo(): before = lax.ppermute(last, axis, up)  29.1 us
    ppermute x6, starting transfers between devices, with_halo(): before = lax.ppermute(last, axis, up)  22 us
    all_to_all x1, starting transfers between devices, per_device(): lax.all_to_all(partial_rows, 'blk', split_axis=0, concat_axis=0, tiled=True)  14.8 us
    ppermute x6, starting transfers between devices, with_halo(): after = lax.ppermute(initial, axis, down)  9.65 us
    slice x5, local copies, waits for them, and re-layouts, with_halo(): initial = lax.slice_in_dim(shard, 0, width, axis=dim)  5.73 us
    ppermute x6, waiting for transfers between devices, with_halo(): after = lax.ppermute(initial, axis, down)  5.32 us
    add x2, other arithmetic, advance(): updated = center + diffusion_rate * laplace  4.42 us
  transfers between devices with their start and end apart: 13, of which 3 were waited for; matrix products, arithmetic and copies ran while one was open for 8% of the time, Pallas kernels for 0%

commit v1 on v0

v1 whole, which is shorter than its diff:
```python
import functools

import jax
import jax.numpy as jnp
from jax import lax
from jax.experimental import pallas as pl
from jax.experimental.pallas import tpu as pltpu
from jax.sharding import PartitionSpec as P

diffusion_rate = 0.2
forcing_step = 0.01
empty_code = 100
f32 = jnp.float32
bf16 = jnp.bfloat16
exact = lax.Precision.HIGHEST
vmem = pl.BlockSpec(memory_space=pltpu.VMEM)
smem = pl.BlockSpec(memory_space=pltpu.SMEM)


def call(body, name, out_shape, in_specs, out_specs=None, scratch=(), flops=0, moved=0):
    many = isinstance(out_shape, (tuple, list))
    if out_specs is None:
        out_specs = [vmem] * len(out_shape) if many else vmem
    return pl.pallas_call(
        body,
        name=name,
        out_shape=out_shape,
        in_specs=in_specs,
        out_specs=out_specs,
        scratch_shapes=list(scratch),
        cost_estimate=pl.CostEstimate(flops=flops, bytes_accessed=moved, transcendentals=0),
    )


def shape(*dims, dtype=f32):
    return jax.ShapeDtypeStruct(dims, dtype)


def lane_iota(dims):
    return lax.broadcasted_iota(jnp.int32, dims, len(dims) - 1)


def line_iota(dims):
    return lax.broadcasted_iota(jnp.int32, dims, len(dims) - 2)


def forward_kernel(block_ref, row_ref, flux_ref, weight_ref, out_ref, slot_ref, used_ref, code_ref):
    blocks = out_ref.shape[0]
    tiles, fields, width = flux_ref.shape
    out_ref[...] = jnp.zeros_like(out_ref)
    for b in range(blocks):
        used_ref[b] = 0
        code_ref[b] = empty_code
        code_ref[blocks + b] = empty_code
    for t in range(tiles):
        b = block_ref[t]
        s = used_ref[b]
        used_ref[b] = s + 1
        slot_ref[t] = s
        code_ref[s * blocks + b] = row_ref[t]
        remapped = jnp.dot(flux_ref[t], weight_ref[t], preferred_element_type=f32)
        start = pl.multiple_of(s * fields, fields)
        out_ref[b, pl.ds(start, fields), :] = remapped.astype(bf16)
    line = line_iota((8, width))
    extra = jnp.where(line % 2 == 1, 8.0, 0.0).astype(f32)
    for b in range(blocks):
        first = code_ref[b].astype(f32)
        second = code_ref[blocks + b].astype(f32)
        code = jnp.where(line < 2, first, jnp.where(line < 4, second, float(empty_code))) + extra
        out_ref[b, 2 * fields : 2 * fields + 8, :] = code.astype(bf16)


def rows_kernel(x_ref, mask_ref, top_ref, bottom_ref):
    planes, rows, width = x_ref.shape
    mask = mask_ref[...].astype(f32)
    for i in range(2):
        for out_ref, r in ((top_ref, i), (bottom_ref, rows - 2 + i)):
            out_ref[i, 0:planes, :] = x_ref[:, r, :]
            out_ref[i, planes : planes + 8, :] = jnp.broadcast_to(mask[r : r + 1, :], (8, width))


def columns_kernel(x_ref, mask_ref, before_ref, after_ref, slab_ref, first_ref, last_ref):
    planes, rows, width = x_ref.shape
    mask = mask_ref[...].astype(f32)
    for i in range(2):
        slab_ref[i] = before_ref[i]
        slab_ref[rows + 2 + i] = after_ref[i]
    for r in range(rows):
        slab_ref[r + 2, 0:planes, :] = x_ref[:, r, :]
        slab_ref[r + 2, planes : planes + 8, :] = jnp.broadcast_to(mask[r : r + 1, :], (8, width))
    lane = lane_iota((planes + 8, width))
    first = jnp.zeros((planes + 8, width), f32)
    last = jnp.zeros((planes + 8, width), f32)
    for r in range(rows + 4):
        here = (lane == 2 * r) | (lane == 2 * r + 1)
        slab = slab_ref[r]
        first = jnp.where(here, pltpu.roll(slab, 2 * r, 1) if r else slab, first)
        last = jnp.where(here, pltpu.roll(slab, 2 * r + 2, 1), last)
    first_ref[...] = first
    last_ref[...] = last


def spread(weight, planes):
    return jnp.broadcast_to(weight[None], (planes // 8, 8, weight.shape[-1])).reshape(planes, -1)


def weights_of(inside, neighbours):
    pairs = [diffusion_rate * inside * n for n in neighbours]
    return [inside - (pairs[0] + pairs[1] + pairs[2] + pairs[3])] + pairs


def combine(weights, values, planes):
    total = spread(weights[0], planes) * values[0]
    for w, v in zip(weights[1:], values[1:]):
        total = total + spread(w, planes) * v
    return total


def stencil_kernel(
    slab_ref, first_ref, last_ref, left_ref, right_ref, mixing_ref,
    twice_ref, once_top_ref, twice_top_ref, weights_ref, work_ref,
):
    rows = slab_ref.shape[0] - 4
    planes = slab_ref.shape[1] - 8
    width = slab_ref.shape[2]
    levels = planes // 2
    lane = lane_iota((planes + 8, width))
    at_start = lane == 0
    at_end = lane == width - 1

    def beside(center, left_value, right_value):
        size = center.shape[0]
        left = jnp.where(at_start[:size], left_value, pltpu.roll(center, 1, 1))
        right = jnp.where(at_end[:size], right_value, pltpu.roll(center, width - 1, 1))
        return left, right

    left_all, right_all = left_ref[...], right_ref[...]

    def edge(own, outer_shift, beyond):
        around = (
            pltpu.roll(own, 2, 1),
            pltpu.roll(own, width - 2, 1),
            pltpu.roll(own, outer_shift, 1),
            beyond,
        )
        w = weights_of(own[planes:], [a[planes:] for a in around])
        return combine(w, [own[:planes]] + [a[:planes] for a in around], planes)

    left_once = edge(left_all, 1, pltpu.roll(first_ref[...], 1, 1))
    right_once = edge(right_all, width - 1, pltpu.roll(last_ref[...], width - 1, 1))

    saved = []
    for r in range(1, rows + 3):
        center = slab_ref[r]
        left, right = beside(
            center,
            pltpu.roll(left_all, width - (2 * r + 1), 1),
            pltpu.roll(right_all, (width - 1 - 2 * r) % width, 1),
        )
        around = (slab_ref[r - 1], slab_ref[r + 1], left, right)
        w = weights_of(center[planes:], [a[planes:] for a in around])
        saved.append(w)
        work_ref[r] = combine(w, [center[:planes]] + [a[:planes] for a in around], planes)

    mixing = mixing_ref[...]
    top_rows = mixing[0:8, :]
    chosen = jnp.where(line_iota((8, width)) == 0, 1.0, 0.0).astype(f32)
    over_first = (((0,), (0,)), ((), ()))
    once_column = lax.dot_general(top_rows, chosen, over_first, precision=exact, preferred_element_type=f32)
    top_twice = jnp.dot(top_rows, mixing, precision=exact, preferred_element_type=f32)
    twice_column = lax.dot_general(top_twice, chosen, over_first, precision=exact, preferred_element_type=f32)

    for r in range(2, rows + 2):
        center = work_ref[r]
        left, right = beside(
            center,
            pltpu.roll(left_once, width - (2 * r + 1), 1),
            pltpu.roll(right_once, (width - 1 - 2 * r) % width, 1),
        )
        w = saved[r - 1]
        result = combine(w, [center, work_ref[r - 1], work_ref[r + 1], left, right], planes)
        i = r - 2
        for n in range(5):
            weights_ref[n, i : i + 1, :] = w[n][0:1, :]
        for k in range(2):
            part = result[k * levels : (k + 1) * levels]
            twice_ref[k, i] = part
            twice_top_ref[k, i : i + 1, :] = jnp.sum(twice_column * part, axis=0, keepdims=True)
            before = center[k * levels : (k + 1) * levels]
            once_top_ref[k, i : i + 1, :] = jnp.sum(once_column * before, axis=0, keepdims=True)


def drive_kernel(received_ref, top_ref, mask_ref, wet_ref, sum_ref, rate_ref, first_ref):
    devices, lines, width = received_ref.shape
    rows = mask_ref.shape[0]
    fields = (lines - 8) // 2
    totals = [jnp.zeros((fields, width), f32) for _ in range(rows)]
    for d in range(devices):
        codes = received_ref[d, 2 * fields : 2 * fields + 8, :].astype(f32)
        for s in range(2):
            value = received_ref[d, s * fields : (s + 1) * fields, :].astype(f32)
            code = jnp.broadcast_to(codes[2 * s : 2 * s + 1, :], (fields, width))
            for r in range(rows):
                totals[r] = totals[r] + jnp.where(code == float(r), value, 0.0)
    mask = mask_ref[...].astype(f32)
    wet = wet_ref[...]
    half = fields // 2
    even = line_iota((half, width)) % 2 == 0
    for k in range(2):
        sums, rates = [], []
        for r in range(rows):
            part = totals[r][k * half : (k + 1) * half]
            following = pltpu.roll(part, half - 1, 0)
            sums.append(jnp.sum(jnp.where(even, part * following, 0.0), axis=0, keepdims=True))
            rates.append(jnp.sum(jnp.where(even, part, 0.0), axis=0, keepdims=True))
        drive_sum = jnp.concatenate(sums, axis=0) / wet
        drive_rate = jnp.concatenate(rates, axis=0) / wet
        sum_ref[k] = drive_sum
        rate_ref[k] = drive_rate
        first_ref[k] = mask * (forcing_step * (drive_sum - drive_rate * top_ref[k]))


def surface_kernel(
    mixing_ref, received_ref, first_ref, before_ref, after_ref, left_ref, right_ref,
    once_top_ref, twice_top_ref, weights_ref, sum_ref, rate_ref, mask_ref,
    spread_ref, second_ref, back_ref,
):
    devices, lines, width = received_ref.shape
    rows = mask_ref.shape[0]
    mask = mask_ref[...].astype(f32)
    once = mixing_ref[0:1, :]
    mixing_00 = mixing_ref[0:1, 0:1]
    column = mixing_ref[...]
    row_squared = jnp.dot(mixing_ref[0:8, :], column, precision=exact, preferred_element_type=f32)
    twice_00 = row_squared[0:1, 0:1]
    line = line_iota((rows, width))
    lane = lane_iota((rows, width))
    surfaces = []
    for k in range(2):
        own = first_ref[k]
        up = pltpu.roll(jnp.where(line == rows - 1, before_ref[k], own), 1, 0)
        down = pltpu.roll(jnp.where(line == 0, after_ref[k], own), rows - 1, 0)
        left = pltpu.roll(jnp.where(lane == width - 1, left_ref[k], own), 1, 1)
        right = pltpu.roll(jnp.where(lane == 0, right_ref[k], own), width - 1, 1)
        moved = (
            weights_ref[0] * own + weights_ref[1] * up + weights_ref[2] * down
            + weights_ref[3] * left + weights_ref[4] * right
        )
        once_top = once_top_ref[k] + mixing_00 * own
        second = mask * (forcing_step * (sum_ref[k] - rate_ref[k] * once_top))
        spread_ref[k] = moved
        second_ref[k] = second
        surfaces.append(twice_top_ref[k] + twice_00 * moved + mixing_00 * second)
    surface = jnp.concatenate(surfaces + [jnp.zeros((width - 2 * rows, width), f32)], axis=0).astype(bf16)
    codes = received_ref[:, lines - 8 : lines, :].astype(f32)
    wanted = (codes == lane_iota(codes.shape).astype(f32)).astype(f32).reshape(devices * 8, width).astype(bf16)
    picked = jnp.dot(wanted, surface, preferred_element_type=f32)
    back_ref[...] = picked.reshape(devices, 8, width).astype(bf16)


def ocean_kernel(mixing_ref, twice_ref, spread_ref, second_ref, out_ref):
    levels = mixing_ref.shape[0]
    rows, width = spread_ref.shape[1:]
    mixing = mixing_ref[...]
    squared = jnp.dot(mixing, mixing, precision=exact, preferred_element_type=f32)
    once = jnp.broadcast_to(mixing[:, 0:1], (levels, width))
    twice = jnp.broadcast_to(squared[:, 0:1], (levels, width))
    for k in range(2):
        for r in range(rows):
            free = jnp.dot(squared, twice_ref[k, r], precision=exact, preferred_element_type=f32)
            forced = twice * spread_ref[k, r : r + 1, :] + once * second_ref[k, r : r + 1, :]
            out_ref[k, :, r, :] = free + forced


def backward_kernel(block_ref, slot_ref, returned_ref, weight_ref, out_ref):
    tiles, width, _ = weight_ref.shape
    line = line_iota((8, width))
    for t in range(tiles):
        values = returned_ref[block_ref[t]].astype(f32)
        values = jnp.where(line == 4, 1.0, values).astype(bf16)
        mapped = lax.dot_general(
            values, weight_ref[t], (((1,), (1,)), ((), ())), preferred_element_type=f32
        )
        numerator = jnp.where(slot_ref[t] == 0, mapped[0:2], mapped[2:4])
        out_ref[t] = numerator / mapped[4:5]


def per_device(
    atm_flux, remap_weights, dest_block, dest_row, ocean_state, land_mask, wet_fraction, mixing
):
    blocks = lax.axis_size("blk")
    sections = lax.axis_size("sec")
    rows, width = land_mask.shape
    tiles, fields = atm_flux.shape[1:3]
    tracers, levels = ocean_state.shape[:2]
    planes = tracers * levels
    weights = remap_weights[0]
    block = dest_block.reshape(tiles)
    row = dest_row.reshape(tiles)
    state = ocean_state.reshape(planes, rows, width)
    up_sec = [(i, i + 1) for i in range(sections - 1)]
    down_sec = [(i + 1, i) for i in range(sections - 1)]
    up_blk = [(i, i + 1) for i in range(blocks - 1)]
    down_blk = [(i + 1, i) for i in range(blocks - 1)]

    packed, slot = call(
        forward_kernel, "forward",
        (shape(blocks, 2 * fields + 8, width, dtype=bf16), shape(tiles, dtype=jnp.int32)),
        [smem, smem, vmem, vmem], [vmem, smem],
        [pltpu.SMEM((blocks,), jnp.int32), pltpu.SMEM((2 * blocks,), jnp.int32)],
        flops=2 * tiles * fields * width * width, moved=3 << 20,
    )(block, row, atm_flux[0], weights)
    received = lax.all_to_all(packed, "blk", split_axis=0, concat_axis=0, tiled=True)

    top, bottom = call(
        rows_kernel, "rows", (shape(2, planes + 8, width),) * 2, [vmem, vmem], moved=1 << 20
    )(state, land_mask)
    before = lax.ppermute(bottom, "sec", up_sec)
    after = lax.ppermute(top, "sec", down_sec)
    slab, first_columns, last_columns = call(
        columns_kernel, "columns",
        (shape(rows + 4, planes + 8, width), shape(planes + 8, width), shape(planes + 8, width)),
        [vmem] * 4, moved=2 << 20,
    )(state, land_mask, before, after)
    left = lax.ppermute(last_columns, "blk", up_blk)
    right = lax.ppermute(first_columns, "blk", down_blk)
    twice, once_top, twice_top, step_weights = call(
        stencil_kernel, "stencil",
        (
            shape(tracers, rows, levels, width), shape(tracers, rows, width),
            shape(tracers, rows, width), shape(5, rows, width),
        ),
        [vmem] * 6, scratch=[pltpu.VMEM((rows + 4, planes, width), f32)], flops=20 << 20, moved=3 << 20,
    )(slab, first_columns, last_columns, left, right, mixing)

    drive_sum, drive_rate, first = call(
        drive_kernel, "drive", (shape(tracers, rows, width),) * 3, [vmem] * 4, moved=1 << 20
    )(received, ocean_state[:, 0], land_mask, wet_fraction)
    first_before = lax.ppermute(first, "sec", up_sec)
    first_after = lax.ppermute(first, "sec", down_sec)
    first_left = lax.ppermute(first, "blk", up_blk)
    first_right = lax.ppermute(first, "blk", down_blk)
    spread_first, second, back = call(
        surface_kernel, "surface",
        (shape(tracers, rows, width), shape(tracers, rows, width), shape(blocks, 8, width, dtype=bf16)),
        [vmem] * 13, moved=1 << 20,
    )(
        mixing, received, first, first_before, first_after, first_left, first_right,
        once_top, twice_top, step_weights, drive_sum, drive_rate, land_mask,
    )
    returned = lax.all_to_all(back, "blk", split_axis=0, concat_axis=0, tiled=True)
    ocean = call(
        ocean_kernel, "ocean", shape(tracers, levels, rows, width), [vmem] * 4,
        flops=12 * planes * levels * rows * width, moved=2 << 20,
    )(mixing, twice, spread_first, second)
    atmosphere = call(
        backward_kernel, "backward", shape(tiles, tracers, width), [smem, smem, vmem, vmem],
        flops=16 * tiles * width * width, moved=3 << 20,
    )(block, slot, returned, weights)
    return (ocean, atmosphere[None])


def solution(mesh):
    placed = (
        P("sec", "blk", None, None),
        P("sec", "blk", None, None),
        P("sec", "blk", None),
        P("sec", "blk"),
        P(None, None, "sec", "blk"),
        P("sec", "blk"),
        P("sec", "blk"),
        P(),
    )
    return jax.shard_map(
        per_device,
        mesh=mesh,
        in_specs=placed,
        out_specs=(P(None, None, "sec", "blk"), P("sec", "blk", None, None)),
        check_vma=False,
    )
```

time: 171 us -> 92.9 us (0.54)
  the two profiles are of different devices: /device:TPU:1 before, /device:TPU:129 now
where the time goes in v1:
time: 92.9 us; the launch traced here: 92.2 us
  starting transfers between devices  48.3 us (52%)
  Pallas kernels  23.4 us (25%)
  waiting for transfers between devices  15 us (16%)
  local copies, waits for them, and re-layouts  4.68 us (5%)
    all_to_all x1, starting transfers between devices, per_device(): lax.all_to_all(back, 'blk', split_axis=0, concat_axis=0, tiled=True)  12.8 us
    all_to_all x1, starting transfers between devices, per_device(): lax.all_to_all(packed, 'blk', split_axis=0, concat_axis=0, tiled=True)  10.8 us
    all_to_all x1, waiting for transfers between devices, per_device(): lax.all_to_all(back, 'blk', split_axis=0, concat_axis=0, tiled=True)  7.43 us
    ppermute x1, waiting for transfers between devices, per_device(): after = lax.ppermute(top, 'sec', down_sec)  5.85 us
    ppermute x1, starting transfers between devices, per_device(): first_before = lax.ppermute(first, 'sec', up_sec)  4.56 us
    ppermute x1, starting transfers between devices, per_device(): left = lax.ppermute(last_columns, 'blk', up_blk)  4.46 us
    pallas_call x1, Pallas kernels, per_device(): call(stencil_kernel, 'stencil', (shape(tracers, rows, levels, width), sha...  4.16 us
    ppermute x1, starting transfers between devices, per_device(): before = lax.ppermute(bottom, 'sec', up_sec)  3.99 us
  transfers between devices with their start and end apart: 10, of which 3 were waited for; matrix products, arithmetic and copies ran while one was open for 1% of the time, Pallas kernels for 16%

profile of v1, /device:TPU:129, one launch (start us, length us, event | category | flops | bytes accessed | tf_op | source)
XLA Modules:
  0.0 92.2 jit_solution(235244310222384354)
XLA Ops:
  0.6 3.4 %forward.1 = (bf16[64,40,128]{2,1,0:T(8,128)(2,1)}, s32[64]{0:T(128)}) custom-call(s32[64]{0:T(128)} %bitcast.16, s32[64]{0:T(128)} %bitcast.18, bf16[64,16,128]{2,1,0:T(8,128)(2,1)} %bitcast.14, bf16[64,128,128]{2,1,0:T(8,128)(2,1)} %bitcast.10), custom_call_target="tpu_custom_call" | custom-call | flops 33554432 | bytes 3145728 | tf_op jit(solution)/shard_map/forward/pallas_call | solution.py:306
  4.0 10.8 %all-to-all-start = ((bf16[64,40,128]{2,1,0:T(8,128)(2,1)}), bf16[64,40,128]{2,1,0:T(8,128)(2,1)S(1)}, u32[]{:S(2)}, u32[]{:S(2)}) async-start(bf16[64,40,128]{2,1,0:T(8,128)(2,1)} %get-tuple-element.25), calls=%async_computation | async-start | bytes 1310720 | tf_op jit(solution)/shard_map/all_to_all | solution.py:313
  14.8 2.0 %rows.1 = (f32[2,168,128]{2,1,0:T(8,128)}, f32[2,168,128]{2,1,0:T(8,128)}) custom-call(f32[160,8,128]{2,1,0:T(8,128)} %bitcast.12, s32[8,128]{1,0:T(8,128)} %mask_ref.7), custom_call_target="tpu_custom_call" | custom-call | bytes 1048576 | tf_op jit(solution)/shard_map/rows/pallas_call | solution.py:315
  16.8 4.0 %collective-permute-start = (f32[2,168,128]{2,1,0:T(8,128)}, f32[2,168,128]{2,1,0:T(8,128)S(1)}, u32[]{:S(2)}, u32[]{:S(2)}) collective-permute-start(f32[2,168,128]{2,1,0:T(8,128)} %get-tuple-element.19), channel_id=1, source_target_pairs={{0,64},{64,128},{128,192},{192,256},{256,320},{320,384},{384,448},... | collective-permute-start | bytes 516104 | tf_op jit(solution)/shard_map/ppermute | solution.py:318
  20.8 1.9 %collective-permute-start.1 = (f32[2,168,128]{2,1,0:T(8,128)}, f32[2,168,128]{2,1,0:T(8,128)S(1)}, u32[]{:S(2)}, u32[]{:S(2)}) collective-permute-start(f32[2,168,128]{2,1,0:T(8,128)} %get-tuple-element.20), channel_id=1, source_target_pairs={{64,0},{128,64},{192,128},{256,192},{320,256},{384,320},{448,384},... | collective-permute-start | bytes 516104 | tf_op jit(solution)/shard_map/ppermute | solution.py:319
  22.7 1.7 %collective-permute-done.before_ref = f32[2,168,128]{2,1,0:T(8,128)S(1)} collective-permute-done((f32[2,168,128]{2,1,0:T(8,128)}, f32[2,168,128]{2,1,0:T(8,128)S(1)}, u32[]{:S(2)}, u32[]{:S(2)}) %collective-permute-start) | collective-permute-done | bytes 172064 | tf_op jit(solution)/shard_map/ppermute | solution.py:318
  24.4 0.0 copy-start.2
  24.4 5.9 %collective-permute-done.1.after_ref = f32[2,168,128]{2,1,0:T(8,128)S(1)} collective-permute-done((f32[2,168,128]{2,1,0:T(8,128)}, f32[2,168,128]{2,1,0:T(8,128)S(1)}, u32[]{:S(2)}, u32[]{:S(2)}) %collective-permute-start.1) | collective-permute-done | bytes 172064 | tf_op jit(solution)/shard_map/ppermute | solution.py:319
  30.3 0.0 copy-done.2
  30.3 0.0 copy-start.3
  30.3 0.7 copy-done.3
  30.9 2.7 %columns.1 = (f32[12,168,128]{2,1,0:T(8,128)}, f32[168,128]{1,0:T(8,128)}, f32[168,128]{1,0:T(8,128)}) custom-call(f32[160,8,128]{2,1,0:T(8,128)} %bitcast.13, s32[8,128]{1,0:T(8,128)} %mask_ref.7, f32[2,168,128]{2,1,0:T(8,128)} %copy-done.2, f32[2,168,128]{2,1,0:T(8,128)} %copy-done.3), custom_call_target="tpu_custom_call" | custom-call | bytes 2097152 | tf_op jit(solution)/shard_map/columns/pallas_call | solution.py:320
  33.6 4.5 %collective-permute-start.2 = (f32[168,128]{1,0:T(8,128)}, f32[168,128]{1,0:T(8,128)S(1)}, u32[]{:S(2)}, u32[]{:S(2)}) collective-permute-start(f32[168,128]{1,0:T(8,128)} %get-tuple-element.23.last_ref), channel_id=1, source_target_pairs={{0,1},{1,2},{2,3},{3,4},{4,5},{5,6},{6,7},{7,8},{8,9},{9,10},{10,1... | collective-permute-start | bytes 258056 | tf_op jit(solution)/shard_map/ppermute | solution.py:325
  38.1 1.9 %collective-permute-start.3 = (f32[168,128]{1,0:T(8,128)}, f32[168,128]{1,0:T(8,128)S(1)}, u32[]{:S(2)}, u32[]{:S(2)}) collective-permute-start(f32[168,128]{1,0:T(8,128)} %get-tuple-element.22.first_ref), channel_id=1, source_target_pairs={{1,0},{2,1},{3,2},{4,3},{5,4},{6,5},{7,6},{8,7},{9,8},{10,9},{11,1... | collective-permute-start | bytes 258056 | tf_op jit(solution)/shard_map/ppermute | solution.py:326
  40.0 1.3 %slice_bitcast_fusion.top_ref = f32[2,8,128]{2,1,0:T(8,128)} fusion(f32[2,80,8,128]{3,2,1,0:T(8,128)} %param.12), kind=kLoop, calls=%fused_computation | loop fusion | bytes 16384 | tf_op jit(solution)/shard_map/squeeze | solution.py:338
  41.3 0.0 all-to-all-done.received_ref
  41.3 0.0 copy-start
  41.3 0.8 copy-done
  42.2 2.6 %drive.1 = (f32[2,8,128]{2,1,0:T(8,128)}, f32[2,8,128]{2,1,0:T(8,128)}, f32[2,8,128]{2,1,0:T(8,128)}) custom-call(bf16[64,40,128]{2,1,0:T(8,128)(2,1)} %copy-done, f32[2,8,128]{2,1,0:T(8,128)} %slice_bitcast_fusion.top_ref, s32[8,128]{1,0:T(8,128)} %mask_ref.7, f32[8,128]{1,0:T(8,128)} %wet_ref.1), custom_call_target="tpu_custom_call" | custom-call | bytes 1048576 | tf_op jit(solution)/shard_map/drive/pallas_call | solution.py:336
  44.8 4.6 %collective-permute-start.4 = (f32[2,8,128]{2,1,0:T(8,128)}, f32[2,8,128]{2,1,0:T(8,128)S(1)}, u32[]{:S(2)}, u32[]{:S(2)}) collective-permute-start(f32[2,8,128]{2,1,0:T(8,128)} %get-tuple-element.26.first_ref), channel_id=1, source_target_pairs={{0,64},{64,128},{128,192},{192,256},{256,320},{320,384},{384,448},... | collective-permute-start | bytes 24584 | tf_op jit(solution)/shard_map/ppermute | solution.py:339
  49.4 1.9 %collective-permute-start.5 = (f32[2,8,128]{2,1,0:T(8,128)}, f32[2,8,128]{2,1,0:T(8,128)S(1)}, u32[]{:S(2)}, u32[]{:S(2)}) collective-permute-start(f32[2,8,128]{2,1,0:T(8,128)} %get-tuple-element.26.first_ref), channel_id=1, source_target_pairs={{64,0},{128,64},{192,128},{256,192},{320,256},{384,320},{448,384},... | collective-permute-start | bytes 24584 | tf_op jit(solution)/shard_map/ppermute | solution.py:340
  51.3 3.9 %collective-permute-start.6 = (f32[2,8,128]{2,1,0:T(8,128)}, f32[2,8,128]{2,1,0:T(8,128)S(1)}, u32[]{:S(2)}, u32[]{:S(2)}) collective-permute-start(f32[2,8,128]{2,1,0:T(8,128)} %get-tuple-element.26.first_ref), channel_id=1, source_target_pairs={{0,1},{1,2},{2,3},{3,4},{4,5},{5,6},{6,7},{7,8},{8,9},{9,10},{10,1... | collective-permute-start | bytes 24584 | tf_op jit(solution)/shard_map/ppermute | solution.py:341
  55.2 0.0 collective-permute-done.2.left_ref
  55.2 0.0 copy-start.4
  55.2 1.9 %collective-permute-start.7 = (f32[2,8,128]{2,1,0:T(8,128)}, f32[2,8,128]{2,1,0:T(8,128)S(1)}, u32[]{:S(2)}, u32[]{:S(2)}) collective-permute-start(f32[2,8,128]{2,1,0:T(8,128)} %get-tuple-element.26.first_ref), channel_id=1, source_target_pairs={{1,0},{2,1},{3,2},{4,3},{5,4},{6,5},{7,6},{8,7},{9,8},{10,9},{11,1... | collective-permute-start | bytes 24584 | tf_op jit(solution)/shard_map/ppermute | solution.py:342
  57.2 0.0 collective-permute-done.3.right_ref
  57.2 0.0 copy-start.5
  57.2 0.0 copy-done.4
  57.2 0.6 copy-done.5
  57.8 4.2 %stencil.1 = (f32[2,8,80,128]{3,2,1,0:T(8,128)}, f32[2,8,128]{2,1,0:T(8,128)}, f32[2,8,128]{2,1,0:T(8,128)}, f32[5,8,128]{2,1,0:T(8,128)}) custom-call(f32[12,168,128]{2,1,0:T(8,128)} %get-tuple-element.21.slab_ref, f32[168,128]{1,0:T(8,128)} %get-tuple-element.22.first_ref, f32[168,128]{1,0:T(8,128)} %get-tuple-element.23.last_ref, f32[168,128]{1,0:T(8,128)} %copy-done.4, ...), custom_call_target="tpu_custom_call" | custom-call | flops 20971520 | bytes 3145728 | tf_op jit(solution)/shard_map/stencil/pallas_call | solution.py:327
  62.0 0.0 collective-permute-done.4.before_ref
  62.0 0.0 copy-start.6
  62.0 0.0 collective-permute-done.5.after_ref
  62.0 0.0 copy-start.7
  62.0 0.0 collective-permute-done.6.left_ref
  62.0 0.0 copy-start.8
  62.0 0.0 collective-permute-done.7.right_ref
  62.0 0.0 copy-start.9
  62.0 0.5 copy-done.6
  62.6 0.0 copy-done.7
  62.6 0.0 copy-done.8
  62.6 0.0 copy-done.9
  62.6 2.2 %surface.1 = (f32[2,8,128]{2,1,0:T(8,128)}, f32[2,8,128]{2,1,0:T(8,128)}, bf16[64,8,128]{2,1,0:T(8,128)(2,1)}) custom-call(f32[80,80]{1,0:T(8,128)} %mixing_ref.5, bf16[64,40,128]{2,1,0:T(8,128)(2,1)} %copy-done, f32[2,8,128]{2,1,0:T(8,128)} %get-tuple-element.26.first_ref, f32[2,8,128]{2,1,0:T(8,128)} %copy-done.6, f32[2,8,128]{2,1,0:T(8,128)} %copy-done.7, ...), custom_call_target="tpu_custom_call" | custom-call | bytes 1048576 | tf_op jit(solution)/shard_map/surface/pallas_call | solution.py:343
  64.8 12.8 %all-to-all-start.1 = ((bf16[64,8,128]{2,1,0:T(8,128)(2,1)}), bf16[64,8,128]{2,1,0:T(8,128)(2,1)S(1)}, u32[]{:S(2)}, u32[]{:S(2)}) async-start(bf16[64,8,128]{2,1,0:T(8,128)(2,1)} %get-tuple-element.35), calls=%async_computation.1 | async-start | bytes 262144 | tf_op jit(solution)/shard_map/all_to_all | solution.py:351
  77.6 2.9 %ocean.1 = f32[2,80,8,128]{3,2,1,0:T(8,128)} custom-call(f32[80,80]{1,0:T(8,128)} %mixing_ref.5, f32[2,8,80,128]{3,2,1,0:T(8,128)} %get-tuple-element.24.twice_ref, f32[2,8,128]{2,1,0:T(8,128)} %get-tuple-element.32.spread_ref, f32[2,8,128]{2,1,0:T(8,128)} %get-tuple-element.33.second_ref), custom_call_target="tpu_custom_call" | custom-call | flops 157286400 | bytes 2097152 | tf_op jit(solution)/shard_map/ocean/pallas_call | solution.py:352
  80.6 7.4 %all-to-all-done.1.returned_ref = bf16[64,8,128]{2,1,0:T(8,128)(2,1)S(1)} async-done(((bf16[64,8,128]{2,1,0:T(8,128)(2,1)}), bf16[64,8,128]{2,1,0:T(8,128)(2,1)S(1)}, u32[]{:S(2)}, u32[]{:S(2)}) %all-to-all-start.1) | async-done | bytes 131104 | tf_op jit(solution)/shard_map/all_to_all | solution.py:351
  88.0 0.0 copy-start.1
  88.0 0.6 copy-done.1
  88.6 3.5 %backward.1 = f32[64,2,128]{2,1,0:T(2,128)} custom-call(s32[64]{0:T(128)} %bitcast.17, s32[64]{0:T(128)} %get-tuple-element.34.slot_ref, bf16[64,8,128]{2,1,0:T(8,128)(2,1)} %copy-done.1, bf16[64,128,128]{2,1,0:T(8,128)(2,1)} %bitcast.11), custom_call_target="tpu_custom_call" | custom-call | flops 16777216 | bytes 3145728 | tf_op jit(solution)/shard_map/backward/pallas_call | solution.py:356
Async XLA Ops:
  4.0 37.3 %all-to-all-start = ((bf16[64,40,128]{2,1,0:T(8,128)(2,1)}), bf16[64,40,128]{2,1,0:T(8,128)(2,1)S(1)}, u32[]{:S(2)}, u32[]{:S(2)}) async-start(bf16[64,40,128]{2,1,0:T(8,128)(2,1)} %get-tuple-element.25), calls=%async_computation | async-start | bytes 1310720 | tf_op jit(solution)/shard_map/all_to_all | solution.py:313
  16.8 7.6 %collective-permute-start = (f32[2,168,128]{2,1,0:T(8,128)}, f32[2,168,128]{2,1,0:T(8,128)S(1)}, u32[]{:S(2)}, u32[]{:S(2)}) collective-permute-start(f32[2,168,128]{2,1,0:T(8,128)} %get-tuple-element.19), channel_id=1, source_target_pairs={{0,64},{64,128},{128,192},{192,256},{256,320},{320,384},{384,448},... | collective-permute-start | bytes 516104 | tf_op jit(solution)/shard_map/ppermute | solution.py:318
  20.8 9.4 %collective-permute-start.1 = (f32[2,168,128]{2,1,0:T(8,128)}, f32[2,168,128]{2,1,0:T(8,128)S(1)}, u32[]{:S(2)}, u32[]{:S(2)}) collective-permute-start(f32[2,168,128]{2,1,0:T(8,128)} %get-tuple-element.20), channel_id=1, source_target_pairs={{64,0},{128,64},{192,128},{256,192},{320,256},{384,320},{448,384},... | collective-permute-start | bytes 516104 | tf_op jit(solution)/shard_map/ppermute | solution.py:319
  24.4 5.9 %copy-start.2 = (f32[2,168,128]{2,1,0:T(8,128)}, f32[2,168,128]{2,1,0:T(8,128)S(1)}, u32[]{:S(2)}) copy-start(f32[2,168,128]{2,1,0:T(8,128)S(1)} %collective-permute-done.before_ref) | copy-start | bytes 516100
  30.3 0.7 copy-start.3
  33.6 21.6 %collective-permute-start.2 = (f32[168,128]{1,0:T(8,128)}, f32[168,128]{1,0:T(8,128)S(1)}, u32[]{:S(2)}, u32[]{:S(2)}) collective-permute-start(f32[168,128]{1,0:T(8,128)} %get-tuple-element.23.last_ref), channel_id=1, source_target_pairs={{0,1},{1,2},{2,3},{3,4},{4,5},{5,6},{6,7},{7,8},{8,9},{9,10},{10,1... | collective-permute-start | bytes 258056 | tf_op jit(solution)/shard_map/ppermute | solution.py:325
  38.1 19.1 %collective-permute-start.3 = (f32[168,128]{1,0:T(8,128)}, f32[168,128]{1,0:T(8,128)S(1)}, u32[]{:S(2)}, u32[]{:S(2)}) collective-permute-start(f32[168,128]{1,0:T(8,128)} %get-tuple-element.22.first_ref), channel_id=1, source_target_pairs={{1,0},{2,1},{3,2},{4,3},{5,4},{6,5},{7,6},{8,7},{9,8},{10,9},{11,1... | collective-permute-start | bytes 258056 | tf_op jit(solution)/shard_map/ppermute | solution.py:326
  41.3 0.8 copy-start
  44.8 17.2 %collective-permute-start.4 = (f32[2,8,128]{2,1,0:T(8,128)}, f32[2,8,128]{2,1,0:T(8,128)S(1)}, u32[]{:S(2)}, u32[]{:S(2)}) collective-permute-start(f32[2,8,128]{2,1,0:T(8,128)} %get-tuple-element.26.first_ref), channel_id=1, source_target_pairs={{0,64},{64,128},{128,192},{192,256},{256,320},{320,384},{384,448},... | collective-permute-start | bytes 24584 | tf_op jit(solution)/shard_map/ppermute | solution.py:339
  49.4 12.6 %collective-permute-start.5 = (f32[2,8,128]{2,1,0:T(8,128)}, f32[2,8,128]{2,1,0:T(8,128)S(1)}, u32[]{:S(2)}, u32[]{:S(2)}) collective-permute-start(f32[2,8,128]{2,1,0:T(8,128)} %get-tuple-element.26.first_ref), channel_id=1, source_target_pairs={{64,0},{128,64},{192,128},{256,192},{320,256},{384,320},{448,384},... | collective-permute-start | bytes 24584 | tf_op jit(solution)/shard_map/ppermute | solution.py:340
  51.3 10.7 %collective-permute-start.6 = (f32[2,8,128]{2,1,0:T(8,128)}, f32[2,8,128]{2,1,0:T(8,128)S(1)}, u32[]{:S(2)}, u32[]{:S(2)}) collective-permute-start(f32[2,8,128]{2,1,0:T(8,128)} %get-tuple-element.26.first_ref), channel_id=1, source_target_pairs={{0,1},{1,2},{2,3},{3,4},{4,5},{5,6},{6,7},{7,8},{8,9},{9,10},{10,1... | collective-permute-start | bytes 24584 | tf_op jit(solution)/shard_map/ppermute | solution.py:341
  55.2 2.0 %copy-start.4 = (f32[168,128]{1,0:T(8,128)}, f32[168,128]{1,0:T(8,128)S(1)}, u32[]{:S(2)}) copy-start(f32[168,128]{1,0:T(8,128)S(1)} %collective-permute-done.2.left_ref) | copy-start | bytes 258052
  55.2 6.8 %collective-permute-start.7 = (f32[2,8,128]{2,1,0:T(8,128)}, f32[2,8,128]{2,1,0:T(8,128)S(1)}, u32[]{:S(2)}, u32[]{:S(2)}) collective-permute-start(f32[2,8,128]{2,1,0:T(8,128)} %get-tuple-element.26.first_ref), channel_id=1, source_target_pairs={{1,0},{2,1},{3,2},{4,3},{5,4},{6,5},{7,6},{8,7},{9,8},{10,9},{11,1... | collective-permute-start | bytes 24584 | tf_op jit(solution)/shard_map/ppermute | solution.py:342
  57.2 0.6 copy-start.5
  62.0 0.6 copy-start.6
  62.0 0.6 copy-start.7
  62.0 0.6 copy-start.8
  62.0 0.6 copy-start.9
  64.8 23.2 %all-to-all-start.1 = ((bf16[64,8,128]{2,1,0:T(8,128)(2,1)}), bf16[64,8,128]{2,1,0:T(8,128)(2,1)S(1)}, u32[]{:S(2)}, u32[]{:S(2)}) async-start(bf16[64,8,128]{2,1,0:T(8,128)(2,1)} %get-tuple-element.35), calls=%async_computation.1 | async-start | bytes 262144 | tf_op jit(solution)/shard_map/all_to_all | solution.py:351
  88.0 0.6 copy-start.1

commit v2 on v1

--- a/solution.py
+++ b/solution.py
@@ -28,6 +28,7 @@
         in_specs=in_specs,
         out_specs=out_specs,
         scratch_shapes=list(scratch),
+        compiler_params=pltpu.CompilerParams(vmem_limit_bytes=16 << 20),
         cost_estimate=pl.CostEstimate(flops=flops, bytes_accessed=moved, transcendentals=0),
     )
 

time: 92.9 us -> 87.2 us (0.939)
  Pallas kernels: 23.4 us -> 10.7 us
  local copies, waits for them, and re-layouts: 4.68 us -> 10.6 us
    unnamed x20 -> x38, local copies, waits for them, and re-layouts: 3.38 us -> 10.6 us
    pallas_call x1, Pallas kernels: 4.16 us -> 2.06 us  [per_device(): call(stencil_kernel, 'stencil', (shape(tracers, rows, levels, width), sha...]
    pallas_call x1, Pallas kernels: 2.69 us -> 0.62 us  [per_device(): call(columns_kernel, 'columns', (shape(rows + 4, planes + 8, width), shap...]
    pallas_call x1, Pallas kernels: 1.99 us -> 0.18 us  [per_device(): call(rows_kernel, 'rows', (shape(2, planes + 8, width),) * 2, [vmem, vmem...]
    pallas_call x1, Pallas kernels: 2.15 us -> 0.41 us  [per_device(): call(surface_kernel, 'surface', (shape(tracers, rows, width), shape(trace...]
    pallas_call x1, Pallas kernels: 2.62 us -> 0.93 us  [per_device(): call(drive_kernel, 'drive', (shape(tracers, rows, width),) * 3, [vmem] *...]
    squeeze x1, local copies, waits for them, and re-layouts: 1.3 us -> 0.01 us  [per_device(): ocean_state[:, 0]]
    pallas_call x1, Pallas kernels: 3.37 us -> 2.22 us  [per_device(): call(forward_kernel, 'forward', (shape(blocks, 2 * fields + 8, width, dty...]
  transfers between devices with their start and end apart: 10 -> 10, of which waited for: 3 -> 3; matrix products, arithmetic and copies ran while one was open for 1% -> 0% of each run, Pallas kernels for 16% -> 7%
where the time goes in v2:
time: 87.2 us; the launch traced here: 86.5 us
  starting transfers between devices  48.4 us (56%)
  waiting for transfers between devices  15.8 us (18%)
  Pallas kernels  10.7 us (12%)
  local copies, waits for them, and re-layouts  10.6 us (12%)
  between operations  0.92 us (1%)
    all_to_all x1, starting transfers between devices, per_device(): lax.all_to_all(back, 'blk', split_axis=0, concat_axis=0, tiled=True)  12.8 us
    all_to_all x1, starting transfers between devices, per_device(): lax.all_to_all(packed, 'blk', split_axis=0, concat_axis=0, tiled=True)  10.8 us
    unnamed x38, local copies, waits for them, and re-layouts  10.6 us
    all_to_all x1, waiting for transfers between devices, per_device(): lax.all_to_all(back, 'blk', split_axis=0, concat_axis=0, tiled=True)  8.5 us
    ppermute x1, waiting for transfers between devices, per_device(): after = lax.ppermute(top, 'sec', down_sec)  5.86 us
    ppermute x1, starting transfers between devices, per_device(): first_before = lax.ppermute(first, 'sec', up_sec)  4.7 us
    ppermute x1, starting transfers between devices, per_device(): left = lax.ppermute(last_columns, 'blk', up_blk)  4.46 us
    ppermute x1, starting transfers between devices, per_device(): before = lax.ppermute(bottom, 'sec', up_sec)  4 us
  transfers between devices with their start and end apart: 10, of which 3 were waited for; matrix products, arithmetic and copies ran while one was open for 0% of the time, Pallas kernels for 7%

profile of v2, /device:TPU:129, one launch (start us, length us, event | category | flops | bytes accessed | tf_op | source)
XLA Modules:
  0.0 86.5 jit_solution(7049156274148238337)
XLA Ops:
  0.6 0.0 copy-start.14
  0.6 0.0 copy-start
  0.7 1.6 %copy-done = bf16[1,64,128,128]{3,2,1,0:T(8,128)(2,1)S(1)} copy-done((bf16[1,64,128,128]{3,2,1,0:T(8,128)(2,1)S(1)}, bf16[1,64,128,128]{3,2,1,0:T(8,128)(2,1)}, u32[]{:S(2)}) %copy-start) | copy-done | bytes 2097176
  2.2 0.0 copy-start.6
  2.2 0.9 %copy-done.6 = bf16[1,64,16,128]{3,2,1,0:T(8,128)(2,1)S(1)} copy-done((bf16[1,64,16,128]{3,2,1,0:T(8,128)(2,1)S(1)}, bf16[1,64,16,128]{3,2,1,0:T(8,128)(2,1)}, u32[]{:S(2)}) %copy-start.6) | copy-done | bytes 262168
  3.2 0.0 copy-start.16
  3.2 0.7 copy-done.16
  3.8 0.0 copy-start.18
  3.8 0.7 copy-done.18
  4.5 0.0 copy-start.2
  4.5 0.0 copy-start.15
  4.5 2.2 %forward.1 = (bf16[64,40,128]{2,1,0:T(8,128)(2,1)}, s32[64]{0:T(128)S(1)}) custom-call(s32[64]{0:T(128)S(1)} %bitcast.15, s32[64]{0:T(128)S(1)} %bitcast.17, bf16[64,16,128]{2,1,0:T(8,128)(2,1)S(1)} %bitcast.14, bf16[64,128,128]{2,1,0:T(8,128)(2,1)S(1)} %bitcast.10), custom_call_target="tpu_custom_call" | custom-call | flops 33554432 | bytes 3145728 | tf_op jit(solution)/shard_map/forward/pallas_call | solution.py:307
  6.7 0.0 copy-start.5
  6.7 10.8 %all-to-all-start = ((bf16[64,40,128]{2,1,0:T(8,128)(2,1)}), bf16[64,40,128]{2,1,0:T(8,128)(2,1)S(1)}, u32[]{:S(2)}, u32[]{:S(2)}) async-start(bf16[64,40,128]{2,1,0:T(8,128)(2,1)} %get-tuple-element.25), calls=%async_computation | async-start | bytes 1310720 | tf_op jit(solution)/shard_map/all_to_all | solution.py:314
  17.6 0.0 copy-done.14
  17.6 0.0 copy-done.2
  17.6 0.2 rows.1
  17.8 4.0 %collective-permute-start = (f32[2,168,128]{2,1,0:T(8,128)S(1)}, f32[2,168,128]{2,1,0:T(8,128)S(1)}, u32[]{:S(2)}, u32[]{:S(2)}) collective-permute-start(f32[2,168,128]{2,1,0:T(8,128)S(1)} %get-tuple-element.19), channel_id=1, source_target_pairs={{0,64},{64,128},{128,192},{192,256},{256,320},{320,384},{384,448},... | collective-permute-start | bytes 516104 | tf_op jit(solution)/shard_map/ppermute | solution.py:319
  21.8 1.9 %collective-permute-start.1 = (f32[2,168,128]{2,1,0:T(8,128)S(1)}, f32[2,168,128]{2,1,0:T(8,128)S(1)}, u32[]{:S(2)}, u32[]{:S(2)}) collective-permute-start(f32[2,168,128]{2,1,0:T(8,128)S(1)} %get-tuple-element.20), channel_id=1, source_target_pairs={{64,0},{128,64},{192,128},{256,192},{320,256},{384,320},{448,384},... | collective-permute-start | bytes 516104 | tf_op jit(solution)/shard_map/ppermute | solution.py:320
  23.7 1.5 %collective-permute-done.before_ref = f32[2,168,128]{2,1,0:T(8,128)S(1)} collective-permute-done((f32[2,168,128]{2,1,0:T(8,128)S(1)}, f32[2,168,128]{2,1,0:T(8,128)S(1)}, u32[]{:S(2)}, u32[]{:S(2)}) %collective-permute-start) | collective-permute-done | bytes 172064 | tf_op jit(solution)/shard_map/ppermute | solution.py:319
  25.1 5.9 %collective-permute-done.1.after_ref = f32[2,168,128]{2,1,0:T(8,128)S(1)} collective-permute-done((f32[2,168,128]{2,1,0:T(8,128)S(1)}, f32[2,168,128]{2,1,0:T(8,128)S(1)}, u32[]{:S(2)}, u32[]{:S(2)}) %collective-permute-start.1) | collective-permute-done | bytes 172064 | tf_op jit(solution)/shard_map/ppermute | solution.py:320
  31.0 0.6 columns.1
  31.6 0.0 copy-start.3
  31.6 1.0 %copy-done.3 = f32[12,168,128]{2,1,0:T(8,128)} copy-done((f32[12,168,128]{2,1,0:T(8,128)}, f32[12,168,128]{2,1,0:T(8,128)S(1)}, u32[]{:S(2)}) %copy-start.3) | copy-done | bytes 1032216
  32.6 4.5 %collective-permute-start.2 = (f32[168,128]{1,0:T(8,128)S(1)}, f32[168,128]{1,0:T(8,128)S(1)}, u32[]{:S(2)}, u32[]{:S(2)}) collective-permute-start(f32[168,128]{1,0:T(8,128)S(1)} %get-tuple-element.23.last_ref), channel_id=1, source_target_pairs={{0,1},{1,2},{2,3},{3,4},{4,5},{5,6},{6,7},{7,8},{8,9},{9,10},{10,1... | collective-permute-start | bytes 258056 | tf_op jit(solution)/shard_map/ppermute | solution.py:326
  37.1 1.9 %collective-permute-start.3 = (f32[168,128]{1,0:T(8,128)S(1)}, f32[168,128]{1,0:T(8,128)S(1)}, u32[]{:S(2)}, u32[]{:S(2)}) collective-permute-start(f32[168,128]{1,0:T(8,128)S(1)} %get-tuple-element.22.first_ref), channel_id=1, source_target_pairs={{1,0},{2,1},{3,2},{4,3},{5,4},{6,5},{7,6},{8,7},{9,8},{10,9},{11,1... | collective-permute-start | bytes 258056 | tf_op jit(solution)/shard_map/ppermute | solution.py:327
  39.0 0.0 all-to-all-done.received_ref
  39.0 0.0 copy-done.15
  39.0 0.0 copy-start.17
  39.1 0.9 %drive.1 = (f32[2,8,128]{2,1,0:T(8,128)S(1)}, f32[2,8,128]{2,1,0:T(8,128)S(1)}, f32[2,8,128]{2,1,0:T(8,128)S(1)}) custom-call(bf16[64,40,128]{2,1,0:T(8,128)(2,1)S(1)} %all-to-all-done.received_ref, f32[2,8,128]{2,1,0:T(8,128)S(1)} %slice_bitcast_fusion.top_ref, s32[8,128]{1,0:T(8,128)S(1)} %copy-done.14, f32[8,128]{1,0:T(8,128)S(1)} %copy-done.15), custom_call_target="tpu_custom_call" | custom-call | bytes 1048576 | tf_op jit(solution)/shard_map/drive/pallas_call | solution.py:337
  40.0 0.0 copy-start.1
  40.0 4.7 %collective-permute-start.4 = (f32[2,8,128]{2,1,0:T(8,128)S(1)}, f32[2,8,128]{2,1,0:T(8,128)S(1)}, u32[]{:S(2)}, u32[]{:S(2)}) collective-permute-start(f32[2,8,128]{2,1,0:T(8,128)S(1)} %get-tuple-element.26.first_ref), channel_id=1, source_target_pairs={{0,64},{64,128},{128,192},{192,256},{256,320},{320,384},{384,448},... | collective-permute-start | bytes 24584 | tf_op jit(solution)/shard_map/ppermute | solution.py:340
  44.7 1.9 %collective-permute-start.5 = (f32[2,8,128]{2,1,0:T(8,128)S(1)}, f32[2,8,128]{2,1,0:T(8,128)S(1)}, u32[]{:S(2)}, u32[]{:S(2)}) collective-permute-start(f32[2,8,128]{2,1,0:T(8,128)S(1)} %get-tuple-element.26.first_ref), channel_id=1, source_target_pairs={{64,0},{128,64},{192,128},{256,192},{320,256},{384,320},{448,384},... | collective-permute-start | bytes 24584 | tf_op jit(solution)/shard_map/ppermute | solution.py:341
  46.6 3.9 %collective-permute-start.6 = (f32[2,8,128]{2,1,0:T(8,128)S(1)}, f32[2,8,128]{2,1,0:T(8,128)S(1)}, u32[]{:S(2)}, u32[]{:S(2)}) collective-permute-start(f32[2,8,128]{2,1,0:T(8,128)S(1)} %get-tuple-element.26.first_ref), channel_id=1, source_target_pairs={{0,1},{1,2},{2,3},{3,4},{4,5},{5,6},{6,7},{7,8},{8,9},{9,10},{10,1... | collective-permute-start | bytes 24584 | tf_op jit(solution)/shard_map/ppermute | solution.py:342
  50.6 0.0 collective-permute-done.2.left_ref
  50.6 0.0 copy-start.10
  50.6 0.6 copy-done.10
  51.2 1.9 %collective-permute-start.7 = (f32[2,8,128]{2,1,0:T(8,128)S(1)}, f32[2,8,128]{2,1,0:T(8,128)S(1)}, u32[]{:S(2)}, u32[]{:S(2)}) collective-permute-start(f32[2,8,128]{2,1,0:T(8,128)S(1)} %get-tuple-element.26.first_ref), channel_id=1, source_target_pairs={{1,0},{2,1},{3,2},{4,3},{5,4},{6,5},{7,6},{8,7},{9,8},{10,9},{11,1... | collective-permute-start | bytes 24584 | tf_op jit(solution)/shard_map/ppermute | solution.py:343
  53.1 0.0 collective-permute-done.3.right_ref
  53.1 0.0 copy-done.8
  53.2 0.0 copy-start.12
  53.2 0.6 copy-done.12
  53.8 0.0 copy-done.5
  53.8 0.0 copy-start.4
  53.8 1.2 %copy-done.4 = f32[12,168,128]{2,1,0:T(8,128)S(1)} copy-done((f32[12,168,128]{2,1,0:T(8,128)S(1)}, f32[12,168,128]{2,1,0:T(8,128)}, u32[]{:S(2)}) %copy-start.4) | copy-done | bytes 1032216
  55.0 0.0 copy-start.9
  55.0 0.9 %copy-done.9 = f32[168,128]{1,0:T(8,128)S(1)} copy-done((f32[168,128]{1,0:T(8,128)S(1)}, f32[168,128]{1,0:T(8,128)}, u32[]{:S(2)}) %copy-start.9) | copy-done | bytes 86040
  55.9 0.0 copy-start.11
  55.9 0.9 %copy-done.11 = f32[168,128]{1,0:T(8,128)S(1)} copy-done((f32[168,128]{1,0:T(8,128)S(1)}, f32[168,128]{1,0:T(8,128)}, u32[]{:S(2)}) %copy-start.11) | copy-done | bytes 86040
  56.8 0.9 %copy-done.13 = f32[168,128]{1,0:T(8,128)S(1)} copy-done((f32[168,128]{1,0:T(8,128)S(1)}, f32[168,128]{1,0:T(8,128)}, u32[]{:S(2)}) %copy-start.13) | copy-done | bytes 86040
  57.7 2.1 %stencil.1 = (f32[2,8,80,128]{3,2,1,0:T(8,128)S(1)}, f32[2,8,128]{2,1,0:T(8,128)S(1)}, f32[2,8,128]{2,1,0:T(8,128)S(1)}, f32[5,8,128]{2,1,0:T(8,128)S(1)}) custom-call(f32[12,168,128]{2,1,0:T(8,128)S(1)} %copy-done.4, f32[168,128]{1,0:T(8,128)S(1)} %get-tuple-element.22.first_ref, f32[168,128]{1,0:T(8,128)S(1)} %copy-done.9, f32[168,128]{1,0:T(8,128)S(1)} %copy-done.11, ...), custom_call_target="tpu_custom_call" | custom-call | flops 20971520 | bytes 3145728 | tf_op jit(solution)/shard_map/stencil/pallas_call | solution.py:328
  59.7 0.0 collective-permute-done.4.before_ref
  59.8 0.0 collective-permute-done.5.after_ref
  59.8 0.0 collective-permute-done.6.left_ref
  59.8 0.0 collective-permute-done.7.right_ref
  59.8 0.4 surface.1
  60.2 0.0 copy-start.7
  60.2 0.6 copy-done.7
  60.9 12.8 %all-to-all-start.1 = ((bf16[64,8,128]{2,1,0:T(8,128)(2,1)}), bf16[64,8,128]{2,1,0:T(8,128)(2,1)S(1)}, u32[]{:S(2)}, u32[]{:S(2)}) async-start(bf16[64,8,128]{2,1,0:T(8,128)(2,1)} %copy-done.7), calls=%async_computation.1 | async-start | bytes 262144 | tf_op jit(solution)/shard_map/all_to_all | solution.py:352
  73.7 1.9 %ocean.1 = f32[2,80,8,128]{3,2,1,0:T(8,128)} custom-call(f32[80,80]{1,0:T(8,128)S(1)} %copy-done.5, f32[2,8,80,128]{3,2,1,0:T(8,128)S(1)} %get-tuple-element.24.twice_ref, f32[2,8,128]{2,1,0:T(8,128)S(1)} %get-tuple-element.32.spread_ref, f32[2,8,128]{2,1,0:T(8,128)S(1)} %get-tuple-element.33.second_ref), custom_call_target="tpu_custom_call" | custom-call | flops 157286400 | bytes 2097152 | tf_op jit(solution)/shard_map/ocean/pallas_call | solution.py:353
  75.6 8.5 %all-to-all-done.1.returned_ref = bf16[64,8,128]{2,1,0:T(8,128)(2,1)S(1)} async-done(((bf16[64,8,128]{2,1,0:T(8,128)(2,1)}), bf16[64,8,128]{2,1,0:T(8,128)(2,1)S(1)}, u32[]{:S(2)}, u32[]{:S(2)}) %all-to-all-start.1) | async-done | bytes 131104 | tf_op jit(solution)/shard_map/all_to_all | solution.py:352
  84.1 0.0 copy-done.17
  84.1 0.0 copy-done.1
  84.1 2.4 %backward.1 = f32[64,2,128]{2,1,0:T(2,128)} custom-call(s32[64]{0:T(128)S(1)} %bitcast.16, s32[64]{0:T(128)S(1)} %get-tuple-element.34.slot_ref, bf16[64,8,128]{2,1,0:T(8,128)(2,1)S(1)} %all-to-all-done.1.returned_ref, bf16[64,128,128]{2,1,0:T(8,128)(2,1)S(1)} %bitcast.11), custom_call_target="tpu_custom_call" | custom-call | flops 16777216 | bytes 3145728 | tf_op jit(solution)/shard_map/backward/pallas_call | solution.py:357
  (3 shorter events, 0.0 us)
Async XLA Ops:
  0.6 16.9 %copy-start.14 = (s32[8,128]{1,0:T(8,128)S(1)}, s32[8,128]{1,0:T(8,128)}, u32[]{:S(2)}) copy-start(s32[8,128]{1,0:T(8,128)} %mask_ref.7) | copy-start | bytes 12292
  0.6 1.6 %copy-start = (bf16[1,64,128,128]{3,2,1,0:T(8,128)(2,1)S(1)}, bf16[1,64,128,128]{3,2,1,0:T(8,128)(2,1)}, u32[]{:S(2)}) copy-start(bf16[1,64,128,128]{3,2,1,0:T(8,128)(2,1)} %param.9) | copy-start | bytes 6291460
  2.2 0.9 %copy-start.6 = (bf16[1,64,16,128]{3,2,1,0:T(8,128)(2,1)S(1)}, bf16[1,64,16,128]{3,2,1,0:T(8,128)(2,1)}, u32[]{:S(2)}) copy-start(bf16[1,64,16,128]{3,2,1,0:T(8,128)(2,1)} %param.8) | copy-start | bytes 786436
  3.2 0.7 copy-start.16
  3.8 0.7 copy-start.18
  4.5 13.1 %copy-start.2 = (f32[2,80,8,128]{3,2,1,0:T(8,128)S(1)}, f32[2,80,8,128]{3,2,1,0:T(8,128)}, u32[]{:S(2)}) copy-start(f32[2,80,8,128]{3,2,1,0:T(8,128)} %param.12) | copy-start | bytes 1966084
  4.5 34.5 %copy-start.15 = (f32[8,128]{1,0:T(8,128)S(1)}, f32[8,128]{1,0:T(8,128)}, u32[]{:S(2)}) copy-start(f32[8,128]{1,0:T(8,128)} %wet_ref.1) | copy-start | bytes 12292
  6.7 47.1 %copy-start.5 = (f32[80,80]{1,0:T(8,128)S(1)}, f32[80,80]{1,0:T(8,128)}, u32[]{:S(2)}) copy-start(f32[80,80]{1,0:T(8,128)} %mixing_ref.5) | copy-start | bytes 76804
  6.7 32.3 %all-to-all-start = ((bf16[64,40,128]{2,1,0:T(8,128)(2,1)}), bf16[64,40,128]{2,1,0:T(8,128)(2,1)S(1)}, u32[]{:S(2)}, u32[]{:S(2)}) async-start(bf16[64,40,128]{2,1,0:T(8,128)(2,1)} %get-tuple-element.25), calls=%async_computation | async-start | bytes 1310720 | tf_op jit(solution)/shard_map/all_to_all | solution.py:314
  17.8 7.4 %collective-permute-start = (f32[2,168,128]{2,1,0:T(8,128)S(1)}, f32[2,168,128]{2,1,0:T(8,128)S(1)}, u32[]{:S(2)}, u32[]{:S(2)}) collective-permute-start(f32[2,168,128]{2,1,0:T(8,128)S(1)} %get-tuple-element.19), channel_id=1, source_target_pairs={{0,64},{64,128},{128,192},{192,256},{256,320},{320,384},{384,448},... | collective-permute-start | bytes 516104 | tf_op jit(solution)/shard_map/ppermute | solution.py:319
  21.8 9.2 %collective-permute-start.1 = (f32[2,168,128]{2,1,0:T(8,128)S(1)}, f32[2,168,128]{2,1,0:T(8,128)S(1)}, u32[]{:S(2)}, u32[]{:S(2)}) collective-permute-start(f32[2,168,128]{2,1,0:T(8,128)S(1)} %get-tuple-element.20), channel_id=1, source_target_pairs={{64,0},{128,64},{192,128},{256,192},{320,256},{384,320},{448,384},... | collective-permute-start | bytes 516104 | tf_op jit(solution)/shard_map/ppermute | solution.py:320
  31.6 1.0 %copy-start.3 = (f32[12,168,128]{2,1,0:T(8,128)}, f32[12,168,128]{2,1,0:T(8,128)S(1)}, u32[]{:S(2)}) copy-start(f32[12,168,128]{2,1,0:T(8,128)S(1)} %get-tuple-element.21.slab_ref) | copy-start | bytes 3096580
  32.6 20.5 %copy-start.8 = (f32[168,128]{1,0:T(8,128)}, f32[168,128]{1,0:T(8,128)S(1)}, u32[]{:S(2)}) copy-start(f32[168,128]{1,0:T(8,128)S(1)} %get-tuple-element.23.last_ref) | copy-start | bytes 258052
  32.6 18.0 %collective-permute-start.2 = (f32[168,128]{1,0:T(8,128)S(1)}, f32[168,128]{1,0:T(8,128)S(1)}, u32[]{:S(2)}, u32[]{:S(2)}) collective-permute-start(f32[168,128]{1,0:T(8,128)S(1)} %get-tuple-element.23.last_ref), channel_id=1, source_target_pairs={{0,1},{1,2},{2,3},{3,4},{4,5},{5,6},{6,7},{7,8},{8,9},{9,10},{10,1... | collective-permute-start | bytes 258056 | tf_op jit(solution)/shard_map/ppermute | solution.py:326
  37.1 16.1 %collective-permute-start.3 = (f32[168,128]{1,0:T(8,128)S(1)}, f32[168,128]{1,0:T(8,128)S(1)}, u32[]{:S(2)}, u32[]{:S(2)}) collective-permute-start(f32[168,128]{1,0:T(8,128)S(1)} %get-tuple-element.22.first_ref), channel_id=1, source_target_pairs={{1,0},{2,1},{3,2},{4,3},{5,4},{6,5},{7,6},{8,7},{9,8},{10,9},{11,1... | collective-permute-start | bytes 258056 | tf_op jit(solution)/shard_map/ppermute | solution.py:327
  39.0 45.0 %copy-start.17 = (s32[1,64,1]{1,2,0:T(1,128)S(1)}, s32[1,64,1]{1,2,0:T(1,128)}, u32[]{:S(2)}) copy-start(s32[1,64,1]{1,2,0:T(1,128)} %param.10) | copy-start | bytes 772
  40.0 44.1 %copy-start.1 = (bf16[1,64,128,128]{3,2,1,0:T(8,128)(2,1)S(1)}, bf16[1,64,128,128]{3,2,1,0:T(8,128)(2,1)}, u32[]{:S(2)}) copy-start(bf16[1,64,128,128]{3,2,1,0:T(8,128)(2,1)} %param.9) | copy-start | bytes 6291460
  40.0 19.8 %collective-permute-start.4 = (f32[2,8,128]{2,1,0:T(8,128)S(1)}, f32[2,8,128]{2,1,0:T(8,128)S(1)}, u32[]{:S(2)}, u32[]{:S(2)}) collective-permute-start(f32[2,8,128]{2,1,0:T(8,128)S(1)} %get-tuple-element.26.first_ref), channel_id=1, source_target_pairs={{0,64},{64,128},{128,192},{192,256},{256,320},{320,384},{384,448},... | collective-permute-start | bytes 24584 | tf_op jit(solution)/shard_map/ppermute | solution.py:340
  44.7 15.0 %collective-permute-start.5 = (f32[2,8,128]{2,1,0:T(8,128)S(1)}, f32[2,8,128]{2,1,0:T(8,128)S(1)}, u32[]{:S(2)}, u32[]{:S(2)}) collective-permute-start(f32[2,8,128]{2,1,0:T(8,128)S(1)} %get-tuple-element.26.first_ref), channel_id=1, source_target_pairs={{64,0},{128,64},{192,128},{256,192},{320,256},{384,320},{448,384},... | collective-permute-start | bytes 24584 | tf_op jit(solution)/shard_map/ppermute | solution.py:341
  46.6 13.1 %collective-permute-start.6 = (f32[2,8,128]{2,1,0:T(8,128)S(1)}, f32[2,8,128]{2,1,0:T(8,128)S(1)}, u32[]{:S(2)}, u32[]{:S(2)}) collective-permute-start(f32[2,8,128]{2,1,0:T(8,128)S(1)} %get-tuple-element.26.first_ref), channel_id=1, source_target_pairs={{0,1},{1,2},{2,3},{3,4},{4,5},{5,6},{6,7},{7,8},{8,9},{9,10},{10,1... | collective-permute-start | bytes 24584 | tf_op jit(solution)/shard_map/ppermute | solution.py:342
  50.6 0.6 copy-start.10
  51.2 8.6 %collective-permute-start.7 = (f32[2,8,128]{2,1,0:T(8,128)S(1)}, f32[2,8,128]{2,1,0:T(8,128)S(1)}, u32[]{:S(2)}, u32[]{:S(2)}) collective-permute-start(f32[2,8,128]{2,1,0:T(8,128)S(1)} %get-tuple-element.26.first_ref), channel_id=1, source_target_pairs={{1,0},{2,1},{3,2},{4,3},{5,4},{6,5},{7,6},{8,7},{9,8},{10,9},{11,1... | collective-permute-start | bytes 24584 | tf_op jit(solution)/shard_map/ppermute | solution.py:343
  53.2 0.6 copy-start.12
  53.8 1.2 %copy-start.4 = (f32[12,168,128]{2,1,0:T(8,128)S(1)}, f32[12,168,128]{2,1,0:T(8,128)}, u32[]{:S(2)}) copy-start(f32[12,168,128]{2,1,0:T(8,128)} %copy-done.3) | copy-start | bytes 3096580
  55.0 0.9 %copy-start.9 = (f32[168,128]{1,0:T(8,128)S(1)}, f32[168,128]{1,0:T(8,128)}, u32[]{:S(2)}) copy-start(f32[168,128]{1,0:T(8,128)} %copy-done.8) | copy-start | bytes 258052
  55.9 0.9 %copy-start.11 = (f32[168,128]{1,0:T(8,128)S(1)}, f32[168,128]{1,0:T(8,128)}, u32[]{:S(2)}) copy-start(f32[168,128]{1,0:T(8,128)} %copy-done.10) | copy-start | bytes 258052
  56.8 0.9 %copy-start.13 = (f32[168,128]{1,0:T(8,128)S(1)}, f32[168,128]{1,0:T(8,128)}, u32[]{:S(2)}) copy-start(f32[168,128]{1,0:T(8,128)} %copy-done.12) | copy-start | bytes 258052
  60.2 0.6 copy-start.7
  60.9 23.2 %all-to-all-start.1 = ((bf16[64,8,128]{2,1,0:T(8,128)(2,1)}), bf16[64,8,128]{2,1,0:T(8,128)(2,1)S(1)}, u32[]{:S(2)}, u32[]{:S(2)}) async-start(bf16[64,8,128]{2,1,0:T(8,128)(2,1)} %copy-done.7), calls=%async_computation.1 | async-start | bytes 262144 | tf_op jit(solution)/shard_map/all_to_all | solution.py:352

commit v3 on v2

--- a/solution.py
+++ b/solution.py
@@ -15,6 +15,7 @@
 exact = lax.Precision.HIGHEST
 vmem = pl.BlockSpec(memory_space=pltpu.VMEM)
 smem = pl.BlockSpec(memory_space=pltpu.SMEM)
+hbm = pl.BlockSpec(memory_space=pltpu.HBM)
 
 
 def call(body, name, out_shape, in_specs, out_specs=None, scratch=(), flops=0, moved=0):
@@ -45,23 +46,37 @@
     return lax.broadcasted_iota(jnp.int32, dims, len(dims) - 2)
 
 
-def forward_kernel(block_ref, row_ref, flux_ref, weight_ref, out_ref, slot_ref, used_ref, code_ref):
+def forward_kernel(
+    block_hbm, row_hbm, flux_hbm, weight_hbm, out_ref, slot_ref,
+    block_ref, row_ref, flux_ref, weight_ref, used_ref, code_ref, small_sems, weight_sems,
+):
     blocks = out_ref.shape[0]
     tiles, fields, width = flux_ref.shape
+    chunks = weight_sems.shape[0]
+    size = tiles // chunks
+    copies = [
+        pltpu.make_async_copy(block_hbm, block_ref, small_sems.at[0]),
+        pltpu.make_async_copy(row_hbm, row_ref, small_sems.at[1]),
+        pltpu.make_async_copy(flux_hbm, flux_ref, small_sems.at[2]),
+    ]
+    for c in range(chunks):
+        part = pl.ds(c * size, size)
+        copies.append(pltpu.make_async_copy(weight_hbm.at[part], weight_ref.at[part], weight_sems.at[c]))
+    for copy in copies:
+        copy.start()
     out_ref[...] = jnp.zeros_like(out_ref)
     for b in range(blocks):
         used_ref[b] = 0
         code_ref[b] = empty_code
         code_ref[blocks + b] = empty_code
+    copies[0].wait()
+    copies[1].wait()
     for t in range(tiles):
         b = block_ref[t]
         s = used_ref[b]
         used_ref[b] = s + 1
         slot_ref[t] = s
         code_ref[s * blocks + b] = row_ref[t]
-        remapped = jnp.dot(flux_ref[t], weight_ref[t], preferred_element_type=f32)
-        start = pl.multiple_of(s * fields, fields)
-        out_ref[b, pl.ds(start, fields), :] = remapped.astype(bf16)
     line = line_iota((8, width))
     extra = jnp.where(line % 2 == 1, 8.0, 0.0).astype(f32)
     for b in range(blocks):
@@ -69,6 +84,17 @@
         second = code_ref[blocks + b].astype(f32)
         code = jnp.where(line < 2, first, jnp.where(line < 4, second, float(empty_code))) + extra
         out_ref[b, 2 * fields : 2 * fields + 8, :] = code.astype(bf16)
+    copies[2].wait()
+    for t in range(0, tiles, 2):
+        if t % size == 0:
+            copies[3 + t // size].wait()
+        both = jnp.concatenate([weight_ref[t], weight_ref[t + 1]], axis=1)
+        fluxes = flux_ref[t : t + 2].reshape(2 * fields, width)
+        remapped = jnp.dot(fluxes, both, preferred_element_type=f32)
+        for i in range(2):
+            start = pl.multiple_of(slot_ref[t + i] * fields, fields)
+            value = remapped[i * fields : (i + 1) * fields, i * width : (i + 1) * width]
+            out_ref[block_ref[t + i], pl.ds(start, fields), :] = value.astype(bf16)
 
 
 def rows_kernel(x_ref, mask_ref, top_ref, bottom_ref):
@@ -80,8 +106,15 @@
             out_ref[i, planes : planes + 8, :] = jnp.broadcast_to(mask[r : r + 1, :], (8, width))
 
 
+def packing(rows, planes, width):
+    span = 2 * (rows + 4)
+    per = width // span
+    return span, per, planes // 8, -(-planes // 8 // per)
+
+
 def columns_kernel(x_ref, mask_ref, before_ref, after_ref, slab_ref, first_ref, last_ref):
     planes, rows, width = x_ref.shape
+    span, per, groups, packs = packing(rows, planes, width)
     mask = mask_ref[...].astype(f32)
     for i in range(2):
         slab_ref[i] = before_ref[i]
@@ -89,16 +122,30 @@
     for r in range(rows):
         slab_ref[r + 2, 0:planes, :] = x_ref[:, r, :]
         slab_ref[r + 2, planes : planes + 8, :] = jnp.broadcast_to(mask[r : r + 1, :], (8, width))
-    lane = lane_iota((planes + 8, width))
-    first = jnp.zeros((planes + 8, width), f32)
-    last = jnp.zeros((planes + 8, width), f32)
-    for r in range(rows + 4):
-        here = (lane == 2 * r) | (lane == 2 * r + 1)
-        slab = slab_ref[r]
-        first = jnp.where(here, pltpu.roll(slab, 2 * r, 1) if r else slab, first)
-        last = jnp.where(here, pltpu.roll(slab, 2 * r + 2, 1), last)
-    first_ref[...] = first
-    last_ref[...] = last
+    lane = lane_iota((8, width))
+
+    def turn(value, by):
+        return pltpu.roll(value, by % width, 1) if by % width else value
+
+    for pack in range(packs + 1):
+        first = jnp.zeros((8, width), f32)
+        last = jnp.zeros((8, width), f32)
+        if pack < packs:
+            members = [(q, q % per) for q in range(pack * per, min(groups, (pack + 1) * per))]
+        else:
+            members = [(groups, 0)]
+        for q, place in members:
+            for r in range(rows + 4):
+                value = slab_ref[r, 8 * q : 8 * q + 8, :]
+                start = span * place + 2 * r
+                here = (lane == start) | (lane == start + 1)
+                first = jnp.where(here, turn(value, start), first)
+                last = jnp.where(here, turn(value, start + 2), last)
+        if pack == packs:
+            first = sum((turn(first, span * i) for i in range(1, per)), first)
+            last = sum((turn(last, span * i) for i in range(1, per)), last)
+        first_ref[8 * pack : 8 * pack + 8, :] = first
+        last_ref[8 * pack : 8 * pack + 8, :] = last
 
 
 def spread(weight, planes):
@@ -125,14 +172,23 @@
     planes = slab_ref.shape[1] - 8
     width = slab_ref.shape[2]
     levels = planes // 2
+    span, per, groups, packs = packing(rows, planes, width)
+    packed = 8 * packs
     lane = lane_iota((planes + 8, width))
     at_start = lane == 0
     at_end = lane == width - 1
 
-    def beside(center, left_value, right_value):
+    def beside(center, left_packed, right_packed, r):
         size = center.shape[0]
-        left = jnp.where(at_start[:size], left_value, pltpu.roll(center, 1, 1))
-        right = jnp.where(at_end[:size], right_value, pltpu.roll(center, width - 1, 1))
+        lefts, rights = [], []
+        for q in range(size // 8):
+            pack, place = (q // per, q % per) if q < groups else (packs, 0)
+            start = span * place + 2 * r
+            part = slice(8 * pack, 8 * pack + 8)
+            lefts.append(pltpu.roll(left_packed[part], width - (start + 1), 1))
+            rights.append(pltpu.roll(right_packed[part], (width - 1 - start) % width, 1))
+        left = jnp.where(at_start[:size], jnp.concatenate(lefts, 0), pltpu.roll(center, 1, 1))
+        right = jnp.where(at_end[:size], jnp.concatenate(rights, 0), pltpu.roll(center, width - 1, 1))
         return left, right
 
     left_all, right_all = left_ref[...], right_ref[...]
@@ -144,8 +200,8 @@
             pltpu.roll(own, outer_shift, 1),
             beyond,
         )
-        w = weights_of(own[planes:], [a[planes:] for a in around])
-        return combine(w, [own[:planes]] + [a[:planes] for a in around], planes)
+        w = weights_of(own[packed:], [a[packed:] for a in around])
+        return combine(w, [own[:packed]] + [a[:packed] for a in around], packed)
 
     left_once = edge(left_all, 1, pltpu.roll(first_ref[...], 1, 1))
     right_once = edge(right_all, width - 1, pltpu.roll(last_ref[...], width - 1, 1))
@@ -153,11 +209,7 @@
     saved = []
     for r in range(1, rows + 3):
         center = slab_ref[r]
-        left, right = beside(
-            center,
-            pltpu.roll(left_all, width - (2 * r + 1), 1),
-            pltpu.roll(right_all, (width - 1 - 2 * r) % width, 1),
-        )
+        left, right = beside(center, left_all, right_all, r)
         around = (slab_ref[r - 1], slab_ref[r + 1], left, right)
         w = weights_of(center[planes:], [a[planes:] for a in around])
         saved.append(w)
@@ -170,14 +222,12 @@
     once_column = lax.dot_general(top_rows, chosen, over_first, precision=exact, preferred_element_type=f32)
     top_twice = jnp.dot(top_rows, mixing, precision=exact, preferred_element_type=f32)
     twice_column = lax.dot_general(top_twice, chosen, over_first, precision=exact, preferred_element_type=f32)
+    weights_ref[5] = jnp.broadcast_to(twice_column[0:1, :], (rows, width))
+    weights_ref[6] = jnp.broadcast_to(once_column[0:1, :], (rows, width))
 
     for r in range(2, rows + 2):
         center = work_ref[r]
-        left, right = beside(
-            center,
-            pltpu.roll(left_once, width - (2 * r + 1), 1),
-            pltpu.roll(right_once, (width - 1 - 2 * r) % width, 1),
-        )
+        left, right = beside(center, left_once, right_once, r)
         w = saved[r - 1]
         result = combine(w, [center, work_ref[r - 1], work_ref[r + 1], left, right], planes)
         i = r - 2
@@ -191,7 +241,10 @@
             once_top_ref[k, i : i + 1, :] = jnp.sum(once_column * before, axis=0, keepdims=True)
 
 
-def drive_kernel(received_ref, top_ref, mask_ref, wet_ref, sum_ref, rate_ref, first_ref):
+def drive_kernel(
+    received_ref, top_ref, mask_ref, wet_ref, once_top_ref, twice_top_ref, weights_ref,
+    first_ref, second_ref, base_ref,
+):
     devices, lines, width = received_ref.shape
     rows = mask_ref.shape[0]
     fields = (lines - 8) // 2
@@ -205,6 +258,7 @@
                 totals[r] = totals[r] + jnp.where(code == float(r), value, 0.0)
     mask = mask_ref[...].astype(f32)
     wet = wet_ref[...]
+    mixing_00 = weights_ref[6]
     half = fields // 2
     even = line_iota((half, width)) % 2 == 0
     for k in range(2):
@@ -216,24 +270,20 @@
             rates.append(jnp.sum(jnp.where(even, part, 0.0), axis=0, keepdims=True))
         drive_sum = jnp.concatenate(sums, axis=0) / wet
         drive_rate = jnp.concatenate(rates, axis=0) / wet
-        sum_ref[k] = drive_sum
-        rate_ref[k] = drive_rate
-        first_ref[k] = mask * (forcing_step * (drive_sum - drive_rate * top_ref[k]))
+        first = mask * (forcing_step * (drive_sum - drive_rate * top_ref[k]))
+        once_top = once_top_ref[k] + mixing_00 * first
+        second = mask * (forcing_step * (drive_sum - drive_rate * once_top))
+        first_ref[k] = first
+        second_ref[k] = second
+        base_ref[k] = twice_top_ref[k] + mixing_00 * second
 
 
 def surface_kernel(
-    mixing_ref, received_ref, first_ref, before_ref, after_ref, left_ref, right_ref,
-    once_top_ref, twice_top_ref, weights_ref, sum_ref, rate_ref, mask_ref,
-    spread_ref, second_ref, back_ref,
+    received_ref, first_ref, before_ref, after_ref, left_ref, right_ref, base_ref, weights_ref,
+    spread_ref, back_ref,
 ):
     devices, lines, width = received_ref.shape
-    rows = mask_ref.shape[0]
-    mask = mask_ref[...].astype(f32)
-    once = mixing_ref[0:1, :]
-    mixing_00 = mixing_ref[0:1, 0:1]
-    column = mixing_ref[...]
-    row_squared = jnp.dot(mixing_ref[0:8, :], column, precision=exact, preferred_element_type=f32)
-    twice_00 = row_squared[0:1, 0:1]
+    rows = first_ref.shape[1]
     line = line_iota((rows, width))
     lane = lane_iota((rows, width))
     surfaces = []
@@ -247,11 +297,8 @@
             weights_ref[0] * own + weights_ref[1] * up + weights_ref[2] * down
             + weights_ref[3] * left + weights_ref[4] * right
         )
-        once_top = once_top_ref[k] + mixing_00 * own
-        second = mask * (forcing_step * (sum_ref[k] - rate_ref[k] * once_top))
         spread_ref[k] = moved
-        second_ref[k] = second
-        surfaces.append(twice_top_ref[k] + twice_00 * moved + mixing_00 * second)
+        surfaces.append(base_ref[k] + weights_ref[5] * moved)
     surface = jnp.concatenate(surfaces + [jnp.zeros((width - 2 * rows, width), f32)], axis=0).astype(bf16)
     codes = received_ref[:, lines - 8 : lines, :].astype(f32)
     wanted = (codes == lane_iota(codes.shape).astype(f32)).astype(f32).reshape(devices * 8, width).astype(bf16)
@@ -259,7 +306,20 @@
     back_ref[...] = picked.reshape(devices, 8, width).astype(bf16)
 
 
-def ocean_kernel(mixing_ref, twice_ref, spread_ref, second_ref, out_ref):
+def own_columns(weight_ref, lines):
+    tiles, width, _ = weight_ref.shape
+    pair = lane_iota((width, width)) // 2
+    total = jnp.zeros((width, width), f32)
+    step = min(16, tiles)
+    for start in range(0, tiles, step):
+        part = weight_ref[start : start + step].reshape(step * width, width)
+        mapped = lax.dot_general(part, lines, (((1,), (1,)), ((), ())), preferred_element_type=f32)
+        for i in range(step):
+            total = jnp.where(pair == start + i, mapped[i * width : (i + 1) * width], total)
+    return total.T
+
+
+def ocean_kernel(mixing_ref, twice_ref, spread_ref, second_ref, weight_ref, out_ref, sums_ref):
     levels = mixing_ref.shape[0]
     rows, width = spread_ref.shape[1:]
     mixing = mixing_ref[...]
@@ -271,19 +331,17 @@
             free = jnp.dot(squared, twice_ref[k, r], precision=exact, preferred_element_type=f32)
             forced = twice * spread_ref[k, r : r + 1, :] + once * second_ref[k, r : r + 1, :]
             out_ref[k, :, r, :] = free + forced
-
-
-def backward_kernel(block_ref, slot_ref, returned_ref, weight_ref, out_ref):
-    tiles, width, _ = weight_ref.shape
-    line = line_iota((8, width))
+    sums_ref[...] = own_columns(weight_ref, jnp.ones((width, width), bf16))
+
+
+def backward_kernel(block_ref, slot_ref, returned_ref, weight_ref, sums_ref, out_ref, lines_ref, rows_ref):
+    tiles = weight_ref.shape[0]
+    lines_ref[...] = returned_ref[...].astype(f32)
     for t in range(tiles):
-        values = returned_ref[block_ref[t]].astype(f32)
-        values = jnp.where(line == 4, 1.0, values).astype(bf16)
-        mapped = lax.dot_general(
-            values, weight_ref[t], (((1,), (1,)), ((), ())), preferred_element_type=f32
-        )
-        numerator = jnp.where(slot_ref[t] == 0, mapped[0:2], mapped[2:4])
-        out_ref[t] = numerator / mapped[4:5]
+        rows_ref[2 * t : 2 * t + 2, :] = lines_ref[block_ref[t], pl.ds(2 * slot_ref[t], 2), :]
+    result = own_columns(weight_ref, rows_ref[...].astype(bf16)) / sums_ref[...]
+    for t in range(tiles):
+        out_ref[t] = result[2 * t : 2 * t + 2]
 
 
 def per_device(
@@ -295,6 +353,7 @@
     tiles, fields = atm_flux.shape[1:3]
     tracers, levels = ocean_state.shape[:2]
     planes = tracers * levels
+    packed_lines = 8 * (packing(rows, planes, width)[3] + 1)
     weights = remap_weights[0]
     block = dest_block.reshape(tiles)
     row = dest_row.reshape(tiles)
@@ -307,8 +366,13 @@
     packed, slot = call(
         forward_kernel, "forward",
         (shape(blocks, 2 * fields + 8, width, dtype=bf16), shape(tiles, dtype=jnp.int32)),
-        [smem, smem, vmem, vmem], [vmem, smem],
-        [pltpu.SMEM((blocks,), jnp.int32), pltpu.SMEM((2 * blocks,), jnp.int32)],
+        [hbm] * 4, [vmem, smem],
+        [
+            pltpu.SMEM((tiles,), jnp.int32), pltpu.SMEM((tiles,), jnp.int32),
+            pltpu.VMEM((tiles, fields, width), bf16), pltpu.VMEM((tiles, width, width), bf16),
+            pltpu.SMEM((blocks,), jnp.int32), pltpu.SMEM((2 * blocks,), jnp.int32),
+            pltpu.SemaphoreType.DMA((3,)), pltpu.SemaphoreType.DMA((min(4, tiles // 2),)),
+        ],
         flops=2 * tiles * fields * width * width, moved=3 << 20,
     )(block, row, atm_flux[0], weights)
     received = lax.all_to_all(packed, "blk", split_axis=0, concat_axis=0, tiled=True)
@@ -320,7 +384,7 @@
     after = lax.ppermute(top, "sec", down_sec)
     slab, first_columns, last_columns = call(
         columns_kernel, "columns",
-        (shape(rows + 4, planes + 8, width), shape(planes + 8, width), shape(planes + 8, width)),
+        (shape(rows + 4, planes + 8, width), shape(packed_lines, width), shape(packed_lines, width)),
         [vmem] * 4, moved=2 << 20,
     )(state, land_mask, before, after)
     left = lax.ppermute(last_columns, "blk", up_blk)
@@ -329,35 +393,33 @@
         stencil_kernel, "stencil",
         (
             shape(tracers, rows, levels, width), shape(tracers, rows, width),
-            shape(tracers, rows, width), shape(5, rows, width),
+            shape(tracers, rows, width), shape(7, rows, width),
         ),
         [vmem] * 6, scratch=[pltpu.VMEM((rows + 4, planes, width), f32)], flops=20 << 20, moved=3 << 20,
     )(slab, first_columns, last_columns, left, right, mixing)
 
-    drive_sum, drive_rate, first = call(
-        drive_kernel, "drive", (shape(tracers, rows, width),) * 3, [vmem] * 4, moved=1 << 20
-    )(received, ocean_state[:, 0], land_mask, wet_fraction)
+    first, second, base = call(
+        drive_kernel, "drive", (shape(tracers, rows, width),) * 3, [vmem] * 7, moved=1 << 20
+    )(received, ocean_state[:, 0], land_mask, wet_fraction, once_top, twice_top, step_weights)
     first_before = lax.ppermute(first, "sec", up_sec)
     first_after = lax.ppermute(first, "sec", down_sec)
     first_left = lax.ppermute(first, "blk", up_blk)
     first_right = lax.ppermute(first, "blk", down_blk)
-    spread_first, second, back = call(
+    spread_first, back = call(
         surface_kernel, "surface",
-        (shape(tracers, rows, width), shape(tracers, rows, width), shape(blocks, 8, width, dtype=bf16)),
-        [vmem] * 13, moved=1 << 20,
-    )(
-        mixing, received, first, first_before, first_after, first_left, first_right,
-        once_top, twice_top, step_weights, drive_sum, drive_rate, land_mask,
-    )
+        (shape(tracers, rows, width), shape(blocks, 8, width, dtype=bf16)),
+        [vmem] * 8, moved=1 << 20,
+    )(received, first, first_before, first_after, first_left, first_right, base, step_weights)
     returned = lax.all_to_all(back, "blk", split_axis=0, concat_axis=0, tiled=True)
-    ocean = call(
-        ocean_kernel, "ocean", shape(tracers, levels, rows, width), [vmem] * 4,
+    ocean, sums = call(
+        ocean_kernel, "ocean", (shape(tracers, levels, rows, width), shape(width, width)), [vmem] * 5,
         flops=12 * planes * levels * rows * width, moved=2 << 20,
-    )(mixing, twice, spread_first, second)
+    )(mixing, twice, spread_first, second, weights)
     atmosphere = call(
-        backward_kernel, "backward", shape(tiles, tracers, width), [smem, smem, vmem, vmem],
+        backward_kernel, "backward", shape(tiles, tracers, width), [smem, smem, vmem, vmem, vmem],
+        scratch=[pltpu.VMEM((blocks, 8, width), f32), pltpu.VMEM((width, width), f32)],
         flops=16 * tiles * width * width, moved=3 << 20,
-    )(block, slot, returned, weights)
+    )(block, slot, returned, weights, sums)
     return (ocean, atmosphere[None])
 
 

time: 87.2 us -> 83.7 us (0.960)
  local copies, waits for them, and re-layouts: 10.6 us -> 4.53 us
  waiting for transfers between devices: 15.8 us -> 21.3 us
  starting transfers between devices: 48.4 us -> 45.5 us
    unnamed x38 -> x22, local copies, waits for them, and re-layouts: 10.6 us -> 4.52 us
    ppermute x1, waiting for transfers between devices: 0.01 us -> 3.15 us  [per_device(): right = lax.ppermute(first_columns, 'blk', down_blk)]
    ppermute x1, waiting for transfers between devices: 0.01 us -> 2.82 us  [per_device(): first_right = lax.ppermute(first, 'blk', down_blk)]
    ppermute x1, starting transfers between devices: 3.92 us -> 2.21 us  [per_device(): first_left = lax.ppermute(first, 'blk', up_blk)]
    all_to_all x1, starting transfers between devices: 12.8 us -> 11.4 us  [per_device(): lax.all_to_all(back, 'blk', split_axis=0, concat_axis=0, tiled=True)]
  transfers between devices with their start and end apart: 10 -> 10, of which waited for: 3 -> 5; matrix products, arithmetic and copies ran while one was open for 0% -> 0% of each run, Pallas kernels for 7% -> 6%
where the time goes in v3:
time: 83.7 us; the launch traced here: 83.2 us
  starting transfers between devices  45.5 us (54%)
  waiting for transfers between devices  21.3 us (25%)
  Pallas kernels  11.1 us (13%)
  local copies, waits for them, and re-layouts  4.53 us (5%)
  between operations  0.88 us (1%)
    all_to_all x1, starting transfers between devices, per_device(): lax.all_to_all(back, 'blk', split_axis=0, concat_axis=0, tiled=True)  11.4 us
    all_to_all x1, starting transfers between devices, per_device(): lax.all_to_all(packed, 'blk', split_axis=0, concat_axis=0, tiled=True)  10.8 us
    all_to_all x1, waiting for transfers between devices, per_device(): lax.all_to_all(back, 'blk', split_axis=0, concat_axis=0, tiled=True)  7.99 us
    ppermute x1, waiting for transfers between devices, per_device(): after = lax.ppermute(top, 'sec', down_sec)  5.86 us
    ppermute x1, starting transfers between devices, per_device(): first_before = lax.ppermute(first, 'sec', up_sec)  4.57 us
    unnamed x22, local copies, waits for them, and re-layouts  4.52 us
    ppermute x1, starting transfers between devices, per_device(): left = lax.ppermute(last_columns, 'blk', up_blk)  4.47 us
    ppermute x1, starting transfers between devices, per_device(): before = lax.ppermute(bottom, 'sec', up_sec)  4.14 us
  transfers between devices with their start and end apart: 10, of which 5 were waited for; matrix products, arithmetic and copies ran while one was open for 0% of the time, Pallas kernels for 6%

profile of v3, /device:TPU:129, one launch (start us, length us, event | category | flops | bytes accessed | tf_op | source)
XLA Modules:
  0.0 83.2 jit_solution(6716423796174303933)
XLA Ops:
  0.6 0.0 copy-start.6
  0.6 0.0 copy-start
  0.7 1.6 %copy-done = bf16[1,64,128,128]{3,2,1,0:T(8,128)(2,1)S(1)} copy-done((bf16[1,64,128,128]{3,2,1,0:T(8,128)(2,1)S(1)}, bf16[1,64,128,128]{3,2,1,0:T(8,128)(2,1)}, u32[]{:S(2)}) %copy-start) | copy-done | bytes 2097176
  2.2 0.0 copy-start.3
  2.2 0.9 %copy-done.3 = bf16[1,64,16,128]{3,2,1,0:T(8,128)(2,1)S(1)} copy-done((bf16[1,64,16,128]{3,2,1,0:T(8,128)(2,1)S(1)}, bf16[1,64,16,128]{3,2,1,0:T(8,128)(2,1)}, u32[]{:S(2)}) %copy-start.3) | copy-done | bytes 262168
  3.2 0.0 copy-start.8
  3.2 0.7 copy-done.8
  3.8 0.0 copy-start.10
  3.8 0.7 copy-done.10
  4.5 0.0 copy-start.2
  4.5 0.0 copy-start.4
  4.5 2.6 %forward.1 = (bf16[64,40,128]{2,1,0:T(8,128)(2,1)}, s32[64]{0:T(128)S(1)}) custom-call(s32[64]{0:T(128)S(1)} %bitcast.16, s32[64]{0:T(128)S(1)} %bitcast.18, bf16[64,16,128]{2,1,0:T(8,128)(2,1)S(1)} %bitcast.15, bf16[64,128,128]{2,1,0:T(8,128)(2,1)S(1)} %bitcast.10), custom_call_target="tpu_custom_call" | custom-call | flops 33554432 | bytes 3145728 | tf_op jit(solution)/shard_map/forward/pallas_call | solution.py:366
  7.2 0.0 copy-start.7
  7.2 10.8 %all-to-all-start = ((bf16[64,40,128]{2,1,0:T(8,128)(2,1)}), bf16[64,40,128]{2,1,0:T(8,128)(2,1)S(1)}, u32[]{:S(2)}, u32[]{:S(2)}) async-start(bf16[64,40,128]{2,1,0:T(8,128)(2,1)} %get-tuple-element.26), calls=%async_computation | async-start | bytes 1310720 | tf_op jit(solution)/shard_map/all_to_all | solution.py:378
  18.0 0.0 copy-done.6
  18.0 0.0 copy-done.2
  18.0 0.2 rows.1
  18.2 0.0 copy-start.1
  18.2 4.1 %collective-permute-start = (f32[2,168,128]{2,1,0:T(8,128)S(1)}, f32[2,168,128]{2,1,0:T(8,128)S(1)}, u32[]{:S(2)}, u32[]{:S(2)}) collective-permute-start(f32[2,168,128]{2,1,0:T(8,128)S(1)} %get-tuple-element.20), channel_id=1, source_target_pairs={{0,64},{64,128},{128,192},{192,256},{256,320},{320,384},{384,448},... | collective-permute-start | bytes 516104 | tf_op jit(solution)/shard_map/ppermute | solution.py:383
  22.3 1.9 %collective-permute-start.1 = (f32[2,168,128]{2,1,0:T(8,128)S(1)}, f32[2,168,128]{2,1,0:T(8,128)S(1)}, u32[]{:S(2)}, u32[]{:S(2)}) collective-permute-start(f32[2,168,128]{2,1,0:T(8,128)S(1)} %get-tuple-element.21), channel_id=1, source_target_pairs={{64,0},{128,64},{192,128},{256,192},{320,256},{384,320},{448,384},... | collective-permute-start | bytes 516104 | tf_op jit(solution)/shard_map/ppermute | solution.py:384
  24.3 1.4 %collective-permute-done.before_ref = f32[2,168,128]{2,1,0:T(8,128)S(1)} collective-permute-done((f32[2,168,128]{2,1,0:T(8,128)S(1)}, f32[2,168,128]{2,1,0:T(8,128)S(1)}, u32[]{:S(2)}, u32[]{:S(2)}) %collective-permute-start) | collective-permute-done | bytes 172064 | tf_op jit(solution)/shard_map/ppermute | solution.py:383
  25.7 5.9 %collective-permute-done.1.after_ref = f32[2,168,128]{2,1,0:T(8,128)S(1)} collective-permute-done((f32[2,168,128]{2,1,0:T(8,128)S(1)}, f32[2,168,128]{2,1,0:T(8,128)S(1)}, u32[]{:S(2)}, u32[]{:S(2)}) %collective-permute-start.1) | collective-permute-done | bytes 172064 | tf_op jit(solution)/shard_map/ppermute | solution.py:384
  31.6 0.8 columns.1
  32.4 4.5 %collective-permute-start.2 = (f32[40,128]{1,0:T(8,128)S(1)}, f32[40,128]{1,0:T(8,128)S(1)}, u32[]{:S(2)}, u32[]{:S(2)}) collective-permute-start(f32[40,128]{1,0:T(8,128)S(1)} %get-tuple-element.24.last_ref), channel_id=1, source_target_pairs={{0,1},{1,2},{2,3},{3,4},{4,5},{5,6},{6,7},{7,8},{8,9},{9,10},{10,1... | collective-permute-start | bytes 61448 | tf_op jit(solution)/shard_map/ppermute | solution.py:390
  36.8 1.9 %collective-permute-start.3 = (f32[40,128]{1,0:T(8,128)S(1)}, f32[40,128]{1,0:T(8,128)S(1)}, u32[]{:S(2)}, u32[]{:S(2)}) collective-permute-start(f32[40,128]{1,0:T(8,128)S(1)} %get-tuple-element.23.first_ref), channel_id=1, source_target_pairs={{1,0},{2,1},{3,2},{4,3},{5,4},{6,5},{7,6},{8,7},{9,8},{10,9},{11,1... | collective-permute-start | bytes 61448 | tf_op jit(solution)/shard_map/ppermute | solution.py:391
  38.8 0.0 collective-permute-done.2.left_ref
  38.8 3.2 %collective-permute-done.3.right_ref = f32[40,128]{1,0:T(8,128)S(1)} collective-permute-done((f32[40,128]{1,0:T(8,128)S(1)}, f32[40,128]{1,0:T(8,128)S(1)}, u32[]{:S(2)}, u32[]{:S(2)}) %collective-permute-start.3) | collective-permute-done | bytes 20512 | tf_op jit(solution)/shard_map/ppermute | solution.py:391
  41.9 0.0 copy-done.4
  41.9 1.8 %stencil.1 = (f32[2,8,80,128]{3,2,1,0:T(8,128)S(1)}, f32[2,8,128]{2,1,0:T(8,128)S(1)}, f32[2,8,128]{2,1,0:T(8,128)S(1)}, f32[7,8,128]{2,1,0:T(8,128)S(1)}) custom-call(f32[12,168,128]{2,1,0:T(8,128)S(1)} %get-tuple-element.22.slab_ref, f32[40,128]{1,0:T(8,128)S(1)} %get-tuple-element.23.first_ref, f32[40,128]{1,0:T(8,128)S(1)} %get-tuple-element.24.last_ref, ...), custom_call_target="tpu_custom_call" | custom-call | flops 20971520 | bytes 3145728 | tf_op jit(solution)/shard_map/stencil/pallas_call | solution.py:392
  43.8 0.0 all-to-all-done.received_ref
  43.8 0.0 copy-done.7
  43.8 0.0 copy-start.9
  43.8 0.9 %drive.1 = (f32[2,8,128]{2,1,0:T(8,128)S(1)}, f32[2,8,128]{2,1,0:T(8,128)S(1)}, f32[2,8,128]{2,1,0:T(8,128)S(1)}) custom-call(bf16[64,40,128]{2,1,0:T(8,128)(2,1)S(1)} %all-to-all-done.received_ref, f32[2,8,128]{2,1,0:T(8,128)S(1)} %slice_bitcast_fusion.top_ref, s32[8,128]{1,0:T(8,128)S(1)} %copy-done.6, f32[8,128]{1,0:T(8,128)S(1)} %copy-done.7, ...), custom_call_target="tpu_custom_call" | custom-call | bytes 1048576 | tf_op jit(solution)/shard_map/drive/pallas_call | solution.py:401
  44.7 4.6 %collective-permute-start.4 = (f32[2,8,128]{2,1,0:T(8,128)S(1)}, f32[2,8,128]{2,1,0:T(8,128)S(1)}, u32[]{:S(2)}, u32[]{:S(2)}) collective-permute-start(f32[2,8,128]{2,1,0:T(8,128)S(1)} %get-tuple-element.30.first_ref), channel_id=1, source_target_pairs={{0,64},{64,128},{128,192},{192,256},{256,320},{320,384},{384,448},... | collective-permute-start | bytes 24584 | tf_op jit(solution)/shard_map/ppermute | solution.py:404
  49.3 1.9 %collective-permute-start.5 = (f32[2,8,128]{2,1,0:T(8,128)S(1)}, f32[2,8,128]{2,1,0:T(8,128)S(1)}, u32[]{:S(2)}, u32[]{:S(2)}) collective-permute-start(f32[2,8,128]{2,1,0:T(8,128)S(1)} %get-tuple-element.30.first_ref), channel_id=1, source_target_pairs={{64,0},{128,64},{192,128},{256,192},{320,256},{384,320},{448,384},... | collective-permute-start | bytes 24584 | tf_op jit(solution)/shard_map/ppermute | solution.py:405
  51.2 2.2 %collective-permute-start.6 = (f32[2,8,128]{2,1,0:T(8,128)S(1)}, f32[2,8,128]{2,1,0:T(8,128)S(1)}, u32[]{:S(2)}, u32[]{:S(2)}) collective-permute-start(f32[2,8,128]{2,1,0:T(8,128)S(1)} %get-tuple-element.30.first_ref), channel_id=1, source_target_pairs={{0,1},{1,2},{2,3},{3,4},{4,5},{5,6},{6,7},{7,8},{8,9},{9,10},{10,1... | collective-permute-start | bytes 24584 | tf_op jit(solution)/shard_map/ppermute | solution.py:406
  53.5 2.1 %collective-permute-start.7 = (f32[2,8,128]{2,1,0:T(8,128)S(1)}, f32[2,8,128]{2,1,0:T(8,128)S(1)}, u32[]{:S(2)}, u32[]{:S(2)}) collective-permute-start(f32[2,8,128]{2,1,0:T(8,128)S(1)} %get-tuple-element.30.first_ref), channel_id=1, source_target_pairs={{1,0},{2,1},{3,2},{4,3},{5,4},{6,5},{7,6},{8,7},{9,8},{10,9},{11,1... | collective-permute-start | bytes 24584 | tf_op jit(solution)/shard_map/ppermute | solution.py:407
  55.6 0.0 collective-permute-done.4.before_ref
  55.6 0.0 collective-permute-done.5.after_ref
  55.6 0.0 collective-permute-done.6.left_ref
  55.6 2.8 %collective-permute-done.7.right_ref = f32[2,8,128]{2,1,0:T(8,128)S(1)} collective-permute-done((f32[2,8,128]{2,1,0:T(8,128)S(1)}, f32[2,8,128]{2,1,0:T(8,128)S(1)}, u32[]{:S(2)}, u32[]{:S(2)}) %collective-permute-start.7) | collective-permute-done | bytes 8224 | tf_op jit(solution)/shard_map/ppermute | solution.py:407
  58.4 0.2 surface.1
  58.7 0.0 copy-start.5
  58.7 0.6 copy-done.5
  59.3 11.4 %all-to-all-start.1 = ((bf16[64,8,128]{2,1,0:T(8,128)(2,1)}), bf16[64,8,128]{2,1,0:T(8,128)(2,1)S(1)}, u32[]{:S(2)}, u32[]{:S(2)}) async-start(bf16[64,8,128]{2,1,0:T(8,128)(2,1)} %copy-done.5), calls=%async_computation.1 | async-start | bytes 262144 | tf_op jit(solution)/shard_map/all_to_all | solution.py:413
  70.7 0.0 copy-done.1
  70.7 2.4 %ocean.1 = (f32[2,80,8,128]{3,2,1,0:T(8,128)}, f32[128,128]{1,0:T(8,128)S(1)}) custom-call(f32[80,80]{1,0:T(8,128)S(1)} %copy-done.4, f32[2,8,80,128]{3,2,1,0:T(8,128)S(1)} %get-tuple-element.25.twice_ref, f32[2,8,128]{2,1,0:T(8,128)S(1)} %get-tuple-element.32.spread_ref, f32[2,8,128]{2,1,0:T(8,128)S(1)} %get-tuple-element.33.second_ref, ...), custom_call_target="tpu_custom_call" | custom-call | flops 157286400 | bytes 2097152 | tf_op jit(solution)/shard_map/ocean/pallas_call | solution.py:414
  73.1 8.0 %all-to-all-done.1.returned_ref = bf16[64,8,128]{2,1,0:T(8,128)(2,1)S(1)} async-done(((bf16[64,8,128]{2,1,0:T(8,128)(2,1)}), bf16[64,8,128]{2,1,0:T(8,128)(2,1)S(1)}, u32[]{:S(2)}, u32[]{:S(2)}) %all-to-all-start.1) | async-done | bytes 131104 | tf_op jit(solution)/shard_map/all_to_all | solution.py:413
  81.1 0.0 copy-done.9
  81.1 2.1 %backward.1 = f32[64,2,128]{2,1,0:T(2,128)} custom-call(s32[64]{0:T(128)S(1)} %bitcast.17, s32[64]{0:T(128)S(1)} %get-tuple-element.35.slot_ref, bf16[64,8,128]{2,1,0:T(8,128)(2,1)S(1)} %all-to-all-done.1.returned_ref, bf16[64,128,128]{2,1,0:T(8,128)(2,1)S(1)} %bitcast.12, f32[128,128]{1,0:T(8,128)S(1)} %get-tuple-element.37.sums_ref), custom_call_target="tpu_custom_call" | custom-call | flops 16777216 | bytes 3145728 | tf_op jit(solution)/shard_map/backward/pallas_call | solution.py:418
  (1 shorter events, 0.0 us)
Async XLA Ops:
  0.6 17.4 %copy-start.6 = (s32[8,128]{1,0:T(8,128)S(1)}, s32[8,128]{1,0:T(8,128)}, u32[]{:S(2)}) copy-start(s32[8,128]{1,0:T(8,128)} %mask_ref.5) | copy-start | bytes 12292
  0.6 1.6 %copy-start = (bf16[1,64,128,128]{3,2,1,0:T(8,128)(2,1)S(1)}, bf16[1,64,128,128]{3,2,1,0:T(8,128)(2,1)}, u32[]{:S(2)}) copy-start(bf16[1,64,128,128]{3,2,1,0:T(8,128)(2,1)} %param.9) | copy-start | bytes 6291460
  2.2 0.9 %copy-start.3 = (bf16[1,64,16,128]{3,2,1,0:T(8,128)(2,1)S(1)}, bf16[1,64,16,128]{3,2,1,0:T(8,128)(2,1)}, u32[]{:S(2)}) copy-start(bf16[1,64,16,128]{3,2,1,0:T(8,128)(2,1)} %param.8) | copy-start | bytes 786436
  3.2 0.7 copy-start.8
  3.8 0.7 copy-start.10
  4.5 13.5 %copy-start.2 = (f32[2,80,8,128]{3,2,1,0:T(8,128)S(1)}, f32[2,80,8,128]{3,2,1,0:T(8,128)}, u32[]{:S(2)}) copy-start(f32[2,80,8,128]{3,2,1,0:T(8,128)} %param.12) | copy-start | bytes 1966084
  4.5 37.4 %copy-start.4 = (f32[80,80]{1,0:T(8,128)S(1)}, f32[80,80]{1,0:T(8,128)}, u32[]{:S(2)}) copy-start(f32[80,80]{1,0:T(8,128)} %mixing_ref.3) | copy-start | bytes 76804
  7.2 36.6 %copy-start.7 = (f32[8,128]{1,0:T(8,128)S(1)}, f32[8,128]{1,0:T(8,128)}, u32[]{:S(2)}) copy-start(f32[8,128]{1,0:T(8,128)} %wet_ref.1) | copy-start | bytes 12292
  7.2 36.6 %all-to-all-start = ((bf16[64,40,128]{2,1,0:T(8,128)(2,1)}), bf16[64,40,128]{2,1,0:T(8,128)(2,1)S(1)}, u32[]{:S(2)}, u32[]{:S(2)}) async-start(bf16[64,40,128]{2,1,0:T(8,128)(2,1)} %get-tuple-element.26), calls=%async_computation | async-start | bytes 1310720 | tf_op jit(solution)/shard_map/all_to_all | solution.py:378
  18.2 52.5 %copy-start.1 = (bf16[1,64,128,128]{3,2,1,0:T(8,128)(2,1)S(1)}, bf16[1,64,128,128]{3,2,1,0:T(8,128)(2,1)}, u32[]{:S(2)}) copy-start(bf16[1,64,128,128]{3,2,1,0:T(8,128)(2,1)} %param.9) | copy-start | bytes 6291460
  18.2 7.5 %collective-permute-start = (f32[2,168,128]{2,1,0:T(8,128)S(1)}, f32[2,168,128]{2,1,0:T(8,128)S(1)}, u32[]{:S(2)}, u32[]{:S(2)}) collective-permute-start(f32[2,168,128]{2,1,0:T(8,128)S(1)} %get-tuple-element.20), channel_id=1, source_target_pairs={{0,64},{64,128},{128,192},{192,256},{256,320},{320,384},{384,448},... | collective-permute-start | bytes 516104 | tf_op jit(solution)/shard_map/ppermute | solution.py:383
  22.3 9.2 %collective-permute-start.1 = (f32[2,168,128]{2,1,0:T(8,128)S(1)}, f32[2,168,128]{2,1,0:T(8,128)S(1)}, u32[]{:S(2)}, u32[]{:S(2)}) collective-permute-start(f32[2,168,128]{2,1,0:T(8,128)S(1)} %get-tuple-element.21), channel_id=1, source_target_pairs={{64,0},{128,64},{192,128},{256,192},{320,256},{384,320},{448,384},... | collective-permute-start | bytes 516104 | tf_op jit(solution)/shard_map/ppermute | solution.py:384
  32.4 6.4 %collective-permute-start.2 = (f32[40,128]{1,0:T(8,128)S(1)}, f32[40,128]{1,0:T(8,128)S(1)}, u32[]{:S(2)}, u32[]{:S(2)}) collective-permute-start(f32[40,128]{1,0:T(8,128)S(1)} %get-tuple-element.24.last_ref), channel_id=1, source_target_pairs={{0,1},{1,2},{2,3},{3,4},{4,5},{5,6},{6,7},{7,8},{8,9},{9,10},{10,1... | collective-permute-start | bytes 61448 | tf_op jit(solution)/shard_map/ppermute | solution.py:390
  36.8 5.1 %collective-permute-start.3 = (f32[40,128]{1,0:T(8,128)S(1)}, f32[40,128]{1,0:T(8,128)S(1)}, u32[]{:S(2)}, u32[]{:S(2)}) collective-permute-start(f32[40,128]{1,0:T(8,128)S(1)} %get-tuple-element.23.first_ref), channel_id=1, source_target_pairs={{1,0},{2,1},{3,2},{4,3},{5,4},{6,5},{7,6},{8,7},{9,8},{10,9},{11,1... | collective-permute-start | bytes 61448 | tf_op jit(solution)/shard_map/ppermute | solution.py:391
  43.8 37.3 %copy-start.9 = (s32[1,64,1]{1,2,0:T(1,128)S(1)}, s32[1,64,1]{1,2,0:T(1,128)}, u32[]{:S(2)}) copy-start(s32[1,64,1]{1,2,0:T(1,128)} %param.10) | copy-start | bytes 772
  44.7 10.8 %collective-permute-start.4 = (f32[2,8,128]{2,1,0:T(8,128)S(1)}, f32[2,8,128]{2,1,0:T(8,128)S(1)}, u32[]{:S(2)}, u32[]{:S(2)}) collective-permute-start(f32[2,8,128]{2,1,0:T(8,128)S(1)} %get-tuple-element.30.first_ref), channel_id=1, source_target_pairs={{0,64},{64,128},{128,192},{192,256},{256,320},{320,384},{384,448},... | collective-permute-start | bytes 24584 | tf_op jit(solution)/shard_map/ppermute | solution.py:404
  49.3 6.3 %collective-permute-start.5 = (f32[2,8,128]{2,1,0:T(8,128)S(1)}, f32[2,8,128]{2,1,0:T(8,128)S(1)}, u32[]{:S(2)}, u32[]{:S(2)}) collective-permute-start(f32[2,8,128]{2,1,0:T(8,128)S(1)} %get-tuple-element.30.first_ref), channel_id=1, source_target_pairs={{64,0},{128,64},{192,128},{256,192},{320,256},{384,320},{448,384},... | collective-permute-start | bytes 24584 | tf_op jit(solution)/shard_map/ppermute | solution.py:405
  51.2 4.4 %collective-permute-start.6 = (f32[2,8,128]{2,1,0:T(8,128)S(1)}, f32[2,8,128]{2,1,0:T(8,128)S(1)}, u32[]{:S(2)}, u32[]{:S(2)}) collective-permute-start(f32[2,8,128]{2,1,0:T(8,128)S(1)} %get-tuple-element.30.first_ref), channel_id=1, source_target_pairs={{0,1},{1,2},{2,3},{3,4},{4,5},{5,6},{6,7},{7,8},{8,9},{9,10},{10,1... | collective-permute-start | bytes 24584 | tf_op jit(solution)/shard_map/ppermute | solution.py:406
  53.5 5.0 %collective-permute-start.7 = (f32[2,8,128]{2,1,0:T(8,128)S(1)}, f32[2,8,128]{2,1,0:T(8,128)S(1)}, u32[]{:S(2)}, u32[]{:S(2)}) collective-permute-start(f32[2,8,128]{2,1,0:T(8,128)S(1)} %get-tuple-element.30.first_ref), channel_id=1, source_target_pairs={{1,0},{2,1},{3,2},{4,3},{5,4},{6,5},{7,6},{8,7},{9,8},{10,9},{11,1... | collective-permute-start | bytes 24584 | tf_op jit(solution)/shard_map/ppermute | solution.py:407
  58.7 0.7 copy-start.5
  59.3 21.8 %all-to-all-start.1 = ((bf16[64,8,128]{2,1,0:T(8,128)(2,1)}), bf16[64,8,128]{2,1,0:T(8,128)(2,1)S(1)}, u32[]{:S(2)}, u32[]{:S(2)}) async-start(bf16[64,8,128]{2,1,0:T(8,128)(2,1)} %copy-done.5), calls=%async_computation.1 | async-start | bytes 262144 | tf_op jit(solution)/shard_map/all_to_all | solution.py:413

commit v4 on v3

--- a/solution.py
+++ b/solution.py
@@ -32,6 +32,10 @@
         compiler_params=pltpu.CompilerParams(vmem_limit_bytes=16 << 20),
         cost_estimate=pl.CostEstimate(flops=flops, bytes_accessed=moved, transcendentals=0),
     )
+
+
+def in_hbm(*values):
+    return [pltpu.with_memory_space_constraint(v, pltpu.HBM) for v in values]
 
 
 def shape(*dims, dtype=f32):
@@ -365,7 +369,7 @@
 
     packed, slot = call(
         forward_kernel, "forward",
-        (shape(blocks, 2 * fields + 8, width, dtype=bf16), shape(tiles, dtype=jnp.int32)),
+        (pltpu.HBM((blocks, 2 * fields + 8, width), bf16), shape(tiles, dtype=jnp.int32)),
         [hbm] * 4, [vmem, smem],
         [
             pltpu.SMEM((tiles,), jnp.int32), pltpu.SMEM((tiles,), jnp.int32),
@@ -374,7 +378,7 @@
             pltpu.SemaphoreType.DMA((3,)), pltpu.SemaphoreType.DMA((min(4, tiles // 2),)),
         ],
         flops=2 * tiles * fields * width * width, moved=3 << 20,
-    )(block, row, atm_flux[0], weights)
+    )(*in_hbm(block, row, atm_flux[0], weights))
     received = lax.all_to_all(packed, "blk", split_axis=0, concat_axis=0, tiled=True)
 
     top, bottom = call(
@@ -407,7 +411,7 @@
     first_right = lax.ppermute(first, "blk", down_blk)
     spread_first, back = call(
         surface_kernel, "surface",
-        (shape(tracers, rows, width), shape(blocks, 8, width, dtype=bf16)),
+        (shape(tracers, rows, width), pltpu.HBM((blocks, 8, width), bf16)),
         [vmem] * 8, moved=1 << 20,
     )(received, first, first_before, first_after, first_left, first_right, base, step_weights)
     returned = lax.all_to_all(back, "blk", split_axis=0, concat_axis=0, tiled=True)

time: 83.7 us -> 80.5 us (0.962)
  local copies, waits for them, and re-layouts: 4.53 us -> 0.03 us
  Pallas kernels: 11.1 us -> 12.3 us
    unnamed x22 -> x12, local copies, waits for them, and re-layouts: 4.52 us -> 0.03 us
    pallas_call x2, Pallas kernels: 2.88 us -> 4.12 us  [the longest x1 3.24 us: per_device(): call(forward_kernel, 'forward', (pltpu.HBM((blocks, 2 * fields + 8, width...]
where the time goes in v4:
time: 80.5 us; the launch traced here: 80 us
  starting transfers between devices  45.5 us (57%)
  waiting for transfers between devices  21.3 us (26%)
  Pallas kernels  12.3 us (15%)
  between operations  0.87 us (1%)
    all_to_all x1, starting transfers between devices, per_device(): lax.all_to_all(back, 'blk', split_axis=0, concat_axis=0, tiled=True)  11.4 us
    all_to_all x1, starting transfers between devices, per_device(): lax.all_to_all(packed, 'blk', split_axis=0, concat_axis=0, tiled=True)  10.8 us
    all_to_all x1, waiting for transfers between devices, per_device(): lax.all_to_all(back, 'blk', split_axis=0, concat_axis=0, tiled=True)  7.98 us
    ppermute x1, waiting for transfers between devices, per_device(): after = lax.ppermute(top, 'sec', down_sec)  5.85 us
    ppermute x1, starting transfers between devices, per_device(): first_before = lax.ppermute(first, 'sec', up_sec)  4.57 us
    ppermute x1, starting transfers between devices, per_device(): left = lax.ppermute(last_columns, 'blk', up_blk)  4.47 us
    ppermute x1, starting transfers between devices, per_device(): before = lax.ppermute(bottom, 'sec', up_sec)  4.13 us
    pallas_call x1, Pallas kernels, per_device(): call(forward_kernel, 'forward', (pltpu.HBM((blocks, 2 * fields + 8, width...  3.24 us
  transfers between devices with their start and end apart: 10, of which 5 were waited for; matrix products, arithmetic and copies ran while one was open for 0% of the time, Pallas kernels for 6%

profile of v4, /device:TPU:129, one launch (start us, length us, event | category | flops | bytes accessed | tf_op | source)
XLA Modules:
  0.0 80.0 jit_solution(1795827033903263311)
XLA Ops:
  0.6 0.0 copy-start.1
  0.6 0.0 copy-start.3
  0.7 0.0 copy-start.2
  0.7 3.2 %forward.1 = (bf16[64,40,128]{2,1,0:T(8,128)(2,1)}, s32[64]{0:T(128)S(1)}) custom-call(s32[64]{0:T(128)} %bitcast.15, s32[64]{0:T(128)} %bitcast.19, bf16[64,16,128]{2,1,0:T(8,128)(2,1)} %bitcast.17, bf16[64,128,128]{2,1,0:T(8,128)(2,1)} %bitcast.10), custom_call_target="tpu_custom_call" | custom-call | flops 33554432 | bytes 3145728 | tf_op jit(solution)/shard_map/forward/pallas_call | solution.py:370
  3.9 0.0 copy-start.4
  3.9 10.8 %all-to-all-start = ((bf16[64,40,128]{2,1,0:T(8,128)(2,1)}), bf16[64,40,128]{2,1,0:T(8,128)(2,1)S(1)}, u32[]{:S(2)}, u32[]{:S(2)}) async-start(bf16[64,40,128]{2,1,0:T(8,128)(2,1)} %get-tuple-element.26), calls=%async_computation | async-start | bytes 1310720 | tf_op jit(solution)/shard_map/all_to_all | solution.py:382
  14.7 0.0 copy-done.1
  14.7 0.0 copy-done.3
  14.8 0.2 rows.1
  14.9 0.0 copy-start
  14.9 4.1 %collective-permute-start = (f32[2,168,128]{2,1,0:T(8,128)S(1)}, f32[2,168,128]{2,1,0:T(8,128)S(1)}, u32[]{:S(2)}, u32[]{:S(2)}) collective-permute-start(f32[2,168,128]{2,1,0:T(8,128)S(1)} %get-tuple-element.20), channel_id=1, source_target_pairs={{0,64},{64,128},{128,192},{192,256},{256,320},{320,384},{384,448},... | collective-permute-start | bytes 516104 | tf_op jit(solution)/shard_map/ppermute | solution.py:387
  19.1 1.9 %collective-permute-start.1 = (f32[2,168,128]{2,1,0:T(8,128)S(1)}, f32[2,168,128]{2,1,0:T(8,128)S(1)}, u32[]{:S(2)}, u32[]{:S(2)}) collective-permute-start(f32[2,168,128]{2,1,0:T(8,128)S(1)} %get-tuple-element.21), channel_id=1, source_target_pairs={{64,0},{128,64},{192,128},{256,192},{320,256},{384,320},{448,384},... | collective-permute-start | bytes 516104 | tf_op jit(solution)/shard_map/ppermute | solution.py:388
  21.0 1.5 %collective-permute-done.before_ref = f32[2,168,128]{2,1,0:T(8,128)S(1)} collective-permute-done((f32[2,168,128]{2,1,0:T(8,128)S(1)}, f32[2,168,128]{2,1,0:T(8,128)S(1)}, u32[]{:S(2)}, u32[]{:S(2)}) %collective-permute-start) | collective-permute-done | bytes 172064 | tf_op jit(solution)/shard_map/ppermute | solution.py:387
  22.5 5.9 %collective-permute-done.1.after_ref = f32[2,168,128]{2,1,0:T(8,128)S(1)} collective-permute-done((f32[2,168,128]{2,1,0:T(8,128)S(1)}, f32[2,168,128]{2,1,0:T(8,128)S(1)}, u32[]{:S(2)}, u32[]{:S(2)}) %collective-permute-start.1) | collective-permute-done | bytes 172064 | tf_op jit(solution)/shard_map/ppermute | solution.py:388
  28.3 0.8 columns.1
  29.1 4.5 %collective-permute-start.2 = (f32[40,128]{1,0:T(8,128)S(1)}, f32[40,128]{1,0:T(8,128)S(1)}, u32[]{:S(2)}, u32[]{:S(2)}) collective-permute-start(f32[40,128]{1,0:T(8,128)S(1)} %get-tuple-element.24.last_ref), channel_id=1, source_target_pairs={{0,1},{1,2},{2,3},{3,4},{4,5},{5,6},{6,7},{7,8},{8,9},{9,10},{10,1... | collective-permute-start | bytes 61448 | tf_op jit(solution)/shard_map/ppermute | solution.py:394
  33.6 1.9 %collective-permute-start.3 = (f32[40,128]{1,0:T(8,128)S(1)}, f32[40,128]{1,0:T(8,128)S(1)}, u32[]{:S(2)}, u32[]{:S(2)}) collective-permute-start(f32[40,128]{1,0:T(8,128)S(1)} %get-tuple-element.23.first_ref), channel_id=1, source_target_pairs={{1,0},{2,1},{3,2},{4,3},{5,4},{6,5},{7,6},{8,7},{9,8},{10,9},{11,1... | collective-permute-start | bytes 61448 | tf_op jit(solution)/shard_map/ppermute | solution.py:395
  35.5 0.0 collective-permute-done.2.left_ref
  35.5 3.2 %collective-permute-done.3.right_ref = f32[40,128]{1,0:T(8,128)S(1)} collective-permute-done((f32[40,128]{1,0:T(8,128)S(1)}, f32[40,128]{1,0:T(8,128)S(1)}, u32[]{:S(2)}, u32[]{:S(2)}) %collective-permute-start.3) | collective-permute-done | bytes 20512 | tf_op jit(solution)/shard_map/ppermute | solution.py:395
  38.7 0.0 copy-done.2
  38.7 1.9 %stencil.1 = (f32[2,8,80,128]{3,2,1,0:T(8,128)S(1)}, f32[2,8,128]{2,1,0:T(8,128)S(1)}, f32[2,8,128]{2,1,0:T(8,128)S(1)}, f32[7,8,128]{2,1,0:T(8,128)S(1)}) custom-call(f32[12,168,128]{2,1,0:T(8,128)S(1)} %get-tuple-element.22.slab_ref, f32[40,128]{1,0:T(8,128)S(1)} %get-tuple-element.23.first_ref, f32[40,128]{1,0:T(8,128)S(1)} %get-tuple-element.24.last_ref, ...), custom_call_target="tpu_custom_call" | custom-call | flops 20971520 | bytes 3145728 | tf_op jit(solution)/shard_map/stencil/pallas_call | solution.py:396
  40.5 0.0 all-to-all-done.received_ref
  40.6 0.0 copy-done.4
  40.6 0.0 copy-start.5
  40.6 0.9 %drive.1 = (f32[2,8,128]{2,1,0:T(8,128)S(1)}, f32[2,8,128]{2,1,0:T(8,128)S(1)}, f32[2,8,128]{2,1,0:T(8,128)S(1)}) custom-call(bf16[64,40,128]{2,1,0:T(8,128)(2,1)S(1)} %all-to-all-done.received_ref, f32[2,8,128]{2,1,0:T(8,128)S(1)} %slice_bitcast_fusion.top_ref, s32[8,128]{1,0:T(8,128)S(1)} %copy-done.3, f32[8,128]{1,0:T(8,128)S(1)} %copy-done.4, ...), custom_call_target="tpu_custom_call" | custom-call | bytes 1048576 | tf_op jit(solution)/shard_map/drive/pallas_call | solution.py:405
  41.5 4.6 %collective-permute-start.4 = (f32[2,8,128]{2,1,0:T(8,128)S(1)}, f32[2,8,128]{2,1,0:T(8,128)S(1)}, u32[]{:S(2)}, u32[]{:S(2)}) collective-permute-start(f32[2,8,128]{2,1,0:T(8,128)S(1)} %get-tuple-element.30.first_ref), channel_id=1, source_target_pairs={{0,64},{64,128},{128,192},{192,256},{256,320},{320,384},{384,448},... | collective-permute-start | bytes 24584 | tf_op jit(solution)/shard_map/ppermute | solution.py:408
  46.1 1.9 %collective-permute-start.5 = (f32[2,8,128]{2,1,0:T(8,128)S(1)}, f32[2,8,128]{2,1,0:T(8,128)S(1)}, u32[]{:S(2)}, u32[]{:S(2)}) collective-permute-start(f32[2,8,128]{2,1,0:T(8,128)S(1)} %get-tuple-element.30.first_ref), channel_id=1, source_target_pairs={{64,0},{128,64},{192,128},{256,192},{320,256},{384,320},{448,384},... | collective-permute-start | bytes 24584 | tf_op jit(solution)/shard_map/ppermute | solution.py:409
  48.0 2.2 %collective-permute-start.6 = (f32[2,8,128]{2,1,0:T(8,128)S(1)}, f32[2,8,128]{2,1,0:T(8,128)S(1)}, u32[]{:S(2)}, u32[]{:S(2)}) collective-permute-start(f32[2,8,128]{2,1,0:T(8,128)S(1)} %get-tuple-element.30.first_ref), channel_id=1, source_target_pairs={{0,1},{1,2},{2,3},{3,4},{4,5},{5,6},{6,7},{7,8},{8,9},{9,10},{10,1... | collective-permute-start | bytes 24584 | tf_op jit(solution)/shard_map/ppermute | solution.py:410
  50.2 2.1 %collective-permute-start.7 = (f32[2,8,128]{2,1,0:T(8,128)S(1)}, f32[2,8,128]{2,1,0:T(8,128)S(1)}, u32[]{:S(2)}, u32[]{:S(2)}) collective-permute-start(f32[2,8,128]{2,1,0:T(8,128)S(1)} %get-tuple-element.30.first_ref), channel_id=1, source_target_pairs={{1,0},{2,1},{3,2},{4,3},{5,4},{6,5},{7,6},{8,7},{9,8},{10,9},{11,1... | collective-permute-start | bytes 24584 | tf_op jit(solution)/shard_map/ppermute | solution.py:411
  52.4 0.0 collective-permute-done.4.before_ref
  52.4 0.0 collective-permute-done.5.after_ref
  52.4 0.0 collective-permute-done.6.left_ref
  52.4 2.8 %collective-permute-done.7.right_ref = f32[2,8,128]{2,1,0:T(8,128)S(1)} collective-permute-done((f32[2,8,128]{2,1,0:T(8,128)S(1)}, f32[2,8,128]{2,1,0:T(8,128)S(1)}, u32[]{:S(2)}, u32[]{:S(2)}) %collective-permute-start.7) | collective-permute-done | bytes 8224 | tf_op jit(solution)/shard_map/ppermute | solution.py:411
  55.2 0.9 %surface.1 = (f32[2,8,128]{2,1,0:T(8,128)S(1)}, bf16[64,8,128]{2,1,0:T(8,128)(2,1)}) custom-call(bf16[64,40,128]{2,1,0:T(8,128)(2,1)S(1)} %all-to-all-done.received_ref, f32[2,8,128]{2,1,0:T(8,128)S(1)} %get-tuple-element.30.first_ref, f32[2,8,128]{2,1,0:T(8,128)S(1)} %collective-permute-done.4.before_ref, ...), custom_call_target="tpu_custom_call" | custom-call | bytes 1048576 | tf_op jit(solution)/shard_map/surface/pallas_call | solution.py:412
  56.1 11.4 %all-to-all-start.1 = ((bf16[64,8,128]{2,1,0:T(8,128)(2,1)}), bf16[64,8,128]{2,1,0:T(8,128)(2,1)S(1)}, u32[]{:S(2)}, u32[]{:S(2)}) async-start(bf16[64,8,128]{2,1,0:T(8,128)(2,1)} %get-tuple-element.36), calls=%async_computation.1 | async-start | bytes 262144 | tf_op jit(solution)/shard_map/all_to_all | solution.py:417
  67.5 0.0 copy-done
  67.5 2.4 %ocean.1 = (f32[2,80,8,128]{3,2,1,0:T(8,128)}, f32[128,128]{1,0:T(8,128)S(1)}) custom-call(f32[80,80]{1,0:T(8,128)S(1)} %copy-done.2, f32[2,8,80,128]{3,2,1,0:T(8,128)S(1)} %get-tuple-element.25.twice_ref, f32[2,8,128]{2,1,0:T(8,128)S(1)} %get-tuple-element.32.spread_ref, f32[2,8,128]{2,1,0:T(8,128)S(1)} %get-tuple-element.33.second_ref, ...), custom_call_target="tpu_custom_call" | custom-call | flops 157286400 | bytes 2097152 | tf_op jit(solution)/shard_map/ocean/pallas_call | solution.py:418
  69.9 8.0 %all-to-all-done.1.returned_ref = bf16[64,8,128]{2,1,0:T(8,128)(2,1)S(1)} async-done(((bf16[64,8,128]{2,1,0:T(8,128)(2,1)}), bf16[64,8,128]{2,1,0:T(8,128)(2,1)S(1)}, u32[]{:S(2)}, u32[]{:S(2)}) %all-to-all-start.1) | async-done | bytes 131104 | tf_op jit(solution)/shard_map/all_to_all | solution.py:417
  77.9 0.0 copy-done.5
  77.9 2.1 %backward.1 = f32[64,2,128]{2,1,0:T(2,128)} custom-call(s32[64]{0:T(128)S(1)} %bitcast.16, s32[64]{0:T(128)S(1)} %get-tuple-element.35.slot_ref, bf16[64,8,128]{2,1,0:T(8,128)(2,1)S(1)} %all-to-all-done.1.returned_ref, bf16[64,128,128]{2,1,0:T(8,128)(2,1)S(1)} %bitcast.12, f32[128,128]{1,0:T(8,128)S(1)} %get-tuple-element.37.sums_ref), custom_call_target="tpu_custom_call" | custom-call | flops 16777216 | bytes 3145728 | tf_op jit(solution)/shard_map/backward/pallas_call | solution.py:422
  (1 shorter events, 0.0 us)
Async XLA Ops:
  0.6 14.1 %copy-start.1 = (f32[2,80,8,128]{3,2,1,0:T(8,128)S(1)}, f32[2,80,8,128]{3,2,1,0:T(8,128)}, u32[]{:S(2)}) copy-start(f32[2,80,8,128]{3,2,1,0:T(8,128)} %param.12) | copy-start | bytes 1966084
  0.6 14.1 %copy-start.3 = (s32[8,128]{1,0:T(8,128)S(1)}, s32[8,128]{1,0:T(8,128)}, u32[]{:S(2)}) copy-start(s32[8,128]{1,0:T(8,128)} %mask_ref.5) | copy-start | bytes 12292
  0.7 38.0 %copy-start.2 = (f32[80,80]{1,0:T(8,128)S(1)}, f32[80,80]{1,0:T(8,128)}, u32[]{:S(2)}) copy-start(f32[80,80]{1,0:T(8,128)} %mixing_ref.3) | copy-start | bytes 76804
  3.9 36.7 %copy-start.4 = (f32[8,128]{1,0:T(8,128)S(1)}, f32[8,128]{1,0:T(8,128)}, u32[]{:S(2)}) copy-start(f32[8,128]{1,0:T(8,128)} %wet_ref.1) | copy-start | bytes 12292
  3.9 36.6 %all-to-all-start = ((bf16[64,40,128]{2,1,0:T(8,128)(2,1)}), bf16[64,40,128]{2,1,0:T(8,128)(2,1)S(1)}, u32[]{:S(2)}, u32[]{:S(2)}) async-start(bf16[64,40,128]{2,1,0:T(8,128)(2,1)} %get-tuple-element.26), calls=%async_computation | async-start | bytes 1310720 | tf_op jit(solution)/shard_map/all_to_all | solution.py:382
  14.9 52.6 %copy-start = (bf16[1,64,128,128]{3,2,1,0:T(8,128)(2,1)S(1)}, bf16[1,64,128,128]{3,2,1,0:T(8,128)(2,1)}, u32[]{:S(2)}) copy-start(bf16[1,64,128,128]{3,2,1,0:T(8,128)(2,1)} %param.9) | copy-start | bytes 6291460
  14.9 7.5 %collective-permute-start = (f32[2,168,128]{2,1,0:T(8,128)S(1)}, f32[2,168,128]{2,1,0:T(8,128)S(1)}, u32[]{:S(2)}, u32[]{:S(2)}) collective-permute-start(f32[2,168,128]{2,1,0:T(8,128)S(1)} %get-tuple-element.20), channel_id=1, source_target_pairs={{0,64},{64,128},{128,192},{192,256},{256,320},{320,384},{384,448},... | collective-permute-start | bytes 516104 | tf_op jit(solution)/shard_map/ppermute | solution.py:387
  19.1 9.2 %collective-permute-start.1 = (f32[2,168,128]{2,1,0:T(8,128)S(1)}, f32[2,168,128]{2,1,0:T(8,128)S(1)}, u32[]{:S(2)}, u32[]{:S(2)}) collective-permute-start(f32[2,168,128]{2,1,0:T(8,128)S(1)} %get-tuple-element.21), channel_id=1, source_target_pairs={{64,0},{128,64},{192,128},{256,192},{320,256},{384,320},{448,384},... | collective-permute-start | bytes 516104 | tf_op jit(solution)/shard_map/ppermute | solution.py:388
  29.1 6.4 %collective-permute-start.2 = (f32[40,128]{1,0:T(8,128)S(1)}, f32[40,128]{1,0:T(8,128)S(1)}, u32[]{:S(2)}, u32[]{:S(2)}) collective-permute-start(f32[40,128]{1,0:T(8,128)S(1)} %get-tuple-element.24.last_ref), channel_id=1, source_target_pairs={{0,1},{1,2},{2,3},{3,4},{4,5},{5,6},{6,7},{7,8},{8,9},{9,10},{10,1... | collective-permute-start | bytes 61448 | tf_op jit(solution)/shard_map/ppermute | solution.py:394
  33.6 5.1 %collective-permute-start.3 = (f32[40,128]{1,0:T(8,128)S(1)}, f32[40,128]{1,0:T(8,128)S(1)}, u32[]{:S(2)}, u32[]{:S(2)}) collective-permute-start(f32[40,128]{1,0:T(8,128)S(1)} %get-tuple-element.23.first_ref), channel_id=1, source_target_pairs={{1,0},{2,1},{3,2},{4,3},{5,4},{6,5},{7,6},{8,7},{9,8},{10,9},{11,1... | collective-permute-start | bytes 61448 | tf_op jit(solution)/shard_map/ppermute | solution.py:395
  40.6 37.3 %copy-start.5 = (s32[1,64,1]{1,2,0:T(1,128)S(1)}, s32[1,64,1]{1,2,0:T(1,128)}, u32[]{:S(2)}) copy-start(s32[1,64,1]{1,2,0:T(1,128)} %param.10) | copy-start | bytes 772
  41.5 10.8 %collective-permute-start.4 = (f32[2,8,128]{2,1,0:T(8,128)S(1)}, f32[2,8,128]{2,1,0:T(8,128)S(1)}, u32[]{:S(2)}, u32[]{:S(2)}) collective-permute-start(f32[2,8,128]{2,1,0:T(8,128)S(1)} %get-tuple-element.30.first_ref), channel_id=1, source_target_pairs={{0,64},{64,128},{128,192},{192,256},{256,320},{320,384},{384,448},... | collective-permute-start | bytes 24584 | tf_op jit(solution)/shard_map/ppermute | solution.py:408
  46.1 6.3 %collective-permute-start.5 = (f32[2,8,128]{2,1,0:T(8,128)S(1)}, f32[2,8,128]{2,1,0:T(8,128)S(1)}, u32[]{:S(2)}, u32[]{:S(2)}) collective-permute-start(f32[2,8,128]{2,1,0:T(8,128)S(1)} %get-tuple-element.30.first_ref), channel_id=1, source_target_pairs={{64,0},{128,64},{192,128},{256,192},{320,256},{384,320},{448,384},... | collective-permute-start | bytes 24584 | tf_op jit(solution)/shard_map/ppermute | solution.py:409
  48.0 4.4 %collective-permute-start.6 = (f32[2,8,128]{2,1,0:T(8,128)S(1)}, f32[2,8,128]{2,1,0:T(8,128)S(1)}, u32[]{:S(2)}, u32[]{:S(2)}) collective-permute-start(f32[2,8,128]{2,1,0:T(8,128)S(1)} %get-tuple-element.30.first_ref), channel_id=1, source_target_pairs={{0,1},{1,2},{2,3},{3,4},{4,5},{5,6},{6,7},{7,8},{8,9},{9,10},{10,1... | collective-permute-start | bytes 24584 | tf_op jit(solution)/shard_map/ppermute | solution.py:410
  50.2 5.0 %collective-permute-start.7 = (f32[2,8,128]{2,1,0:T(8,128)S(1)}, f32[2,8,128]{2,1,0:T(8,128)S(1)}, u32[]{:S(2)}, u32[]{:S(2)}) collective-permute-start(f32[2,8,128]{2,1,0:T(8,128)S(1)} %get-tuple-element.30.first_ref), channel_id=1, source_target_pairs={{1,0},{2,1},{3,2},{4,3},{5,4},{6,5},{7,6},{8,7},{9,8},{10,9},{11,1... | collective-permute-start | bytes 24584 | tf_op jit(solution)/shard_map/ppermute | solution.py:411
  56.1 21.8 %all-to-all-start.1 = ((bf16[64,8,128]{2,1,0:T(8,128)(2,1)}), bf16[64,8,128]{2,1,0:T(8,128)(2,1)S(1)}, u32[]{:S(2)}, u32[]{:S(2)}) async-start(bf16[64,8,128]{2,1,0:T(8,128)(2,1)} %get-tuple-element.36), calls=%async_computation.1 | async-start | bytes 262144 | tf_op jit(solution)/shard_map/all_to_all | solution.py:417

commit v5 on v4

--- a/solution.py
+++ b/solution.py
@@ -52,7 +52,8 @@
 
 def forward_kernel(
     block_hbm, row_hbm, flux_hbm, weight_hbm, out_ref, slot_ref,
-    block_ref, row_ref, flux_ref, weight_ref, used_ref, code_ref, small_sems, weight_sems,
+    block_ref, row_ref, flux_ref, weight_ref, used_ref, code_ref, mapped_ref, edge_ref,
+    small_sems, weight_sems,
 ):
     blocks = out_ref.shape[0]
     tiles, fields, width = flux_ref.shape
@@ -69,26 +70,13 @@
     for copy in copies:
         copy.start()
     out_ref[...] = jnp.zeros_like(out_ref)
+    edge_ref[...] = jnp.zeros_like(edge_ref)
     for b in range(blocks):
         used_ref[b] = 0
         code_ref[b] = empty_code
         code_ref[blocks + b] = empty_code
-    copies[0].wait()
-    copies[1].wait()
-    for t in range(tiles):
-        b = block_ref[t]
-        s = used_ref[b]
-        used_ref[b] = s + 1
-        slot_ref[t] = s
-        code_ref[s * blocks + b] = row_ref[t]
-    line = line_iota((8, width))
-    extra = jnp.where(line % 2 == 1, 8.0, 0.0).astype(f32)
-    for b in range(blocks):
-        first = code_ref[b].astype(f32)
-        second = code_ref[blocks + b].astype(f32)
-        code = jnp.where(line < 2, first, jnp.where(line < 4, second, float(empty_code))) + extra
-        out_ref[b, 2 * fields : 2 * fields + 8, :] = code.astype(bf16)
-    copies[2].wait()
+    for copy in copies[:3]:
+        copy.wait()
     for t in range(0, tiles, 2):
         if t % size == 0:
             copies[3 + t // size].wait()
@@ -96,9 +84,37 @@
         fluxes = flux_ref[t : t + 2].reshape(2 * fields, width)
         remapped = jnp.dot(fluxes, both, preferred_element_type=f32)
         for i in range(2):
-            start = pl.multiple_of(slot_ref[t + i] * fields, fields)
-            value = remapped[i * fields : (i + 1) * fields, i * width : (i + 1) * width]
-            out_ref[block_ref[t + i], pl.ds(start, fields), :] = value.astype(bf16)
+            b = block_ref[t + i]
+            s = used_ref[b]
+            used_ref[b] = s + 1
+            slot_ref[t + i] = s
+            code_ref[s * blocks + b] = row_ref[t + i]
+            start = pl.multiple_of(s * fields, fields)
+            value = remapped[i * fields : (i + 1) * fields, i * width : (i + 1) * width].astype(bf16)
+            out_ref[b, pl.ds(start, fields), :] = value
+            mapped_ref[(t + i) * fields : (t + i + 1) * fields, :] = value
+    line = line_iota((8, width))
+    lane = lane_iota((8, width))
+    chosen = ((line == 0) & (lane == width - 1)) | ((line == 4) & (lane == 0))
+    edges = lax.dot_general(
+        jnp.where(chosen, 1.0, 0.0).astype(bf16), mapped_ref[...],
+        (((1,), (1,)), ((), ())), preferred_element_type=f32,
+    )
+    per = width // fields
+    for t in range(tiles):
+        b, r, s = block_ref[t], row_ref[t], slot_ref[t]
+        group = edges[:, t // per * width : (t // per + 1) * width]
+        turned = pltpu.roll(group, lax.rem(r + per - t % per, per) * fields, 1)
+        placed = jnp.where(lane // fields == r, turned, 0.0)
+        edge_ref[b + 2, pl.ds(4 + s, 1), :] = placed[0:1]
+        edge_ref[b, pl.ds(6 + s, 1), :] = placed[4:5]
+    extra = jnp.where(line % 2 == 1, 8.0, 0.0).astype(f32)
+    for b in range(blocks):
+        first = code_ref[b].astype(f32)
+        second = code_ref[blocks + b].astype(f32)
+        code = jnp.where(line < 2, first, second) + extra
+        last = jnp.where(line < 4, code, edge_ref[b + 1])
+        out_ref[b, 2 * fields : 2 * fields + 8, :] = last.astype(bf16)
 
 
 def rows_kernel(x_ref, mask_ref, top_ref, bottom_ref):
@@ -116,8 +132,15 @@
     return span, per, planes // 8, -(-planes // 8 // per)
 
 
-def columns_kernel(x_ref, mask_ref, before_ref, after_ref, slab_ref, first_ref, last_ref):
+def odd_block():
+    return lax.rem(lax.axis_index("blk"), 2) == 1
+
+
+def columns_kernel(
+    x_ref, mask_ref, wet_ref, before_ref, after_ref, slab_ref, first_ref, last_ref, near_ref, far_ref
+):
     planes, rows, width = x_ref.shape
+    levels = planes // 2
     span, per, groups, packs = packing(rows, planes, width)
     mask = mask_ref[...].astype(f32)
     for i in range(2):
@@ -150,6 +173,20 @@
             last = sum((turn(last, span * i) for i in range(1, per)), last)
         first_ref[8 * pack : 8 * pack + 8, :] = first
         last_ref[8 * pack : 8 * pack + 8, :] = last
+    first = jnp.zeros((8, width), f32)
+    last = jnp.zeros((8, width), f32)
+    for r in range(rows):
+        for k in range(2):
+            parts = [x_ref[k * levels, r : r + 1, :], mask[r : r + 1, :], wet_ref[r : r + 1, :]]
+            value = jnp.concatenate(parts + [jnp.zeros((5, width), f32)], axis=0)
+            start = 16 * r + 8 * k
+            first = jnp.where(lane == start, turn(value, start), first)
+            last = jnp.where(lane == start, turn(value, start + 1), last)
+    first_ref[8 * packs + 8 : 8 * packs + 16, :] = first
+    last_ref[8 * packs + 8 : 8 * packs + 16, :] = last
+    odd = odd_block()
+    near_ref[...] = jnp.where(odd, first_ref[...], last_ref[...])
+    far_ref[...] = jnp.where(odd, last_ref[...], first_ref[...])
 
 
 def spread(weight, planes):
@@ -169,8 +206,8 @@
 
 
 def stencil_kernel(
-    slab_ref, first_ref, last_ref, left_ref, right_ref, mixing_ref,
-    twice_ref, once_top_ref, twice_top_ref, weights_ref, work_ref,
+    slab_ref, first_ref, last_ref, near_ref, far_ref, mixing_ref,
+    twice_ref, once_top_ref, twice_top_ref, weights_ref, beside_ref, work_ref,
 ):
     rows = slab_ref.shape[0] - 4
     planes = slab_ref.shape[1] - 8
@@ -195,7 +232,13 @@
         right = jnp.where(at_end[:size], jnp.concatenate(rights, 0), pltpu.roll(center, width - 1, 1))
         return left, right
 
-    left_all, right_all = left_ref[...], right_ref[...]
+    odd = odd_block()
+    left_all = jnp.where(odd, near_ref[...], far_ref[...])
+    right_all = jnp.where(odd, far_ref[...], near_ref[...])
+    beside_ref[0] = left_all[packed + 8 :]
+    beside_ref[1] = right_all[packed + 8 :]
+    left_all, right_all = left_all[: packed + 8], right_all[: packed + 8]
+    first_all, last_all = first_ref[: packed + 8, :], last_ref[: packed + 8, :]
 
     def edge(own, outer_shift, beyond):
         around = (
@@ -207,8 +250,8 @@
         w = weights_of(own[packed:], [a[packed:] for a in around])
         return combine(w, [own[:packed]] + [a[:packed] for a in around], packed)
 
-    left_once = edge(left_all, 1, pltpu.roll(first_ref[...], 1, 1))
-    right_once = edge(right_all, width - 1, pltpu.roll(last_ref[...], width - 1, 1))
+    left_once = edge(left_all, 1, pltpu.roll(first_all, 1, 1))
+    right_once = edge(right_all, width - 1, pltpu.roll(last_all, width - 1, 1))
 
     saved = []
     for r in range(1, rows + 3):
@@ -246,15 +289,17 @@
 
 
 def drive_kernel(
-    received_ref, top_ref, mask_ref, wet_ref, once_top_ref, twice_top_ref, weights_ref,
-    first_ref, second_ref, base_ref,
+    received_ref, top_ref, mask_ref, wet_ref, once_top_ref, twice_top_ref, weights_ref, beside_ref,
+    first_ref, second_ref, base_ref, left_ref, right_ref,
 ):
     devices, lines, width = received_ref.shape
     rows = mask_ref.shape[0]
     fields = (lines - 8) // 2
     totals = [jnp.zeros((fields, width), f32) for _ in range(rows)]
+    edges = jnp.zeros((8, width), f32)
     for d in range(devices):
         codes = received_ref[d, 2 * fields : 2 * fields + 8, :].astype(f32)
+        edges = edges + codes
         for s in range(2):
             value = received_ref[d, s * fields : (s + 1) * fields, :].astype(f32)
             code = jnp.broadcast_to(codes[2 * s : 2 * s + 1, :], (fields, width))
@@ -280,6 +325,23 @@
         first_ref[k] = first
         second_ref[k] = second
         base_ref[k] = twice_top_ref[k] + mixing_00 * second
+    line = line_iota((8, width))
+    lane = lane_iota((8, width))
+    for n, out_ref in enumerate((left_ref, right_ref)):
+        flux = edges[4 + 2 * n : 5 + 2 * n] + edges[5 + 2 * n : 6 + 2 * n]
+        flux = jnp.broadcast_to(flux, (8, width))
+        first_of_pair = lane % 2 == 0
+        drive_sum = jnp.where(first_of_pair, flux * pltpu.roll(flux, width - 1, 1), 0.0)
+        drive_rate = jnp.where(first_of_pair, flux, 0.0)
+        for step in (2, 4):
+            drive_sum = drive_sum + pltpu.roll(drive_sum, width - step, 1)
+            drive_rate = drive_rate + pltpu.roll(drive_rate, width - step, 1)
+        there = [jnp.broadcast_to(beside_ref[n, i : i + 1, :], (8, width)) for i in range(3)]
+        share = jnp.where(there[2] > 0.0, there[2], 1.0)
+        first = there[1] * (forcing_step * (drive_sum / share - drive_rate / share * there[0]))
+        for k in range(2):
+            column = jnp.where(lane == 16 * line + 8 * k, first, 0.0)
+            out_ref[k] = jnp.broadcast_to(jnp.sum(column, axis=1, keepdims=True), (rows, width))
 
 
 def surface_kernel(
@@ -323,7 +385,10 @@
     return total.T
 
 
-def ocean_kernel(mixing_ref, twice_ref, spread_ref, second_ref, weight_ref, out_ref, sums_ref):
+def ocean_kernel(
+    block_ref, slot_ref, mixing_ref, twice_ref, spread_ref, second_ref, weight_ref,
+    out_ref, sums_ref, picks_ref,
+):
     levels = mixing_ref.shape[0]
     rows, width = spread_ref.shape[1:]
     mixing = mixing_ref[...]
@@ -336,14 +401,25 @@
             forced = twice * spread_ref[k, r : r + 1, :] + once * second_ref[k, r : r + 1, :]
             out_ref[k, :, r, :] = free + forced
     sums_ref[...] = own_columns(weight_ref, jnp.ones((width, width), bf16))
-
-
-def backward_kernel(block_ref, slot_ref, returned_ref, weight_ref, sums_ref, out_ref, lines_ref, rows_ref):
     tiles = weight_ref.shape[0]
-    lines_ref[...] = returned_ref[...].astype(f32)
-    for t in range(tiles):
-        rows_ref[2 * t : 2 * t + 2, :] = lines_ref[block_ref[t], pl.ds(2 * slot_ref[t], 2), :]
-    result = own_columns(weight_ref, rows_ref[...].astype(bf16)) / sums_ref[...]
+    columns = picks_ref.shape[1]
+    if 2 * tiles < width:
+        picks_ref[...] = jnp.zeros_like(picks_ref)
+    line = line_iota((16, columns))
+    lane = lane_iota((16, columns))
+    for start in range(0, tiles, 8):
+        target = line % 2
+        for i in range(8):
+            place = 8 * block_ref[start + i] + 2 * slot_ref[start + i]
+            target = target + jnp.where(line // 2 == i, place, 0)
+        picks_ref[2 * start : 2 * start + 16, :] = jnp.where(lane == target, 1.0, 0.0).astype(bf16)
+
+
+def backward_kernel(picks_ref, returned_ref, weight_ref, sums_ref, out_ref):
+    tiles, width, _ = weight_ref.shape
+    lines = returned_ref[...].astype(f32).reshape(picks_ref.shape[1], width).astype(bf16)
+    picked = jnp.dot(picks_ref[...], lines, preferred_element_type=f32).astype(bf16)
+    result = own_columns(weight_ref, picked) / sums_ref[...]
     for t in range(tiles):
         out_ref[t] = result[2 * t : 2 * t + 2]
 
@@ -357,15 +433,15 @@
     tiles, fields = atm_flux.shape[1:3]
     tracers, levels = ocean_state.shape[:2]
     planes = tracers * levels
-    packed_lines = 8 * (packing(rows, planes, width)[3] + 1)
+    packed_lines = 8 * (packing(rows, planes, width)[3] + 2)
     weights = remap_weights[0]
     block = dest_block.reshape(tiles)
     row = dest_row.reshape(tiles)
     state = ocean_state.reshape(planes, rows, width)
     up_sec = [(i, i + 1) for i in range(sections - 1)]
     down_sec = [(i + 1, i) for i in range(sections - 1)]
-    up_blk = [(i, i + 1) for i in range(blocks - 1)]
-    down_blk = [(i + 1, i) for i in range(blocks - 1)]
+    pairs = [[(i, i + 1) for i in range(start, blocks - 1, 2)] for start in range(2)]
+    swaps = [pair + [(j, i) for i, j in pair] for pair in pairs]
 
     packed, slot = call(
         forward_kernel, "forward",
@@ -375,6 +451,7 @@
             pltpu.SMEM((tiles,), jnp.int32), pltpu.SMEM((tiles,), jnp.int32),
             pltpu.VMEM((tiles, fields, width), bf16), pltpu.VMEM((tiles, width, width), bf16),
             pltpu.SMEM((blocks,), jnp.int32), pltpu.SMEM((2 * blocks,), jnp.int32),
+            pltpu.VMEM((tiles * fields, width), bf16), pltpu.VMEM((blocks + 2, 8, width), f32),
             pltpu.SemaphoreType.DMA((3,)), pltpu.SemaphoreType.DMA((min(4, tiles // 2),)),
         ],
         flops=2 * tiles * fields * width * width, moved=3 << 20,
@@ -386,44 +463,45 @@
     )(state, land_mask)
     before = lax.ppermute(bottom, "sec", up_sec)
     after = lax.ppermute(top, "sec", down_sec)
-    slab, first_columns, last_columns = call(
+    packed_shape = shape(packed_lines, width)
+    slab, first_columns, last_columns, near, far = call(
         columns_kernel, "columns",
-        (shape(rows + 4, planes + 8, width), shape(packed_lines, width), shape(packed_lines, width)),
-        [vmem] * 4, moved=2 << 20,
-    )(state, land_mask, before, after)
-    left = lax.ppermute(last_columns, "blk", up_blk)
-    right = lax.ppermute(first_columns, "blk", down_blk)
-    twice, once_top, twice_top, step_weights = call(
+        (shape(rows + 4, planes + 8, width),) + (packed_shape,) * 4, [vmem] * 5, moved=2 << 20,
+    )(state, land_mask, wet_fraction, before, after)
+    near = lax.ppermute(near, "blk", swaps[0])
+    far = lax.ppermute(far, "blk", swaps[1])
+    surface_shape = shape(tracers, rows, width)
+    twice, once_top, twice_top, step_weights, beside = call(
         stencil_kernel, "stencil",
         (
-            shape(tracers, rows, levels, width), shape(tracers, rows, width),
-            shape(tracers, rows, width), shape(7, rows, width),
+            shape(tracers, rows, levels, width), surface_shape, surface_shape,
+            shape(7, rows, width), shape(2, 8, width),
         ),
         [vmem] * 6, scratch=[pltpu.VMEM((rows + 4, planes, width), f32)], flops=20 << 20, moved=3 << 20,
-    )(slab, first_columns, last_columns, left, right, mixing)
-
-    first, second, base = call(
-        drive_kernel, "drive", (shape(tracers, rows, width),) * 3, [vmem] * 7, moved=1 << 20
-    )(received, ocean_state[:, 0], land_mask, wet_fraction, once_top, twice_top, step_weights)
+    )(slab, first_columns, last_columns, near, far, mixing)
+
+    first, second, base, first_left, first_right = call(
+        drive_kernel, "drive", (surface_shape,) * 5, [vmem] * 8, moved=1 << 20
+    )(received, ocean_state[:, 0], land_mask, wet_fraction, once_top, twice_top, step_weights, beside)
     first_before = lax.ppermute(first, "sec", up_sec)
     first_after = lax.ppermute(first, "sec", down_sec)
-    first_left = lax.ppermute(first, "blk", up_blk)
-    first_right = lax.ppermute(first, "blk", down_blk)
     spread_first, back = call(
-        surface_kernel, "surface",
-        (shape(tracers, rows, width), pltpu.HBM((blocks, 8, width), bf16)),
+        surface_kernel, "surface", (surface_shape, pltpu.HBM((blocks, 8, width), bf16)),
         [vmem] * 8, moved=1 << 20,
     )(received, first, first_before, first_after, first_left, first_right, base, step_weights)
     returned = lax.all_to_all(back, "blk", split_axis=0, concat_axis=0, tiled=True)
-    ocean, sums = call(
-        ocean_kernel, "ocean", (shape(tracers, levels, rows, width), shape(width, width)), [vmem] * 5,
-        flops=12 * planes * levels * rows * width, moved=2 << 20,
-    )(mixing, twice, spread_first, second, weights)
+    ocean, sums, picks = call(
+        ocean_kernel, "ocean",
+        (
+            shape(tracers, levels, rows, width), shape(width, width),
+            shape(width, 8 * blocks, dtype=bf16),
+        ),
+        [smem, smem] + [vmem] * 5, flops=12 * planes * levels * rows * width, moved=2 << 20,
+    )(block, slot, mixing, twice, spread_first, second, weights)
     atmosphere = call(
-        backward_kernel, "backward", shape(tiles, tracers, width), [smem, smem, vmem, vmem, vmem],
-        scratch=[pltpu.VMEM((blocks, 8, width), f32), pltpu.VMEM((width, width), f32)],
+        backward_kernel, "backward", shape(tiles, tracers, width), [vmem] * 4,
         flops=16 * tiles * width * width, moved=3 << 20,
-    )(block, slot, returned, weights, sums)
+    )(picks, returned, weights, sums)
     return (ocean, atmosphere[None])
 
 

time: 80.5 us -> 76.2 us (0.947)
  the two profiles are of different devices: /device:TPU:129 before, /device:TPU:193 now
where the time goes in v5:
time: 76.2 us; the launch traced here: 75.8 us
  starting transfers between devices  42.7 us (56%)
  waiting for transfers between devices  19.2 us (25%)
  Pallas kernels  12.9 us (17%)
  between operations  0.84 us (1%)
    all_to_all x1, starting transfers between devices, per_device(): lax.all_to_all(back, 'blk', split_axis=0, concat_axis=0, tiled=True)  12.6 us
    all_to_all x1, starting transfers between devices, per_device(): lax.all_to_all(packed, 'blk', split_axis=0, concat_axis=0, tiled=True)  10.8 us
    all_to_all x1, waiting for transfers between devices, per_device(): lax.all_to_all(back, 'blk', split_axis=0, concat_axis=0, tiled=True)  7.28 us
    ppermute x1, starting transfers between devices, per_device(): before = lax.ppermute(bottom, 'sec', up_sec)  5.34 us
    ppermute x1, waiting for transfers between devices, per_device(): after = lax.ppermute(top, 'sec', down_sec)  5 us
    ppermute x1, waiting for transfers between devices, per_device(): first_after = lax.ppermute(first, 'sec', down_sec)  3.67 us
    pallas_call x1, Pallas kernels, per_device(): call(forward_kernel, 'forward', (pltpu.HBM((blocks, 2 * fields + 8, width...  3.58 us
    ppermute x1, starting transfers between devices, per_device(): near = lax.ppermute(near, 'blk', swaps[0])  3.53 us
  transfers between devices with their start and end apart: 8, of which 5 were waited for; matrix products, arithmetic and copies ran while one was open for 0% of the time, Pallas kernels for 8%

profile of v5, /device:TPU:193, one launch (start us, length us, event | category | flops | bytes accessed | tf_op | source)
XLA Modules:
  0.0 75.8 jit_solution(11990870307432200269)
XLA Ops:
  0.6 0.0 copy-start.1
  0.6 0.0 copy-start.3
  0.7 0.0 copy-start.4
  0.7 0.0 copy-start.2
  0.7 3.6 %forward.1 = (bf16[64,40,128]{2,1,0:T(8,128)(2,1)}, s32[64]{0:T(128)S(1)}) custom-call(s32[64]{0:T(128)} %bitcast.15, s32[64]{0:T(128)} %bitcast.19, bf16[64,16,128]{2,1,0:T(8,128)(2,1)} %bitcast.17, bf16[64,128,128]{2,1,0:T(8,128)(2,1)} %bitcast.10), custom_call_target="tpu_custom_call" | custom-call | flops 33554432 | bytes 3145728 | tf_op jit(solution)/shard_map/forward/pallas_call | solution.py:446
  4.3 10.8 %all-to-all-start = ((bf16[64,40,128]{2,1,0:T(8,128)(2,1)}), bf16[64,40,128]{2,1,0:T(8,128)(2,1)S(1)}, u32[]{:S(2)}, u32[]{:S(2)}) async-start(bf16[64,40,128]{2,1,0:T(8,128)(2,1)} %get-tuple-element.35), calls=%async_computation | async-start | bytes 1310720 | tf_op jit(solution)/shard_map/all_to_all | solution.py:459
  15.1 0.0 copy-done.1
  15.1 0.0 copy-done.3
  15.1 0.2 rows.1
  15.3 0.0 copy-start
  15.3 0.0 copy-start.5
  15.3 5.3 %collective-permute-start = (f32[2,168,128]{2,1,0:T(8,128)S(1)}, f32[2,168,128]{2,1,0:T(8,128)S(1)}, u32[]{:S(2)}, u32[]{:S(2)}) collective-permute-start(f32[2,168,128]{2,1,0:T(8,128)S(1)} %get-tuple-element.27), channel_id=1, source_target_pairs={{0,64},{64,128},{128,192},{192,256},{256,320},{320,384},{384,448},... | collective-permute-start | bytes 516104 | tf_op jit(solution)/shard_map/ppermute | solution.py:464
  20.6 1.9 %collective-permute-start.1 = (f32[2,168,128]{2,1,0:T(8,128)S(1)}, f32[2,168,128]{2,1,0:T(8,128)S(1)}, u32[]{:S(2)}, u32[]{:S(2)}) collective-permute-start(f32[2,168,128]{2,1,0:T(8,128)S(1)} %get-tuple-element.28), channel_id=1, source_target_pairs={{64,0},{128,64},{192,128},{256,192},{320,256},{384,320},{448,384},... | collective-permute-start | bytes 516104 | tf_op jit(solution)/shard_map/ppermute | solution.py:465
  22.6 1.3 %collective-permute-done.before_ref = f32[2,168,128]{2,1,0:T(8,128)S(1)} collective-permute-done((f32[2,168,128]{2,1,0:T(8,128)S(1)}, f32[2,168,128]{2,1,0:T(8,128)S(1)}, u32[]{:S(2)}, u32[]{:S(2)}) %collective-permute-start) | collective-permute-done | bytes 172064 | tf_op jit(solution)/shard_map/ppermute | solution.py:464
  23.9 5.0 %collective-permute-done.1.after_ref = f32[2,168,128]{2,1,0:T(8,128)S(1)} collective-permute-done((f32[2,168,128]{2,1,0:T(8,128)S(1)}, f32[2,168,128]{2,1,0:T(8,128)S(1)}, u32[]{:S(2)}, u32[]{:S(2)}) %collective-permute-start.1) | collective-permute-done | bytes 172064 | tf_op jit(solution)/shard_map/ppermute | solution.py:465
  28.9 0.0 copy-done.4
  28.9 0.8 %columns.1 = (f32[12,168,128]{2,1,0:T(8,128)S(1)}, f32[48,128]{1,0:T(8,128)S(1)}, f32[48,128]{1,0:T(8,128)S(1)}, f32[48,128]{1,0:T(8,128)S(1)}, f32[48,128]{1,0:T(8,128)S(1)}) custom-call(f32[160,8,128]{2,1,0:T(8,128)S(1)} %bitcast.14, s32[8,128]{1,0:T(8,128)S(1)} %copy-done.3, f32[8,128]{1,0:T(8,128)S(1)} %copy-done.4, ...), custom_call_target="tpu_custom_call" | custom-call | bytes 2097152 | tf_op jit(solution)/shard_map/columns/pallas_call | solution.py:467
  29.7 3.5 %collective-permute-start.2 = (f32[48,128]{1,0:T(8,128)S(1)}, f32[48,128]{1,0:T(8,128)S(1)}, u32[]{:S(2)}, u32[]{:S(2)}) collective-permute-start(f32[48,128]{1,0:T(8,128)S(1)} %get-tuple-element.32), channel_id=1, source_target_pairs={{0,1},{2,3},{4,5},{6,7},{8,9},{10,11},{12,13},{14,15},{16,17},{18,... | collective-permute-start | bytes 73736 | tf_op jit(solution)/shard_map/ppermute | solution.py:471
  33.3 3.2 %collective-permute-start.3 = (f32[48,128]{1,0:T(8,128)S(1)}, f32[48,128]{1,0:T(8,128)S(1)}, u32[]{:S(2)}, u32[]{:S(2)}) collective-permute-start(f32[48,128]{1,0:T(8,128)S(1)} %get-tuple-element.33), channel_id=1, source_target_pairs={{1,2},{3,4},{5,6},{7,8},{9,10},{11,12},{13,14},{15,16},{17,18},{19... | collective-permute-start | bytes 73736 | tf_op jit(solution)/shard_map/ppermute | solution.py:472
  36.5 0.0 collective-permute-done.2.near_ref
  36.5 1.9 %collective-permute-done.3.far_ref = f32[48,128]{1,0:T(8,128)S(1)} collective-permute-done((f32[48,128]{1,0:T(8,128)S(1)}, f32[48,128]{1,0:T(8,128)S(1)}, u32[]{:S(2)}, u32[]{:S(2)}) %collective-permute-start.3) | collective-permute-done | bytes 24608 | tf_op jit(solution)/shard_map/ppermute | solution.py:472
  38.4 0.0 copy-done.2
  38.4 1.9 %stencil.1 = (f32[2,8,80,128]{3,2,1,0:T(8,128)S(1)}, f32[2,8,128]{2,1,0:T(8,128)S(1)}, f32[2,8,128]{2,1,0:T(8,128)S(1)}, f32[7,8,128]{2,1,0:T(8,128)S(1)}, f32[2,8,128]{2,1,0:T(8,128)S(1)}) custom-call(f32[12,168,128]{2,1,0:T(8,128)S(1)} %get-tuple-element.29.slab_ref, f32[48,128]{1,0:T(8,128)S(1)} %get-tuple-element.30.first_ref, ...), custom_call_target="tpu_custom_call" | custom-call | flops 20971520 | bytes 3145728 | tf_op jit(solution)/shard_map/stencil/pallas_call | solution.py:474
  40.3 0.0 all-to-all-done.received_ref
  40.3 0.9 %drive.1 = (f32[2,8,128]{2,1,0:T(8,128)S(1)}, f32[2,8,128]{2,1,0:T(8,128)S(1)}, f32[2,8,128]{2,1,0:T(8,128)S(1)}, f32[2,8,128]{2,1,0:T(8,128)S(1)}, f32[2,8,128]{2,1,0:T(8,128)S(1)}) custom-call(bf16[64,40,128]{2,1,0:T(8,128)(2,1)S(1)} %all-to-all-done.received_ref, f32[2,8,128]{2,1,0:T(8,128)S(1)} %slice_bitcast_fusion.top_ref, s32[8,128]{1,0:T(8,128)S(1)} %copy-done.3, ...), custom_call_target="tpu_custom_call" | custom-call | bytes 1048576 | tf_op jit(solution)/shard_map/drive/pallas_call | solution.py:483
  41.2 3.4 %collective-permute-start.4 = (f32[2,8,128]{2,1,0:T(8,128)S(1)}, f32[2,8,128]{2,1,0:T(8,128)S(1)}, u32[]{:S(2)}, u32[]{:S(2)}) collective-permute-start(f32[2,8,128]{2,1,0:T(8,128)S(1)} %get-tuple-element.40.first_ref), channel_id=1, source_target_pairs={{0,64},{64,128},{128,192},{192,256},{256,320},{320,384},{384,448},... | collective-permute-start | bytes 24584 | tf_op jit(solution)/shard_map/ppermute | solution.py:486
  44.6 1.9 %collective-permute-start.5 = (f32[2,8,128]{2,1,0:T(8,128)S(1)}, f32[2,8,128]{2,1,0:T(8,128)S(1)}, u32[]{:S(2)}, u32[]{:S(2)}) collective-permute-start(f32[2,8,128]{2,1,0:T(8,128)S(1)} %get-tuple-element.40.first_ref), channel_id=1, source_target_pairs={{64,0},{128,64},{192,128},{256,192},{320,256},{384,320},{448,384},... | collective-permute-start | bytes 24584 | tf_op jit(solution)/shard_map/ppermute | solution.py:487
  46.6 0.0 collective-permute-done.4.before_ref
  46.6 3.7 %collective-permute-done.5.after_ref = f32[2,8,128]{2,1,0:T(8,128)S(1)} collective-permute-done((f32[2,8,128]{2,1,0:T(8,128)S(1)}, f32[2,8,128]{2,1,0:T(8,128)S(1)}, u32[]{:S(2)}, u32[]{:S(2)}) %collective-permute-start.5) | collective-permute-done | bytes 8224 | tf_op jit(solution)/shard_map/ppermute | solution.py:487
  50.3 0.9 %surface.1 = (f32[2,8,128]{2,1,0:T(8,128)S(1)}, bf16[64,8,128]{2,1,0:T(8,128)(2,1)}) custom-call(bf16[64,40,128]{2,1,0:T(8,128)(2,1)S(1)} %all-to-all-done.received_ref, f32[2,8,128]{2,1,0:T(8,128)S(1)} %get-tuple-element.40.first_ref, f32[2,8,128]{2,1,0:T(8,128)S(1)} %collective-permute-done.4.before_ref, ...), custom_call_target="tpu_custom_call" | custom-call | bytes 1048576 | tf_op jit(solution)/shard_map/surface/pallas_call | solution.py:488
  51.1 12.6 %all-to-all-start.1 = ((bf16[64,8,128]{2,1,0:T(8,128)(2,1)}), bf16[64,8,128]{2,1,0:T(8,128)(2,1)S(1)}, u32[]{:S(2)}, u32[]{:S(2)}) async-start(bf16[64,8,128]{2,1,0:T(8,128)(2,1)} %get-tuple-element.48), calls=%async_computation.1 | async-start | bytes 262144 | tf_op jit(solution)/shard_map/all_to_all | solution.py:492
  63.8 0.0 copy-done
  63.8 0.0 copy-done.5
  63.8 3.1 %ocean.1 = (f32[2,80,8,128]{3,2,1,0:T(8,128)}, f32[128,128]{1,0:T(8,128)S(1)}, bf16[128,512]{1,0:T(8,128)(2,1)S(1)}) custom-call(s32[64]{0:T(128)S(1)} %bitcast.16, s32[64]{0:T(128)S(1)} %get-tuple-element.26.slot_ref, f32[80,80]{1,0:T(8,128)S(1)} %copy-done.2, f32[2,8,80,128]{3,2,1,0:T(8,128)S(1)} %get-tuple-element.34.twice_ref, ...), custom_call_target="tpu_custom_call" | custom-call | flops 157286400 | bytes 2097152 | tf_op jit(solution)/shard_map/ocean/pallas_call | solution.py:493
  66.8 7.3 %all-to-all-done.1.returned_ref = bf16[64,8,128]{2,1,0:T(8,128)(2,1)S(1)} async-done(((bf16[64,8,128]{2,1,0:T(8,128)(2,1)}), bf16[64,8,128]{2,1,0:T(8,128)(2,1)S(1)}, u32[]{:S(2)}, u32[]{:S(2)}) %all-to-all-start.1) | async-done | bytes 131104 | tf_op jit(solution)/shard_map/all_to_all | solution.py:492
  74.1 1.6 %backward.1 = f32[64,2,128]{2,1,0:T(2,128)} custom-call(bf16[128,512]{1,0:T(8,128)(2,1)S(1)} %get-tuple-element.47.picks_ref, bf16[64,8,128]{2,1,0:T(8,128)(2,1)S(1)} %all-to-all-done.1.returned_ref, bf16[64,128,128]{2,1,0:T(8,128)(2,1)S(1)} %bitcast.12, f32[128,128]{1,0:T(8,128)S(1)} %get-tuple-element.49.sums_ref), custom_call_target="tpu_custom_call" | custom-call | flops 16777216 | bytes 3145728 | tf_op jit(solution)/shard_map/backward/pallas_call | solution.py:501
  (1 shorter events, 0.0 us)
Async XLA Ops:
  0.6 14.4 %copy-start.1 = (f32[2,80,8,128]{3,2,1,0:T(8,128)S(1)}, f32[2,80,8,128]{3,2,1,0:T(8,128)}, u32[]{:S(2)}) copy-start(f32[2,80,8,128]{3,2,1,0:T(8,128)} %param.12) | copy-start | bytes 1966084
  0.6 14.4 %copy-start.3 = (s32[8,128]{1,0:T(8,128)S(1)}, s32[8,128]{1,0:T(8,128)}, u32[]{:S(2)}) copy-start(s32[8,128]{1,0:T(8,128)} %mask_ref.5) | copy-start | bytes 12292
  0.7 28.3 %copy-start.4 = (f32[8,128]{1,0:T(8,128)S(1)}, f32[8,128]{1,0:T(8,128)}, u32[]{:S(2)}) copy-start(f32[8,128]{1,0:T(8,128)} %wet_ref.3) | copy-start | bytes 12292
  0.7 37.8 %copy-start.2 = (f32[80,80]{1,0:T(8,128)S(1)}, f32[80,80]{1,0:T(8,128)}, u32[]{:S(2)}) copy-start(f32[80,80]{1,0:T(8,128)} %mixing_ref.3) | copy-start | bytes 76804
  4.3 36.0 %all-to-all-start = ((bf16[64,40,128]{2,1,0:T(8,128)(2,1)}), bf16[64,40,128]{2,1,0:T(8,128)(2,1)S(1)}, u32[]{:S(2)}, u32[]{:S(2)}) async-start(bf16[64,40,128]{2,1,0:T(8,128)(2,1)} %get-tuple-element.35), calls=%async_computation | async-start | bytes 1310720 | tf_op jit(solution)/shard_map/all_to_all | solution.py:459
  15.3 48.5 %copy-start = (bf16[1,64,128,128]{3,2,1,0:T(8,128)(2,1)S(1)}, bf16[1,64,128,128]{3,2,1,0:T(8,128)(2,1)}, u32[]{:S(2)}) copy-start(bf16[1,64,128,128]{3,2,1,0:T(8,128)(2,1)} %param.9) | copy-start | bytes 6291460
  15.3 48.5 %copy-start.5 = (s32[1,64,1]{1,2,0:T(1,128)S(1)}, s32[1,64,1]{1,2,0:T(1,128)}, u32[]{:S(2)}) copy-start(s32[1,64,1]{1,2,0:T(1,128)} %param.10) | copy-start | bytes 772
  15.3 8.6 %collective-permute-start = (f32[2,168,128]{2,1,0:T(8,128)S(1)}, f32[2,168,128]{2,1,0:T(8,128)S(1)}, u32[]{:S(2)}, u32[]{:S(2)}) collective-permute-start(f32[2,168,128]{2,1,0:T(8,128)S(1)} %get-tuple-element.27), channel_id=1, source_target_pairs={{0,64},{64,128},{128,192},{192,256},{256,320},{320,384},{384,448},... | collective-permute-start | bytes 516104 | tf_op jit(solution)/shard_map/ppermute | solution.py:464
  20.6 8.3 %collective-permute-start.1 = (f32[2,168,128]{2,1,0:T(8,128)S(1)}, f32[2,168,128]{2,1,0:T(8,128)S(1)}, u32[]{:S(2)}, u32[]{:S(2)}) collective-permute-start(f32[2,168,128]{2,1,0:T(8,128)S(1)} %get-tuple-element.28), channel_id=1, source_target_pairs={{64,0},{128,64},{192,128},{256,192},{320,256},{384,320},{448,384},... | collective-permute-start | bytes 516104 | tf_op jit(solution)/shard_map/ppermute | solution.py:465
  29.7 6.7 %collective-permute-start.2 = (f32[48,128]{1,0:T(8,128)S(1)}, f32[48,128]{1,0:T(8,128)S(1)}, u32[]{:S(2)}, u32[]{:S(2)}) collective-permute-start(f32[48,128]{1,0:T(8,128)S(1)} %get-tuple-element.32), channel_id=1, source_target_pairs={{0,1},{2,3},{4,5},{6,7},{8,9},{10,11},{12,13},{14,15},{16,17},{18,... | collective-permute-start | bytes 73736 | tf_op jit(solution)/shard_map/ppermute | solution.py:471
  33.3 5.1 %collective-permute-start.3 = (f32[48,128]{1,0:T(8,128)S(1)}, f32[48,128]{1,0:T(8,128)S(1)}, u32[]{:S(2)}, u32[]{:S(2)}) collective-permute-start(f32[48,128]{1,0:T(8,128)S(1)} %get-tuple-element.33), channel_id=1, source_target_pairs={{1,2},{3,4},{5,6},{7,8},{9,10},{11,12},{13,14},{15,16},{17,18},{19... | collective-permute-start | bytes 73736 | tf_op jit(solution)/shard_map/ppermute | solution.py:472
  41.2 5.4 %collective-permute-start.4 = (f32[2,8,128]{2,1,0:T(8,128)S(1)}, f32[2,8,128]{2,1,0:T(8,128)S(1)}, u32[]{:S(2)}, u32[]{:S(2)}) collective-permute-start(f32[2,8,128]{2,1,0:T(8,128)S(1)} %get-tuple-element.40.first_ref), channel_id=1, source_target_pairs={{0,64},{64,128},{128,192},{192,256},{256,320},{320,384},{384,448},... | collective-permute-start | bytes 24584 | tf_op jit(solution)/shard_map/ppermute | solution.py:486
  44.6 5.6 %collective-permute-start.5 = (f32[2,8,128]{2,1,0:T(8,128)S(1)}, f32[2,8,128]{2,1,0:T(8,128)S(1)}, u32[]{:S(2)}, u32[]{:S(2)}) collective-permute-start(f32[2,8,128]{2,1,0:T(8,128)S(1)} %get-tuple-element.40.first_ref), channel_id=1, source_target_pairs={{64,0},{128,64},{192,128},{256,192},{320,256},{384,320},{448,384},... | collective-permute-start | bytes 24584 | tf_op jit(solution)/shard_map/ppermute | solution.py:487
  51.1 23.0 %all-to-all-start.1 = ((bf16[64,8,128]{2,1,0:T(8,128)(2,1)}), bf16[64,8,128]{2,1,0:T(8,128)(2,1)S(1)}, u32[]{:S(2)}, u32[]{:S(2)}) async-start(bf16[64,8,128]{2,1,0:T(8,128)(2,1)} %get-tuple-element.48), calls=%async_computation.1 | async-start | bytes 262144 | tf_op jit(solution)/shard_map/all_to_all | solution.py:492

commit v6 on v5

--- a/solution.py
+++ b/solution.py
@@ -288,10 +288,7 @@
             once_top_ref[k, i : i + 1, :] = jnp.sum(once_column * before, axis=0, keepdims=True)
 
 
-def drive_kernel(
-    received_ref, top_ref, mask_ref, wet_ref, once_top_ref, twice_top_ref, weights_ref, beside_ref,
-    first_ref, second_ref, base_ref, left_ref, right_ref,
-):
+def drive_kernel(received_ref, top_ref, mask_ref, wet_ref, sum_ref, rate_ref, first_ref, edges_ref):
     devices, lines, width = received_ref.shape
     rows = mask_ref.shape[0]
     fields = (lines - 8) // 2
@@ -305,9 +302,9 @@
             code = jnp.broadcast_to(codes[2 * s : 2 * s + 1, :], (fields, width))
             for r in range(rows):
                 totals[r] = totals[r] + jnp.where(code == float(r), value, 0.0)
+    edges_ref[...] = edges
     mask = mask_ref[...].astype(f32)
     wet = wet_ref[...]
-    mixing_00 = weights_ref[6]
     half = fields // 2
     even = line_iota((half, width)) % 2 == 0
     for k in range(2):
@@ -319,52 +316,58 @@
             rates.append(jnp.sum(jnp.where(even, part, 0.0), axis=0, keepdims=True))
         drive_sum = jnp.concatenate(sums, axis=0) / wet
         drive_rate = jnp.concatenate(rates, axis=0) / wet
-        first = mask * (forcing_step * (drive_sum - drive_rate * top_ref[k]))
-        once_top = once_top_ref[k] + mixing_00 * first
-        second = mask * (forcing_step * (drive_sum - drive_rate * once_top))
-        first_ref[k] = first
-        second_ref[k] = second
-        base_ref[k] = twice_top_ref[k] + mixing_00 * second
-    line = line_iota((8, width))
-    lane = lane_iota((8, width))
-    for n, out_ref in enumerate((left_ref, right_ref)):
-        flux = edges[4 + 2 * n : 5 + 2 * n] + edges[5 + 2 * n : 6 + 2 * n]
-        flux = jnp.broadcast_to(flux, (8, width))
-        first_of_pair = lane % 2 == 0
-        drive_sum = jnp.where(first_of_pair, flux * pltpu.roll(flux, width - 1, 1), 0.0)
-        drive_rate = jnp.where(first_of_pair, flux, 0.0)
-        for step in (2, 4):
-            drive_sum = drive_sum + pltpu.roll(drive_sum, width - step, 1)
-            drive_rate = drive_rate + pltpu.roll(drive_rate, width - step, 1)
-        there = [jnp.broadcast_to(beside_ref[n, i : i + 1, :], (8, width)) for i in range(3)]
-        share = jnp.where(there[2] > 0.0, there[2], 1.0)
-        first = there[1] * (forcing_step * (drive_sum / share - drive_rate / share * there[0]))
-        for k in range(2):
-            column = jnp.where(lane == 16 * line + 8 * k, first, 0.0)
-            out_ref[k] = jnp.broadcast_to(jnp.sum(column, axis=1, keepdims=True), (rows, width))
+        sum_ref[k] = drive_sum
+        rate_ref[k] = drive_rate
+        first_ref[k] = mask * (forcing_step * (drive_sum - drive_rate * top_ref[k]))
+
+
+def beside_forcing(edges, there):
+    rows, width = edges.shape
+    line = line_iota(edges.shape)
+    lane = lane_iota(edges.shape)
+    first_of_pair = lane % 2 == 0
+    drive_sum = jnp.where(first_of_pair, edges * pltpu.roll(edges, width - 1, 1), 0.0)
+    drive_rate = jnp.where(first_of_pair, edges, 0.0)
+    for step in (2, 4):
+        drive_sum = drive_sum + pltpu.roll(drive_sum, width - step, 1)
+        drive_rate = drive_rate + pltpu.roll(drive_rate, width - step, 1)
+    top, mask, wet = (jnp.broadcast_to(there[i : i + 1, :], edges.shape) for i in range(3))
+    wet = jnp.where(wet > 0.0, wet, 1.0)
+    first = mask * (forcing_step * (drive_sum / wet - drive_rate / wet * top))
+    columns = [jnp.where(lane == 16 * line + 8 * k, first, 0.0) for k in range(2)]
+    return [jnp.broadcast_to(jnp.sum(c, axis=1, keepdims=True), edges.shape) for c in columns]
 
 
 def surface_kernel(
-    received_ref, first_ref, before_ref, after_ref, left_ref, right_ref, base_ref, weights_ref,
-    spread_ref, back_ref,
+    received_ref, mask_ref, sum_ref, rate_ref, first_ref, edges_ref, before_ref, after_ref,
+    beside_ref, once_top_ref, twice_top_ref, weights_ref, spread_ref, second_ref, back_ref,
 ):
     devices, lines, width = received_ref.shape
     rows = first_ref.shape[1]
     line = line_iota((rows, width))
     lane = lane_iota((rows, width))
+    mask = mask_ref[...].astype(f32)
+    mixing_00 = weights_ref[6]
+    edges = [edges_ref[4 + 2 * n : 5 + 2 * n, :] + edges_ref[5 + 2 * n : 6 + 2 * n, :] for n in range(2)]
+    lefts, rights = (
+        beside_forcing(jnp.broadcast_to(edges[n], (rows, width)), beside_ref[n]) for n in range(2)
+    )
     surfaces = []
     for k in range(2):
         own = first_ref[k]
         up = pltpu.roll(jnp.where(line == rows - 1, before_ref[k], own), 1, 0)
         down = pltpu.roll(jnp.where(line == 0, after_ref[k], own), rows - 1, 0)
-        left = pltpu.roll(jnp.where(lane == width - 1, left_ref[k], own), 1, 1)
-        right = pltpu.roll(jnp.where(lane == 0, right_ref[k], own), width - 1, 1)
+        left = pltpu.roll(jnp.where(lane == width - 1, lefts[k], own), 1, 1)
+        right = pltpu.roll(jnp.where(lane == 0, rights[k], own), width - 1, 1)
         moved = (
             weights_ref[0] * own + weights_ref[1] * up + weights_ref[2] * down
             + weights_ref[3] * left + weights_ref[4] * right
         )
+        once_top = once_top_ref[k] + mixing_00 * own
+        second = mask * (forcing_step * (sum_ref[k] - rate_ref[k] * once_top))
         spread_ref[k] = moved
-        surfaces.append(base_ref[k] + weights_ref[5] * moved)
+        second_ref[k] = second
+        surfaces.append(twice_top_ref[k] + mixing_00 * second + weights_ref[5] * moved)
     surface = jnp.concatenate(surfaces + [jnp.zeros((width - 2 * rows, width), f32)], axis=0).astype(bf16)
     codes = received_ref[:, lines - 8 : lines, :].astype(f32)
     wanted = (codes == lane_iota(codes.shape).astype(f32)).astype(f32).reshape(devices * 8, width).astype(bf16)
@@ -480,15 +483,18 @@
         [vmem] * 6, scratch=[pltpu.VMEM((rows + 4, planes, width), f32)], flops=20 << 20, moved=3 << 20,
     )(slab, first_columns, last_columns, near, far, mixing)
 
-    first, second, base, first_left, first_right = call(
-        drive_kernel, "drive", (surface_shape,) * 5, [vmem] * 8, moved=1 << 20
-    )(received, ocean_state[:, 0], land_mask, wet_fraction, once_top, twice_top, step_weights, beside)
+    drive_sum, drive_rate, first, edges = call(
+        drive_kernel, "drive", (surface_shape,) * 3 + (shape(8, width),), [vmem] * 4, moved=1 << 20
+    )(received, ocean_state[:, 0], land_mask, wet_fraction)
     first_before = lax.ppermute(first, "sec", up_sec)
     first_after = lax.ppermute(first, "sec", down_sec)
-    spread_first, back = call(
-        surface_kernel, "surface", (surface_shape, pltpu.HBM((blocks, 8, width), bf16)),
-        [vmem] * 8, moved=1 << 20,
-    )(received, first, first_before, first_after, first_left, first_right, base, step_weights)
+    spread_first, second, back = call(
+        surface_kernel, "surface",
+        (surface_shape, surface_shape, pltpu.HBM((blocks, 8, width), bf16)), [vmem] * 12, moved=1 << 20,
+    )(
+        received, land_mask, drive_sum, drive_rate, first, edges, first_before, first_after,
+        beside, once_top, twice_top, step_weights,
+    )
     returned = lax.all_to_all(back, "blk", split_axis=0, concat_axis=0, tiled=True)
     ocean, sums, picks = call(
         ocean_kernel, "ocean",

time: 76.2 us -> 72.4 us (0.950)
  waiting for transfers between devices: 19.2 us -> 13.7 us
  local copies, waits for them, and re-layouts: 0.03 us -> 2.24 us
  starting transfers between devices: 42.7 us -> 40.7 us
  Pallas kernels: 12.9 us -> 14.4 us
    ppermute x1, waiting for transfers between devices: 3.67 us -> 0.07 us  [per_device(): first_after = lax.ppermute(first, 'sec', down_sec)]
    unnamed x12 -> x16, local copies, waits for them, and re-layouts: 0.03 us -> 2.23 us
    all_to_all x1, starting transfers between devices: 12.6 us -> 10.5 us  [per_device(): lax.all_to_all(back, 'blk', split_axis=0, concat_axis=0, tiled=True)]
    ppermute x1, waiting for transfers between devices: 1.93 us -> 0.01 us  [per_device(): far = lax.ppermute(far, 'blk', swaps[1])]
  transfers between devices with their start and end apart: 8 -> 8, of which waited for: 5 -> 4; matrix products, arithmetic and copies ran while one was open for 0% -> 0% of each run, Pallas kernels for 8% -> 11%
where the time goes in v6:
time: 72.4 us; the launch traced here: 71.9 us
  starting transfers between devices  40.7 us (56%)
  Pallas kernels  14.4 us (20%)
  waiting for transfers between devices  13.7 us (19%)
  local copies, waits for them, and re-layouts  2.24 us (3%)
  between operations  0.86 us (1%)
    all_to_all x1, starting transfers between devices, per_device(): lax.all_to_all(packed, 'blk', split_axis=0, concat_axis=0, tiled=True)  10.8 us
    all_to_all x1, starting transfers between devices, per_device(): lax.all_to_all(back, 'blk', split_axis=0, concat_axis=0, tiled=True)  10.5 us
    all_to_all x1, waiting for transfers between devices, per_device(): lax.all_to_all(back, 'blk', split_axis=0, concat_axis=0, tiled=True)  7.28 us
    ppermute x1, starting transfers between devices, per_device(): before = lax.ppermute(bottom, 'sec', up_sec)  5.34 us
    ppermute x1, waiting for transfers between devices, per_device(): after = lax.ppermute(top, 'sec', down_sec)  5 us
    pallas_call x1, Pallas kernels, per_device(): call(forward_kernel, 'forward', (pltpu.HBM((blocks, 2 * fields + 8, width...  3.58 us
    ppermute x1, starting transfers between devices, per_device(): near = lax.ppermute(near, 'blk', swaps[0])  3.51 us
    ppermute x1, starting transfers between devices, per_device(): first_before = lax.ppermute(first, 'sec', up_sec)  3.43 us
  transfers between devices with their start and end apart: 8, of which 4 were waited for; matrix products, arithmetic and copies ran while one was open for 0% of the time, Pallas kernels for 11%

profile of v6, /device:TPU:193, one launch (start us, length us, event | category | flops | bytes accessed | tf_op | source)
XLA Modules:
  0.0 71.9 jit_solution(4377639655244786322)
XLA Ops:
  0.6 0.0 copy-start.1
  0.6 0.0 copy-start.5
  0.7 0.0 copy-start.6
  0.7 3.6 %forward.1 = (bf16[64,40,128]{2,1,0:T(8,128)(2,1)}, s32[64]{0:T(128)S(1)}) custom-call(s32[64]{0:T(128)} %bitcast.15, s32[64]{0:T(128)} %bitcast.19, bf16[64,16,128]{2,1,0:T(8,128)(2,1)} %bitcast.17, bf16[64,128,128]{2,1,0:T(8,128)(2,1)} %bitcast.10), custom_call_target="tpu_custom_call" | custom-call | flops 33554432 | bytes 3145728 | tf_op jit(solution)/shard_map/forward/pallas_call | solution.py:449
  4.2 0.0 copy-start.4
  4.3 10.8 %all-to-all-start = ((bf16[64,40,128]{2,1,0:T(8,128)(2,1)}), bf16[64,40,128]{2,1,0:T(8,128)(2,1)S(1)}, u32[]{:S(2)}, u32[]{:S(2)}) async-start(bf16[64,40,128]{2,1,0:T(8,128)(2,1)} %get-tuple-element.35), calls=%async_computation | async-start | bytes 1310720 | tf_op jit(solution)/shard_map/all_to_all | solution.py:462
  15.1 0.0 copy-done.1
  15.1 0.0 copy-done.5
  15.1 0.0 copy-start.7
  15.1 0.2 rows.1
  15.3 0.0 copy-start
  15.3 5.3 %collective-permute-start = (f32[2,168,128]{2,1,0:T(8,128)S(1)}, f32[2,168,128]{2,1,0:T(8,128)S(1)}, u32[]{:S(2)}, u32[]{:S(2)}) collective-permute-start(f32[2,168,128]{2,1,0:T(8,128)S(1)} %get-tuple-element.27), channel_id=1, source_target_pairs={{0,64},{64,128},{128,192},{192,256},{256,320},{320,384},{384,448},... | collective-permute-start | bytes 516104 | tf_op jit(solution)/shard_map/ppermute | solution.py:467
  20.6 1.9 %collective-permute-start.1 = (f32[2,168,128]{2,1,0:T(8,128)S(1)}, f32[2,168,128]{2,1,0:T(8,128)S(1)}, u32[]{:S(2)}, u32[]{:S(2)}) collective-permute-start(f32[2,168,128]{2,1,0:T(8,128)S(1)} %get-tuple-element.28), channel_id=1, source_target_pairs={{64,0},{128,64},{192,128},{256,192},{320,256},{384,320},{448,384},... | collective-permute-start | bytes 516104 | tf_op jit(solution)/shard_map/ppermute | solution.py:468
  22.6 1.3 %collective-permute-done.before_ref = f32[2,168,128]{2,1,0:T(8,128)S(1)} collective-permute-done((f32[2,168,128]{2,1,0:T(8,128)S(1)}, f32[2,168,128]{2,1,0:T(8,128)S(1)}, u32[]{:S(2)}, u32[]{:S(2)}) %collective-permute-start) | collective-permute-done | bytes 172064 | tf_op jit(solution)/shard_map/ppermute | solution.py:467
  23.9 5.0 %collective-permute-done.1.after_ref = f32[2,168,128]{2,1,0:T(8,128)S(1)} collective-permute-done((f32[2,168,128]{2,1,0:T(8,128)S(1)}, f32[2,168,128]{2,1,0:T(8,128)S(1)}, u32[]{:S(2)}, u32[]{:S(2)}) %collective-permute-start.1) | collective-permute-done | bytes 172064 | tf_op jit(solution)/shard_map/ppermute | solution.py:468
  28.9 0.0 copy-done.6
  28.9 1.4 %columns.1 = (f32[12,168,128]{2,1,0:T(8,128)S(1)}, f32[48,128]{1,0:T(8,128)S(1)}, f32[48,128]{1,0:T(8,128)S(1)}, f32[48,128]{1,0:T(8,128)}, f32[48,128]{1,0:T(8,128)}) custom-call(f32[160,8,128]{2,1,0:T(8,128)S(1)} %bitcast.14, s32[8,128]{1,0:T(8,128)S(1)} %copy-done.5, f32[8,128]{1,0:T(8,128)S(1)} %copy-done.6, ...), custom_call_target="tpu_custom_call" | custom-call | bytes 2097152 | tf_op jit(solution)/shard_map/columns/pallas_call | solution.py:470
  30.3 0.0 copy-start.2
  30.3 1.0 %copy-done.2 = f32[12,168,128]{2,1,0:T(8,128)} copy-done((f32[12,168,128]{2,1,0:T(8,128)}, f32[12,168,128]{2,1,0:T(8,128)S(1)}, u32[]{:S(2)}) %copy-start.2) | copy-done | bytes 1032216
  31.3 3.5 %collective-permute-start.2 = (f32[48,128]{1,0:T(8,128)}, f32[48,128]{1,0:T(8,128)S(1)}, u32[]{:S(2)}, u32[]{:S(2)}) collective-permute-start(f32[48,128]{1,0:T(8,128)} %get-tuple-element.32), channel_id=1, source_target_pairs={{0,1},{2,3},{4,5},{6,7},{8,9},{10,11},{12,13},{14,15},{16,17},{18,... | collective-permute-start | bytes 73736 | tf_op jit(solution)/shard_map/ppermute | solution.py:474
  34.8 3.2 %collective-permute-start.3 = (f32[48,128]{1,0:T(8,128)}, f32[48,128]{1,0:T(8,128)}, u32[]{:S(2)}, u32[]{:S(2)}) collective-permute-start(f32[48,128]{1,0:T(8,128)} %get-tuple-element.33), channel_id=1, source_target_pairs={{1,2},{3,4},{5,6},{7,8},{9,10},{11,12},{13,14},{15,16},{17,18},{19... | collective-permute-start | bytes 73736 | tf_op jit(solution)/shard_map/ppermute | solution.py:475
  38.1 0.0 all-to-all-done.received_ref
  38.1 0.8 %drive.1 = (f32[2,8,128]{2,1,0:T(8,128)S(1)}, f32[2,8,128]{2,1,0:T(8,128)S(1)}, f32[2,8,128]{2,1,0:T(8,128)S(1)}, f32[8,128]{1,0:T(8,128)S(1)}) custom-call(bf16[64,40,128]{2,1,0:T(8,128)(2,1)S(1)} %all-to-all-done.received_ref, f32[2,8,128]{2,1,0:T(8,128)S(1)} %slice_bitcast_fusion.top_ref, s32[8,128]{1,0:T(8,128)S(1)} %copy-done.5, f32[8,128]{1,0:T(8,128)S(1)} %copy-done.6), custom_call_target="tpu_custom_call" | custom-call | bytes 1048576 | tf_op jit(solution)/shard_map/drive/pallas_call | solution.py:486
  38.9 3.4 %collective-permute-start.4 = (f32[2,8,128]{2,1,0:T(8,128)S(1)}, f32[2,8,128]{2,1,0:T(8,128)S(1)}, u32[]{:S(2)}, u32[]{:S(2)}) collective-permute-start(f32[2,8,128]{2,1,0:T(8,128)S(1)} %get-tuple-element.38.first_ref), channel_id=1, source_target_pairs={{0,64},{64,128},{128,192},{192,256},{256,320},{320,384},{384,448},... | collective-permute-start | bytes 24584 | tf_op jit(solution)/shard_map/ppermute | solution.py:489
  42.3 1.9 %collective-permute-start.5 = (f32[2,8,128]{2,1,0:T(8,128)S(1)}, f32[2,8,128]{2,1,0:T(8,128)S(1)}, u32[]{:S(2)}, u32[]{:S(2)}) collective-permute-start(f32[2,8,128]{2,1,0:T(8,128)S(1)} %get-tuple-element.38.first_ref), channel_id=1, source_target_pairs={{64,0},{128,64},{192,128},{256,192},{320,256},{384,320},{448,384},... | collective-permute-start | bytes 24584 | tf_op jit(solution)/shard_map/ppermute | solution.py:490
  44.3 0.0 collective-permute-done.2.near_ref
  44.3 0.0 collective-permute-done.3.far_ref
  44.3 0.0 copy-done.4
  44.3 0.0 copy-start.3
  44.3 1.2 %copy-done.3 = f32[12,168,128]{2,1,0:T(8,128)S(1)} copy-done((f32[12,168,128]{2,1,0:T(8,128)S(1)}, f32[12,168,128]{2,1,0:T(8,128)}, u32[]{:S(2)}) %copy-start.3) | copy-done | bytes 1032216
  45.5 2.6 %stencil.1 = (f32[2,8,80,128]{3,2,1,0:T(8,128)S(1)}, f32[2,8,128]{2,1,0:T(8,128)S(1)}, f32[2,8,128]{2,1,0:T(8,128)S(1)}, f32[7,8,128]{2,1,0:T(8,128)S(1)}, f32[2,8,128]{2,1,0:T(8,128)S(1)}) custom-call(f32[12,168,128]{2,1,0:T(8,128)S(1)} %copy-done.3, f32[48,128]{1,0:T(8,128)S(1)} %get-tuple-element.30.first_ref, f32[48,128]{1,0:T(8,128)S(1)} %get-tuple-element.31.last_ref, ...), custom_call_target="tpu_custom_call" | custom-call | flops 20971520 | bytes 3145728 | tf_op jit(solution)/shard_map/stencil/pallas_call | solution.py:477
  48.1 0.0 collective-permute-done.4.before_ref
  48.1 0.1 collective-permute-done.5.after_ref
  48.2 1.2 %surface.1 = (f32[2,8,128]{2,1,0:T(8,128)S(1)}, f32[2,8,128]{2,1,0:T(8,128)S(1)}, bf16[64,8,128]{2,1,0:T(8,128)(2,1)}) custom-call(bf16[64,40,128]{2,1,0:T(8,128)(2,1)S(1)} %all-to-all-done.received_ref, s32[8,128]{1,0:T(8,128)S(1)} %copy-done.5, f32[2,8,128]{2,1,0:T(8,128)S(1)} %get-tuple-element.36.sum_ref, f32[2,8,128]{2,1,0:T(8,128)S(1)} %get-tuple-element.37.rate_ref, ...), custom_call_target="tpu_custom_call" | custom-call | bytes 1048576 | tf_op jit(solution)/shard_map/surface/pallas_call | solution.py:491
  49.3 10.5 %all-to-all-start.1 = ((bf16[64,8,128]{2,1,0:T(8,128)(2,1)}), bf16[64,8,128]{2,1,0:T(8,128)(2,1)S(1)}, u32[]{:S(2)}, u32[]{:S(2)}) async-start(bf16[64,8,128]{2,1,0:T(8,128)(2,1)} %get-tuple-element.48), calls=%async_computation.1 | async-start | bytes 262144 | tf_op jit(solution)/shard_map/all_to_all | solution.py:498
  59.9 0.0 copy-done.7
  59.9 0.0 copy-done
  59.9 3.1 %ocean.1 = (f32[2,80,8,128]{3,2,1,0:T(8,128)}, f32[128,128]{1,0:T(8,128)S(1)}, bf16[128,512]{1,0:T(8,128)(2,1)S(1)}) custom-call(s32[64]{0:T(128)S(1)} %bitcast.16, s32[64]{0:T(128)S(1)} %get-tuple-element.26.slot_ref, f32[80,80]{1,0:T(8,128)S(1)} %copy-done.4, f32[2,8,80,128]{3,2,1,0:T(8,128)S(1)} %get-tuple-element.34.twice_ref, ...), custom_call_target="tpu_custom_call" | custom-call | flops 157286400 | bytes 2097152 | tf_op jit(solution)/shard_map/ocean/pallas_call | solution.py:499
  63.0 7.3 %all-to-all-done.1.returned_ref = bf16[64,8,128]{2,1,0:T(8,128)(2,1)S(1)} async-done(((bf16[64,8,128]{2,1,0:T(8,128)(2,1)}), bf16[64,8,128]{2,1,0:T(8,128)(2,1)S(1)}, u32[]{:S(2)}, u32[]{:S(2)}) %all-to-all-start.1) | async-done | bytes 131104 | tf_op jit(solution)/shard_map/all_to_all | solution.py:498
  70.3 1.6 %backward.1 = f32[64,2,128]{2,1,0:T(2,128)} custom-call(bf16[128,512]{1,0:T(8,128)(2,1)S(1)} %get-tuple-element.47.picks_ref, bf16[64,8,128]{2,1,0:T(8,128)(2,1)S(1)} %all-to-all-done.1.returned_ref, bf16[64,128,128]{2,1,0:T(8,128)(2,1)S(1)} %bitcast.12, f32[128,128]{1,0:T(8,128)S(1)} %get-tuple-element.49.sums_ref), custom_call_target="tpu_custom_call" | custom-call | flops 16777216 | bytes 3145728 | tf_op jit(solution)/shard_map/backward/pallas_call | solution.py:507
  (1 shorter events, 0.0 us)
Async XLA Ops:
  0.6 14.4 %copy-start.1 = (f32[2,80,8,128]{3,2,1,0:T(8,128)S(1)}, f32[2,80,8,128]{3,2,1,0:T(8,128)}, u32[]{:S(2)}) copy-start(f32[2,80,8,128]{3,2,1,0:T(8,128)} %param.12) | copy-start | bytes 1966084
  0.6 14.4 %copy-start.5 = (s32[8,128]{1,0:T(8,128)S(1)}, s32[8,128]{1,0:T(8,128)}, u32[]{:S(2)}) copy-start(s32[8,128]{1,0:T(8,128)} %mask_ref.7) | copy-start | bytes 12292
  0.7 28.3 %copy-start.6 = (f32[8,128]{1,0:T(8,128)S(1)}, f32[8,128]{1,0:T(8,128)}, u32[]{:S(2)}) copy-start(f32[8,128]{1,0:T(8,128)} %wet_ref.3) | copy-start | bytes 12292
  4.2 40.0 %copy-start.4 = (f32[80,80]{1,0:T(8,128)S(1)}, f32[80,80]{1,0:T(8,128)}, u32[]{:S(2)}) copy-start(f32[80,80]{1,0:T(8,128)} %mixing_ref.3) | copy-start | bytes 76804
  4.3 33.8 %all-to-all-start = ((bf16[64,40,128]{2,1,0:T(8,128)(2,1)}), bf16[64,40,128]{2,1,0:T(8,128)(2,1)S(1)}, u32[]{:S(2)}, u32[]{:S(2)}) async-start(bf16[64,40,128]{2,1,0:T(8,128)(2,1)} %get-tuple-element.35), calls=%async_computation | async-start | bytes 1310720 | tf_op jit(solution)/shard_map/all_to_all | solution.py:462
  15.1 44.8 %copy-start.7 = (s32[1,64,1]{1,2,0:T(1,128)S(1)}, s32[1,64,1]{1,2,0:T(1,128)}, u32[]{:S(2)}) copy-start(s32[1,64,1]{1,2,0:T(1,128)} %param.10) | copy-start | bytes 772
  15.3 44.6 %copy-start = (bf16[1,64,128,128]{3,2,1,0:T(8,128)(2,1)S(1)}, bf16[1,64,128,128]{3,2,1,0:T(8,128)(2,1)}, u32[]{:S(2)}) copy-start(bf16[1,64,128,128]{3,2,1,0:T(8,128)(2,1)} %param.9) | copy-start | bytes 6291460
  15.3 8.6 %collective-permute-start = (f32[2,168,128]{2,1,0:T(8,128)S(1)}, f32[2,168,128]{2,1,0:T(8,128)S(1)}, u32[]{:S(2)}, u32[]{:S(2)}) collective-permute-start(f32[2,168,128]{2,1,0:T(8,128)S(1)} %get-tuple-element.27), channel_id=1, source_target_pairs={{0,64},{64,128},{128,192},{192,256},{256,320},{320,384},{384,448},... | collective-permute-start | bytes 516104 | tf_op jit(solution)/shard_map/ppermute | solution.py:467
  20.6 8.3 %collective-permute-start.1 = (f32[2,168,128]{2,1,0:T(8,128)S(1)}, f32[2,168,128]{2,1,0:T(8,128)S(1)}, u32[]{:S(2)}, u32[]{:S(2)}) collective-permute-start(f32[2,168,128]{2,1,0:T(8,128)S(1)} %get-tuple-element.28), channel_id=1, source_target_pairs={{64,0},{128,64},{192,128},{256,192},{320,256},{384,320},{448,384},... | collective-permute-start | bytes 516104 | tf_op jit(solution)/shard_map/ppermute | solution.py:468
  30.3 1.0 %copy-start.2 = (f32[12,168,128]{2,1,0:T(8,128)}, f32[12,168,128]{2,1,0:T(8,128)S(1)}, u32[]{:S(2)}) copy-start(f32[12,168,128]{2,1,0:T(8,128)S(1)} %get-tuple-element.29.slab_ref) | copy-start | bytes 3096580
  31.3 12.9 %collective-permute-start.2 = (f32[48,128]{1,0:T(8,128)}, f32[48,128]{1,0:T(8,128)S(1)}, u32[]{:S(2)}, u32[]{:S(2)}) collective-permute-start(f32[48,128]{1,0:T(8,128)} %get-tuple-element.32), channel_id=1, source_target_pairs={{0,1},{2,3},{4,5},{6,7},{8,9},{10,11},{12,13},{14,15},{16,17},{18,... | collective-permute-start | bytes 73736 | tf_op jit(solution)/shard_map/ppermute | solution.py:474
  34.8 9.4 %collective-permute-start.3 = (f32[48,128]{1,0:T(8,128)}, f32[48,128]{1,0:T(8,128)}, u32[]{:S(2)}, u32[]{:S(2)}) collective-permute-start(f32[48,128]{1,0:T(8,128)} %get-tuple-element.33), channel_id=1, source_target_pairs={{1,2},{3,4},{5,6},{7,8},{9,10},{11,12},{13,14},{15,16},{17,18},{19... | collective-permute-start | bytes 73736 | tf_op jit(solution)/shard_map/ppermute | solution.py:475
  38.9 9.2 %collective-permute-start.4 = (f32[2,8,128]{2,1,0:T(8,128)S(1)}, f32[2,8,128]{2,1,0:T(8,128)S(1)}, u32[]{:S(2)}, u32[]{:S(2)}) collective-permute-start(f32[2,8,128]{2,1,0:T(8,128)S(1)} %get-tuple-element.38.first_ref), channel_id=1, source_target_pairs={{0,64},{64,128},{128,192},{192,256},{256,320},{320,384},{384,448},... | collective-permute-start | bytes 24584 | tf_op jit(solution)/shard_map/ppermute | solution.py:489
  42.3 5.9 %collective-permute-start.5 = (f32[2,8,128]{2,1,0:T(8,128)S(1)}, f32[2,8,128]{2,1,0:T(8,128)S(1)}, u32[]{:S(2)}, u32[]{:S(2)}) collective-permute-start(f32[2,8,128]{2,1,0:T(8,128)S(1)} %get-tuple-element.38.first_ref), channel_id=1, source_target_pairs={{64,0},{128,64},{192,128},{256,192},{320,256},{384,320},{448,384},... | collective-permute-start | bytes 24584 | tf_op jit(solution)/shard_map/ppermute | solution.py:490
  44.3 1.2 %copy-start.3 = (f32[12,168,128]{2,1,0:T(8,128)S(1)}, f32[12,168,128]{2,1,0:T(8,128)}, u32[]{:S(2)}) copy-start(f32[12,168,128]{2,1,0:T(8,128)} %copy-done.2) | copy-start | bytes 3096580
  49.3 20.9 %all-to-all-start.1 = ((bf16[64,8,128]{2,1,0:T(8,128)(2,1)}), bf16[64,8,128]{2,1,0:T(8,128)(2,1)S(1)}, u32[]{:S(2)}, u32[]{:S(2)}) async-start(bf16[64,8,128]{2,1,0:T(8,128)(2,1)} %get-tuple-element.48), calls=%async_computation.1 | async-start | bytes 262144 | tf_op jit(solution)/shard_map/all_to_all | solution.py:498

commit v7 on v6

--- a/solution.py
+++ b/solution.py
@@ -36,6 +36,14 @@
 
 def in_hbm(*values):
     return [pltpu.with_memory_space_constraint(v, pltpu.HBM) for v in values]
+
+
+def in_vmem(*values):
+    return [pltpu.with_memory_space_constraint(v, pltpu.VMEM) for v in values]
+
+
+def held(*dims, dtype=f32):
+    return pltpu.VMEM(dims, dtype)
 
 
 def shape(*dims, dtype=f32):
@@ -122,8 +130,8 @@
     mask = mask_ref[...].astype(f32)
     for i in range(2):
         for out_ref, r in ((top_ref, i), (bottom_ref, rows - 2 + i)):
-            out_ref[i, 0:planes, :] = x_ref[:, r, :]
-            out_ref[i, planes : planes + 8, :] = jnp.broadcast_to(mask[r : r + 1, :], (8, width))
+            lines = jnp.broadcast_to(mask[r : r + 1, :], (out_ref.shape[1] - planes, width))
+            out_ref[i] = jnp.concatenate([x_ref[:, r, :], lines], axis=0).astype(bf16)
 
 
 def packing(rows, planes, width):
@@ -144,8 +152,8 @@
     span, per, groups, packs = packing(rows, planes, width)
     mask = mask_ref[...].astype(f32)
     for i in range(2):
-        slab_ref[i] = before_ref[i]
-        slab_ref[rows + 2 + i] = after_ref[i]
+        slab_ref[i] = before_ref[i].astype(f32)[: planes + 8]
+        slab_ref[rows + 2 + i] = after_ref[i].astype(f32)[: planes + 8]
     for r in range(rows):
         slab_ref[r + 2, 0:planes, :] = x_ref[:, r, :]
         slab_ref[r + 2, planes : planes + 8, :] = jnp.broadcast_to(mask[r : r + 1, :], (8, width))
@@ -462,15 +470,15 @@
     received = lax.all_to_all(packed, "blk", split_axis=0, concat_axis=0, tiled=True)
 
     top, bottom = call(
-        rows_kernel, "rows", (shape(2, planes + 8, width),) * 2, [vmem, vmem], moved=1 << 20
+        rows_kernel, "rows", (held(2, planes + 16, width, dtype=bf16),) * 2, [vmem, vmem], moved=1 << 20
     )(state, land_mask)
     before = lax.ppermute(bottom, "sec", up_sec)
     after = lax.ppermute(top, "sec", down_sec)
-    packed_shape = shape(packed_lines, width)
+    packed_shape = held(packed_lines, width)
     slab, first_columns, last_columns, near, far = call(
         columns_kernel, "columns",
-        (shape(rows + 4, planes + 8, width),) + (packed_shape,) * 4, [vmem] * 5, moved=2 << 20,
-    )(state, land_mask, wet_fraction, before, after)
+        (held(rows + 4, planes + 8, width),) + (packed_shape,) * 4, [vmem] * 5, moved=2 << 20,
+    )(*in_vmem(state, land_mask, wet_fraction, before, after))
     near = lax.ppermute(near, "blk", swaps[0])
     far = lax.ppermute(far, "blk", swaps[1])
     surface_shape = shape(tracers, rows, width)
@@ -481,7 +489,7 @@
             shape(7, rows, width), shape(2, 8, width),
         ),
         [vmem] * 6, scratch=[pltpu.VMEM((rows + 4, planes, width), f32)], flops=20 << 20, moved=3 << 20,
-    )(slab, first_columns, last_columns, near, far, mixing)
+    )(*in_vmem(slab, first_columns, last_columns, near, far, mixing))
 
     drive_sum, drive_rate, first, edges = call(
         drive_kernel, "drive", (surface_shape,) * 3 + (shape(8, width),), [vmem] * 4, moved=1 << 20

time: 72.4 us -> 70.6 us (0.975)
  waiting for transfers between devices: 13.7 us -> 12.1 us
    ppermute x1, waiting for transfers between devices: 1.34 us -> 0.01 us  [per_device(): before = lax.ppermute(bottom, 'sec', up_sec)]
  transfers between devices with their start and end apart: 8 -> 8, of which waited for: 4 -> 2; matrix products, arithmetic and copies ran while one was open for 0% -> 0% of each run, Pallas kernels for 11% -> 11%
where the time goes in v7:
time: 70.6 us; the launch traced here: 70.1 us
  starting transfers between devices  40.5 us (57%)
  Pallas kernels  14.4 us (20%)
  waiting for transfers between devices  12.1 us (17%)
  local copies, waits for them, and re-layouts  2.24 us (3%)
  between operations  0.87 us (1%)
    all_to_all x1, starting transfers between devices, per_device(): lax.all_to_all(packed, 'blk', split_axis=0, concat_axis=0, tiled=True)  10.8 us
    all_to_all x1, starting transfers between devices, per_device(): lax.all_to_all(back, 'blk', split_axis=0, concat_axis=0, tiled=True)  9.89 us
    all_to_all x1, waiting for transfers between devices, per_device(): lax.all_to_all(back, 'blk', split_axis=0, concat_axis=0, tiled=True)  7.28 us
    ppermute x1, starting transfers between devices, per_device(): before = lax.ppermute(bottom, 'sec', up_sec)  5.34 us
    ppermute x1, waiting for transfers between devices, per_device(): after = lax.ppermute(top, 'sec', down_sec)  4.84 us
    ppermute x1, starting transfers between devices, per_device(): first_before = lax.ppermute(first, 'sec', up_sec)  4 us
    pallas_call x1, Pallas kernels, per_device(): call(forward_kernel, 'forward', (pltpu.HBM((blocks, 2 * fields + 8, width...  3.58 us
    ppermute x1, starting transfers between devices, per_device(): near = lax.ppermute(near, 'blk', swaps[0])  3.49 us
  transfers between devices with their start and end apart: 8, of which 2 were waited for; matrix products, arithmetic and copies ran while one was open for 0% of the time, Pallas kernels for 11%

profile of v7, /device:TPU:193, one launch (start us, length us, event | category | flops | bytes accessed | tf_op | source)
XLA Modules:
  0.0 70.1 jit_solution(2882376992946069339)
XLA Ops:
  0.6 0.0 copy-start.1
  0.6 0.0 copy-start.5
  0.7 0.0 copy-start.6
  0.7 3.6 %forward.1 = (bf16[64,40,128]{2,1,0:T(8,128)(2,1)}, s32[64]{0:T(128)S(1)}) custom-call(s32[64]{0:T(128)} %bitcast.15, s32[64]{0:T(128)} %bitcast.19, bf16[64,16,128]{2,1,0:T(8,128)(2,1)} %bitcast.17, bf16[64,128,128]{2,1,0:T(8,128)(2,1)} %bitcast.10), custom_call_target="tpu_custom_call" | custom-call | flops 33554432 | bytes 3145728 | tf_op jit(solution)/shard_map/forward/pallas_call | solution.py:457
  4.2 0.0 copy-start.4
  4.3 10.8 %all-to-all-start = ((bf16[64,40,128]{2,1,0:T(8,128)(2,1)}), bf16[64,40,128]{2,1,0:T(8,128)(2,1)S(1)}, u32[]{:S(2)}, u32[]{:S(2)}) async-start(bf16[64,40,128]{2,1,0:T(8,128)(2,1)} %get-tuple-element.35), calls=%async_computation | async-start | bytes 1310720 | tf_op jit(solution)/shard_map/all_to_all | solution.py:470
  15.1 0.0 copy-done.1
  15.1 0.0 copy-done.5
  15.1 0.0 copy-start
  15.1 0.0 copy-start.7
  15.1 0.2 rows.1
  15.3 5.3 %collective-permute-start = (bf16[2,176,128]{2,1,0:T(8,128)(2,1)S(1)}, bf16[2,176,128]{2,1,0:T(8,128)(2,1)S(1)}, u32[]{:S(2)}, u32[]{:S(2)}) collective-permute-start(bf16[2,176,128]{2,1,0:T(8,128)(2,1)S(1)} %get-tuple-element.27), channel_id=1, source_target_pairs={{0,64},{64,128},{128,192},{192,256},{256,320},{320,384},{384,448},... | collective-permute-start | bytes 270344 | tf_op jit(solution)/shard_map/ppermute | solution.py:475
  20.6 1.9 %collective-permute-start.1 = (bf16[2,176,128]{2,1,0:T(8,128)(2,1)S(1)}, bf16[2,176,128]{2,1,0:T(8,128)(2,1)S(1)}, u32[]{:S(2)}, u32[]{:S(2)}) collective-permute-start(bf16[2,176,128]{2,1,0:T(8,128)(2,1)S(1)} %get-tuple-element.28), channel_id=1, source_target_pairs={{64,0},{128,64},{192,128},{256,192},{320,256},{384,320},{448,384},... | collective-permute-start | bytes 270344 | tf_op jit(solution)/shard_map/ppermute | solution.py:476
  22.6 0.0 collective-permute-done.before_ref
  22.6 4.8 %collective-permute-done.1.after_ref = bf16[2,176,128]{2,1,0:T(8,128)(2,1)S(1)} collective-permute-done((bf16[2,176,128]{2,1,0:T(8,128)(2,1)S(1)}, bf16[2,176,128]{2,1,0:T(8,128)(2,1)S(1)}, u32[]{:S(2)}, u32[]{:S(2)}) %collective-permute-start.1) | collective-permute-done | bytes 90144 | tf_op jit(solution)/shard_map/ppermute | solution.py:476
  27.4 0.0 copy-done.6
  27.4 1.4 %columns.1 = (f32[12,168,128]{2,1,0:T(8,128)S(1)}, f32[48,128]{1,0:T(8,128)S(1)}, f32[48,128]{1,0:T(8,128)S(1)}, f32[48,128]{1,0:T(8,128)}, f32[48,128]{1,0:T(8,128)}) custom-call(f32[160,8,128]{2,1,0:T(8,128)S(1)} %bitcast.14, s32[8,128]{1,0:T(8,128)S(1)} %copy-done.5, f32[8,128]{1,0:T(8,128)S(1)} %copy-done.6, ...), custom_call_target="tpu_custom_call" | custom-call | bytes 2097152 | tf_op jit(solution)/shard_map/columns/pallas_call | solution.py:478
  28.8 0.0 copy-start.2
  28.8 1.0 %copy-done.2 = f32[12,168,128]{2,1,0:T(8,128)} copy-done((f32[12,168,128]{2,1,0:T(8,128)}, f32[12,168,128]{2,1,0:T(8,128)S(1)}, u32[]{:S(2)}) %copy-start.2) | copy-done | bytes 1032216
  29.8 3.5 %collective-permute-start.2 = (f32[48,128]{1,0:T(8,128)}, f32[48,128]{1,0:T(8,128)S(1)}, u32[]{:S(2)}, u32[]{:S(2)}) collective-permute-start(f32[48,128]{1,0:T(8,128)} %get-tuple-element.32), channel_id=1, source_target_pairs={{0,1},{2,3},{4,5},{6,7},{8,9},{10,11},{12,13},{14,15},{16,17},{18,... | collective-permute-start | bytes 73736 | tf_op jit(solution)/shard_map/ppermute | solution.py:482
  33.3 3.1 %collective-permute-start.3 = (f32[48,128]{1,0:T(8,128)}, f32[48,128]{1,0:T(8,128)}, u32[]{:S(2)}, u32[]{:S(2)}) collective-permute-start(f32[48,128]{1,0:T(8,128)} %get-tuple-element.33), channel_id=1, source_target_pairs={{1,2},{3,4},{5,6},{7,8},{9,10},{11,12},{13,14},{15,16},{17,18},{19... | collective-permute-start | bytes 73736 | tf_op jit(solution)/shard_map/ppermute | solution.py:483
  36.4 0.0 all-to-all-done.received_ref
  36.4 0.8 %drive.1 = (f32[2,8,128]{2,1,0:T(8,128)S(1)}, f32[2,8,128]{2,1,0:T(8,128)S(1)}, f32[2,8,128]{2,1,0:T(8,128)S(1)}, f32[8,128]{1,0:T(8,128)S(1)}) custom-call(bf16[64,40,128]{2,1,0:T(8,128)(2,1)S(1)} %all-to-all-done.received_ref, f32[2,8,128]{2,1,0:T(8,128)S(1)} %slice_bitcast_fusion.top_ref, s32[8,128]{1,0:T(8,128)S(1)} %copy-done.5, f32[8,128]{1,0:T(8,128)S(1)} %copy-done.6), custom_call_target="tpu_custom_call" | custom-call | bytes 1048576 | tf_op jit(solution)/shard_map/drive/pallas_call | solution.py:494
  37.2 4.0 %collective-permute-start.4 = (f32[2,8,128]{2,1,0:T(8,128)S(1)}, f32[2,8,128]{2,1,0:T(8,128)S(1)}, u32[]{:S(2)}, u32[]{:S(2)}) collective-permute-start(f32[2,8,128]{2,1,0:T(8,128)S(1)} %get-tuple-element.38.first_ref), channel_id=1, source_target_pairs={{0,64},{64,128},{128,192},{192,256},{256,320},{320,384},{384,448},... | collective-permute-start | bytes 24584 | tf_op jit(solution)/shard_map/ppermute | solution.py:497
  41.2 1.9 %collective-permute-start.5 = (f32[2,8,128]{2,1,0:T(8,128)S(1)}, f32[2,8,128]{2,1,0:T(8,128)S(1)}, u32[]{:S(2)}, u32[]{:S(2)}) collective-permute-start(f32[2,8,128]{2,1,0:T(8,128)S(1)} %get-tuple-element.38.first_ref), channel_id=1, source_target_pairs={{64,0},{128,64},{192,128},{256,192},{320,256},{384,320},{448,384},... | collective-permute-start | bytes 24584 | tf_op jit(solution)/shard_map/ppermute | solution.py:498
  43.2 0.0 collective-permute-done.2.near_ref
  43.2 0.0 collective-permute-done.3.far_ref
  43.2 0.0 copy-done.4
  43.2 0.0 copy-start.3
  43.2 1.2 %copy-done.3 = f32[12,168,128]{2,1,0:T(8,128)S(1)} copy-done((f32[12,168,128]{2,1,0:T(8,128)S(1)}, f32[12,168,128]{2,1,0:T(8,128)}, u32[]{:S(2)}) %copy-start.3) | copy-done | bytes 1032216
  44.4 2.6 %stencil.1 = (f32[2,8,80,128]{3,2,1,0:T(8,128)S(1)}, f32[2,8,128]{2,1,0:T(8,128)S(1)}, f32[2,8,128]{2,1,0:T(8,128)S(1)}, f32[7,8,128]{2,1,0:T(8,128)S(1)}, f32[2,8,128]{2,1,0:T(8,128)S(1)}) custom-call(f32[12,168,128]{2,1,0:T(8,128)S(1)} %copy-done.3, f32[48,128]{1,0:T(8,128)S(1)} %get-tuple-element.30.first_ref, f32[48,128]{1,0:T(8,128)S(1)} %get-tuple-element.31.last_ref, ...), custom_call_target="tpu_custom_call" | custom-call | flops 20971520 | bytes 3145728 | tf_op jit(solution)/shard_map/stencil/pallas_call | solution.py:485
  47.0 0.0 collective-permute-done.4.before_ref
  47.0 0.0 collective-permute-done.5.after_ref
  47.0 1.2 %surface.1 = (f32[2,8,128]{2,1,0:T(8,128)S(1)}, f32[2,8,128]{2,1,0:T(8,128)S(1)}, bf16[64,8,128]{2,1,0:T(8,128)(2,1)}) custom-call(bf16[64,40,128]{2,1,0:T(8,128)(2,1)S(1)} %all-to-all-done.received_ref, s32[8,128]{1,0:T(8,128)S(1)} %copy-done.5, f32[2,8,128]{2,1,0:T(8,128)S(1)} %get-tuple-element.36.sum_ref, f32[2,8,128]{2,1,0:T(8,128)S(1)} %get-tuple-element.37.rate_ref, ...), custom_call_target="tpu_custom_call" | custom-call | bytes 1048576 | tf_op jit(solution)/shard_map/surface/pallas_call | solution.py:499
  48.2 9.9 %all-to-all-start.1 = ((bf16[64,8,128]{2,1,0:T(8,128)(2,1)}), bf16[64,8,128]{2,1,0:T(8,128)(2,1)S(1)}, u32[]{:S(2)}, u32[]{:S(2)}) async-start(bf16[64,8,128]{2,1,0:T(8,128)(2,1)} %get-tuple-element.48), calls=%async_computation.1 | async-start | bytes 262144 | tf_op jit(solution)/shard_map/all_to_all | solution.py:506
  58.1 0.0 copy-done
  58.1 0.0 copy-done.7
  58.1 3.1 %ocean.1 = (f32[2,80,8,128]{3,2,1,0:T(8,128)}, f32[128,128]{1,0:T(8,128)S(1)}, bf16[128,512]{1,0:T(8,128)(2,1)S(1)}) custom-call(s32[64]{0:T(128)S(1)} %bitcast.16, s32[64]{0:T(128)S(1)} %get-tuple-element.26.slot_ref, f32[80,80]{1,0:T(8,128)S(1)} %copy-done.4, f32[2,8,80,128]{3,2,1,0:T(8,128)S(1)} %get-tuple-element.34.twice_ref, ...), custom_call_target="tpu_custom_call" | custom-call | flops 157286400 | bytes 2097152 | tf_op jit(solution)/shard_map/ocean/pallas_call | solution.py:507
  61.2 7.3 %all-to-all-done.1.returned_ref = bf16[64,8,128]{2,1,0:T(8,128)(2,1)S(1)} async-done(((bf16[64,8,128]{2,1,0:T(8,128)(2,1)}), bf16[64,8,128]{2,1,0:T(8,128)(2,1)S(1)}, u32[]{:S(2)}, u32[]{:S(2)}) %all-to-all-start.1) | async-done | bytes 131104 | tf_op jit(solution)/shard_map/all_to_all | solution.py:506
  68.5 1.6 %backward.1 = f32[64,2,128]{2,1,0:T(2,128)} custom-call(bf16[128,512]{1,0:T(8,128)(2,1)S(1)} %get-tuple-element.47.picks_ref, bf16[64,8,128]{2,1,0:T(8,128)(2,1)S(1)} %all-to-all-done.1.returned_ref, bf16[64,128,128]{2,1,0:T(8,128)(2,1)S(1)} %bitcast.12, f32[128,128]{1,0:T(8,128)S(1)} %get-tuple-element.49.sums_ref), custom_call_target="tpu_custom_call" | custom-call | flops 16777216 | bytes 3145728 | tf_op jit(solution)/shard_map/backward/pallas_call | solution.py:515
  (1 shorter events, 0.0 us)
Async XLA Ops:
  0.6 14.4 %copy-start.1 = (f32[2,80,8,128]{3,2,1,0:T(8,128)S(1)}, f32[2,80,8,128]{3,2,1,0:T(8,128)}, u32[]{:S(2)}) copy-start(f32[2,80,8,128]{3,2,1,0:T(8,128)} %param.12) | copy-start | bytes 1966084
  0.6 14.4 %copy-start.5 = (s32[8,128]{1,0:T(8,128)S(1)}, s32[8,128]{1,0:T(8,128)}, u32[]{:S(2)}) copy-start(s32[8,128]{1,0:T(8,128)} %mask_ref.7) | copy-start | bytes 12292
  0.7 26.8 %copy-start.6 = (f32[8,128]{1,0:T(8,128)S(1)}, f32[8,128]{1,0:T(8,128)}, u32[]{:S(2)}) copy-start(f32[8,128]{1,0:T(8,128)} %wet_ref.3) | copy-start | bytes 12292
  4.2 38.9 %copy-start.4 = (f32[80,80]{1,0:T(8,128)S(1)}, f32[80,80]{1,0:T(8,128)}, u32[]{:S(2)}) copy-start(f32[80,80]{1,0:T(8,128)} %mixing_ref.3) | copy-start | bytes 76804
  4.3 32.1 %all-to-all-start = ((bf16[64,40,128]{2,1,0:T(8,128)(2,1)}), bf16[64,40,128]{2,1,0:T(8,128)(2,1)S(1)}, u32[]{:S(2)}, u32[]{:S(2)}) async-start(bf16[64,40,128]{2,1,0:T(8,128)(2,1)} %get-tuple-element.35), calls=%async_computation | async-start | bytes 1310720 | tf_op jit(solution)/shard_map/all_to_all | solution.py:470
  15.1 43.0 %copy-start = (bf16[1,64,128,128]{3,2,1,0:T(8,128)(2,1)S(1)}, bf16[1,64,128,128]{3,2,1,0:T(8,128)(2,1)}, u32[]{:S(2)}) copy-start(bf16[1,64,128,128]{3,2,1,0:T(8,128)(2,1)} %param.9) | copy-start | bytes 6291460
  15.1 43.0 %copy-start.7 = (s32[1,64,1]{1,2,0:T(1,128)S(1)}, s32[1,64,1]{1,2,0:T(1,128)}, u32[]{:S(2)}) copy-start(s32[1,64,1]{1,2,0:T(1,128)} %param.10) | copy-start | bytes 772
  15.3 7.3 %collective-permute-start = (bf16[2,176,128]{2,1,0:T(8,128)(2,1)S(1)}, bf16[2,176,128]{2,1,0:T(8,128)(2,1)S(1)}, u32[]{:S(2)}, u32[]{:S(2)}) collective-permute-start(bf16[2,176,128]{2,1,0:T(8,128)(2,1)S(1)} %get-tuple-element.27), channel_id=1, source_target_pairs={{0,64},{64,128},{128,192},{192,256},{256,320},{320,384},{384,448},... | collective-permute-start | bytes 270344 | tf_op jit(solution)/shard_map/ppermute | solution.py:475
  20.6 6.8 %collective-permute-start.1 = (bf16[2,176,128]{2,1,0:T(8,128)(2,1)S(1)}, bf16[2,176,128]{2,1,0:T(8,128)(2,1)S(1)}, u32[]{:S(2)}, u32[]{:S(2)}) collective-permute-start(bf16[2,176,128]{2,1,0:T(8,128)(2,1)S(1)} %get-tuple-element.28), channel_id=1, source_target_pairs={{64,0},{128,64},{192,128},{256,192},{320,256},{384,320},{448,384},... | collective-permute-start | bytes 270344 | tf_op jit(solution)/shard_map/ppermute | solution.py:476
  28.8 1.0 %copy-start.2 = (f32[12,168,128]{2,1,0:T(8,128)}, f32[12,168,128]{2,1,0:T(8,128)S(1)}, u32[]{:S(2)}) copy-start(f32[12,168,128]{2,1,0:T(8,128)S(1)} %get-tuple-element.29.slab_ref) | copy-start | bytes 3096580
  29.8 13.4 %collective-permute-start.2 = (f32[48,128]{1,0:T(8,128)}, f32[48,128]{1,0:T(8,128)S(1)}, u32[]{:S(2)}, u32[]{:S(2)}) collective-permute-start(f32[48,128]{1,0:T(8,128)} %get-tuple-element.32), channel_id=1, source_target_pairs={{0,1},{2,3},{4,5},{6,7},{8,9},{10,11},{12,13},{14,15},{16,17},{18,... | collective-permute-start | bytes 73736 | tf_op jit(solution)/shard_map/ppermute | solution.py:482
  33.3 9.9 %collective-permute-start.3 = (f32[48,128]{1,0:T(8,128)}, f32[48,128]{1,0:T(8,128)}, u32[]{:S(2)}, u32[]{:S(2)}) collective-permute-start(f32[48,128]{1,0:T(8,128)} %get-tuple-element.33), channel_id=1, source_target_pairs={{1,2},{3,4},{5,6},{7,8},{9,10},{11,12},{13,14},{15,16},{17,18},{19... | collective-permute-start | bytes 73736 | tf_op jit(solution)/shard_map/ppermute | solution.py:483
  37.2 9.8 %collective-permute-start.4 = (f32[2,8,128]{2,1,0:T(8,128)S(1)}, f32[2,8,128]{2,1,0:T(8,128)S(1)}, u32[]{:S(2)}, u32[]{:S(2)}) collective-permute-start(f32[2,8,128]{2,1,0:T(8,128)S(1)} %get-tuple-element.38.first_ref), channel_id=1, source_target_pairs={{0,64},{64,128},{128,192},{192,256},{256,320},{320,384},{384,448},... | collective-permute-start | bytes 24584 | tf_op jit(solution)/shard_map/ppermute | solution.py:497
  41.2 5.8 %collective-permute-start.5 = (f32[2,8,128]{2,1,0:T(8,128)S(1)}, f32[2,8,128]{2,1,0:T(8,128)S(1)}, u32[]{:S(2)}, u32[]{:S(2)}) collective-permute-start(f32[2,8,128]{2,1,0:T(8,128)S(1)} %get-tuple-element.38.first_ref), channel_id=1, source_target_pairs={{64,0},{128,64},{192,128},{256,192},{320,256},{384,320},{448,384},... | collective-permute-start | bytes 24584 | tf_op jit(solution)/shard_map/ppermute | solution.py:498
  43.2 1.2 %copy-start.3 = (f32[12,168,128]{2,1,0:T(8,128)S(1)}, f32[12,168,128]{2,1,0:T(8,128)}, u32[]{:S(2)}) copy-start(f32[12,168,128]{2,1,0:T(8,128)} %copy-done.2) | copy-start | bytes 3096580
  48.2 20.3 %all-to-all-start.1 = ((bf16[64,8,128]{2,1,0:T(8,128)(2,1)}), bf16[64,8,128]{2,1,0:T(8,128)(2,1)S(1)}, u32[]{:S(2)}, u32[]{:S(2)}) async-start(bf16[64,8,128]{2,1,0:T(8,128)(2,1)} %get-tuple-element.48), calls=%async_computation.1 | async-start | bytes 262144 | tf_op jit(solution)/shard_map/all_to_all | solution.py:506

commit v8 on v7

--- a/solution.py
+++ b/solution.py
@@ -144,19 +144,24 @@
     return lax.rem(lax.axis_index("blk"), 2) == 1
 
 
-def columns_kernel(
-    x_ref, mask_ref, wet_ref, before_ref, after_ref, slab_ref, first_ref, last_ref, near_ref, far_ref
-):
+def fill_slab(slab_ref, x_ref, mask, before_ref, after_ref):
     planes, rows, width = x_ref.shape
-    levels = planes // 2
-    span, per, groups, packs = packing(rows, planes, width)
-    mask = mask_ref[...].astype(f32)
     for i in range(2):
         slab_ref[i] = before_ref[i].astype(f32)[: planes + 8]
         slab_ref[rows + 2 + i] = after_ref[i].astype(f32)[: planes + 8]
     for r in range(rows):
         slab_ref[r + 2, 0:planes, :] = x_ref[:, r, :]
         slab_ref[r + 2, planes : planes + 8, :] = jnp.broadcast_to(mask[r : r + 1, :], (8, width))
+
+
+def columns_kernel(
+    x_ref, mask_ref, wet_ref, before_ref, after_ref, first_ref, last_ref, near_ref, far_ref, slab_ref
+):
+    planes, rows, width = x_ref.shape
+    levels = planes // 2
+    span, per, groups, packs = packing(rows, planes, width)
+    mask = mask_ref[...].astype(f32)
+    fill_slab(slab_ref, x_ref, mask, before_ref, after_ref)
     lane = lane_iota((8, width))
 
     def turn(value, by):
@@ -214,12 +219,11 @@
 
 
 def stencil_kernel(
-    slab_ref, first_ref, last_ref, near_ref, far_ref, mixing_ref,
-    twice_ref, once_top_ref, twice_top_ref, weights_ref, beside_ref, work_ref,
+    x_ref, mask_ref, before_ref, after_ref, first_ref, last_ref, near_ref, far_ref, mixing_ref,
+    twice_ref, once_top_ref, twice_top_ref, weights_ref, beside_ref, slab_ref, work_ref,
 ):
-    rows = slab_ref.shape[0] - 4
-    planes = slab_ref.shape[1] - 8
-    width = slab_ref.shape[2]
+    planes, rows, width = x_ref.shape
+    fill_slab(slab_ref, x_ref, mask_ref[...].astype(f32), before_ref, after_ref)
     levels = planes // 2
     span, per, groups, packs = packing(rows, planes, width)
     packed = 8 * packs
@@ -472,12 +476,12 @@
     top, bottom = call(
         rows_kernel, "rows", (held(2, planes + 16, width, dtype=bf16),) * 2, [vmem, vmem], moved=1 << 20
     )(state, land_mask)
+    after = lax.ppermute(top, "sec", down_sec)
     before = lax.ppermute(bottom, "sec", up_sec)
-    after = lax.ppermute(top, "sec", down_sec)
     packed_shape = held(packed_lines, width)
-    slab, first_columns, last_columns, near, far = call(
-        columns_kernel, "columns",
-        (held(rows + 4, planes + 8, width),) + (packed_shape,) * 4, [vmem] * 5, moved=2 << 20,
+    slab = pltpu.VMEM((rows + 4, planes + 8, width), f32)
+    first_columns, last_columns, near, far = call(
+        columns_kernel, "columns", (packed_shape,) * 4, [vmem] * 5, scratch=[slab], moved=2 << 20
     )(*in_vmem(state, land_mask, wet_fraction, before, after))
     near = lax.ppermute(near, "blk", swaps[0])
     far = lax.ppermute(far, "blk", swaps[1])
@@ -488,14 +492,14 @@
             shape(tracers, rows, levels, width), surface_shape, surface_shape,
             shape(7, rows, width), shape(2, 8, width),
         ),
-        [vmem] * 6, scratch=[pltpu.VMEM((rows + 4, planes, width), f32)], flops=20 << 20, moved=3 << 20,
-    )(*in_vmem(slab, first_columns, last_columns, near, far, mixing))
+        [vmem] * 9, scratch=[slab, pltpu.VMEM((rows + 4, planes, width), f32)], flops=20 << 20, moved=3 << 20,
+    )(*in_vmem(state, land_mask, before, after, first_columns, last_columns, near, far, mixing))
 
     drive_sum, drive_rate, first, edges = call(
         drive_kernel, "drive", (surface_shape,) * 3 + (shape(8, width),), [vmem] * 4, moved=1 << 20
     )(received, ocean_state[:, 0], land_mask, wet_fraction)
+    first_after = lax.ppermute(first, "sec", down_sec)
     first_before = lax.ppermute(first, "sec", up_sec)
-    first_after = lax.ppermute(first, "sec", down_sec)
     spread_first, second, back = call(
         surface_kernel, "surface",
         (surface_shape, surface_shape, pltpu.HBM((blocks, 8, width), bf16)), [vmem] * 12, moved=1 << 20,

time: 70.6 us -> 72.8 us (1.031)
  the two profiles are of different devices: /device:TPU:193 before, /device:TPU:129 now
where the time goes in v8:
time: 72.8 us; the launch traced here: 72 us
  starting transfers between devices  39.5 us (54%)
  Pallas kernels  14.4 us (20%)
  waiting for transfers between devices  10.5 us (14%)
  local copies, waits for them, and re-layouts  6.73 us (9%)
  between operations  0.88 us (1%)
    all_to_all x1, starting transfers between devices, per_device(): lax.all_to_all(packed, 'blk', split_axis=0, concat_axis=0, tiled=True)  10.8 us
    all_to_all x1, starting transfers between devices, per_device(): lax.all_to_all(back, 'blk', split_axis=0, concat_axis=0, tiled=True)  9.64 us
    unnamed x32, local copies, waits for them, and re-layouts  6.73 us
    ppermute x1, waiting for transfers between devices, per_device(): after = lax.ppermute(top, 'sec', down_sec)  5.54 us
    all_to_all x1, waiting for transfers between devices, per_device(): lax.all_to_all(back, 'blk', split_axis=0, concat_axis=0, tiled=True)  4.98 us
    ppermute x1, starting transfers between devices, per_device(): first_before = lax.ppermute(first, 'sec', up_sec)  4.71 us
    ppermute x1, starting transfers between devices, per_device(): before = lax.ppermute(bottom, 'sec', up_sec)  4.13 us
    pallas_call x1, Pallas kernels, per_device(): call(forward_kernel, 'forward', (pltpu.HBM((blocks, 2 * fields + 8, width...  3.58 us
  transfers between devices with their start and end apart: 8, of which 2 were waited for; matrix products, arithmetic and copies ran while one was open for 0% of the time, Pallas kernels for 11%

profile of v8, /device:TPU:129, one launch (start us, length us, event | category | flops | bytes accessed | tf_op | source)
XLA Modules:
  0.0 72.0 jit_solution(13129901175892954557)
XLA Ops:
  0.6 0.0 copy-start.1
  0.6 0.0 copy-start.7
  0.7 0.0 copy-start.12
  0.7 3.6 %forward.1 = (bf16[64,40,128]{2,1,0:T(8,128)(2,1)}, s32[64]{0:T(128)S(1)}) custom-call(s32[64]{0:T(128)} %bitcast.16, s32[64]{0:T(128)} %bitcast.20, bf16[64,16,128]{2,1,0:T(8,128)(2,1)} %bitcast.18, bf16[64,128,128]{2,1,0:T(8,128)(2,1)} %bitcast.10), custom_call_target="tpu_custom_call" | custom-call | flops 33554432 | bytes 3145728 | tf_op jit(solution)/shard_map/forward/pallas_call | solution.py:461
  4.2 0.0 copy-start.14
  4.3 0.0 copy-start.6
  4.3 10.8 %all-to-all-start = ((bf16[64,40,128]{2,1,0:T(8,128)(2,1)}), bf16[64,40,128]{2,1,0:T(8,128)(2,1)S(1)}, u32[]{:S(2)}, u32[]{:S(2)}) async-start(bf16[64,40,128]{2,1,0:T(8,128)(2,1)} %get-tuple-element.33), calls=%async_computation | async-start | bytes 1310720 | tf_op jit(solution)/shard_map/all_to_all | solution.py:474
  15.1 0.0 copy-done.1
  15.1 0.0 copy-done.7
  15.1 0.0 copy-start
  15.1 0.2 rows.1
  15.3 4.1 %collective-permute-start = (bf16[2,176,128]{2,1,0:T(8,128)(2,1)S(1)}, bf16[2,176,128]{2,1,0:T(8,128)(2,1)S(1)}, u32[]{:S(2)}, u32[]{:S(2)}) collective-permute-start(bf16[2,176,128]{2,1,0:T(8,128)(2,1)S(1)} %get-tuple-element.26), channel_id=1, source_target_pairs={{0,64},{64,128},{128,192},{192,256},{256,320},{320,384},{384,448},... | collective-permute-start | bytes 270344 | tf_op jit(solution)/shard_map/ppermute | solution.py:480
  19.4 1.9 %collective-permute-start.1 = (bf16[2,176,128]{2,1,0:T(8,128)(2,1)S(1)}, bf16[2,176,128]{2,1,0:T(8,128)(2,1)S(1)}, u32[]{:S(2)}, u32[]{:S(2)}) collective-permute-start(bf16[2,176,128]{2,1,0:T(8,128)(2,1)S(1)} %get-tuple-element.27), channel_id=1, source_target_pairs={{64,0},{128,64},{192,128},{256,192},{320,256},{384,320},{448,384},... | collective-permute-start | bytes 270344 | tf_op jit(solution)/shard_map/ppermute | solution.py:479
  21.4 0.0 collective-permute-done.before_ref
  21.4 5.5 %collective-permute-done.1.after_ref = bf16[2,176,128]{2,1,0:T(8,128)(2,1)S(1)} collective-permute-done((bf16[2,176,128]{2,1,0:T(8,128)(2,1)S(1)}, bf16[2,176,128]{2,1,0:T(8,128)(2,1)S(1)}, u32[]{:S(2)}, u32[]{:S(2)}) %collective-permute-start.1) | collective-permute-done | bytes 90144 | tf_op jit(solution)/shard_map/ppermute | solution.py:479
  26.9 0.0 copy-done.12
  26.9 0.0 copy-start.4
  26.9 1.3 %columns.1 = (f32[48,128]{1,0:T(8,128)S(1)}, f32[48,128]{1,0:T(8,128)S(1)}, f32[48,128]{1,0:T(8,128)}, f32[48,128]{1,0:T(8,128)}) custom-call(f32[160,8,128]{2,1,0:T(8,128)S(1)} %bitcast.14, s32[8,128]{1,0:T(8,128)S(1)} %copy-done.7, f32[8,128]{1,0:T(8,128)S(1)} %copy-done.12, bf16[2,176,128]{2,1,0:T(8,128)(2,1)S(1)} %collective-permute-done.before_ref, ...), custom_call_target="tpu_custom_call" | custom-call | bytes 2097152 | tf_op jit(solution)/shard_map/columns/pallas_call | solution.py:483
  28.3 0.0 copy-start.8
  28.3 0.6 copy-done.8
  28.9 0.0 copy-start.10
  28.9 0.6 copy-done.10
  29.5 3.2 %collective-permute-start.2 = (f32[48,128]{1,0:T(8,128)}, f32[48,128]{1,0:T(8,128)}, u32[]{:S(2)}, u32[]{:S(2)}) collective-permute-start(f32[48,128]{1,0:T(8,128)} %get-tuple-element.30), channel_id=1, source_target_pairs={{0,1},{2,3},{4,5},{6,7},{8,9},{10,11},{12,13},{14,15},{16,17},{18,... | collective-permute-start | bytes 73736 | tf_op jit(solution)/shard_map/ppermute | solution.py:486
  32.7 0.0 copy-done.14
  32.7 3.2 %collective-permute-start.3 = (f32[48,128]{1,0:T(8,128)}, f32[48,128]{1,0:T(8,128)}, u32[]{:S(2)}, u32[]{:S(2)}) collective-permute-start(f32[48,128]{1,0:T(8,128)} %get-tuple-element.31), channel_id=1, source_target_pairs={{1,2},{3,4},{5,6},{7,8},{9,10},{11,12},{13,14},{15,16},{17,18},{19... | collective-permute-start | bytes 73736 | tf_op jit(solution)/shard_map/ppermute | solution.py:487
  35.9 0.0 copy-done.4
  35.9 0.0 all-to-all-done.received_ref
  35.9 0.8 %drive.1 = (f32[2,8,128]{2,1,0:T(8,128)S(1)}, f32[2,8,128]{2,1,0:T(8,128)S(1)}, f32[2,8,128]{2,1,0:T(8,128)S(1)}, f32[8,128]{1,0:T(8,128)S(1)}) custom-call(bf16[64,40,128]{2,1,0:T(8,128)(2,1)S(1)} %all-to-all-done.received_ref, f32[2,8,128]{2,1,0:T(8,128)S(1)} %slice_bitcast_fusion.top_ref, s32[8,128]{1,0:T(8,128)S(1)} %copy-done.7, f32[8,128]{1,0:T(8,128)S(1)} %copy-done.12), custom_call_target="tpu_custom_call" | custom-call | bytes 1048576 | tf_op jit(solution)/shard_map/drive/pallas_call | solution.py:498
  36.7 4.7 %collective-permute-start.4 = (f32[2,8,128]{2,1,0:T(8,128)S(1)}, f32[2,8,128]{2,1,0:T(8,128)S(1)}, u32[]{:S(2)}, u32[]{:S(2)}) collective-permute-start(f32[2,8,128]{2,1,0:T(8,128)S(1)} %get-tuple-element.36.first_ref), channel_id=1, source_target_pairs={{0,64},{64,128},{128,192},{192,256},{256,320},{320,384},{384,448},... | collective-permute-start | bytes 24584 | tf_op jit(solution)/shard_map/ppermute | solution.py:502
  41.4 1.9 %collective-permute-start.5 = (f32[2,8,128]{2,1,0:T(8,128)S(1)}, f32[2,8,128]{2,1,0:T(8,128)S(1)}, u32[]{:S(2)}, u32[]{:S(2)}) collective-permute-start(f32[2,8,128]{2,1,0:T(8,128)S(1)} %get-tuple-element.36.first_ref), channel_id=1, source_target_pairs={{64,0},{128,64},{192,128},{256,192},{320,256},{384,320},{448,384},... | collective-permute-start | bytes 24584 | tf_op jit(solution)/shard_map/ppermute | solution.py:501
  43.4 0.0 collective-permute-done.2.near_ref
  43.4 0.0 collective-permute-done.3.far_ref
  43.4 0.0 copy-done.6
  43.4 0.0 copy-start.5
  43.4 0.9 %copy-done.5 = bf16[2,176,128]{2,1,0:T(8,128)(2,1)S(1)} copy-done((bf16[2,176,128]{2,1,0:T(8,128)(2,1)S(1)}, bf16[2,176,128]{2,1,0:T(8,128)(2,1)}, u32[]{:S(2)}) %copy-start.5) | copy-done | bytes 90136
  44.3 0.0 copy-start.9
  44.3 0.7 %copy-done.9 = f32[48,128]{1,0:T(8,128)S(1)} copy-done((f32[48,128]{1,0:T(8,128)S(1)}, f32[48,128]{1,0:T(8,128)}, u32[]{:S(2)}) %copy-start.9) | copy-done | bytes 24600
  45.0 0.0 copy-start.11
  45.0 0.7 %copy-done.11 = f32[48,128]{1,0:T(8,128)S(1)} copy-done((f32[48,128]{1,0:T(8,128)S(1)}, f32[48,128]{1,0:T(8,128)}, u32[]{:S(2)}) %copy-start.11) | copy-done | bytes 24600
  45.8 2.6 %stencil.1 = (f32[2,8,80,128]{3,2,1,0:T(8,128)S(1)}, f32[2,8,128]{2,1,0:T(8,128)S(1)}, f32[2,8,128]{2,1,0:T(8,128)S(1)}, f32[7,8,128]{2,1,0:T(8,128)S(1)}, f32[2,8,128]{2,1,0:T(8,128)S(1)}) custom-call(f32[160,8,128]{2,1,0:T(8,128)S(1)} %bitcast.15, s32[8,128]{1,0:T(8,128)S(1)} %copy-done.7, bf16[2,176,128]{2,1,0:T(8,128)(2,1)S(1)} %collective-permute-done.before_ref, ...), custom_call_target="tpu_custom_call" | custom-call | flops 20971520 | bytes 3145728 | tf_op jit(solution)/shard_map/stencil/pallas_call | solution.py:489
  48.4 0.0 copy-start.2
  48.4 0.8 %copy-done.2 = f32[2,8,80,128]{3,2,1,0:T(8,128)} copy-done((f32[2,8,80,128]{3,2,1,0:T(8,128)}, f32[2,8,80,128]{3,2,1,0:T(8,128)S(1)}, u32[]{:S(2)}) %copy-start.2) | copy-done | bytes 655384
  49.2 0.0 collective-permute-done.4.before_ref
  49.2 0.0 collective-permute-done.5.after_ref
  49.2 1.2 %surface.1 = (f32[2,8,128]{2,1,0:T(8,128)S(1)}, f32[2,8,128]{2,1,0:T(8,128)S(1)}, bf16[64,8,128]{2,1,0:T(8,128)(2,1)}) custom-call(bf16[64,40,128]{2,1,0:T(8,128)(2,1)S(1)} %all-to-all-done.received_ref, s32[8,128]{1,0:T(8,128)S(1)} %copy-done.7, f32[2,8,128]{2,1,0:T(8,128)S(1)} %get-tuple-element.34.sum_ref, f32[2,8,128]{2,1,0:T(8,128)S(1)} %get-tuple-element.35.rate_ref, ...), custom_call_target="tpu_custom_call" | custom-call | bytes 1048576 | tf_op jit(solution)/shard_map/surface/pallas_call | solution.py:503
  50.4 9.6 %all-to-all-start.1 = ((bf16[64,8,128]{2,1,0:T(8,128)(2,1)}), bf16[64,8,128]{2,1,0:T(8,128)(2,1)S(1)}, u32[]{:S(2)}, u32[]{:S(2)}) async-start(bf16[64,8,128]{2,1,0:T(8,128)(2,1)} %get-tuple-element.46), calls=%async_computation.1 | async-start | bytes 262144 | tf_op jit(solution)/shard_map/all_to_all | solution.py:510
  60.0 0.0 copy-done
  60.0 0.0 copy-start.3
  60.1 1.1 %copy-done.3 = f32[2,8,80,128]{3,2,1,0:T(8,128)S(1)} copy-done((f32[2,8,80,128]{3,2,1,0:T(8,128)S(1)}, f32[2,8,80,128]{3,2,1,0:T(8,128)}, u32[]{:S(2)}) %copy-start.3) | copy-done | bytes 655384
  61.1 0.0 copy-start.13
  61.1 0.7 copy-done.13
  61.8 0.0 copy-start.15
  61.8 0.6 copy-done.15
  62.4 3.0 %ocean.1 = (f32[2,80,8,128]{3,2,1,0:T(8,128)}, f32[128,128]{1,0:T(8,128)S(1)}, bf16[128,512]{1,0:T(8,128)(2,1)S(1)}) custom-call(s32[64]{0:T(128)S(1)} %bitcast.17, s32[64]{0:T(128)S(1)} %copy-done.15, f32[80,80]{1,0:T(8,128)S(1)} %copy-done.6, f32[2,8,80,128]{3,2,1,0:T(8,128)S(1)} %copy-done.3, f32[2,8,128]{2,1,0:T(8,128)S(1)} %get-tuple-element.42.spread_ref, ...), custom_call_target="tpu_custom_call" | custom-call | flops 157286400 | bytes 2097152 | tf_op jit(solution)/shard_map/ocean/pallas_call | solution.py:511
  65.4 5.0 %all-to-all-done.1.returned_ref = bf16[64,8,128]{2,1,0:T(8,128)(2,1)S(1)} async-done(((bf16[64,8,128]{2,1,0:T(8,128)(2,1)}), bf16[64,8,128]{2,1,0:T(8,128)(2,1)S(1)}, u32[]{:S(2)}, u32[]{:S(2)}) %all-to-all-start.1) | async-done | bytes 131104 | tf_op jit(solution)/shard_map/all_to_all | solution.py:510
  70.4 1.6 %backward.1 = f32[64,2,128]{2,1,0:T(2,128)} custom-call(bf16[128,512]{1,0:T(8,128)(2,1)S(1)} %get-tuple-element.45.picks_ref, bf16[64,8,128]{2,1,0:T(8,128)(2,1)S(1)} %all-to-all-done.1.returned_ref, bf16[64,128,128]{2,1,0:T(8,128)(2,1)S(1)} %bitcast.12, f32[128,128]{1,0:T(8,128)S(1)} %get-tuple-element.47.sums_ref), custom_call_target="tpu_custom_call" | custom-call | flops 16777216 | bytes 3145728 | tf_op jit(solution)/shard_map/backward/pallas_call | solution.py:519
  (1 shorter events, 0.0 us)
Async XLA Ops:
  0.6 14.5 %copy-start.1 = (f32[2,80,8,128]{3,2,1,0:T(8,128)S(1)}, f32[2,80,8,128]{3,2,1,0:T(8,128)}, u32[]{:S(2)}) copy-start(f32[2,80,8,128]{3,2,1,0:T(8,128)} %param.12) | copy-start | bytes 1966084
  0.6 14.5 %copy-start.7 = (s32[8,128]{1,0:T(8,128)S(1)}, s32[8,128]{1,0:T(8,128)}, u32[]{:S(2)}) copy-start(s32[8,128]{1,0:T(8,128)} %mask_ref.9) | copy-start | bytes 12292
  0.7 26.3 %copy-start.12 = (f32[8,128]{1,0:T(8,128)S(1)}, f32[8,128]{1,0:T(8,128)}, u32[]{:S(2)}) copy-start(f32[8,128]{1,0:T(8,128)} %wet_ref.3) | copy-start | bytes 12292
  4.2 28.4 %copy-start.14 = (s32[64]{0:T(128)}, s32[64]{0:T(128)S(1)}, u32[]{:S(2)}) copy-start(s32[64]{0:T(128)S(1)} %get-tuple-element.25.slot_ref) | copy-start | bytes 772
  4.3 39.1 %copy-start.6 = (f32[80,80]{1,0:T(8,128)S(1)}, f32[80,80]{1,0:T(8,128)}, u32[]{:S(2)}) copy-start(f32[80,80]{1,0:T(8,128)} %mixing_ref.3) | copy-start | bytes 76804
  4.3 31.6 %all-to-all-start = ((bf16[64,40,128]{2,1,0:T(8,128)(2,1)}), bf16[64,40,128]{2,1,0:T(8,128)(2,1)S(1)}, u32[]{:S(2)}, u32[]{:S(2)}) async-start(bf16[64,40,128]{2,1,0:T(8,128)(2,1)} %get-tuple-element.33), calls=%async_computation | async-start | bytes 1310720 | tf_op jit(solution)/shard_map/all_to_all | solution.py:474
  15.1 44.9 %copy-start = (bf16[1,64,128,128]{3,2,1,0:T(8,128)(2,1)S(1)}, bf16[1,64,128,128]{3,2,1,0:T(8,128)(2,1)}, u32[]{:S(2)}) copy-start(bf16[1,64,128,128]{3,2,1,0:T(8,128)(2,1)} %param.9) | copy-start | bytes 6291460
  15.3 6.1 %collective-permute-start = (bf16[2,176,128]{2,1,0:T(8,128)(2,1)S(1)}, bf16[2,176,128]{2,1,0:T(8,128)(2,1)S(1)}, u32[]{:S(2)}, u32[]{:S(2)}) collective-permute-start(bf16[2,176,128]{2,1,0:T(8,128)(2,1)S(1)} %get-tuple-element.26), channel_id=1, source_target_pairs={{0,64},{64,128},{128,192},{192,256},{256,320},{320,384},{384,448},... | collective-permute-start | bytes 270344 | tf_op jit(solution)/shard_map/ppermute | solution.py:480
  19.4 7.5 %collective-permute-start.1 = (bf16[2,176,128]{2,1,0:T(8,128)(2,1)S(1)}, bf16[2,176,128]{2,1,0:T(8,128)(2,1)S(1)}, u32[]{:S(2)}, u32[]{:S(2)}) collective-permute-start(bf16[2,176,128]{2,1,0:T(8,128)(2,1)S(1)} %get-tuple-element.27), channel_id=1, source_target_pairs={{64,0},{128,64},{192,128},{256,192},{320,256},{384,320},{448,384},... | collective-permute-start | bytes 270344 | tf_op jit(solution)/shard_map/ppermute | solution.py:479
  26.9 9.0 %copy-start.4 = (bf16[2,176,128]{2,1,0:T(8,128)(2,1)}, bf16[2,176,128]{2,1,0:T(8,128)(2,1)S(1)}, u32[]{:S(2)}) copy-start(bf16[2,176,128]{2,1,0:T(8,128)(2,1)S(1)} %collective-permute-done.1.after_ref) | copy-start | bytes 270340
  28.3 0.6 copy-start.8
  28.9 0.6 copy-start.10
  29.5 13.9 %collective-permute-start.2 = (f32[48,128]{1,0:T(8,128)}, f32[48,128]{1,0:T(8,128)}, u32[]{:S(2)}, u32[]{:S(2)}) collective-permute-start(f32[48,128]{1,0:T(8,128)} %get-tuple-element.30), channel_id=1, source_target_pairs={{0,1},{2,3},{4,5},{6,7},{8,9},{10,11},{12,13},{14,15},{16,17},{18,... | collective-permute-start | bytes 73736 | tf_op jit(solution)/shard_map/ppermute | solution.py:486
  32.7 10.7 %collective-permute-start.3 = (f32[48,128]{1,0:T(8,128)}, f32[48,128]{1,0:T(8,128)}, u32[]{:S(2)}, u32[]{:S(2)}) collective-permute-start(f32[48,128]{1,0:T(8,128)} %get-tuple-element.31), channel_id=1, source_target_pairs={{1,2},{3,4},{5,6},{7,8},{9,10},{11,12},{13,14},{15,16},{17,18},{19... | collective-permute-start | bytes 73736 | tf_op jit(solution)/shard_map/ppermute | solution.py:487
  36.7 12.5 %collective-permute-start.4 = (f32[2,8,128]{2,1,0:T(8,128)S(1)}, f32[2,8,128]{2,1,0:T(8,128)S(1)}, u32[]{:S(2)}, u32[]{:S(2)}) collective-permute-start(f32[2,8,128]{2,1,0:T(8,128)S(1)} %get-tuple-element.36.first_ref), channel_id=1, source_target_pairs={{0,64},{64,128},{128,192},{192,256},{256,320},{320,384},{384,448},... | collective-permute-start | bytes 24584 | tf_op jit(solution)/shard_map/ppermute | solution.py:502
  41.4 7.8 %collective-permute-start.5 = (f32[2,8,128]{2,1,0:T(8,128)S(1)}, f32[2,8,128]{2,1,0:T(8,128)S(1)}, u32[]{:S(2)}, u32[]{:S(2)}) collective-permute-start(f32[2,8,128]{2,1,0:T(8,128)S(1)} %get-tuple-element.36.first_ref), channel_id=1, source_target_pairs={{64,0},{128,64},{192,128},{256,192},{320,256},{384,320},{448,384},... | collective-permute-start | bytes 24584 | tf_op jit(solution)/shard_map/ppermute | solution.py:501
  43.4 0.9 %copy-start.5 = (bf16[2,176,128]{2,1,0:T(8,128)(2,1)S(1)}, bf16[2,176,128]{2,1,0:T(8,128)(2,1)}, u32[]{:S(2)}) copy-start(bf16[2,176,128]{2,1,0:T(8,128)(2,1)} %copy-done.4) | copy-start | bytes 270340
  44.3 0.7 %copy-start.9 = (f32[48,128]{1,0:T(8,128)S(1)}, f32[48,128]{1,0:T(8,128)}, u32[]{:S(2)}) copy-start(f32[48,128]{1,0:T(8,128)} %copy-done.8) | copy-start | bytes 73732
  45.0 0.7 %copy-start.11 = (f32[48,128]{1,0:T(8,128)S(1)}, f32[48,128]{1,0:T(8,128)}, u32[]{:S(2)}) copy-start(f32[48,128]{1,0:T(8,128)} %copy-done.10) | copy-start | bytes 73732
  48.4 0.8 %copy-start.2 = (f32[2,8,80,128]{3,2,1,0:T(8,128)}, f32[2,8,80,128]{3,2,1,0:T(8,128)S(1)}, u32[]{:S(2)}) copy-start(f32[2,8,80,128]{3,2,1,0:T(8,128)S(1)} %get-tuple-element.32.twice_ref) | copy-start | bytes 1966084
  50.4 20.0 %all-to-all-start.1 = ((bf16[64,8,128]{2,1,0:T(8,128)(2,1)}), bf16[64,8,128]{2,1,0:T(8,128)(2,1)S(1)}, u32[]{:S(2)}, u32[]{:S(2)}) async-start(bf16[64,8,128]{2,1,0:T(8,128)(2,1)} %get-tuple-element.46), calls=%async_computation.1 | async-start | bytes 262144 | tf_op jit(solution)/shard_map/all_to_all | solution.py:510
  60.0 1.1 %copy-start.3 = (f32[2,8,80,128]{3,2,1,0:T(8,128)S(1)}, f32[2,8,80,128]{3,2,1,0:T(8,128)}, u32[]{:S(2)}) copy-start(f32[2,8,80,128]{3,2,1,0:T(8,128)} %copy-done.2) | copy-start | bytes 1966084
  61.1 0.7 copy-start.13
  61.8 0.6 copy-start.15

commit v9 on v8

--- a/solution.py
+++ b/solution.py
@@ -300,9 +300,10 @@
             once_top_ref[k, i : i + 1, :] = jnp.sum(once_column * before, axis=0, keepdims=True)
 
 
-def drive_kernel(received_ref, top_ref, mask_ref, wet_ref, sum_ref, rate_ref, first_ref, edges_ref):
+def drive_kernel(received_ref, x_ref, mask_ref, wet_ref, sum_ref, rate_ref, first_ref, edges_ref):
     devices, lines, width = received_ref.shape
     rows = mask_ref.shape[0]
+    levels = x_ref.shape[0] // 2
     fields = (lines - 8) // 2
     totals = [jnp.zeros((fields, width), f32) for _ in range(rows)]
     edges = jnp.zeros((8, width), f32)
@@ -330,7 +331,7 @@
         drive_rate = jnp.concatenate(rates, axis=0) / wet
         sum_ref[k] = drive_sum
         rate_ref[k] = drive_rate
-        first_ref[k] = mask * (forcing_step * (drive_sum - drive_rate * top_ref[k]))
+        first_ref[k] = mask * (forcing_step * (drive_sum - drive_rate * x_ref[k * levels]))
 
 
 def beside_forcing(edges, there):
@@ -401,9 +402,11 @@
 
 
 def ocean_kernel(
-    block_ref, slot_ref, mixing_ref, twice_ref, spread_ref, second_ref, weight_ref,
-    out_ref, sums_ref, picks_ref,
+    block_ref, slot_ref, mixing_ref, twice_ref, spread_ref, second_ref, weight_hbm,
+    out_ref, sums_ref, picks_ref, weight_ref, weight_sem,
 ):
+    fetch = pltpu.make_async_copy(weight_hbm, weight_ref, weight_sem)
+    fetch.start()
     levels = mixing_ref.shape[0]
     rows, width = spread_ref.shape[1:]
     mixing = mixing_ref[...]
@@ -415,6 +418,7 @@
             free = jnp.dot(squared, twice_ref[k, r], precision=exact, preferred_element_type=f32)
             forced = twice * spread_ref[k, r : r + 1, :] + once * second_ref[k, r : r + 1, :]
             out_ref[k, :, r, :] = free + forced
+    fetch.wait()
     sums_ref[...] = own_columns(weight_ref, jnp.ones((width, width), bf16))
     tiles = weight_ref.shape[0]
     columns = picks_ref.shape[1]
@@ -497,7 +501,7 @@
 
     drive_sum, drive_rate, first, edges = call(
         drive_kernel, "drive", (surface_shape,) * 3 + (shape(8, width),), [vmem] * 4, moved=1 << 20
-    )(received, ocean_state[:, 0], land_mask, wet_fraction)
+    )(*in_vmem(received, state, land_mask, wet_fraction))
     first_after = lax.ppermute(first, "sec", down_sec)
     first_before = lax.ppermute(first, "sec", up_sec)
     spread_first, second, back = call(
@@ -508,18 +512,19 @@
         beside, once_top, twice_top, step_weights,
     )
     returned = lax.all_to_all(back, "blk", split_axis=0, concat_axis=0, tiled=True)
-    ocean, sums, picks = call(
+    ocean, sums, picks, fetched = call(
         ocean_kernel, "ocean",
         (
-            shape(tracers, levels, rows, width), shape(width, width),
-            shape(width, 8 * blocks, dtype=bf16),
+            shape(tracers, levels, rows, width), held(width, width),
+            held(width, 8 * blocks, dtype=bf16), held(tiles, width, width, dtype=bf16),
         ),
-        [smem, smem] + [vmem] * 5, flops=12 * planes * levels * rows * width, moved=2 << 20,
-    )(block, slot, mixing, twice, spread_first, second, weights)
+        [smem, smem] + [vmem] * 4 + [hbm], scratch=[pltpu.SemaphoreType.DMA(())],
+        flops=12 * planes * levels * rows * width, moved=2 << 20,
+    )(block, slot, *in_vmem(mixing, twice, spread_first, second), *in_hbm(weights))
     atmosphere = call(
         backward_kernel, "backward", shape(tiles, tracers, width), [vmem] * 4,
         flops=16 * tiles * width * width, moved=3 << 20,
-    )(picks, returned, weights, sums)
+    )(*in_vmem(picks, returned, fetched, sums))
     return (ocean, atmosphere[None])
 
 

time: 72.8 us -> 67.5 us (0.927)
  the two profiles are of different devices: /device:TPU:129 before, /device:TPU:193 now
where the time goes in v9:
time: 67.5 us; the launch traced here: 66.9 us
  starting transfers between devices  40.4 us (60%)
  Pallas kernels  13.6 us (20%)
  waiting for transfers between devices  12 us (18%)
  between operations  0.84 us (1%)
    all_to_all x1, starting transfers between devices, per_device(): lax.all_to_all(packed, 'blk', split_axis=0, concat_axis=0, tiled=True)  10.8 us
    all_to_all x1, starting transfers between devices, per_device(): lax.all_to_all(back, 'blk', split_axis=0, concat_axis=0, tiled=True)  8.72 us
    all_to_all x1, waiting for transfers between devices, per_device(): lax.all_to_all(back, 'blk', split_axis=0, concat_axis=0, tiled=True)  6.56 us
    ppermute x1, starting transfers between devices, per_device(): before = lax.ppermute(bottom, 'sec', up_sec)  5.21 us
    ppermute x1, starting transfers between devices, per_device(): first_before = lax.ppermute(first, 'sec', up_sec)  5.21 us
    ppermute x1, waiting for transfers between devices, per_device(): after = lax.ppermute(top, 'sec', down_sec)  4.84 us
    pallas_call x1, Pallas kernels, per_device(): call(ocean_kernel, 'ocean', (shape(tracers, levels, rows, width), held(wi...  3.78 us
    pallas_call x1, Pallas kernels, per_device(): call(forward_kernel, 'forward', (pltpu.HBM((blocks, 2 * fields + 8, width...  3.58 us
  transfers between devices with their start and end apart: 8, of which 3 were waited for; matrix products, arithmetic and copies ran while one was open for 0% of the time, Pallas kernels for 11%

profile of v9, /device:TPU:193, one launch (start us, length us, event | category | flops | bytes accessed | tf_op | source)
XLA Modules:
  0.0 66.9 jit_solution(4213244803473181949)
XLA Ops:
  0.6 0.0 copy-start.2
  0.6 0.0 copy-start
  0.7 0.0 copy-start.3
  0.7 3.6 %forward.1 = (bf16[64,40,128]{2,1,0:T(8,128)(2,1)}, s32[64]{0:T(128)S(1)}) custom-call(s32[64]{0:T(128)} %bitcast.10, s32[64]{0:T(128)} %bitcast.16, bf16[64,16,128]{2,1,0:T(8,128)(2,1)} %bitcast.14, bf16[64,128,128]{2,1,0:T(8,128)(2,1)} %bitcast.12), custom_call_target="tpu_custom_call" | custom-call | flops 33554432 | bytes 3145728 | tf_op jit(solution)/shard_map/forward/pallas_call | solution.py:465
  4.2 0.0 copy-start.1
  4.3 10.8 %all-to-all-start = ((bf16[64,40,128]{2,1,0:T(8,128)(2,1)}), bf16[64,40,128]{2,1,0:T(8,128)(2,1)S(1)}, u32[]{:S(2)}, u32[]{:S(2)}) async-start(bf16[64,40,128]{2,1,0:T(8,128)(2,1)} %get-tuple-element.34), calls=%async_computation | async-start | bytes 1310720 | tf_op jit(solution)/shard_map/all_to_all | solution.py:478
  15.1 0.0 copy-done.2
  15.1 0.0 copy-done
  15.1 0.2 rows.1
  15.3 5.2 %collective-permute-start = (bf16[2,176,128]{2,1,0:T(8,128)(2,1)S(1)}, bf16[2,176,128]{2,1,0:T(8,128)(2,1)S(1)}, u32[]{:S(2)}, u32[]{:S(2)}) collective-permute-start(bf16[2,176,128]{2,1,0:T(8,128)(2,1)S(1)} %get-tuple-element.27), channel_id=1, source_target_pairs={{0,64},{64,128},{128,192},{192,256},{256,320},{320,384},{384,448},... | collective-permute-start | bytes 270344 | tf_op jit(solution)/shard_map/ppermute | solution.py:484
  20.5 0.0 copy-start.4
  20.5 1.9 %collective-permute-start.1 = (bf16[2,176,128]{2,1,0:T(8,128)(2,1)S(1)}, bf16[2,176,128]{2,1,0:T(8,128)(2,1)S(1)}, u32[]{:S(2)}, u32[]{:S(2)}) collective-permute-start(bf16[2,176,128]{2,1,0:T(8,128)(2,1)S(1)} %get-tuple-element.28), channel_id=1, source_target_pairs={{64,0},{128,64},{192,128},{256,192},{320,256},{384,320},{448,384},... | collective-permute-start | bytes 270344 | tf_op jit(solution)/shard_map/ppermute | solution.py:483
  22.4 0.0 collective-permute-done.before_ref
  22.4 4.8 %collective-permute-done.1.after_ref = bf16[2,176,128]{2,1,0:T(8,128)(2,1)S(1)} collective-permute-done((bf16[2,176,128]{2,1,0:T(8,128)(2,1)S(1)}, bf16[2,176,128]{2,1,0:T(8,128)(2,1)S(1)}, u32[]{:S(2)}, u32[]{:S(2)}) %collective-permute-start.1) | collective-permute-done | bytes 90144 | tf_op jit(solution)/shard_map/ppermute | solution.py:483
  27.3 0.0 copy-done.3
  27.3 0.7 %columns.1 = (f32[48,128]{1,0:T(8,128)S(1)}, f32[48,128]{1,0:T(8,128)S(1)}, f32[48,128]{1,0:T(8,128)S(1)}, f32[48,128]{1,0:T(8,128)S(1)}) custom-call(f32[160,8,128]{2,1,0:T(8,128)S(1)} %bitcast.7, s32[8,128]{1,0:T(8,128)S(1)} %copy-done.2, f32[8,128]{1,0:T(8,128)S(1)} %copy-done.3, bf16[2,176,128]{2,1,0:T(8,128)(2,1)S(1)} %collective-permute-done.before_ref, ...), custom_call_target="tpu_custom_call" | custom-call | bytes 2097152 | tf_op jit(solution)/shard_map/columns/pallas_call | solution.py:487
  28.0 3.5 %collective-permute-start.2 = (f32[48,128]{1,0:T(8,128)S(1)}, f32[48,128]{1,0:T(8,128)S(1)}, u32[]{:S(2)}, u32[]{:S(2)}) collective-permute-start(f32[48,128]{1,0:T(8,128)S(1)} %get-tuple-element.31), channel_id=1, source_target_pairs={{0,1},{2,3},{4,5},{6,7},{8,9},{10,11},{12,13},{14,15},{16,17},{18,... | collective-permute-start | bytes 73736 | tf_op jit(solution)/shard_map/ppermute | solution.py:490
  31.5 3.1 %collective-permute-start.3 = (f32[48,128]{1,0:T(8,128)S(1)}, f32[48,128]{1,0:T(8,128)S(1)}, u32[]{:S(2)}, u32[]{:S(2)}) collective-permute-start(f32[48,128]{1,0:T(8,128)S(1)} %get-tuple-element.32), channel_id=1, source_target_pairs={{1,2},{3,4},{5,6},{7,8},{9,10},{11,12},{13,14},{15,16},{17,18},{19... | collective-permute-start | bytes 73736 | tf_op jit(solution)/shard_map/ppermute | solution.py:491
  34.6 0.6 all-to-all-done.received_ref
  35.2 0.8 %drive.1 = (f32[2,8,128]{2,1,0:T(8,128)S(1)}, f32[2,8,128]{2,1,0:T(8,128)S(1)}, f32[2,8,128]{2,1,0:T(8,128)S(1)}, f32[8,128]{1,0:T(8,128)S(1)}) custom-call(bf16[64,40,128]{2,1,0:T(8,128)(2,1)S(1)} %all-to-all-done.received_ref, f32[160,8,128]{2,1,0:T(8,128)S(1)} %bitcast.8, s32[8,128]{1,0:T(8,128)S(1)} %copy-done.2, f32[8,128]{1,0:T(8,128)S(1)} %copy-done.3), custom_call_target="tpu_custom_call" | custom-call | bytes 1048576 | tf_op jit(solution)/shard_map/drive/pallas_call | solution.py:502
  36.0 1.9 %collective-permute-start.5 = (f32[2,8,128]{2,1,0:T(8,128)S(1)}, f32[2,8,128]{2,1,0:T(8,128)S(1)}, u32[]{:S(2)}, u32[]{:S(2)}) collective-permute-start(f32[2,8,128]{2,1,0:T(8,128)S(1)} %get-tuple-element.37.first_ref), channel_id=1, source_target_pairs={{64,0},{128,64},{192,128},{256,192},{320,256},{384,320},{448,384},... | collective-permute-start | bytes 24584 | tf_op jit(solution)/shard_map/ppermute | solution.py:505
  37.9 5.2 %collective-permute-start.4 = (f32[2,8,128]{2,1,0:T(8,128)S(1)}, f32[2,8,128]{2,1,0:T(8,128)S(1)}, u32[]{:S(2)}, u32[]{:S(2)}) collective-permute-start(f32[2,8,128]{2,1,0:T(8,128)S(1)} %get-tuple-element.37.first_ref), channel_id=1, source_target_pairs={{0,64},{64,128},{128,192},{192,256},{256,320},{320,384},{384,448},... | collective-permute-start | bytes 24584 | tf_op jit(solution)/shard_map/ppermute | solution.py:506
  43.2 0.0 collective-permute-done.2.near_ref
  43.2 0.0 collective-permute-done.3.far_ref
  43.2 0.0 copy-done.1
  43.2 1.8 %stencil.1 = (f32[2,8,80,128]{3,2,1,0:T(8,128)S(1)}, f32[2,8,128]{2,1,0:T(8,128)S(1)}, f32[2,8,128]{2,1,0:T(8,128)S(1)}, f32[7,8,128]{2,1,0:T(8,128)S(1)}, f32[2,8,128]{2,1,0:T(8,128)S(1)}) custom-call(f32[160,8,128]{2,1,0:T(8,128)S(1)} %bitcast.9, s32[8,128]{1,0:T(8,128)S(1)} %copy-done.2, bf16[2,176,128]{2,1,0:T(8,128)(2,1)S(1)} %collective-permute-done.before_ref, ...), custom_call_target="tpu_custom_call" | custom-call | flops 20971520 | bytes 3145728 | tf_op jit(solution)/shard_map/stencil/pallas_call | solution.py:493
  45.0 0.0 collective-permute-done.5.after_ref
  45.0 0.0 collective-permute-done.4.before_ref
  45.0 1.2 %surface.1 = (f32[2,8,128]{2,1,0:T(8,128)S(1)}, f32[2,8,128]{2,1,0:T(8,128)S(1)}, bf16[64,8,128]{2,1,0:T(8,128)(2,1)}) custom-call(bf16[64,40,128]{2,1,0:T(8,128)(2,1)S(1)} %all-to-all-done.received_ref, s32[8,128]{1,0:T(8,128)S(1)} %copy-done.2, f32[2,8,128]{2,1,0:T(8,128)S(1)} %get-tuple-element.35.sum_ref, f32[2,8,128]{2,1,0:T(8,128)S(1)} %get-tuple-element.36.rate_ref, ...), custom_call_target="tpu_custom_call" | custom-call | bytes 1048576 | tf_op jit(solution)/shard_map/surface/pallas_call | solution.py:507
  46.2 8.7 %all-to-all-start.1 = ((bf16[64,8,128]{2,1,0:T(8,128)(2,1)}), bf16[64,8,128]{2,1,0:T(8,128)(2,1)S(1)}, u32[]{:S(2)}, u32[]{:S(2)}) async-start(bf16[64,8,128]{2,1,0:T(8,128)(2,1)} %get-tuple-element.47), calls=%async_computation.1 | async-start | bytes 262144 | tf_op jit(solution)/shard_map/all_to_all | solution.py:514
  54.9 0.0 copy-done.4
  54.9 3.8 %ocean.1 = (f32[2,80,8,128]{3,2,1,0:T(8,128)}, f32[128,128]{1,0:T(8,128)S(1)}, bf16[128,512]{1,0:T(8,128)(2,1)S(1)}, bf16[64,128,128]{2,1,0:T(8,128)(2,1)S(1)}) custom-call(s32[64]{0:T(128)S(1)} %bitcast.11, s32[64]{0:T(128)S(1)} %get-tuple-element.26.slot_ref, f32[80,80]{1,0:T(8,128)S(1)} %copy-done.1, f32[2,8,80,128]{3,2,1,0:T(8,128)S(1)} %get-tuple-element.33.twice_ref, ...), custom_call_target="tpu_custom_call" | custom-call | flops 157286400 | bytes 2097152 | tf_op jit(solution)/shard_map/ocean/pallas_call | solution.py:515
  58.7 6.6 %all-to-all-done.1.returned_ref = bf16[64,8,128]{2,1,0:T(8,128)(2,1)S(1)} async-done(((bf16[64,8,128]{2,1,0:T(8,128)(2,1)}), bf16[64,8,128]{2,1,0:T(8,128)(2,1)S(1)}, u32[]{:S(2)}, u32[]{:S(2)}) %all-to-all-start.1) | async-done | bytes 131104 | tf_op jit(solution)/shard_map/all_to_all | solution.py:514
  65.3 1.6 %backward.1 = f32[64,2,128]{2,1,0:T(2,128)} custom-call(bf16[128,512]{1,0:T(8,128)(2,1)S(1)} %get-tuple-element.46.picks_ref, bf16[64,8,128]{2,1,0:T(8,128)(2,1)S(1)} %all-to-all-done.1.returned_ref, bf16[64,128,128]{2,1,0:T(8,128)(2,1)S(1)} %get-tuple-element.48.weight_ref, f32[128,128]{1,0:T(8,128)S(1)} %get-tuple-element.49.sums_ref), custom_call_target="tpu_custom_call" | custom-call | flops 16777216 | bytes 3145728 | tf_op jit(solution)/shard_map/backward/pallas_call | solution.py:524
Async XLA Ops:
  0.6 14.4 %copy-start.2 = (s32[8,128]{1,0:T(8,128)S(1)}, s32[8,128]{1,0:T(8,128)}, u32[]{:S(2)}) copy-start(s32[8,128]{1,0:T(8,128)} %mask_ref.9) | copy-start | bytes 12292
  0.6 14.4 %copy-start = (f32[2,80,8,128]{3,2,1,0:T(8,128)S(1)}, f32[2,80,8,128]{3,2,1,0:T(8,128)}, u32[]{:S(2)}) copy-start(f32[2,80,8,128]{3,2,1,0:T(8,128)} %param.12) | copy-start | bytes 1966084
  0.7 26.6 %copy-start.3 = (f32[8,128]{1,0:T(8,128)S(1)}, f32[8,128]{1,0:T(8,128)}, u32[]{:S(2)}) copy-start(f32[8,128]{1,0:T(8,128)} %wet_ref.3) | copy-start | bytes 12292
  4.2 38.9 %copy-start.1 = (f32[80,80]{1,0:T(8,128)S(1)}, f32[80,80]{1,0:T(8,128)}, u32[]{:S(2)}) copy-start(f32[80,80]{1,0:T(8,128)} %mixing_ref.3) | copy-start | bytes 76804
  4.3 30.9 %all-to-all-start = ((bf16[64,40,128]{2,1,0:T(8,128)(2,1)}), bf16[64,40,128]{2,1,0:T(8,128)(2,1)S(1)}, u32[]{:S(2)}, u32[]{:S(2)}) async-start(bf16[64,40,128]{2,1,0:T(8,128)(2,1)} %get-tuple-element.34), calls=%async_computation | async-start | bytes 1310720 | tf_op jit(solution)/shard_map/all_to_all | solution.py:478
  15.3 7.2 %collective-permute-start = (bf16[2,176,128]{2,1,0:T(8,128)(2,1)S(1)}, bf16[2,176,128]{2,1,0:T(8,128)(2,1)S(1)}, u32[]{:S(2)}, u32[]{:S(2)}) collective-permute-start(bf16[2,176,128]{2,1,0:T(8,128)(2,1)S(1)} %get-tuple-element.27), channel_id=1, source_target_pairs={{0,64},{64,128},{128,192},{192,256},{256,320},{320,384},{384,448},... | collective-permute-start | bytes 270344 | tf_op jit(solution)/shard_map/ppermute | solution.py:484
  20.5 34.4 %copy-start.4 = (s32[1,64,1]{1,2,0:T(1,128)S(1)}, s32[1,64,1]{1,2,0:T(1,128)}, u32[]{:S(2)}) copy-start(s32[1,64,1]{1,2,0:T(1,128)} %param.10) | copy-start | bytes 772
  20.5 6.8 %collective-permute-start.1 = (bf16[2,176,128]{2,1,0:T(8,128)(2,1)S(1)}, bf16[2,176,128]{2,1,0:T(8,128)(2,1)S(1)}, u32[]{:S(2)}, u32[]{:S(2)}) collective-permute-start(bf16[2,176,128]{2,1,0:T(8,128)(2,1)S(1)} %get-tuple-element.28), channel_id=1, source_target_pairs={{64,0},{128,64},{192,128},{256,192},{320,256},{384,320},{448,384},... | collective-permute-start | bytes 270344 | tf_op jit(solution)/shard_map/ppermute | solution.py:483
  28.0 15.1 %collective-permute-start.2 = (f32[48,128]{1,0:T(8,128)S(1)}, f32[48,128]{1,0:T(8,128)S(1)}, u32[]{:S(2)}, u32[]{:S(2)}) collective-permute-start(f32[48,128]{1,0:T(8,128)S(1)} %get-tuple-element.31), channel_id=1, source_target_pairs={{0,1},{2,3},{4,5},{6,7},{8,9},{10,11},{12,13},{14,15},{16,17},{18,... | collective-permute-start | bytes 73736 | tf_op jit(solution)/shard_map/ppermute | solution.py:490
  31.5 11.6 %collective-permute-start.3 = (f32[48,128]{1,0:T(8,128)S(1)}, f32[48,128]{1,0:T(8,128)S(1)}, u32[]{:S(2)}, u32[]{:S(2)}) collective-permute-start(f32[48,128]{1,0:T(8,128)S(1)} %get-tuple-element.32), channel_id=1, source_target_pairs={{1,2},{3,4},{5,6},{7,8},{9,10},{11,12},{13,14},{15,16},{17,18},{19... | collective-permute-start | bytes 73736 | tf_op jit(solution)/shard_map/ppermute | solution.py:491
  36.0 9.0 %collective-permute-start.5 = (f32[2,8,128]{2,1,0:T(8,128)S(1)}, f32[2,8,128]{2,1,0:T(8,128)S(1)}, u32[]{:S(2)}, u32[]{:S(2)}) collective-permute-start(f32[2,8,128]{2,1,0:T(8,128)S(1)} %get-tuple-element.37.first_ref), channel_id=1, source_target_pairs={{64,0},{128,64},{192,128},{256,192},{320,256},{384,320},{448,384},... | collective-permute-start | bytes 24584 | tf_op jit(solution)/shard_map/ppermute | solution.py:505
  37.9 7.1 %collective-permute-start.4 = (f32[2,8,128]{2,1,0:T(8,128)S(1)}, f32[2,8,128]{2,1,0:T(8,128)S(1)}, u32[]{:S(2)}, u32[]{:S(2)}) collective-permute-start(f32[2,8,128]{2,1,0:T(8,128)S(1)} %get-tuple-element.37.first_ref), channel_id=1, source_target_pairs={{0,64},{64,128},{128,192},{192,256},{256,320},{320,384},{384,448},... | collective-permute-start | bytes 24584 | tf_op jit(solution)/shard_map/ppermute | solution.py:506
  46.2 19.1 %all-to-all-start.1 = ((bf16[64,8,128]{2,1,0:T(8,128)(2,1)}), bf16[64,8,128]{2,1,0:T(8,128)(2,1)S(1)}, u32[]{:S(2)}, u32[]{:S(2)}) async-start(bf16[64,8,128]{2,1,0:T(8,128)(2,1)} %get-tuple-element.47), calls=%async_computation.1 | async-start | bytes 262144 | tf_op jit(solution)/shard_map/all_to_all | solution.py:514

commit v10 on v9

--- a/solution.py
+++ b/solution.py
@@ -300,7 +300,7 @@
             once_top_ref[k, i : i + 1, :] = jnp.sum(once_column * before, axis=0, keepdims=True)
 
 
-def drive_kernel(received_ref, x_ref, mask_ref, wet_ref, sum_ref, rate_ref, first_ref, edges_ref):
+def drive_kernel(received_ref, x_ref, mask_ref, wet_ref, weights_ref, sum_ref, rate_ref, first_ref, edges_ref):
     devices, lines, width = received_ref.shape
     rows = mask_ref.shape[0]
     levels = x_ref.shape[0] // 2
@@ -500,8 +500,8 @@
     )(*in_vmem(state, land_mask, before, after, first_columns, last_columns, near, far, mixing))
 
     drive_sum, drive_rate, first, edges = call(
-        drive_kernel, "drive", (surface_shape,) * 3 + (shape(8, width),), [vmem] * 4, moved=1 << 20
-    )(*in_vmem(received, state, land_mask, wet_fraction))
+        drive_kernel, "drive", (surface_shape,) * 3 + (shape(8, width),), [vmem] * 5, moved=1 << 20
+    )(*in_vmem(received, state, land_mask, wet_fraction, step_weights))
     first_after = lax.ppermute(first, "sec", down_sec)
     first_before = lax.ppermute(first, "sec", up_sec)
     spread_first, second, back = call(

time: 67.5 us -> 72.4 us (1.073)
  starting transfers between devices: 40.4 us -> 43.3 us
  waiting for transfers between devices: 12 us -> 14.2 us
    all_to_all x1, starting transfers between devices: 8.72 us -> 12.2 us  [per_device(): lax.all_to_all(back, 'blk', split_axis=0, concat_axis=0, tiled=True)]
    ppermute x1, waiting for transfers between devices: 0.01 us -> 2.03 us  [per_device(): far = lax.ppermute(far, 'blk', swaps[1])]
    ppermute x1, waiting for transfers between devices: 0.01 us -> 0.76 us  [per_device(): first_before = lax.ppermute(first, 'sec', up_sec)]
  transfers between devices with their start and end apart: 8 -> 8, of which waited for: 3 -> 4; matrix products, arithmetic and copies ran while one was open for 0% -> 0% of each run, Pallas kernels for 11% -> 9%
where the time goes in v10:
time: 72.4 us; the launch traced here: 71.9 us
  starting transfers between devices  43.3 us (60%)
  waiting for transfers between devices  14.2 us (20%)
  Pallas kernels  13.6 us (19%)
  between operations  0.83 us (1%)
    all_to_all x1, starting transfers between devices, per_device(): lax.all_to_all(back, 'blk', split_axis=0, concat_axis=0, tiled=True)  12.2 us
    all_to_all x1, starting transfers between devices, per_device(): lax.all_to_all(packed, 'blk', split_axis=0, concat_axis=0, tiled=True)  10.8 us
    all_to_all x1, waiting for transfers between devices, per_device(): lax.all_to_all(back, 'blk', split_axis=0, concat_axis=0, tiled=True)  6.56 us
    ppermute x1, starting transfers between devices, per_device(): before = lax.ppermute(bottom, 'sec', up_sec)  5.21 us
    ppermute x1, waiting for transfers between devices, per_device(): after = lax.ppermute(top, 'sec', down_sec)  4.84 us
    ppermute x1, starting transfers between devices, per_device(): first_before = lax.ppermute(first, 'sec', up_sec)  4.57 us
    pallas_call x1, Pallas kernels, per_device(): call(ocean_kernel, 'ocean', (shape(tracers, levels, rows, width), held(wi...  3.79 us
    pallas_call x1, Pallas kernels, per_device(): call(forward_kernel, 'forward', (pltpu.HBM((blocks, 2 * fields + 8, width...  3.58 us
  transfers between devices with their start and end apart: 8, of which 4 were waited for; matrix products, arithmetic and copies ran while one was open for 0% of the time, Pallas kernels for 9%

profile of v10, /device:TPU:193, one launch (start us, length us, event | category | flops | bytes accessed | tf_op | source)
XLA Modules:
  0.0 71.9 jit_solution(8599695210336239031)
XLA Ops:
  0.6 0.0 copy-start.2
  0.6 0.0 copy-start
  0.7 0.0 copy-start.3
  0.7 0.0 copy-start.1
  0.7 3.6 %forward.1 = (bf16[64,40,128]{2,1,0:T(8,128)(2,1)}, s32[64]{0:T(128)S(1)}) custom-call(s32[64]{0:T(128)} %bitcast.10, s32[64]{0:T(128)} %bitcast.16, bf16[64,16,128]{2,1,0:T(8,128)(2,1)} %bitcast.14, bf16[64,128,128]{2,1,0:T(8,128)(2,1)} %bitcast.12), custom_call_target="tpu_custom_call" | custom-call | flops 33554432 | bytes 3145728 | tf_op jit(solution)/shard_map/forward/pallas_call | solution.py:465
  4.3 10.8 %all-to-all-start = ((bf16[64,40,128]{2,1,0:T(8,128)(2,1)}), bf16[64,40,128]{2,1,0:T(8,128)(2,1)S(1)}, u32[]{:S(2)}, u32[]{:S(2)}) async-start(bf16[64,40,128]{2,1,0:T(8,128)(2,1)} %get-tuple-element.34), calls=%async_computation | async-start | bytes 1310720 | tf_op jit(solution)/shard_map/all_to_all | solution.py:478
  15.1 0.0 copy-done.2
  15.1 0.0 copy-done
  15.1 0.2 rows.1
  15.3 5.2 %collective-permute-start = (bf16[2,176,128]{2,1,0:T(8,128)(2,1)S(1)}, bf16[2,176,128]{2,1,0:T(8,128)(2,1)S(1)}, u32[]{:S(2)}, u32[]{:S(2)}) collective-permute-start(bf16[2,176,128]{2,1,0:T(8,128)(2,1)S(1)} %get-tuple-element.27), channel_id=1, source_target_pairs={{0,64},{64,128},{128,192},{192,256},{256,320},{320,384},{384,448},... | collective-permute-start | bytes 270344 | tf_op jit(solution)/shard_map/ppermute | solution.py:484
  20.5 0.0 copy-start.4
  20.5 1.9 %collective-permute-start.1 = (bf16[2,176,128]{2,1,0:T(8,128)(2,1)S(1)}, bf16[2,176,128]{2,1,0:T(8,128)(2,1)S(1)}, u32[]{:S(2)}, u32[]{:S(2)}) collective-permute-start(bf16[2,176,128]{2,1,0:T(8,128)(2,1)S(1)} %get-tuple-element.28), channel_id=1, source_target_pairs={{64,0},{128,64},{192,128},{256,192},{320,256},{384,320},{448,384},... | collective-permute-start | bytes 270344 | tf_op jit(solution)/shard_map/ppermute | solution.py:483
  22.4 0.0 collective-permute-done.before_ref
  22.4 4.8 %collective-permute-done.1.after_ref = bf16[2,176,128]{2,1,0:T(8,128)(2,1)S(1)} collective-permute-done((bf16[2,176,128]{2,1,0:T(8,128)(2,1)S(1)}, bf16[2,176,128]{2,1,0:T(8,128)(2,1)S(1)}, u32[]{:S(2)}, u32[]{:S(2)}) %collective-permute-start.1) | collective-permute-done | bytes 90144 | tf_op jit(solution)/shard_map/ppermute | solution.py:483
  27.3 0.0 copy-done.3
  27.3 0.7 %columns.1 = (f32[48,128]{1,0:T(8,128)S(1)}, f32[48,128]{1,0:T(8,128)S(1)}, f32[48,128]{1,0:T(8,128)S(1)}, f32[48,128]{1,0:T(8,128)S(1)}) custom-call(f32[160,8,128]{2,1,0:T(8,128)S(1)} %bitcast.7, s32[8,128]{1,0:T(8,128)S(1)} %copy-done.2, f32[8,128]{1,0:T(8,128)S(1)} %copy-done.3, bf16[2,176,128]{2,1,0:T(8,128)(2,1)S(1)} %collective-permute-done.before_ref, ...), custom_call_target="tpu_custom_call" | custom-call | bytes 2097152 | tf_op jit(solution)/shard_map/columns/pallas_call | solution.py:487
  28.0 3.5 %collective-permute-start.2 = (f32[48,128]{1,0:T(8,128)S(1)}, f32[48,128]{1,0:T(8,128)S(1)}, u32[]{:S(2)}, u32[]{:S(2)}) collective-permute-start(f32[48,128]{1,0:T(8,128)S(1)} %get-tuple-element.31), channel_id=1, source_target_pairs={{0,1},{2,3},{4,5},{6,7},{8,9},{10,11},{12,13},{14,15},{16,17},{18,... | collective-permute-start | bytes 73736 | tf_op jit(solution)/shard_map/ppermute | solution.py:490
  31.5 3.1 %collective-permute-start.3 = (f32[48,128]{1,0:T(8,128)S(1)}, f32[48,128]{1,0:T(8,128)S(1)}, u32[]{:S(2)}, u32[]{:S(2)}) collective-permute-start(f32[48,128]{1,0:T(8,128)S(1)} %get-tuple-element.32), channel_id=1, source_target_pairs={{1,2},{3,4},{5,6},{7,8},{9,10},{11,12},{13,14},{15,16},{17,18},{19... | collective-permute-start | bytes 73736 | tf_op jit(solution)/shard_map/ppermute | solution.py:491
  34.6 0.0 collective-permute-done.2.near_ref
  34.6 2.0 %collective-permute-done.3.far_ref = f32[48,128]{1,0:T(8,128)S(1)} collective-permute-done((f32[48,128]{1,0:T(8,128)S(1)}, f32[48,128]{1,0:T(8,128)S(1)}, u32[]{:S(2)}, u32[]{:S(2)}) %collective-permute-start.3) | collective-permute-done | bytes 24608 | tf_op jit(solution)/shard_map/ppermute | solution.py:491
  36.7 0.0 copy-done.1
  36.7 1.8 %stencil.1 = (f32[2,8,80,128]{3,2,1,0:T(8,128)S(1)}, f32[2,8,128]{2,1,0:T(8,128)S(1)}, f32[2,8,128]{2,1,0:T(8,128)S(1)}, f32[7,8,128]{2,1,0:T(8,128)S(1)}, f32[2,8,128]{2,1,0:T(8,128)S(1)}) custom-call(f32[160,8,128]{2,1,0:T(8,128)S(1)} %bitcast.8, s32[8,128]{1,0:T(8,128)S(1)} %copy-done.2, bf16[2,176,128]{2,1,0:T(8,128)(2,1)S(1)} %collective-permute-done.before_ref, ...), custom_call_target="tpu_custom_call" | custom-call | flops 20971520 | bytes 3145728 | tf_op jit(solution)/shard_map/stencil/pallas_call | solution.py:493
  38.5 0.0 all-to-all-done.received_ref
  38.5 0.8 %drive.1 = (f32[2,8,128]{2,1,0:T(8,128)S(1)}, f32[2,8,128]{2,1,0:T(8,128)S(1)}, f32[2,8,128]{2,1,0:T(8,128)S(1)}, f32[8,128]{1,0:T(8,128)S(1)}) custom-call(bf16[64,40,128]{2,1,0:T(8,128)(2,1)S(1)} %all-to-all-done.received_ref, f32[160,8,128]{2,1,0:T(8,128)S(1)} %bitcast.9, s32[8,128]{1,0:T(8,128)S(1)} %copy-done.2, f32[8,128]{1,0:T(8,128)S(1)} %copy-done.3, ...), custom_call_target="tpu_custom_call" | custom-call | bytes 1048576 | tf_op jit(solution)/shard_map/drive/pallas_call | solution.py:502
  39.3 1.9 %collective-permute-start.5 = (f32[2,8,128]{2,1,0:T(8,128)S(1)}, f32[2,8,128]{2,1,0:T(8,128)S(1)}, u32[]{:S(2)}, u32[]{:S(2)}) collective-permute-start(f32[2,8,128]{2,1,0:T(8,128)S(1)} %get-tuple-element.38.first_ref), channel_id=1, source_target_pairs={{64,0},{128,64},{192,128},{256,192},{320,256},{384,320},{448,384},... | collective-permute-start | bytes 24584 | tf_op jit(solution)/shard_map/ppermute | solution.py:505
  41.2 4.6 %collective-permute-start.4 = (f32[2,8,128]{2,1,0:T(8,128)S(1)}, f32[2,8,128]{2,1,0:T(8,128)S(1)}, u32[]{:S(2)}, u32[]{:S(2)}) collective-permute-start(f32[2,8,128]{2,1,0:T(8,128)S(1)} %get-tuple-element.38.first_ref), channel_id=1, source_target_pairs={{0,64},{64,128},{128,192},{192,256},{256,320},{320,384},{384,448},... | collective-permute-start | bytes 24584 | tf_op jit(solution)/shard_map/ppermute | solution.py:506
  45.8 0.0 collective-permute-done.5.after_ref
  45.8 0.8 %collective-permute-done.4.before_ref = f32[2,8,128]{2,1,0:T(8,128)S(1)} collective-permute-done((f32[2,8,128]{2,1,0:T(8,128)S(1)}, f32[2,8,128]{2,1,0:T(8,128)S(1)}, u32[]{:S(2)}, u32[]{:S(2)}) %collective-permute-start.4) | collective-permute-done | bytes 8224 | tf_op jit(solution)/shard_map/ppermute | solution.py:506
  46.6 1.2 %surface.1 = (f32[2,8,128]{2,1,0:T(8,128)S(1)}, f32[2,8,128]{2,1,0:T(8,128)S(1)}, bf16[64,8,128]{2,1,0:T(8,128)(2,1)}) custom-call(bf16[64,40,128]{2,1,0:T(8,128)(2,1)S(1)} %all-to-all-done.received_ref, s32[8,128]{1,0:T(8,128)S(1)} %copy-done.2, f32[2,8,128]{2,1,0:T(8,128)S(1)} %get-tuple-element.36.sum_ref, f32[2,8,128]{2,1,0:T(8,128)S(1)} %get-tuple-element.37.rate_ref, ...), custom_call_target="tpu_custom_call" | custom-call | bytes 1048576 | tf_op jit(solution)/shard_map/surface/pallas_call | solution.py:507
  47.7 12.2 %all-to-all-start.1 = ((bf16[64,8,128]{2,1,0:T(8,128)(2,1)}), bf16[64,8,128]{2,1,0:T(8,128)(2,1)S(1)}, u32[]{:S(2)}, u32[]{:S(2)}) async-start(bf16[64,8,128]{2,1,0:T(8,128)(2,1)} %get-tuple-element.47), calls=%async_computation.1 | async-start | bytes 262144 | tf_op jit(solution)/shard_map/all_to_all | solution.py:514
  60.0 0.0 copy-done.4
  60.0 3.8 %ocean.1 = (f32[2,80,8,128]{3,2,1,0:T(8,128)}, f32[128,128]{1,0:T(8,128)S(1)}, bf16[128,512]{1,0:T(8,128)(2,1)S(1)}, bf16[64,128,128]{2,1,0:T(8,128)(2,1)S(1)}) custom-call(s32[64]{0:T(128)S(1)} %bitcast.11, s32[64]{0:T(128)S(1)} %get-tuple-element.26.slot_ref, f32[80,80]{1,0:T(8,128)S(1)} %copy-done.1, f32[2,8,80,128]{3,2,1,0:T(8,128)S(1)} %get-tuple-element.33.twice_ref, ...), custom_call_target="tpu_custom_call" | custom-call | flops 157286400 | bytes 2097152 | tf_op jit(solution)/shard_map/ocean/pallas_call | solution.py:515
  63.8 6.6 %all-to-all-done.1.returned_ref = bf16[64,8,128]{2,1,0:T(8,128)(2,1)S(1)} async-done(((bf16[64,8,128]{2,1,0:T(8,128)(2,1)}), bf16[64,8,128]{2,1,0:T(8,128)(2,1)S(1)}, u32[]{:S(2)}, u32[]{:S(2)}) %all-to-all-start.1) | async-done | bytes 131104 | tf_op jit(solution)/shard_map/all_to_all | solution.py:514
  70.3 1.6 %backward.1 = f32[64,2,128]{2,1,0:T(2,128)} custom-call(bf16[128,512]{1,0:T(8,128)(2,1)S(1)} %get-tuple-element.46.picks_ref, bf16[64,8,128]{2,1,0:T(8,128)(2,1)S(1)} %all-to-all-done.1.returned_ref, bf16[64,128,128]{2,1,0:T(8,128)(2,1)S(1)} %get-tuple-element.48.weight_ref, f32[128,128]{1,0:T(8,128)S(1)} %get-tuple-element.49.sums_ref), custom_call_target="tpu_custom_call" | custom-call | flops 16777216 | bytes 3145728 | tf_op jit(solution)/shard_map/backward/pallas_call | solution.py:524
Async XLA Ops:
  0.6 14.4 %copy-start.2 = (s32[8,128]{1,0:T(8,128)S(1)}, s32[8,128]{1,0:T(8,128)}, u32[]{:S(2)}) copy-start(s32[8,128]{1,0:T(8,128)} %mask_ref.9) | copy-start | bytes 12292
  0.6 14.4 %copy-start = (f32[2,80,8,128]{3,2,1,0:T(8,128)S(1)}, f32[2,80,8,128]{3,2,1,0:T(8,128)}, u32[]{:S(2)}) copy-start(f32[2,80,8,128]{3,2,1,0:T(8,128)} %param.12) | copy-start | bytes 1966084
  0.7 26.6 %copy-start.3 = (f32[8,128]{1,0:T(8,128)S(1)}, f32[8,128]{1,0:T(8,128)}, u32[]{:S(2)}) copy-start(f32[8,128]{1,0:T(8,128)} %wet_ref.3) | copy-start | bytes 12292
  0.7 36.0 %copy-start.1 = (f32[80,80]{1,0:T(8,128)S(1)}, f32[80,80]{1,0:T(8,128)}, u32[]{:S(2)}) copy-start(f32[80,80]{1,0:T(8,128)} %mixing_ref.3) | copy-start | bytes 76804
  4.3 34.2 %all-to-all-start = ((bf16[64,40,128]{2,1,0:T(8,128)(2,1)}), bf16[64,40,128]{2,1,0:T(8,128)(2,1)S(1)}, u32[]{:S(2)}, u32[]{:S(2)}) async-start(bf16[64,40,128]{2,1,0:T(8,128)(2,1)} %get-tuple-element.34), calls=%async_computation | async-start | bytes 1310720 | tf_op jit(solution)/shard_map/all_to_all | solution.py:478
  15.3 7.2 %collective-permute-start = (bf16[2,176,128]{2,1,0:T(8,128)(2,1)S(1)}, bf16[2,176,128]{2,1,0:T(8,128)(2,1)S(1)}, u32[]{:S(2)}, u32[]{:S(2)}) collective-permute-start(bf16[2,176,128]{2,1,0:T(8,128)(2,1)S(1)} %get-tuple-element.27), channel_id=1, source_target_pairs={{0,64},{64,128},{128,192},{192,256},{256,320},{320,384},{384,448},... | collective-permute-start | bytes 270344 | tf_op jit(solution)/shard_map/ppermute | solution.py:484
  20.5 39.5 %copy-start.4 = (s32[1,64,1]{1,2,0:T(1,128)S(1)}, s32[1,64,1]{1,2,0:T(1,128)}, u32[]{:S(2)}) copy-start(s32[1,64,1]{1,2,0:T(1,128)} %param.10) | copy-start | bytes 772
  20.5 6.8 %collective-permute-start.1 = (bf16[2,176,128]{2,1,0:T(8,128)(2,1)S(1)}, bf16[2,176,128]{2,1,0:T(8,128)(2,1)S(1)}, u32[]{:S(2)}, u32[]{:S(2)}) collective-permute-start(bf16[2,176,128]{2,1,0:T(8,128)(2,1)S(1)} %get-tuple-element.28), channel_id=1, source_target_pairs={{64,0},{128,64},{192,128},{256,192},{320,256},{384,320},{448,384},... | collective-permute-start | bytes 270344 | tf_op jit(solution)/shard_map/ppermute | solution.py:483
  28.0 6.6 %collective-permute-start.2 = (f32[48,128]{1,0:T(8,128)S(1)}, f32[48,128]{1,0:T(8,128)S(1)}, u32[]{:S(2)}, u32[]{:S(2)}) collective-permute-start(f32[48,128]{1,0:T(8,128)S(1)} %get-tuple-element.31), channel_id=1, source_target_pairs={{0,1},{2,3},{4,5},{6,7},{8,9},{10,11},{12,13},{14,15},{16,17},{18,... | collective-permute-start | bytes 73736 | tf_op jit(solution)/shard_map/ppermute | solution.py:490
  31.5 5.1 %collective-permute-start.3 = (f32[48,128]{1,0:T(8,128)S(1)}, f32[48,128]{1,0:T(8,128)S(1)}, u32[]{:S(2)}, u32[]{:S(2)}) collective-permute-start(f32[48,128]{1,0:T(8,128)S(1)} %get-tuple-element.32), channel_id=1, source_target_pairs={{1,2},{3,4},{5,6},{7,8},{9,10},{11,12},{13,14},{15,16},{17,18},{19... | collective-permute-start | bytes 73736 | tf_op jit(solution)/shard_map/ppermute | solution.py:491
  39.3 6.5 %collective-permute-start.5 = (f32[2,8,128]{2,1,0:T(8,128)S(1)}, f32[2,8,128]{2,1,0:T(8,128)S(1)}, u32[]{:S(2)}, u32[]{:S(2)}) collective-permute-start(f32[2,8,128]{2,1,0:T(8,128)S(1)} %get-tuple-element.38.first_ref), channel_id=1, source_target_pairs={{64,0},{128,64},{192,128},{256,192},{320,256},{384,320},{448,384},... | collective-permute-start | bytes 24584 | tf_op jit(solution)/shard_map/ppermute | solution.py:505
  41.2 5.4 %collective-permute-start.4 = (f32[2,8,128]{2,1,0:T(8,128)S(1)}, f32[2,8,128]{2,1,0:T(8,128)S(1)}, u32[]{:S(2)}, u32[]{:S(2)}) collective-permute-start(f32[2,8,128]{2,1,0:T(8,128)S(1)} %get-tuple-element.38.first_ref), channel_id=1, source_target_pairs={{0,64},{64,128},{128,192},{192,256},{256,320},{320,384},{384,448},... | collective-permute-start | bytes 24584 | tf_op jit(solution)/shard_map/ppermute | solution.py:506
  47.7 22.6 %all-to-all-start.1 = ((bf16[64,8,128]{2,1,0:T(8,128)(2,1)}), bf16[64,8,128]{2,1,0:T(8,128)(2,1)S(1)}, u32[]{:S(2)}, u32[]{:S(2)}) async-start(bf16[64,8,128]{2,1,0:T(8,128)(2,1)} %get-tuple-element.47), calls=%async_computation.1 | async-start | bytes 262144 | tf_op jit(solution)/shard_map/all_to_all | solution.py:514

commit v11 on v9

--- a/solution.py
+++ b/solution.py
@@ -125,13 +125,30 @@
         out_ref[b, 2 * fields : 2 * fields + 8, :] = last.astype(bf16)
 
 
-def rows_kernel(x_ref, mask_ref, top_ref, bottom_ref):
+def rows_kernel(x_ref, mask_ref, mixing_ref, top_ref, bottom_ref, sums_ref, corner_ref):
     planes, rows, width = x_ref.shape
+    levels = planes // 2
     mask = mask_ref[...].astype(f32)
+    mixing = mixing_ref[...]
+    chosen = jnp.where(line_iota((8, width)) == 0, 1.0, 0.0).astype(f32)
+    over_first = (((0,), (0,)), ((), ()))
+    twice_rows = jnp.dot(mixing[0:8, :], mixing, precision=exact, preferred_element_type=f32)
+    columns = [
+        lax.dot_general(m, chosen, over_first, precision=exact, preferred_element_type=f32)
+        for m in (twice_rows, mixing[0:8, :])
+    ]
+    for n in range(2):
+        corner_ref[n] = jnp.broadcast_to(columns[n][0:1, :], (rows, width))
+    sums = []
+    for r in range(rows):
+        parts = [x_ref[k * levels : (k + 1) * levels, r, :] for k in range(2)]
+        lines = [jnp.sum(c * p, axis=0, keepdims=True) for c in columns for p in parts]
+        sums.append(jnp.concatenate(lines + [jnp.zeros((4, width), f32)], axis=0))
+        sums_ref[r] = sums[r]
     for i in range(2):
         for out_ref, r in ((top_ref, i), (bottom_ref, rows - 2 + i)):
-            lines = jnp.broadcast_to(mask[r : r + 1, :], (out_ref.shape[1] - planes, width))
-            out_ref[i] = jnp.concatenate([x_ref[:, r, :], lines], axis=0).astype(bf16)
+            lines = jnp.broadcast_to(mask[r : r + 1, :], (8, width))
+            out_ref[i] = jnp.concatenate([x_ref[:, r, :], lines, sums[r]], axis=0).astype(bf16)
 
 
 def packing(rows, planes, width):
@@ -146,34 +163,40 @@
 
 def fill_slab(slab_ref, x_ref, mask, before_ref, after_ref):
     planes, rows, width = x_ref.shape
+    lines = slab_ref.shape[1]
     for i in range(2):
-        slab_ref[i] = before_ref[i].astype(f32)[: planes + 8]
-        slab_ref[rows + 2 + i] = after_ref[i].astype(f32)[: planes + 8]
+        slab_ref[i] = before_ref[i].astype(f32)[:lines]
+        slab_ref[rows + 2 + i] = after_ref[i].astype(f32)[:lines]
     for r in range(rows):
         slab_ref[r + 2, 0:planes, :] = x_ref[:, r, :]
         slab_ref[r + 2, planes : planes + 8, :] = jnp.broadcast_to(mask[r : r + 1, :], (8, width))
 
 
 def columns_kernel(
-    x_ref, mask_ref, wet_ref, before_ref, after_ref, first_ref, last_ref, near_ref, far_ref, slab_ref
+    x_ref, mask_ref, wet_ref, sums_ref, before_ref, after_ref,
+    first_ref, last_ref, near_ref, far_ref, light_ref, slab_ref,
 ):
     planes, rows, width = x_ref.shape
     levels = planes // 2
     span, per, groups, packs = packing(rows, planes, width)
     mask = mask_ref[...].astype(f32)
     fill_slab(slab_ref, x_ref, mask, before_ref, after_ref)
+    for r in range(rows):
+        slab_ref[r + 2, planes + 8 :, :] = sums_ref[r]
+    for r in range(rows + 4):
+        light_ref[r] = slab_ref[r, planes:, :]
     lane = lane_iota((8, width))
 
     def turn(value, by):
         return pltpu.roll(value, by % width, 1) if by % width else value
 
-    for pack in range(packs + 1):
+    for pack in range(packs + 2):
         first = jnp.zeros((8, width), f32)
         last = jnp.zeros((8, width), f32)
         if pack < packs:
             members = [(q, q % per) for q in range(pack * per, min(groups, (pack + 1) * per))]
         else:
-            members = [(groups, 0)]
+            members = [(groups + pack - packs, 0)]
         for q, place in members:
             for r in range(rows + 4):
                 value = slab_ref[r, 8 * q : 8 * q + 8, :]
@@ -195,8 +218,8 @@
             start = 16 * r + 8 * k
             first = jnp.where(lane == start, turn(value, start), first)
             last = jnp.where(lane == start, turn(value, start + 1), last)
-    first_ref[8 * packs + 8 : 8 * packs + 16, :] = first
-    last_ref[8 * packs + 8 : 8 * packs + 16, :] = last
+    first_ref[8 * packs + 16 : 8 * packs + 24, :] = first
+    last_ref[8 * packs + 16 : 8 * packs + 24, :] = last
     odd = odd_block()
     near_ref[...] = jnp.where(odd, first_ref[...], last_ref[...])
     far_ref[...] = jnp.where(odd, last_ref[...], first_ref[...])
@@ -218,24 +241,18 @@
     return total
 
 
-def stencil_kernel(
-    x_ref, mask_ref, before_ref, after_ref, first_ref, last_ref, near_ref, far_ref, mixing_ref,
-    twice_ref, once_top_ref, twice_top_ref, weights_ref, beside_ref, slab_ref, work_ref,
-):
-    planes, rows, width = x_ref.shape
-    fill_slab(slab_ref, x_ref, mask_ref[...].astype(f32), before_ref, after_ref)
-    levels = planes // 2
-    span, per, groups, packs = packing(rows, planes, width)
-    packed = 8 * packs
+def two_steps(rows, planes, per, packed, slab, work, store, first, last, left_all, right_all):
+    width = first.shape[1]
     lane = lane_iota((planes + 8, width))
     at_start = lane == 0
     at_end = lane == width - 1
+    span = 2 * (rows + 4)
 
     def beside(center, left_packed, right_packed, r):
         size = center.shape[0]
         lefts, rights = [], []
         for q in range(size // 8):
-            pack, place = (q // per, q % per) if q < groups else (packs, 0)
+            pack, place = (q // per, q % per) if q < planes // 8 else (packed // 8, 0)
             start = span * place + 2 * r
             part = slice(8 * pack, 8 * pack + 8)
             lefts.append(pltpu.roll(left_packed[part], width - (start + 1), 1))
@@ -243,14 +260,6 @@
         left = jnp.where(at_start[:size], jnp.concatenate(lefts, 0), pltpu.roll(center, 1, 1))
         right = jnp.where(at_end[:size], jnp.concatenate(rights, 0), pltpu.roll(center, width - 1, 1))
         return left, right
-
-    odd = odd_block()
-    left_all = jnp.where(odd, near_ref[...], far_ref[...])
-    right_all = jnp.where(odd, far_ref[...], near_ref[...])
-    beside_ref[0] = left_all[packed + 8 :]
-    beside_ref[1] = right_all[packed + 8 :]
-    left_all, right_all = left_all[: packed + 8], right_all[: packed + 8]
-    first_all, last_all = first_ref[: packed + 8, :], last_ref[: packed + 8, :]
 
     def edge(own, outer_shift, beyond):
         around = (
@@ -262,42 +271,73 @@
         w = weights_of(own[packed:], [a[packed:] for a in around])
         return combine(w, [own[:packed]] + [a[:packed] for a in around], packed)
 
-    left_once = edge(left_all, 1, pltpu.roll(first_all, 1, 1))
-    right_once = edge(right_all, width - 1, pltpu.roll(last_all, width - 1, 1))
+    left_once = edge(left_all, 1, pltpu.roll(first, 1, 1))
+    right_once = edge(right_all, width - 1, pltpu.roll(last, width - 1, 1))
 
     saved = []
     for r in range(1, rows + 3):
-        center = slab_ref[r]
+        center = slab(r)
         left, right = beside(center, left_all, right_all, r)
-        around = (slab_ref[r - 1], slab_ref[r + 1], left, right)
+        around = (slab(r - 1), slab(r + 1), left, right)
         w = weights_of(center[planes:], [a[planes:] for a in around])
         saved.append(w)
-        work_ref[r] = combine(w, [center[:planes]] + [a[:planes] for a in around], planes)
-
-    mixing = mixing_ref[...]
-    top_rows = mixing[0:8, :]
-    chosen = jnp.where(line_iota((8, width)) == 0, 1.0, 0.0).astype(f32)
-    over_first = (((0,), (0,)), ((), ()))
-    once_column = lax.dot_general(top_rows, chosen, over_first, precision=exact, preferred_element_type=f32)
-    top_twice = jnp.dot(top_rows, mixing, precision=exact, preferred_element_type=f32)
-    twice_column = lax.dot_general(top_twice, chosen, over_first, precision=exact, preferred_element_type=f32)
-    weights_ref[5] = jnp.broadcast_to(twice_column[0:1, :], (rows, width))
-    weights_ref[6] = jnp.broadcast_to(once_column[0:1, :], (rows, width))
-
+        work[r] = combine(w, [center[:planes]] + [a[:planes] for a in around], planes)
     for r in range(2, rows + 2):
-        center = work_ref[r]
+        center = work[r]
         left, right = beside(center, left_once, right_once, r)
         w = saved[r - 1]
-        result = combine(w, [center, work_ref[r - 1], work_ref[r + 1], left, right], planes)
-        i = r - 2
+        store(r - 2, center, combine(w, [center, work[r - 1], work[r + 1], left, right], planes), w)
+
+
+def light_kernel(
+    light_ref, first_ref, last_ref, near_ref, far_ref,
+    once_top_ref, twice_top_ref, weights_ref, beside_ref,
+):
+    rows = light_ref.shape[0] - 4
+    lines = first_ref.shape[0]
+
+    def columns(value):
+        return jnp.concatenate([value[lines - 16 : lines - 8], value[lines - 24 : lines - 16]], axis=0)
+
+    odd = odd_block()
+    left_all = jnp.where(odd, near_ref[...], far_ref[...])
+    right_all = jnp.where(odd, far_ref[...], near_ref[...])
+    beside_ref[0] = left_all[lines - 8 :]
+    beside_ref[1] = right_all[lines - 8 :]
+
+    def store(i, once, twice, w):
         for n in range(5):
             weights_ref[n, i : i + 1, :] = w[n][0:1, :]
         for k in range(2):
-            part = result[k * levels : (k + 1) * levels]
-            twice_ref[k, i] = part
-            twice_top_ref[k, i : i + 1, :] = jnp.sum(twice_column * part, axis=0, keepdims=True)
-            before = center[k * levels : (k + 1) * levels]
-            once_top_ref[k, i : i + 1, :] = jnp.sum(once_column * before, axis=0, keepdims=True)
+            twice_top_ref[k, i : i + 1, :] = twice[k : k + 1]
+            once_top_ref[k, i : i + 1, :] = once[2 + k : 3 + k]
+
+    two_steps(
+        rows, 8, 1, 8, lambda r: jnp.concatenate([light_ref[r, 8:, :], light_ref[r, :8, :]], axis=0),
+        {}, store, columns(first_ref[...]), columns(last_ref[...]), columns(left_all), columns(right_all),
+    )
+
+
+def stencil_kernel(
+    x_ref, mask_ref, before_ref, after_ref, first_ref, last_ref, near_ref, far_ref, later_ref,
+    twice_ref, slab_ref, work_ref,
+):
+    planes, rows, width = x_ref.shape
+    levels = planes // 2
+    fill_slab(slab_ref, x_ref, mask_ref[...].astype(f32), before_ref, after_ref)
+    span, per, groups, packs = packing(rows, planes, width)
+    used = slice(0, 8 * packs + 8)
+    odd = odd_block()
+    near, far = near_ref[used], far_ref[used]
+
+    def store(i, once, twice, w):
+        for k in range(2):
+            twice_ref[k, i] = twice[k * levels : (k + 1) * levels]
+
+    two_steps(
+        rows, planes, per, 8 * packs, lambda r: slab_ref[r], work_ref, store,
+        first_ref[used], last_ref[used], jnp.where(odd, near, far), jnp.where(odd, far, near),
+    )
 
 
 def drive_kernel(received_ref, x_ref, mask_ref, wet_ref, sum_ref, rate_ref, first_ref, edges_ref):
@@ -353,14 +393,14 @@
 
 def surface_kernel(
     received_ref, mask_ref, sum_ref, rate_ref, first_ref, edges_ref, before_ref, after_ref,
-    beside_ref, once_top_ref, twice_top_ref, weights_ref, spread_ref, second_ref, back_ref,
+    beside_ref, once_top_ref, twice_top_ref, weights_ref, corner_ref, spread_ref, second_ref, back_ref,
 ):
     devices, lines, width = received_ref.shape
     rows = first_ref.shape[1]
     line = line_iota((rows, width))
     lane = lane_iota((rows, width))
     mask = mask_ref[...].astype(f32)
-    mixing_00 = weights_ref[6]
+    mixing_00 = corner_ref[1]
     edges = [edges_ref[4 + 2 * n : 5 + 2 * n, :] + edges_ref[5 + 2 * n : 6 + 2 * n, :] for n in range(2)]
     lefts, rights = (
         beside_forcing(jnp.broadcast_to(edges[n], (rows, width)), beside_ref[n]) for n in range(2)
@@ -380,7 +420,7 @@
         second = mask * (forcing_step * (sum_ref[k] - rate_ref[k] * once_top))
         spread_ref[k] = moved
         second_ref[k] = second
-        surfaces.append(twice_top_ref[k] + mixing_00 * second + weights_ref[5] * moved)
+        surfaces.append(twice_top_ref[k] + mixing_00 * second + corner_ref[0] * moved)
     surface = jnp.concatenate(surfaces + [jnp.zeros((width - 2 * rows, width), f32)], axis=0).astype(bf16)
     codes = received_ref[:, lines - 8 : lines, :].astype(f32)
     wanted = (codes == lane_iota(codes.shape).astype(f32)).astype(f32).reshape(devices * 8, width).astype(bf16)
@@ -452,7 +492,7 @@
     tiles, fields = atm_flux.shape[1:3]
     tracers, levels = ocean_state.shape[:2]
     planes = tracers * levels
-    packed_lines = 8 * (packing(rows, planes, width)[3] + 2)
+    packed_lines = 8 * (packing(rows, planes, width)[3] + 3)
     weights = remap_weights[0]
     block = dest_block.reshape(tiles)
     row = dest_row.reshape(tiles)
@@ -471,33 +511,31 @@
             pltpu.VMEM((tiles, fields, width), bf16), pltpu.VMEM((tiles, width, width), bf16),
             pltpu.SMEM((blocks,), jnp.int32), pltpu.SMEM((2 * blocks,), jnp.int32),
             pltpu.VMEM((tiles * fields, width), bf16), pltpu.VMEM((blocks + 2, 8, width), f32),
-            pltpu.SemaphoreType.DMA((3,)), pltpu.SemaphoreType.DMA((min(4, tiles // 2),)),
+            pltpu.SemaphoreType.DMA((3,)), pltpu.SemaphoreType.DMA((2,)),
         ],
         flops=2 * tiles * fields * width * width, moved=3 << 20,
     )(*in_hbm(block, row, atm_flux[0], weights))
     received = lax.all_to_all(packed, "blk", split_axis=0, concat_axis=0, tiled=True)
 
-    top, bottom = call(
-        rows_kernel, "rows", (held(2, planes + 16, width, dtype=bf16),) * 2, [vmem, vmem], moved=1 << 20
-    )(state, land_mask)
+    surface_shape = shape(tracers, rows, width)
+    message = held(2, planes + 16, width, dtype=bf16)
+    top, bottom, sums, corner = call(
+        rows_kernel, "rows", (message, message, held(rows, 8, width), held(2, rows, width)),
+        [vmem] * 3, moved=1 << 20,
+    )(*in_vmem(state, land_mask, mixing))
     after = lax.ppermute(top, "sec", down_sec)
     before = lax.ppermute(bottom, "sec", up_sec)
     packed_shape = held(packed_lines, width)
-    slab = pltpu.VMEM((rows + 4, planes + 8, width), f32)
-    first_columns, last_columns, near, far = call(
-        columns_kernel, "columns", (packed_shape,) * 4, [vmem] * 5, scratch=[slab], moved=2 << 20
-    )(*in_vmem(state, land_mask, wet_fraction, before, after))
+    first_columns, last_columns, near, far, light = call(
+        columns_kernel, "columns", (packed_shape,) * 4 + (held(rows + 4, 16, width),), [vmem] * 6,
+        scratch=[pltpu.VMEM((rows + 4, planes + 16, width), f32)], moved=2 << 20,
+    )(*in_vmem(state, land_mask, wet_fraction, sums, before, after))
     near = lax.ppermute(near, "blk", swaps[0])
     far = lax.ppermute(far, "blk", swaps[1])
-    surface_shape = shape(tracers, rows, width)
-    twice, once_top, twice_top, step_weights, beside = call(
-        stencil_kernel, "stencil",
-        (
-            shape(tracers, rows, levels, width), surface_shape, surface_shape,
-            shape(7, rows, width), shape(2, 8, width),
-        ),
-        [vmem] * 9, scratch=[slab, pltpu.VMEM((rows + 4, planes, width), f32)], flops=20 << 20, moved=3 << 20,
-    )(*in_vmem(state, land_mask, before, after, first_columns, last_columns, near, far, mixing))
+    once_top, twice_top, step_weights, beside = call(
+        light_kernel, "light",
+        (surface_shape, surface_shape, shape(5, rows, width), shape(2, 8, width)), [vmem] * 5, moved=1 << 20,
+    )(*in_vmem(light, first_columns, last_columns, near, far))
 
     drive_sum, drive_rate, first, edges = call(
         drive_kernel, "drive", (surface_shape,) * 3 + (shape(8, width),), [vmem] * 4, moved=1 << 20
@@ -506,12 +544,19 @@
     first_before = lax.ppermute(first, "sec", up_sec)
     spread_first, second, back = call(
         surface_kernel, "surface",
-        (surface_shape, surface_shape, pltpu.HBM((blocks, 8, width), bf16)), [vmem] * 12, moved=1 << 20,
+        (surface_shape, surface_shape, pltpu.HBM((blocks, 8, width), bf16)), [vmem] * 13, moved=1 << 20,
     )(
         received, land_mask, drive_sum, drive_rate, first, edges, first_before, first_after,
-        beside, once_top, twice_top, step_weights,
+        beside, once_top, twice_top, step_weights, corner,
     )
     returned = lax.all_to_all(back, "blk", split_axis=0, concat_axis=0, tiled=True)
+    twice = call(
+        stencil_kernel, "stencil", held(tracers, rows, levels, width), [vmem] * 9,
+        scratch=[
+            pltpu.VMEM((rows + 4, planes + 8, width), f32), pltpu.VMEM((rows + 4, planes, width), f32),
+        ],
+        flops=20 << 20, moved=3 << 20,
+    )(*in_vmem(state, land_mask, before, after, first_columns, last_columns, near, far, spread_first))
     ocean, sums, picks, fetched = call(
         ocean_kernel, "ocean",
         (

time: 67.5 us -> 67.3 us (level)
  waiting for transfers between devices: 12 us -> 10.1 us
  starting transfers between devices: 40.4 us -> 41.5 us
  Pallas kernels: 13.6 us -> 14.3 us
    all_to_all x1, waiting for transfers between devices: 6.56 us -> 4.79 us  [per_device(): lax.all_to_all(back, 'blk', split_axis=0, concat_axis=0, tiled=True)]
    all_to_all x1, starting transfers between devices: 8.72 us -> 10.1 us  [per_device(): lax.all_to_all(back, 'blk', split_axis=0, concat_axis=0, tiled=True)]
    pallas_call x3 -> x4, Pallas kernels: 2.7 us -> 3.7 us  [the longest x1 1.75 us: per_device(): call(stencil_kernel, 'stencil', held(tracers, rows, levels, width), [vmem...]
  transfers between devices with their start and end apart: 8 -> 8, of which waited for: 3 -> 3; matrix products, arithmetic and copies ran while one was open for 0% -> 0% of each run, Pallas kernels for 11% -> 12%
where the time goes in v11:
time: 67.3 us; the launch traced here: 66.8 us
  starting transfers between devices  41.5 us (62%)
  Pallas kernels  14.3 us (21%)
  waiting for transfers between devices  10.1 us (15%)
  between operations  0.86 us (1%)
    all_to_all x1, starting transfers between devices, per_device(): lax.all_to_all(packed, 'blk', split_axis=0, concat_axis=0, tiled=True)  10.8 us
    all_to_all x1, starting transfers between devices, per_device(): lax.all_to_all(back, 'blk', split_axis=0, concat_axis=0, tiled=True)  10.1 us
    ppermute x1, starting transfers between devices, per_device(): before = lax.ppermute(bottom, 'sec', up_sec)  5.21 us
    ppermute x1, starting transfers between devices, per_device(): first_before = lax.ppermute(first, 'sec', up_sec)  4.96 us
    ppermute x1, waiting for transfers between devices, per_device(): after = lax.ppermute(top, 'sec', down_sec)  4.84 us
    all_to_all x1, waiting for transfers between devices, per_device(): lax.all_to_all(back, 'blk', split_axis=0, concat_axis=0, tiled=True)  4.79 us
    pallas_call x1, Pallas kernels, per_device(): call(ocean_kernel, 'ocean', (shape(tracers, levels, rows, width), held(wi...  3.79 us
    ppermute x1, starting transfers between devices, per_device(): near = lax.ppermute(near, 'blk', swaps[0])  3.5 us
  transfers between devices with their start and end apart: 8, of which 3 were waited for; matrix products, arithmetic and copies ran while one was open for 0% of the time, Pallas kernels for 12%

profile of v11, /device:TPU:193, one launch (start us, length us, event | category | flops | bytes accessed | tf_op | source)
XLA Modules:
  0.0 66.8 jit_solution(3962641422445886774)
XLA Ops:
  0.6 0.0 copy-start.2
  0.6 0.0 copy-start.1
  0.7 0.0 copy-start
  0.7 0.0 copy-start.3
  0.7 3.3 %forward.1 = (bf16[64,40,128]{2,1,0:T(8,128)(2,1)}, s32[64]{0:T(128)S(1)}) custom-call(s32[64]{0:T(128)} %bitcast.10, s32[64]{0:T(128)} %bitcast.16, bf16[64,16,128]{2,1,0:T(8,128)(2,1)} %bitcast.14, bf16[64,128,128]{2,1,0:T(8,128)(2,1)} %bitcast.12), custom_call_target="tpu_custom_call" | custom-call | flops 33554432 | bytes 3145728 | tf_op jit(solution)/shard_map/forward/pallas_call | solution.py:505
  3.9 10.8 %all-to-all-start = ((bf16[64,40,128]{2,1,0:T(8,128)(2,1)}), bf16[64,40,128]{2,1,0:T(8,128)(2,1)S(1)}, u32[]{:S(2)}, u32[]{:S(2)}) async-start(bf16[64,40,128]{2,1,0:T(8,128)(2,1)} %get-tuple-element.36), calls=%async_computation | async-start | bytes 1310720 | tf_op jit(solution)/shard_map/all_to_all | solution.py:518
  14.7 0.0 copy-done.2
  14.8 0.0 copy-done.1
  14.8 0.0 copy-done
  14.8 0.9 %rows.1 = (bf16[2,176,128]{2,1,0:T(8,128)(2,1)S(1)}, bf16[2,176,128]{2,1,0:T(8,128)(2,1)S(1)}, f32[8,8,128]{2,1,0:T(8,128)S(1)}, f32[2,8,128]{2,1,0:T(8,128)S(1)}) custom-call(f32[160,8,128]{2,1,0:T(8,128)S(1)} %bitcast.6, s32[8,128]{1,0:T(8,128)S(1)} %copy-done.2, f32[80,80]{1,0:T(8,128)S(1)} %copy-done.1), custom_call_target="tpu_custom_call" | custom-call | bytes 1048576 | tf_op jit(solution)/shard_map/rows/pallas_call | solution.py:522
  15.7 5.2 %collective-permute-start = (bf16[2,176,128]{2,1,0:T(8,128)(2,1)S(1)}, bf16[2,176,128]{2,1,0:T(8,128)(2,1)S(1)}, u32[]{:S(2)}, u32[]{:S(2)}) collective-permute-start(bf16[2,176,128]{2,1,0:T(8,128)(2,1)S(1)} %get-tuple-element.29), channel_id=1, source_target_pairs={{0,64},{64,128},{128,192},{192,256},{256,320},{320,384},{384,448},... | collective-permute-start | bytes 270344 | tf_op jit(solution)/shard_map/ppermute | solution.py:527
  20.9 1.9 %collective-permute-start.1 = (bf16[2,176,128]{2,1,0:T(8,128)(2,1)S(1)}, bf16[2,176,128]{2,1,0:T(8,128)(2,1)S(1)}, u32[]{:S(2)}, u32[]{:S(2)}) collective-permute-start(bf16[2,176,128]{2,1,0:T(8,128)(2,1)S(1)} %get-tuple-element.30), channel_id=1, source_target_pairs={{64,0},{128,64},{192,128},{256,192},{320,256},{384,320},{448,384},... | collective-permute-start | bytes 270344 | tf_op jit(solution)/shard_map/ppermute | solution.py:526
  22.9 0.0 collective-permute-done.before_ref
  22.9 4.8 %collective-permute-done.1.after_ref = bf16[2,176,128]{2,1,0:T(8,128)(2,1)S(1)} collective-permute-done((bf16[2,176,128]{2,1,0:T(8,128)(2,1)S(1)}, bf16[2,176,128]{2,1,0:T(8,128)(2,1)S(1)}, u32[]{:S(2)}, u32[]{:S(2)}) %collective-permute-start.1) | collective-permute-done | bytes 90144 | tf_op jit(solution)/shard_map/ppermute | solution.py:526
  27.7 0.0 copy-done.3
  27.7 0.8 %columns.1 = (f32[56,128]{1,0:T(8,128)S(1)}, f32[56,128]{1,0:T(8,128)S(1)}, f32[56,128]{1,0:T(8,128)S(1)}, f32[56,128]{1,0:T(8,128)S(1)}, f32[12,16,128]{2,1,0:T(8,128)S(1)}) custom-call(f32[160,8,128]{2,1,0:T(8,128)S(1)} %bitcast.7, s32[8,128]{1,0:T(8,128)S(1)} %copy-done.2, f32[8,128]{1,0:T(8,128)S(1)} %copy-done.3, ...), custom_call_target="tpu_custom_call" | custom-call | bytes 2097152 | tf_op jit(solution)/shard_map/columns/pallas_call | solution.py:529
  28.5 3.5 %collective-permute-start.2 = (f32[56,128]{1,0:T(8,128)S(1)}, f32[56,128]{1,0:T(8,128)S(1)}, u32[]{:S(2)}, u32[]{:S(2)}) collective-permute-start(f32[56,128]{1,0:T(8,128)S(1)} %get-tuple-element.34), channel_id=1, source_target_pairs={{0,1},{2,3},{4,5},{6,7},{8,9},{10,11},{12,13},{14,15},{16,17},{18,... | collective-permute-start | bytes 86024 | tf_op jit(solution)/shard_map/ppermute | solution.py:533
  32.0 0.0 copy-start.4
  32.0 3.1 %collective-permute-start.3 = (f32[56,128]{1,0:T(8,128)S(1)}, f32[56,128]{1,0:T(8,128)S(1)}, u32[]{:S(2)}, u32[]{:S(2)}) collective-permute-start(f32[56,128]{1,0:T(8,128)S(1)} %get-tuple-element.35), channel_id=1, source_target_pairs={{1,2},{3,4},{5,6},{7,8},{9,10},{11,12},{13,14},{15,16},{17,18},{19... | collective-permute-start | bytes 86024 | tf_op jit(solution)/shard_map/ppermute | solution.py:534
  35.1 0.0 all-to-all-done.received_ref
  35.1 0.8 %drive.1 = (f32[2,8,128]{2,1,0:T(8,128)S(1)}, f32[2,8,128]{2,1,0:T(8,128)S(1)}, f32[2,8,128]{2,1,0:T(8,128)S(1)}, f32[8,128]{1,0:T(8,128)S(1)}) custom-call(bf16[64,40,128]{2,1,0:T(8,128)(2,1)S(1)} %all-to-all-done.received_ref, f32[160,8,128]{2,1,0:T(8,128)S(1)} %bitcast.8, s32[8,128]{1,0:T(8,128)S(1)} %copy-done.2, f32[8,128]{1,0:T(8,128)S(1)} %copy-done.3), custom_call_target="tpu_custom_call" | custom-call | bytes 1048576 | tf_op jit(solution)/shard_map/drive/pallas_call | solution.py:540
  35.9 1.9 %collective-permute-start.5 = (f32[2,8,128]{2,1,0:T(8,128)S(1)}, f32[2,8,128]{2,1,0:T(8,128)S(1)}, u32[]{:S(2)}, u32[]{:S(2)}) collective-permute-start(f32[2,8,128]{2,1,0:T(8,128)S(1)} %get-tuple-element.39.first_ref), channel_id=1, source_target_pairs={{64,0},{128,64},{192,128},{256,192},{320,256},{384,320},{448,384},... | collective-permute-start | bytes 24584 | tf_op jit(solution)/shard_map/ppermute | solution.py:543
  37.9 5.0 %collective-permute-start.4 = (f32[2,8,128]{2,1,0:T(8,128)S(1)}, f32[2,8,128]{2,1,0:T(8,128)S(1)}, u32[]{:S(2)}, u32[]{:S(2)}) collective-permute-start(f32[2,8,128]{2,1,0:T(8,128)S(1)} %get-tuple-element.39.first_ref), channel_id=1, source_target_pairs={{0,64},{64,128},{128,192},{192,256},{256,320},{320,384},{384,448},... | collective-permute-start | bytes 24584 | tf_op jit(solution)/shard_map/ppermute | solution.py:544
  42.8 0.0 collective-permute-done.2.near_ref
  42.8 0.0 collective-permute-done.3.far_ref
  42.9 0.3 light.1
  43.1 0.0 collective-permute-done.5.after_ref
  43.1 0.5 collective-permute-done.4.before_ref
  43.6 1.2 %surface.1 = (f32[2,8,128]{2,1,0:T(8,128)S(1)}, f32[2,8,128]{2,1,0:T(8,128)S(1)}, bf16[64,8,128]{2,1,0:T(8,128)(2,1)}) custom-call(bf16[64,40,128]{2,1,0:T(8,128)(2,1)S(1)} %all-to-all-done.received_ref, s32[8,128]{1,0:T(8,128)S(1)} %copy-done.2, f32[2,8,128]{2,1,0:T(8,128)S(1)} %get-tuple-element.37.sum_ref, f32[2,8,128]{2,1,0:T(8,128)S(1)} %get-tuple-element.38.rate_ref, ...), custom_call_target="tpu_custom_call" | custom-call | bytes 1048576 | tf_op jit(solution)/shard_map/surface/pallas_call | solution.py:545
  44.8 10.1 %all-to-all-start.1 = ((bf16[64,8,128]{2,1,0:T(8,128)(2,1)}), bf16[64,8,128]{2,1,0:T(8,128)(2,1)S(1)}, u32[]{:S(2)}, u32[]{:S(2)}) async-start(bf16[64,8,128]{2,1,0:T(8,128)(2,1)} %get-tuple-element.51), calls=%async_computation.1 | async-start | bytes 262144 | tf_op jit(solution)/shard_map/all_to_all | solution.py:552
  54.9 1.8 %stencil.1.twice_ref = f32[2,8,80,128]{3,2,1,0:T(8,128)S(1)} custom-call(f32[160,8,128]{2,1,0:T(8,128)S(1)} %bitcast.9, s32[8,128]{1,0:T(8,128)S(1)} %copy-done.2, bf16[2,176,128]{2,1,0:T(8,128)(2,1)S(1)} %collective-permute-done.before_ref, bf16[2,176,128]{2,1,0:T(8,128)(2,1)S(1)} %collective-permute-done.1.after_ref, ...), custom_call_target="tpu_custom_call" | custom-call | flops 20971520 | bytes 3145728 | tf_op jit(solution)/shard_map/stencil/pallas_call | solution.py:553
  56.6 0.0 copy-done.4
  56.6 3.8 %ocean.1 = (f32[2,80,8,128]{3,2,1,0:T(8,128)}, f32[128,128]{1,0:T(8,128)S(1)}, bf16[128,512]{1,0:T(8,128)(2,1)S(1)}, bf16[64,128,128]{2,1,0:T(8,128)(2,1)S(1)}) custom-call(s32[64]{0:T(128)S(1)} %bitcast.11, s32[64]{0:T(128)S(1)} %get-tuple-element.28.slot_ref, f32[80,80]{1,0:T(8,128)S(1)} %copy-done.1, f32[2,8,80,128]{3,2,1,0:T(8,128)S(1)} %stencil.1.twice_ref, ...), custom_call_target="tpu_custom_call" | custom-call | flops 157286400 | bytes 2097152 | tf_op jit(solution)/shard_map/ocean/pallas_call | solution.py:560
  60.4 4.8 %all-to-all-done.1.returned_ref = bf16[64,8,128]{2,1,0:T(8,128)(2,1)S(1)} async-done(((bf16[64,8,128]{2,1,0:T(8,128)(2,1)}), bf16[64,8,128]{2,1,0:T(8,128)(2,1)S(1)}, u32[]{:S(2)}, u32[]{:S(2)}) %all-to-all-start.1) | async-done | bytes 131104 | tf_op jit(solution)/shard_map/all_to_all | solution.py:552
  65.2 1.6 %backward.1 = f32[64,2,128]{2,1,0:T(2,128)} custom-call(bf16[128,512]{1,0:T(8,128)(2,1)S(1)} %get-tuple-element.50.picks_ref, bf16[64,8,128]{2,1,0:T(8,128)(2,1)S(1)} %all-to-all-done.1.returned_ref, bf16[64,128,128]{2,1,0:T(8,128)(2,1)S(1)} %get-tuple-element.52.weight_ref, f32[128,128]{1,0:T(8,128)S(1)} %get-tuple-element.53.sums_ref), custom_call_target="tpu_custom_call" | custom-call | flops 16777216 | bytes 3145728 | tf_op jit(solution)/shard_map/backward/pallas_call | solution.py:569
Async XLA Ops:
  0.6 14.1 %copy-start.2 = (s32[8,128]{1,0:T(8,128)S(1)}, s32[8,128]{1,0:T(8,128)}, u32[]{:S(2)}) copy-start(s32[8,128]{1,0:T(8,128)} %mask_ref.9) | copy-start | bytes 12292
  0.6 14.1 %copy-start.1 = (f32[80,80]{1,0:T(8,128)S(1)}, f32[80,80]{1,0:T(8,128)}, u32[]{:S(2)}) copy-start(f32[80,80]{1,0:T(8,128)} %mixing_ref.3) | copy-start | bytes 76804
  0.7 14.1 %copy-start = (f32[2,80,8,128]{3,2,1,0:T(8,128)S(1)}, f32[2,80,8,128]{3,2,1,0:T(8,128)}, u32[]{:S(2)}) copy-start(f32[2,80,8,128]{3,2,1,0:T(8,128)} %param.12) | copy-start | bytes 1966084
  0.7 27.0 %copy-start.3 = (f32[8,128]{1,0:T(8,128)S(1)}, f32[8,128]{1,0:T(8,128)}, u32[]{:S(2)}) copy-start(f32[8,128]{1,0:T(8,128)} %wet_ref.3) | copy-start | bytes 12292
  3.9 31.2 %all-to-all-start = ((bf16[64,40,128]{2,1,0:T(8,128)(2,1)}), bf16[64,40,128]{2,1,0:T(8,128)(2,1)S(1)}, u32[]{:S(2)}, u32[]{:S(2)}) async-start(bf16[64,40,128]{2,1,0:T(8,128)(2,1)} %get-tuple-element.36), calls=%async_computation | async-start | bytes 1310720 | tf_op jit(solution)/shard_map/all_to_all | solution.py:518
  15.7 7.2 %collective-permute-start = (bf16[2,176,128]{2,1,0:T(8,128)(2,1)S(1)}, bf16[2,176,128]{2,1,0:T(8,128)(2,1)S(1)}, u32[]{:S(2)}, u32[]{:S(2)}) collective-permute-start(bf16[2,176,128]{2,1,0:T(8,128)(2,1)S(1)} %get-tuple-element.29), channel_id=1, source_target_pairs={{0,64},{64,128},{128,192},{192,256},{256,320},{320,384},{384,448},... | collective-permute-start | bytes 270344 | tf_op jit(solution)/shard_map/ppermute | solution.py:527
  20.9 6.8 %collective-permute-start.1 = (bf16[2,176,128]{2,1,0:T(8,128)(2,1)S(1)}, bf16[2,176,128]{2,1,0:T(8,128)(2,1)S(1)}, u32[]{:S(2)}, u32[]{:S(2)}) collective-permute-start(bf16[2,176,128]{2,1,0:T(8,128)(2,1)S(1)} %get-tuple-element.30), channel_id=1, source_target_pairs={{64,0},{128,64},{192,128},{256,192},{320,256},{384,320},{448,384},... | collective-permute-start | bytes 270344 | tf_op jit(solution)/shard_map/ppermute | solution.py:526
  28.5 14.4 %collective-permute-start.2 = (f32[56,128]{1,0:T(8,128)S(1)}, f32[56,128]{1,0:T(8,128)S(1)}, u32[]{:S(2)}, u32[]{:S(2)}) collective-permute-start(f32[56,128]{1,0:T(8,128)S(1)} %get-tuple-element.34), channel_id=1, source_target_pairs={{0,1},{2,3},{4,5},{6,7},{8,9},{10,11},{12,13},{14,15},{16,17},{18,... | collective-permute-start | bytes 86024 | tf_op jit(solution)/shard_map/ppermute | solution.py:533
  32.0 24.7 %copy-start.4 = (s32[1,64,1]{1,2,0:T(1,128)S(1)}, s32[1,64,1]{1,2,0:T(1,128)}, u32[]{:S(2)}) copy-start(s32[1,64,1]{1,2,0:T(1,128)} %param.10) | copy-start | bytes 772
  32.0 10.8 %collective-permute-start.3 = (f32[56,128]{1,0:T(8,128)S(1)}, f32[56,128]{1,0:T(8,128)S(1)}, u32[]{:S(2)}, u32[]{:S(2)}) collective-permute-start(f32[56,128]{1,0:T(8,128)S(1)} %get-tuple-element.35), channel_id=1, source_target_pairs={{1,2},{3,4},{5,6},{7,8},{9,10},{11,12},{13,14},{15,16},{17,18},{19... | collective-permute-start | bytes 86024 | tf_op jit(solution)/shard_map/ppermute | solution.py:534
  35.9 7.2 %collective-permute-start.5 = (f32[2,8,128]{2,1,0:T(8,128)S(1)}, f32[2,8,128]{2,1,0:T(8,128)S(1)}, u32[]{:S(2)}, u32[]{:S(2)}) collective-permute-start(f32[2,8,128]{2,1,0:T(8,128)S(1)} %get-tuple-element.39.first_ref), channel_id=1, source_target_pairs={{64,0},{128,64},{192,128},{256,192},{320,256},{384,320},{448,384},... | collective-permute-start | bytes 24584 | tf_op jit(solution)/shard_map/ppermute | solution.py:543
  37.9 5.7 %collective-permute-start.4 = (f32[2,8,128]{2,1,0:T(8,128)S(1)}, f32[2,8,128]{2,1,0:T(8,128)S(1)}, u32[]{:S(2)}, u32[]{:S(2)}) collective-permute-start(f32[2,8,128]{2,1,0:T(8,128)S(1)} %get-tuple-element.39.first_ref), channel_id=1, source_target_pairs={{0,64},{64,128},{128,192},{192,256},{256,320},{320,384},{384,448},... | collective-permute-start | bytes 24584 | tf_op jit(solution)/shard_map/ppermute | solution.py:544
  44.8 20.5 %all-to-all-start.1 = ((bf16[64,8,128]{2,1,0:T(8,128)(2,1)}), bf16[64,8,128]{2,1,0:T(8,128)(2,1)S(1)}, u32[]{:S(2)}, u32[]{:S(2)}) async-start(bf16[64,8,128]{2,1,0:T(8,128)(2,1)} %get-tuple-element.51), calls=%async_computation.1 | async-start | bytes 262144 | tf_op jit(solution)/shard_map/all_to_all | solution.py:552

commit v12 on v11

--- a/solution.py
+++ b/solution.py
@@ -425,7 +425,7 @@
     codes = received_ref[:, lines - 8 : lines, :].astype(f32)
     wanted = (codes == lane_iota(codes.shape).astype(f32)).astype(f32).reshape(devices * 8, width).astype(bf16)
     picked = jnp.dot(wanted, surface, preferred_element_type=f32)
-    back_ref[...] = picked.reshape(devices, 8, width).astype(bf16)
+    back_ref[...] = picked.reshape(devices, 8, width)[:, :4].astype(bf16)
 
 
 def own_columns(weight_ref, lines):
@@ -443,7 +443,7 @@
 
 def ocean_kernel(
     block_ref, slot_ref, mixing_ref, twice_ref, spread_ref, second_ref, weight_hbm,
-    out_ref, sums_ref, picks_ref, weight_ref, weight_sem,
+    out_ref, shares_ref, picks_ref, weight_ref, weight_sem,
 ):
     fetch = pltpu.make_async_copy(weight_hbm, weight_ref, weight_sem)
     fetch.start()
@@ -459,7 +459,7 @@
             forced = twice * spread_ref[k, r : r + 1, :] + once * second_ref[k, r : r + 1, :]
             out_ref[k, :, r, :] = free + forced
     fetch.wait()
-    sums_ref[...] = own_columns(weight_ref, jnp.ones((width, width), bf16))
+    shares_ref[...] = 1.0 / own_columns(weight_ref, jnp.ones((width, width), bf16))
     tiles = weight_ref.shape[0]
     columns = picks_ref.shape[1]
     if 2 * tiles < width:
@@ -474,11 +474,13 @@
         picks_ref[2 * start : 2 * start + 16, :] = jnp.where(lane == target, 1.0, 0.0).astype(bf16)
 
 
-def backward_kernel(picks_ref, returned_ref, weight_ref, sums_ref, out_ref):
+def backward_kernel(picks_ref, returned_ref, weight_ref, shares_ref, out_ref):
     tiles, width, _ = weight_ref.shape
-    lines = returned_ref[...].astype(f32).reshape(picks_ref.shape[1], width).astype(bf16)
+    lines = returned_ref[...].astype(f32)
+    lines = jnp.concatenate([lines, jnp.zeros_like(lines)], axis=1)
+    lines = lines.reshape(picks_ref.shape[1], width).astype(bf16)
     picked = jnp.dot(picks_ref[...], lines, preferred_element_type=f32).astype(bf16)
-    result = own_columns(weight_ref, picked) / sums_ref[...]
+    result = own_columns(weight_ref, picked) * shares_ref[...]
     for t in range(tiles):
         out_ref[t] = result[2 * t : 2 * t + 2]
 
@@ -544,7 +546,7 @@
     first_before = lax.ppermute(first, "sec", up_sec)
     spread_first, second, back = call(
         surface_kernel, "surface",
-        (surface_shape, surface_shape, pltpu.HBM((blocks, 8, width), bf16)), [vmem] * 13, moved=1 << 20,
+        (surface_shape, surface_shape, pltpu.HBM((blocks, 4, width), bf16)), [vmem] * 13, moved=1 << 20,
     )(
         received, land_mask, drive_sum, drive_rate, first, edges, first_before, first_after,
         beside, once_top, twice_top, step_weights, corner,
@@ -557,7 +559,7 @@
         ],
         flops=20 << 20, moved=3 << 20,
     )(*in_vmem(state, land_mask, before, after, first_columns, last_columns, near, far, spread_first))
-    ocean, sums, picks, fetched = call(
+    ocean, shares, picks, fetched = call(
         ocean_kernel, "ocean",
         (
             shape(tracers, levels, rows, width), held(width, width),
@@ -569,7 +571,7 @@
     atmosphere = call(
         backward_kernel, "backward", shape(tiles, tracers, width), [vmem] * 4,
         flops=16 * tiles * width * width, moved=3 << 20,
-    )(*in_vmem(picks, returned, fetched, sums))
+    )(*in_vmem(picks, returned, fetched, shares))
     return (ocean, atmosphere[None])
 
 

time: 67.3 us -> 66.7 us (level)
  transfers between devices with their start and end apart: 8 -> 8, of which waited for: 3 -> 3; matrix products, arithmetic and copies ran while one was open for 0% -> 0% of each run, Pallas kernels for 12% -> 13%
where the time goes in v12:
time: 66.7 us; the launch traced here: 66.3 us
  starting transfers between devices  41.5 us (62%)
  Pallas kernels  14.3 us (21%)
  waiting for transfers between devices  9.55 us (14%)
  between operations  0.86 us (1%)
    all_to_all x1, starting transfers between devices, per_device(): lax.all_to_all(packed, 'blk', split_axis=0, concat_axis=0, tiled=True)  10.8 us
    all_to_all x1, starting transfers between devices, per_device(): lax.all_to_all(back, 'blk', split_axis=0, concat_axis=0, tiled=True)  10.1 us
    ppermute x1, starting transfers between devices, per_device(): before = lax.ppermute(bottom, 'sec', up_sec)  5.21 us
    ppermute x1, starting transfers between devices, per_device(): first_before = lax.ppermute(first, 'sec', up_sec)  4.96 us
    ppermute x1, waiting for transfers between devices, per_device(): after = lax.ppermute(top, 'sec', down_sec)  4.84 us
    all_to_all x1, waiting for transfers between devices, per_device(): lax.all_to_all(back, 'blk', split_axis=0, concat_axis=0, tiled=True)  4.22 us
    pallas_call x1, Pallas kernels, per_device(): call(ocean_kernel, 'ocean', (shape(tracers, levels, rows, width), held(wi...  3.78 us
    ppermute x1, starting transfers between devices, per_device(): near = lax.ppermute(near, 'blk', swaps[0])  3.5 us
  transfers between devices with their start and end apart: 8, of which 3 were waited for; matrix products, arithmetic and copies ran while one was open for 0% of the time, Pallas kernels for 13%

profile of v12, /device:TPU:193, one launch (start us, length us, event | category | flops | bytes accessed | tf_op | source)
XLA Modules:
  0.0 66.3 jit_solution(13926405479645324544)
XLA Ops:
  0.6 0.0 copy-start.2
  0.6 0.0 copy-start.1
  0.7 0.0 copy-start
  0.7 0.0 copy-start.3
  0.7 3.3 %forward.1 = (bf16[64,40,128]{2,1,0:T(8,128)(2,1)}, s32[64]{0:T(128)S(1)}) custom-call(s32[64]{0:T(128)} %bitcast.10, s32[64]{0:T(128)} %bitcast.16, bf16[64,16,128]{2,1,0:T(8,128)(2,1)} %bitcast.14, bf16[64,128,128]{2,1,0:T(8,128)(2,1)} %bitcast.12), custom_call_target="tpu_custom_call" | custom-call | flops 33554432 | bytes 3145728 | tf_op jit(solution)/shard_map/forward/pallas_call | solution.py:507
  3.9 10.8 %all-to-all-start = ((bf16[64,40,128]{2,1,0:T(8,128)(2,1)}), bf16[64,40,128]{2,1,0:T(8,128)(2,1)S(1)}, u32[]{:S(2)}, u32[]{:S(2)}) async-start(bf16[64,40,128]{2,1,0:T(8,128)(2,1)} %get-tuple-element.36), calls=%async_computation | async-start | bytes 1310720 | tf_op jit(solution)/shard_map/all_to_all | solution.py:520
  14.7 0.0 copy-done.2
  14.8 0.0 copy-done.1
  14.8 0.0 copy-done
  14.8 0.9 %rows.1 = (bf16[2,176,128]{2,1,0:T(8,128)(2,1)S(1)}, bf16[2,176,128]{2,1,0:T(8,128)(2,1)S(1)}, f32[8,8,128]{2,1,0:T(8,128)S(1)}, f32[2,8,128]{2,1,0:T(8,128)S(1)}) custom-call(f32[160,8,128]{2,1,0:T(8,128)S(1)} %bitcast.6, s32[8,128]{1,0:T(8,128)S(1)} %copy-done.2, f32[80,80]{1,0:T(8,128)S(1)} %copy-done.1), custom_call_target="tpu_custom_call" | custom-call | bytes 1048576 | tf_op jit(solution)/shard_map/rows/pallas_call | solution.py:524
  15.7 5.2 %collective-permute-start = (bf16[2,176,128]{2,1,0:T(8,128)(2,1)S(1)}, bf16[2,176,128]{2,1,0:T(8,128)(2,1)S(1)}, u32[]{:S(2)}, u32[]{:S(2)}) collective-permute-start(bf16[2,176,128]{2,1,0:T(8,128)(2,1)S(1)} %get-tuple-element.29), channel_id=1, source_target_pairs={{0,64},{64,128},{128,192},{192,256},{256,320},{320,384},{384,448},... | collective-permute-start | bytes 270344 | tf_op jit(solution)/shard_map/ppermute | solution.py:529
  20.9 1.9 %collective-permute-start.1 = (bf16[2,176,128]{2,1,0:T(8,128)(2,1)S(1)}, bf16[2,176,128]{2,1,0:T(8,128)(2,1)S(1)}, u32[]{:S(2)}, u32[]{:S(2)}) collective-permute-start(bf16[2,176,128]{2,1,0:T(8,128)(2,1)S(1)} %get-tuple-element.30), channel_id=1, source_target_pairs={{64,0},{128,64},{192,128},{256,192},{320,256},{384,320},{448,384},... | collective-permute-start | bytes 270344 | tf_op jit(solution)/shard_map/ppermute | solution.py:528
  22.9 0.0 collective-permute-done.before_ref
  22.9 4.8 %collective-permute-done.1.after_ref = bf16[2,176,128]{2,1,0:T(8,128)(2,1)S(1)} collective-permute-done((bf16[2,176,128]{2,1,0:T(8,128)(2,1)S(1)}, bf16[2,176,128]{2,1,0:T(8,128)(2,1)S(1)}, u32[]{:S(2)}, u32[]{:S(2)}) %collective-permute-start.1) | collective-permute-done | bytes 90144 | tf_op jit(solution)/shard_map/ppermute | solution.py:528
  27.7 0.0 copy-done.3
  27.7 0.8 %columns.1 = (f32[56,128]{1,0:T(8,128)S(1)}, f32[56,128]{1,0:T(8,128)S(1)}, f32[56,128]{1,0:T(8,128)S(1)}, f32[56,128]{1,0:T(8,128)S(1)}, f32[12,16,128]{2,1,0:T(8,128)S(1)}) custom-call(f32[160,8,128]{2,1,0:T(8,128)S(1)} %bitcast.7, s32[8,128]{1,0:T(8,128)S(1)} %copy-done.2, f32[8,128]{1,0:T(8,128)S(1)} %copy-done.3, ...), custom_call_target="tpu_custom_call" | custom-call | bytes 2097152 | tf_op jit(solution)/shard_map/columns/pallas_call | solution.py:531
  28.5 0.0 copy-start.4
  28.5 3.5 %collective-permute-start.2 = (f32[56,128]{1,0:T(8,128)S(1)}, f32[56,128]{1,0:T(8,128)S(1)}, u32[]{:S(2)}, u32[]{:S(2)}) collective-permute-start(f32[56,128]{1,0:T(8,128)S(1)} %get-tuple-element.34), channel_id=1, source_target_pairs={{0,1},{2,3},{4,5},{6,7},{8,9},{10,11},{12,13},{14,15},{16,17},{18,... | collective-permute-start | bytes 86024 | tf_op jit(solution)/shard_map/ppermute | solution.py:535
  32.0 3.1 %collective-permute-start.3 = (f32[56,128]{1,0:T(8,128)S(1)}, f32[56,128]{1,0:T(8,128)S(1)}, u32[]{:S(2)}, u32[]{:S(2)}) collective-permute-start(f32[56,128]{1,0:T(8,128)S(1)} %get-tuple-element.35), channel_id=1, source_target_pairs={{1,2},{3,4},{5,6},{7,8},{9,10},{11,12},{13,14},{15,16},{17,18},{19... | collective-permute-start | bytes 86024 | tf_op jit(solution)/shard_map/ppermute | solution.py:536
  35.1 0.0 all-to-all-done.received_ref
  35.1 0.8 %drive.1 = (f32[2,8,128]{2,1,0:T(8,128)S(1)}, f32[2,8,128]{2,1,0:T(8,128)S(1)}, f32[2,8,128]{2,1,0:T(8,128)S(1)}, f32[8,128]{1,0:T(8,128)S(1)}) custom-call(bf16[64,40,128]{2,1,0:T(8,128)(2,1)S(1)} %all-to-all-done.received_ref, f32[160,8,128]{2,1,0:T(8,128)S(1)} %bitcast.8, s32[8,128]{1,0:T(8,128)S(1)} %copy-done.2, f32[8,128]{1,0:T(8,128)S(1)} %copy-done.3), custom_call_target="tpu_custom_call" | custom-call | bytes 1048576 | tf_op jit(solution)/shard_map/drive/pallas_call | solution.py:542
  35.9 1.9 %collective-permute-start.5 = (f32[2,8,128]{2,1,0:T(8,128)S(1)}, f32[2,8,128]{2,1,0:T(8,128)S(1)}, u32[]{:S(2)}, u32[]{:S(2)}) collective-permute-start(f32[2,8,128]{2,1,0:T(8,128)S(1)} %get-tuple-element.39.first_ref), channel_id=1, source_target_pairs={{64,0},{128,64},{192,128},{256,192},{320,256},{384,320},{448,384},... | collective-permute-start | bytes 24584 | tf_op jit(solution)/shard_map/ppermute | solution.py:545
  37.9 5.0 %collective-permute-start.4 = (f32[2,8,128]{2,1,0:T(8,128)S(1)}, f32[2,8,128]{2,1,0:T(8,128)S(1)}, u32[]{:S(2)}, u32[]{:S(2)}) collective-permute-start(f32[2,8,128]{2,1,0:T(8,128)S(1)} %get-tuple-element.39.first_ref), channel_id=1, source_target_pairs={{0,64},{64,128},{128,192},{192,256},{256,320},{320,384},{384,448},... | collective-permute-start | bytes 24584 | tf_op jit(solution)/shard_map/ppermute | solution.py:546
  42.8 0.0 collective-permute-done.2.near_ref
  42.8 0.0 collective-permute-done.3.far_ref
  42.9 0.3 light.1
  43.1 0.0 collective-permute-done.5.after_ref
  43.1 0.5 collective-permute-done.4.before_ref
  43.6 1.2 %surface.1 = (f32[2,8,128]{2,1,0:T(8,128)S(1)}, f32[2,8,128]{2,1,0:T(8,128)S(1)}, bf16[64,4,128]{2,1,0:T(4,128)(2,1)}) custom-call(bf16[64,40,128]{2,1,0:T(8,128)(2,1)S(1)} %all-to-all-done.received_ref, s32[8,128]{1,0:T(8,128)S(1)} %copy-done.2, f32[2,8,128]{2,1,0:T(8,128)S(1)} %get-tuple-element.37.sum_ref, f32[2,8,128]{2,1,0:T(8,128)S(1)} %get-tuple-element.38.rate_ref, ...), custom_call_target="tpu_custom_call" | custom-call | bytes 1048576 | tf_op jit(solution)/shard_map/surface/pallas_call | solution.py:547
  44.8 10.1 %all-to-all-start.1 = ((bf16[64,4,128]{2,1,0:T(4,128)(2,1)}), bf16[64,4,128]{2,1,0:T(4,128)(2,1)S(1)}, u32[]{:S(2)}, u32[]{:S(2)}) async-start(bf16[64,4,128]{2,1,0:T(4,128)(2,1)} %get-tuple-element.51), calls=%async_computation.1 | async-start | bytes 131072 | tf_op jit(solution)/shard_map/all_to_all | solution.py:554
  54.9 1.8 %stencil.1.twice_ref = f32[2,8,80,128]{3,2,1,0:T(8,128)S(1)} custom-call(f32[160,8,128]{2,1,0:T(8,128)S(1)} %bitcast.9, s32[8,128]{1,0:T(8,128)S(1)} %copy-done.2, bf16[2,176,128]{2,1,0:T(8,128)(2,1)S(1)} %collective-permute-done.before_ref, bf16[2,176,128]{2,1,0:T(8,128)(2,1)S(1)} %collective-permute-done.1.after_ref, ...), custom_call_target="tpu_custom_call" | custom-call | flops 20971520 | bytes 3145728 | tf_op jit(solution)/shard_map/stencil/pallas_call | solution.py:555
  56.6 0.0 copy-done.4
  56.6 3.8 %ocean.1 = (f32[2,80,8,128]{3,2,1,0:T(8,128)}, f32[128,128]{1,0:T(8,128)S(1)}, bf16[128,512]{1,0:T(8,128)(2,1)S(1)}, bf16[64,128,128]{2,1,0:T(8,128)(2,1)S(1)}) custom-call(s32[64]{0:T(128)S(1)} %bitcast.11, s32[64]{0:T(128)S(1)} %get-tuple-element.28.slot_ref, f32[80,80]{1,0:T(8,128)S(1)} %copy-done.1, f32[2,8,80,128]{3,2,1,0:T(8,128)S(1)} %stencil.1.twice_ref, ...), custom_call_target="tpu_custom_call" | custom-call | flops 157286400 | bytes 2097152 | tf_op jit(solution)/shard_map/ocean/pallas_call | solution.py:562
  60.4 4.2 %all-to-all-done.1.returned_ref = bf16[64,4,128]{2,1,0:T(4,128)(2,1)S(1)} async-done(((bf16[64,4,128]{2,1,0:T(4,128)(2,1)}), bf16[64,4,128]{2,1,0:T(4,128)(2,1)S(1)}, u32[]{:S(2)}, u32[]{:S(2)}) %all-to-all-start.1) | async-done | bytes 65568 | tf_op jit(solution)/shard_map/all_to_all | solution.py:554
  64.7 1.6 %backward.1 = f32[64,2,128]{2,1,0:T(2,128)} custom-call(bf16[128,512]{1,0:T(8,128)(2,1)S(1)} %get-tuple-element.50.picks_ref, bf16[64,4,128]{2,1,0:T(4,128)(2,1)S(1)} %all-to-all-done.1.returned_ref, bf16[64,128,128]{2,1,0:T(8,128)(2,1)S(1)} %get-tuple-element.52.weight_ref, f32[128,128]{1,0:T(8,128)S(1)} %get-tuple-element.53.shares_ref), custom_call_target="tpu_custom_call" | custom-call | flops 16777216 | bytes 3145728 | tf_op jit(solution)/shard_map/backward/pallas_call | solution.py:571
Async XLA Ops:
  0.6 14.1 %copy-start.2 = (s32[8,128]{1,0:T(8,128)S(1)}, s32[8,128]{1,0:T(8,128)}, u32[]{:S(2)}) copy-start(s32[8,128]{1,0:T(8,128)} %mask_ref.9) | copy-start | bytes 12292
  0.6 14.1 %copy-start.1 = (f32[80,80]{1,0:T(8,128)S(1)}, f32[80,80]{1,0:T(8,128)}, u32[]{:S(2)}) copy-start(f32[80,80]{1,0:T(8,128)} %mixing_ref.3) | copy-start | bytes 76804
  0.7 14.1 %copy-start = (f32[2,80,8,128]{3,2,1,0:T(8,128)S(1)}, f32[2,80,8,128]{3,2,1,0:T(8,128)}, u32[]{:S(2)}) copy-start(f32[2,80,8,128]{3,2,1,0:T(8,128)} %param.12) | copy-start | bytes 1966084
  0.7 27.0 %copy-start.3 = (f32[8,128]{1,0:T(8,128)S(1)}, f32[8,128]{1,0:T(8,128)}, u32[]{:S(2)}) copy-start(f32[8,128]{1,0:T(8,128)} %wet_ref.3) | copy-start | bytes 12292
  3.9 31.2 %all-to-all-start = ((bf16[64,40,128]{2,1,0:T(8,128)(2,1)}), bf16[64,40,128]{2,1,0:T(8,128)(2,1)S(1)}, u32[]{:S(2)}, u32[]{:S(2)}) async-start(bf16[64,40,128]{2,1,0:T(8,128)(2,1)} %get-tuple-element.36), calls=%async_computation | async-start | bytes 1310720 | tf_op jit(solution)/shard_map/all_to_all | solution.py:520
  15.7 7.2 %collective-permute-start = (bf16[2,176,128]{2,1,0:T(8,128)(2,1)S(1)}, bf16[2,176,128]{2,1,0:T(8,128)(2,1)S(1)}, u32[]{:S(2)}, u32[]{:S(2)}) collective-permute-start(bf16[2,176,128]{2,1,0:T(8,128)(2,1)S(1)} %get-tuple-element.29), channel_id=1, source_target_pairs={{0,64},{64,128},{128,192},{192,256},{256,320},{320,384},{384,448},... | collective-permute-start | bytes 270344 | tf_op jit(solution)/shard_map/ppermute | solution.py:529
  20.9 6.8 %collective-permute-start.1 = (bf16[2,176,128]{2,1,0:T(8,128)(2,1)S(1)}, bf16[2,176,128]{2,1,0:T(8,128)(2,1)S(1)}, u32[]{:S(2)}, u32[]{:S(2)}) collective-permute-start(bf16[2,176,128]{2,1,0:T(8,128)(2,1)S(1)} %get-tuple-element.30), channel_id=1, source_target_pairs={{64,0},{128,64},{192,128},{256,192},{320,256},{384,320},{448,384},... | collective-permute-start | bytes 270344 | tf_op jit(solution)/shard_map/ppermute | solution.py:528
  28.5 28.1 %copy-start.4 = (s32[1,64,1]{1,2,0:T(1,128)S(1)}, s32[1,64,1]{1,2,0:T(1,128)}, u32[]{:S(2)}) copy-start(s32[1,64,1]{1,2,0:T(1,128)} %param.10) | copy-start | bytes 772
  28.5 14.3 %collective-permute-start.2 = (f32[56,128]{1,0:T(8,128)S(1)}, f32[56,128]{1,0:T(8,128)S(1)}, u32[]{:S(2)}, u32[]{:S(2)}) collective-permute-start(f32[56,128]{1,0:T(8,128)S(1)} %get-tuple-element.34), channel_id=1, source_target_pairs={{0,1},{2,3},{4,5},{6,7},{8,9},{10,11},{12,13},{14,15},{16,17},{18,... | collective-permute-start | bytes 86024 | tf_op jit(solution)/shard_map/ppermute | solution.py:535
  32.0 10.8 %collective-permute-start.3 = (f32[56,128]{1,0:T(8,128)S(1)}, f32[56,128]{1,0:T(8,128)S(1)}, u32[]{:S(2)}, u32[]{:S(2)}) collective-permute-start(f32[56,128]{1,0:T(8,128)S(1)} %get-tuple-element.35), channel_id=1, source_target_pairs={{1,2},{3,4},{5,6},{7,8},{9,10},{11,12},{13,14},{15,16},{17,18},{19... | collective-permute-start | bytes 86024 | tf_op jit(solution)/shard_map/ppermute | solution.py:536
  35.9 7.2 %collective-permute-start.5 = (f32[2,8,128]{2,1,0:T(8,128)S(1)}, f32[2,8,128]{2,1,0:T(8,128)S(1)}, u32[]{:S(2)}, u32[]{:S(2)}) collective-permute-start(f32[2,8,128]{2,1,0:T(8,128)S(1)} %get-tuple-element.39.first_ref), channel_id=1, source_target_pairs={{64,0},{128,64},{192,128},{256,192},{320,256},{384,320},{448,384},... | collective-permute-start | bytes 24584 | tf_op jit(solution)/shard_map/ppermute | solution.py:545
  37.9 5.7 %collective-permute-start.4 = (f32[2,8,128]{2,1,0:T(8,128)S(1)}, f32[2,8,128]{2,1,0:T(8,128)S(1)}, u32[]{:S(2)}, u32[]{:S(2)}) collective-permute-start(f32[2,8,128]{2,1,0:T(8,128)S(1)} %get-tuple-element.39.first_ref), channel_id=1, source_target_pairs={{0,64},{64,128},{128,192},{192,256},{256,320},{320,384},{384,448},... | collective-permute-start | bytes 24584 | tf_op jit(solution)/shard_map/ppermute | solution.py:546
  44.8 19.9 %all-to-all-start.1 = ((bf16[64,4,128]{2,1,0:T(4,128)(2,1)}), bf16[64,4,128]{2,1,0:T(4,128)(2,1)S(1)}, u32[]{:S(2)}, u32[]{:S(2)}) async-start(bf16[64,4,128]{2,1,0:T(4,128)(2,1)} %get-tuple-element.51), calls=%async_computation.1 | async-start | bytes 131072 | tf_op jit(solution)/shard_map/all_to_all | solution.py:554

commit v13 on v12

--- a/solution.py
+++ b/solution.py
@@ -78,13 +78,25 @@
     for copy in copies:
         copy.start()
     out_ref[...] = jnp.zeros_like(out_ref)
-    edge_ref[...] = jnp.zeros_like(edge_ref)
     for b in range(blocks):
         used_ref[b] = 0
         code_ref[b] = empty_code
         code_ref[blocks + b] = empty_code
     for copy in copies[:3]:
         copy.wait()
+    for t in range(tiles):
+        b = block_ref[t]
+        s = used_ref[b]
+        used_ref[b] = s + 1
+        slot_ref[t] = s
+        code_ref[s * blocks + b] = row_ref[t]
+    line = line_iota((8, width))
+    lane = lane_iota((8, width))
+    extra = jnp.where(line % 2 == 1, 8.0, 0.0).astype(f32)
+    for b in range(blocks):
+        first = code_ref[b].astype(f32)
+        second = code_ref[blocks + b].astype(f32)
+        edge_ref[b + 1] = jnp.where(line < 4, jnp.where(line < 2, first, second) + extra, 0.0)
     for t in range(0, tiles, 2):
         if t % size == 0:
             copies[3 + t // size].wait()
@@ -92,17 +104,10 @@
         fluxes = flux_ref[t : t + 2].reshape(2 * fields, width)
         remapped = jnp.dot(fluxes, both, preferred_element_type=f32)
         for i in range(2):
-            b = block_ref[t + i]
-            s = used_ref[b]
-            used_ref[b] = s + 1
-            slot_ref[t + i] = s
-            code_ref[s * blocks + b] = row_ref[t + i]
-            start = pl.multiple_of(s * fields, fields)
+            start = pl.multiple_of(slot_ref[t + i] * fields, fields)
             value = remapped[i * fields : (i + 1) * fields, i * width : (i + 1) * width].astype(bf16)
-            out_ref[b, pl.ds(start, fields), :] = value
+            out_ref[block_ref[t + i], pl.ds(start, fields), :] = value
             mapped_ref[(t + i) * fields : (t + i + 1) * fields, :] = value
-    line = line_iota((8, width))
-    lane = lane_iota((8, width))
     chosen = ((line == 0) & (lane == width - 1)) | ((line == 4) & (lane == 0))
     edges = lax.dot_general(
         jnp.where(chosen, 1.0, 0.0).astype(bf16), mapped_ref[...],
@@ -116,13 +121,8 @@
         placed = jnp.where(lane // fields == r, turned, 0.0)
         edge_ref[b + 2, pl.ds(4 + s, 1), :] = placed[0:1]
         edge_ref[b, pl.ds(6 + s, 1), :] = placed[4:5]
-    extra = jnp.where(line % 2 == 1, 8.0, 0.0).astype(f32)
     for b in range(blocks):
-        first = code_ref[b].astype(f32)
-        second = code_ref[blocks + b].astype(f32)
-        code = jnp.where(line < 2, first, second) + extra
-        last = jnp.where(line < 4, code, edge_ref[b + 1])
-        out_ref[b, 2 * fields : 2 * fields + 8, :] = last.astype(bf16)
+        out_ref[b, 2 * fields : 2 * fields + 8, :] = edge_ref[b + 1].astype(bf16)
 
 
 def rows_kernel(x_ref, mask_ref, mixing_ref, top_ref, bottom_ref, sums_ref, corner_ref):

time: 66.7 us -> 66.6 us (level)
  no operation moved by 1% of the time
where the time goes in v13:
time: 66.6 us; the launch traced here: 66.1 us
  starting transfers between devices  41.5 us (62%)
  Pallas kernels  14.2 us (21%)
  waiting for transfers between devices  9.54 us (14%)
  between operations  0.86 us (1%)
    all_to_all x1, starting transfers between devices, per_device(): lax.all_to_all(packed, 'blk', split_axis=0, concat_axis=0, tiled=True)  10.8 us
    all_to_all x1, starting transfers between devices, per_device(): lax.all_to_all(back, 'blk', split_axis=0, concat_axis=0, tiled=True)  10.1 us
    ppermute x1, starting transfers between devices, per_device(): before = lax.ppermute(bottom, 'sec', up_sec)  5.21 us
    ppermute x1, starting transfers between devices, per_device(): first_before = lax.ppermute(first, 'sec', up_sec)  4.96 us
    ppermute x1, waiting for transfers between devices, per_device(): after = lax.ppermute(top, 'sec', down_sec)  4.84 us
    all_to_all x1, waiting for transfers between devices, per_device(): lax.all_to_all(back, 'blk', split_axis=0, concat_axis=0, tiled=True)  4.22 us
    pallas_call x1, Pallas kernels, per_device(): call(ocean_kernel, 'ocean', (shape(tracers, levels, rows, width), held(wi...  3.79 us
    ppermute x1, starting transfers between devices, per_device(): near = lax.ppermute(near, 'blk', swaps[0])  3.5 us
  transfers between devices with their start and end apart: 8, of which 3 were waited for; matrix products, arithmetic and copies ran while one was open for 0% of the time, Pallas kernels for 13%

profile of v13, /device:TPU:193, one launch (start us, length us, event | category | flops | bytes accessed | tf_op | source)
XLA Modules:
  0.0 66.1 jit_solution(17394685008887578058)
XLA Ops:
  0.6 0.0 copy-start.2
  0.6 0.0 copy-start.1
  0.7 0.0 copy-start
  0.7 0.0 copy-start.3
  0.7 3.1 %forward.1 = (bf16[64,40,128]{2,1,0:T(8,128)(2,1)}, s32[64]{0:T(128)S(1)}) custom-call(s32[64]{0:T(128)} %bitcast.10, s32[64]{0:T(128)} %bitcast.16, bf16[64,16,128]{2,1,0:T(8,128)(2,1)} %bitcast.14, bf16[64,128,128]{2,1,0:T(8,128)(2,1)} %bitcast.12), custom_call_target="tpu_custom_call" | custom-call | flops 33554432 | bytes 3145728 | tf_op jit(solution)/shard_map/forward/pallas_call | solution.py:507
  3.8 10.8 %all-to-all-start = ((bf16[64,40,128]{2,1,0:T(8,128)(2,1)}), bf16[64,40,128]{2,1,0:T(8,128)(2,1)S(1)}, u32[]{:S(2)}, u32[]{:S(2)}) async-start(bf16[64,40,128]{2,1,0:T(8,128)(2,1)} %get-tuple-element.36), calls=%async_computation | async-start | bytes 1310720 | tf_op jit(solution)/shard_map/all_to_all | solution.py:520
  14.6 0.0 copy-done.2
  14.6 0.0 copy-done.1
  14.6 0.0 copy-done
  14.6 0.9 %rows.1 = (bf16[2,176,128]{2,1,0:T(8,128)(2,1)S(1)}, bf16[2,176,128]{2,1,0:T(8,128)(2,1)S(1)}, f32[8,8,128]{2,1,0:T(8,128)S(1)}, f32[2,8,128]{2,1,0:T(8,128)S(1)}) custom-call(f32[160,8,128]{2,1,0:T(8,128)S(1)} %bitcast.6, s32[8,128]{1,0:T(8,128)S(1)} %copy-done.2, f32[80,80]{1,0:T(8,128)S(1)} %copy-done.1), custom_call_target="tpu_custom_call" | custom-call | bytes 1048576 | tf_op jit(solution)/shard_map/rows/pallas_call | solution.py:524
  15.6 5.2 %collective-permute-start = (bf16[2,176,128]{2,1,0:T(8,128)(2,1)S(1)}, bf16[2,176,128]{2,1,0:T(8,128)(2,1)S(1)}, u32[]{:S(2)}, u32[]{:S(2)}) collective-permute-start(bf16[2,176,128]{2,1,0:T(8,128)(2,1)S(1)} %get-tuple-element.29), channel_id=1, source_target_pairs={{0,64},{64,128},{128,192},{192,256},{256,320},{320,384},{384,448},... | collective-permute-start | bytes 270344 | tf_op jit(solution)/shard_map/ppermute | solution.py:529
  20.8 1.9 %collective-permute-start.1 = (bf16[2,176,128]{2,1,0:T(8,128)(2,1)S(1)}, bf16[2,176,128]{2,1,0:T(8,128)(2,1)S(1)}, u32[]{:S(2)}, u32[]{:S(2)}) collective-permute-start(bf16[2,176,128]{2,1,0:T(8,128)(2,1)S(1)} %get-tuple-element.30), channel_id=1, source_target_pairs={{64,0},{128,64},{192,128},{256,192},{320,256},{384,320},{448,384},... | collective-permute-start | bytes 270344 | tf_op jit(solution)/shard_map/ppermute | solution.py:528
  22.7 0.0 collective-permute-done.before_ref
  22.7 4.8 %collective-permute-done.1.after_ref = bf16[2,176,128]{2,1,0:T(8,128)(2,1)S(1)} collective-permute-done((bf16[2,176,128]{2,1,0:T(8,128)(2,1)S(1)}, bf16[2,176,128]{2,1,0:T(8,128)(2,1)S(1)}, u32[]{:S(2)}, u32[]{:S(2)}) %collective-permute-start.1) | collective-permute-done | bytes 90144 | tf_op jit(solution)/shard_map/ppermute | solution.py:528
  27.6 0.0 copy-done.3
  27.6 0.8 %columns.1 = (f32[56,128]{1,0:T(8,128)S(1)}, f32[56,128]{1,0:T(8,128)S(1)}, f32[56,128]{1,0:T(8,128)S(1)}, f32[56,128]{1,0:T(8,128)S(1)}, f32[12,16,128]{2,1,0:T(8,128)S(1)}) custom-call(f32[160,8,128]{2,1,0:T(8,128)S(1)} %bitcast.7, s32[8,128]{1,0:T(8,128)S(1)} %copy-done.2, f32[8,128]{1,0:T(8,128)S(1)} %copy-done.3, ...), custom_call_target="tpu_custom_call" | custom-call | bytes 2097152 | tf_op jit(solution)/shard_map/columns/pallas_call | solution.py:531
  28.4 0.0 copy-start.4
  28.4 3.5 %collective-permute-start.2 = (f32[56,128]{1,0:T(8,128)S(1)}, f32[56,128]{1,0:T(8,128)S(1)}, u32[]{:S(2)}, u32[]{:S(2)}) collective-permute-start(f32[56,128]{1,0:T(8,128)S(1)} %get-tuple-element.34), channel_id=1, source_target_pairs={{0,1},{2,3},{4,5},{6,7},{8,9},{10,11},{12,13},{14,15},{16,17},{18,... | collective-permute-start | bytes 86024 | tf_op jit(solution)/shard_map/ppermute | solution.py:535
  31.9 3.1 %collective-permute-start.3 = (f32[56,128]{1,0:T(8,128)S(1)}, f32[56,128]{1,0:T(8,128)S(1)}, u32[]{:S(2)}, u32[]{:S(2)}) collective-permute-start(f32[56,128]{1,0:T(8,128)S(1)} %get-tuple-element.35), channel_id=1, source_target_pairs={{1,2},{3,4},{5,6},{7,8},{9,10},{11,12},{13,14},{15,16},{17,18},{19... | collective-permute-start | bytes 86024 | tf_op jit(solution)/shard_map/ppermute | solution.py:536
  35.0 0.0 all-to-all-done.received_ref
  35.0 0.8 %drive.1 = (f32[2,8,128]{2,1,0:T(8,128)S(1)}, f32[2,8,128]{2,1,0:T(8,128)S(1)}, f32[2,8,128]{2,1,0:T(8,128)S(1)}, f32[8,128]{1,0:T(8,128)S(1)}) custom-call(bf16[64,40,128]{2,1,0:T(8,128)(2,1)S(1)} %all-to-all-done.received_ref, f32[160,8,128]{2,1,0:T(8,128)S(1)} %bitcast.8, s32[8,128]{1,0:T(8,128)S(1)} %copy-done.2, f32[8,128]{1,0:T(8,128)S(1)} %copy-done.3), custom_call_target="tpu_custom_call" | custom-call | bytes 1048576 | tf_op jit(solution)/shard_map/drive/pallas_call | solution.py:542
  35.8 1.9 %collective-permute-start.5 = (f32[2,8,128]{2,1,0:T(8,128)S(1)}, f32[2,8,128]{2,1,0:T(8,128)S(1)}, u32[]{:S(2)}, u32[]{:S(2)}) collective-permute-start(f32[2,8,128]{2,1,0:T(8,128)S(1)} %get-tuple-element.39.first_ref), channel_id=1, source_target_pairs={{64,0},{128,64},{192,128},{256,192},{320,256},{384,320},{448,384},... | collective-permute-start | bytes 24584 | tf_op jit(solution)/shard_map/ppermute | solution.py:545
  37.7 5.0 %collective-permute-start.4 = (f32[2,8,128]{2,1,0:T(8,128)S(1)}, f32[2,8,128]{2,1,0:T(8,128)S(1)}, u32[]{:S(2)}, u32[]{:S(2)}) collective-permute-start(f32[2,8,128]{2,1,0:T(8,128)S(1)} %get-tuple-element.39.first_ref), channel_id=1, source_target_pairs={{0,64},{64,128},{128,192},{192,256},{256,320},{320,384},{384,448},... | collective-permute-start | bytes 24584 | tf_op jit(solution)/shard_map/ppermute | solution.py:546
  42.7 0.0 collective-permute-done.2.near_ref
  42.7 0.0 collective-permute-done.3.far_ref
  42.7 0.3 light.1
  43.0 0.0 collective-permute-done.5.after_ref
  43.0 0.5 collective-permute-done.4.before_ref
  43.5 1.2 %surface.1 = (f32[2,8,128]{2,1,0:T(8,128)S(1)}, f32[2,8,128]{2,1,0:T(8,128)S(1)}, bf16[64,4,128]{2,1,0:T(4,128)(2,1)}) custom-call(bf16[64,40,128]{2,1,0:T(8,128)(2,1)S(1)} %all-to-all-done.received_ref, s32[8,128]{1,0:T(8,128)S(1)} %copy-done.2, f32[2,8,128]{2,1,0:T(8,128)S(1)} %get-tuple-element.37.sum_ref, f32[2,8,128]{2,1,0:T(8,128)S(1)} %get-tuple-element.38.rate_ref, ...), custom_call_target="tpu_custom_call" | custom-call | bytes 1048576 | tf_op jit(solution)/shard_map/surface/pallas_call | solution.py:547
  44.6 10.1 %all-to-all-start.1 = ((bf16[64,4,128]{2,1,0:T(4,128)(2,1)}), bf16[64,4,128]{2,1,0:T(4,128)(2,1)S(1)}, u32[]{:S(2)}, u32[]{:S(2)}) async-start(bf16[64,4,128]{2,1,0:T(4,128)(2,1)} %get-tuple-element.51), calls=%async_computation.1 | async-start | bytes 131072 | tf_op jit(solution)/shard_map/all_to_all | solution.py:554
  54.7 1.8 %stencil.1.twice_ref = f32[2,8,80,128]{3,2,1,0:T(8,128)S(1)} custom-call(f32[160,8,128]{2,1,0:T(8,128)S(1)} %bitcast.9, s32[8,128]{1,0:T(8,128)S(1)} %copy-done.2, bf16[2,176,128]{2,1,0:T(8,128)(2,1)S(1)} %collective-permute-done.before_ref, bf16[2,176,128]{2,1,0:T(8,128)(2,1)S(1)} %collective-permute-done.1.after_ref, ...), custom_call_target="tpu_custom_call" | custom-call | flops 20971520 | bytes 3145728 | tf_op jit(solution)/shard_map/stencil/pallas_call | solution.py:555
  56.5 0.0 copy-done.4
  56.5 3.8 %ocean.1 = (f32[2,80,8,128]{3,2,1,0:T(8,128)}, f32[128,128]{1,0:T(8,128)S(1)}, bf16[128,512]{1,0:T(8,128)(2,1)S(1)}, bf16[64,128,128]{2,1,0:T(8,128)(2,1)S(1)}) custom-call(s32[64]{0:T(128)S(1)} %bitcast.11, s32[64]{0:T(128)S(1)} %get-tuple-element.28.slot_ref, f32[80,80]{1,0:T(8,128)S(1)} %copy-done.1, f32[2,8,80,128]{3,2,1,0:T(8,128)S(1)} %stencil.1.twice_ref, ...), custom_call_target="tpu_custom_call" | custom-call | flops 157286400 | bytes 2097152 | tf_op jit(solution)/shard_map/ocean/pallas_call | solution.py:562
  60.3 4.2 %all-to-all-done.1.returned_ref = bf16[64,4,128]{2,1,0:T(4,128)(2,1)S(1)} async-done(((bf16[64,4,128]{2,1,0:T(4,128)(2,1)}), bf16[64,4,128]{2,1,0:T(4,128)(2,1)S(1)}, u32[]{:S(2)}, u32[]{:S(2)}) %all-to-all-start.1) | async-done | bytes 65568 | tf_op jit(solution)/shard_map/all_to_all | solution.py:554
  64.5 1.6 %backward.1 = f32[64,2,128]{2,1,0:T(2,128)} custom-call(bf16[128,512]{1,0:T(8,128)(2,1)S(1)} %get-tuple-element.50.picks_ref, bf16[64,4,128]{2,1,0:T(4,128)(2,1)S(1)} %all-to-all-done.1.returned_ref, bf16[64,128,128]{2,1,0:T(8,128)(2,1)S(1)} %get-tuple-element.52.weight_ref, f32[128,128]{1,0:T(8,128)S(1)} %get-tuple-element.53.shares_ref), custom_call_target="tpu_custom_call" | custom-call | flops 16777216 | bytes 3145728 | tf_op jit(solution)/shard_map/backward/pallas_call | solution.py:571
Async XLA Ops:
  0.6 14.0 %copy-start.2 = (s32[8,128]{1,0:T(8,128)S(1)}, s32[8,128]{1,0:T(8,128)}, u32[]{:S(2)}) copy-start(s32[8,128]{1,0:T(8,128)} %mask_ref.9) | copy-start | bytes 12292
  0.6 14.0 %copy-start.1 = (f32[80,80]{1,0:T(8,128)S(1)}, f32[80,80]{1,0:T(8,128)}, u32[]{:S(2)}) copy-start(f32[80,80]{1,0:T(8,128)} %mixing_ref.3) | copy-start | bytes 76804
  0.7 14.0 %copy-start = (f32[2,80,8,128]{3,2,1,0:T(8,128)S(1)}, f32[2,80,8,128]{3,2,1,0:T(8,128)}, u32[]{:S(2)}) copy-start(f32[2,80,8,128]{3,2,1,0:T(8,128)} %param.12) | copy-start | bytes 1966084
  0.7 26.9 %copy-start.3 = (f32[8,128]{1,0:T(8,128)S(1)}, f32[8,128]{1,0:T(8,128)}, u32[]{:S(2)}) copy-start(f32[8,128]{1,0:T(8,128)} %wet_ref.3) | copy-start | bytes 12292
  3.8 31.2 %all-to-all-start = ((bf16[64,40,128]{2,1,0:T(8,128)(2,1)}), bf16[64,40,128]{2,1,0:T(8,128)(2,1)S(1)}, u32[]{:S(2)}, u32[]{:S(2)}) async-start(bf16[64,40,128]{2,1,0:T(8,128)(2,1)} %get-tuple-element.36), calls=%async_computation | async-start | bytes 1310720 | tf_op jit(solution)/shard_map/all_to_all | solution.py:520
  15.6 7.2 %collective-permute-start = (bf16[2,176,128]{2,1,0:T(8,128)(2,1)S(1)}, bf16[2,176,128]{2,1,0:T(8,128)(2,1)S(1)}, u32[]{:S(2)}, u32[]{:S(2)}) collective-permute-start(bf16[2,176,128]{2,1,0:T(8,128)(2,1)S(1)} %get-tuple-element.29), channel_id=1, source_target_pairs={{0,64},{64,128},{128,192},{192,256},{256,320},{320,384},{384,448},... | collective-permute-start | bytes 270344 | tf_op jit(solution)/shard_map/ppermute | solution.py:529
  20.8 6.8 %collective-permute-start.1 = (bf16[2,176,128]{2,1,0:T(8,128)(2,1)S(1)}, bf16[2,176,128]{2,1,0:T(8,128)(2,1)S(1)}, u32[]{:S(2)}, u32[]{:S(2)}) collective-permute-start(bf16[2,176,128]{2,1,0:T(8,128)(2,1)S(1)} %get-tuple-element.30), channel_id=1, source_target_pairs={{64,0},{128,64},{192,128},{256,192},{320,256},{384,320},{448,384},... | collective-permute-start | bytes 270344 | tf_op jit(solution)/shard_map/ppermute | solution.py:528
  28.4 28.1 %copy-start.4 = (s32[1,64,1]{1,2,0:T(1,128)S(1)}, s32[1,64,1]{1,2,0:T(1,128)}, u32[]{:S(2)}) copy-start(s32[1,64,1]{1,2,0:T(1,128)} %param.10) | copy-start | bytes 772
  28.4 14.3 %collective-permute-start.2 = (f32[56,128]{1,0:T(8,128)S(1)}, f32[56,128]{1,0:T(8,128)S(1)}, u32[]{:S(2)}, u32[]{:S(2)}) collective-permute-start(f32[56,128]{1,0:T(8,128)S(1)} %get-tuple-element.34), channel_id=1, source_target_pairs={{0,1},{2,3},{4,5},{6,7},{8,9},{10,11},{12,13},{14,15},{16,17},{18,... | collective-permute-start | bytes 86024 | tf_op jit(solution)/shard_map/ppermute | solution.py:535
  31.9 10.8 %collective-permute-start.3 = (f32[56,128]{1,0:T(8,128)S(1)}, f32[56,128]{1,0:T(8,128)S(1)}, u32[]{:S(2)}, u32[]{:S(2)}) collective-permute-start(f32[56,128]{1,0:T(8,128)S(1)} %get-tuple-element.35), channel_id=1, source_target_pairs={{1,2},{3,4},{5,6},{7,8},{9,10},{11,12},{13,14},{15,16},{17,18},{19... | collective-permute-start | bytes 86024 | tf_op jit(solution)/shard_map/ppermute | solution.py:536
  35.8 7.2 %collective-permute-start.5 = (f32[2,8,128]{2,1,0:T(8,128)S(1)}, f32[2,8,128]{2,1,0:T(8,128)S(1)}, u32[]{:S(2)}, u32[]{:S(2)}) collective-permute-start(f32[2,8,128]{2,1,0:T(8,128)S(1)} %get-tuple-element.39.first_ref), channel_id=1, source_target_pairs={{64,0},{128,64},{192,128},{256,192},{320,256},{384,320},{448,384},... | collective-permute-start | bytes 24584 | tf_op jit(solution)/shard_map/ppermute | solution.py:545
  37.7 5.7 %collective-permute-start.4 = (f32[2,8,128]{2,1,0:T(8,128)S(1)}, f32[2,8,128]{2,1,0:T(8,128)S(1)}, u32[]{:S(2)}, u32[]{:S(2)}) collective-permute-start(f32[2,8,128]{2,1,0:T(8,128)S(1)} %get-tuple-element.39.first_ref), channel_id=1, source_target_pairs={{0,64},{64,128},{128,192},{192,256},{256,320},{320,384},{384,448},... | collective-permute-start | bytes 24584 | tf_op jit(solution)/shard_map/ppermute | solution.py:546
  44.6 19.9 %all-to-all-start.1 = ((bf16[64,4,128]{2,1,0:T(4,128)(2,1)}), bf16[64,4,128]{2,1,0:T(4,128)(2,1)S(1)}, u32[]{:S(2)}, u32[]{:S(2)}) async-start(bf16[64,4,128]{2,1,0:T(4,128)(2,1)} %get-tuple-element.51), calls=%async_computation.1 | async-start | bytes 131072 | tf_op jit(solution)/shard_map/all_to_all | solution.py:554

commit v14 on v13

--- a/solution.py
+++ b/solution.py
@@ -443,7 +443,7 @@
 
 def ocean_kernel(
     block_ref, slot_ref, mixing_ref, twice_ref, spread_ref, second_ref, weight_hbm,
-    out_ref, shares_ref, picks_ref, weight_ref, weight_sem,
+    out_ref, total_ref, picks_ref, weight_ref, weight_sem,
 ):
     fetch = pltpu.make_async_copy(weight_hbm, weight_ref, weight_sem)
     fetch.start()
@@ -459,7 +459,7 @@
             forced = twice * spread_ref[k, r : r + 1, :] + once * second_ref[k, r : r + 1, :]
             out_ref[k, :, r, :] = free + forced
     fetch.wait()
-    shares_ref[...] = 1.0 / own_columns(weight_ref, jnp.ones((width, width), bf16))
+    total_ref[...] = own_columns(weight_ref, jnp.ones((width, width), bf16))
     tiles = weight_ref.shape[0]
     columns = picks_ref.shape[1]
     if 2 * tiles < width:
@@ -474,15 +474,14 @@
         picks_ref[2 * start : 2 * start + 16, :] = jnp.where(lane == target, 1.0, 0.0).astype(bf16)
 
 
-def backward_kernel(picks_ref, returned_ref, weight_ref, shares_ref, out_ref):
+def backward_kernel(picks_ref, returned_ref, weight_ref, total_ref, out_ref):
     tiles, width, _ = weight_ref.shape
     lines = returned_ref[...].astype(f32)
     lines = jnp.concatenate([lines, jnp.zeros_like(lines)], axis=1)
     lines = lines.reshape(picks_ref.shape[1], width).astype(bf16)
     picked = jnp.dot(picks_ref[...], lines, preferred_element_type=f32).astype(bf16)
-    result = own_columns(weight_ref, picked) * shares_ref[...]
-    for t in range(tiles):
-        out_ref[t] = result[2 * t : 2 * t + 2]
+    result = own_columns(weight_ref, picked) / total_ref[...]
+    out_ref[...] = result[: 2 * tiles]
 
 
 def per_device(
@@ -559,7 +558,7 @@
         ],
         flops=20 << 20, moved=3 << 20,
     )(*in_vmem(state, land_mask, before, after, first_columns, last_columns, near, far, spread_first))
-    ocean, shares, picks, fetched = call(
+    ocean, totals, picks, fetched = call(
         ocean_kernel, "ocean",
         (
             shape(tracers, levels, rows, width), held(width, width),
@@ -569,10 +568,10 @@
         flops=12 * planes * levels * rows * width, moved=2 << 20,
     )(block, slot, *in_vmem(mixing, twice, spread_first, second), *in_hbm(weights))
     atmosphere = call(
-        backward_kernel, "backward", shape(tiles, tracers, width), [vmem] * 4,
+        backward_kernel, "backward", shape(tiles * tracers, width), [vmem] * 4,
         flops=16 * tiles * width * width, moved=3 << 20,
-    )(*in_vmem(picks, returned, fetched, shares))
-    return (ocean, atmosphere[None])
+    )(*in_vmem(picks, returned, fetched, totals))
+    return (ocean, atmosphere.reshape(1, tiles, tracers, width))
 
 
 def solution(mesh):

time: 66.6 us -> 66.6 us (level)
  no operation moved by 1% of the time
where the time goes in v14:
time: 66.6 us; the launch traced here: 66.1 us
  starting transfers between devices  41.5 us (62%)
  Pallas kernels  14.2 us (21%)
  waiting for transfers between devices  9.54 us (14%)
  between operations  0.86 us (1%)
    all_to_all x1, starting transfers between devices, per_device(): lax.all_to_all(packed, 'blk', split_axis=0, concat_axis=0, tiled=True)  10.8 us
    all_to_all x1, starting transfers between devices, per_device(): lax.all_to_all(back, 'blk', split_axis=0, concat_axis=0, tiled=True)  10.1 us
    ppermute x1, starting transfers between devices, per_device(): before = lax.ppermute(bottom, 'sec', up_sec)  5.21 us
    ppermute x1, starting transfers between devices, per_device(): first_before = lax.ppermute(first, 'sec', up_sec)  4.96 us
    ppermute x1, waiting for transfers between devices, per_device(): after = lax.ppermute(top, 'sec', down_sec)  4.84 us
    all_to_all x1, waiting for transfers between devices, per_device(): lax.all_to_all(back, 'blk', split_axis=0, concat_axis=0, tiled=True)  4.22 us
    pallas_call x1, Pallas kernels, per_device(): call(ocean_kernel, 'ocean', (shape(tracers, levels, rows, width), held(wi...  3.79 us
    ppermute x1, starting transfers between devices, per_device(): near = lax.ppermute(near, 'blk', swaps[0])  3.5 us
  transfers between devices with their start and end apart: 8, of which 3 were waited for; matrix products, arithmetic and copies ran while one was open for 0% of the time, Pallas kernels for 13%

profile of v14, /device:TPU:193, one launch (start us, length us, event | category | flops | bytes accessed | tf_op | source)
XLA Modules:
  0.0 66.1 jit_solution(18384536092046031299)
XLA Ops:
  0.6 0.0 copy-start.2
  0.6 0.0 copy-start.1
  0.7 0.0 copy-start
  0.7 0.0 copy-start.3
  0.7 3.1 %forward.1 = (bf16[64,40,128]{2,1,0:T(8,128)(2,1)}, s32[64]{0:T(128)S(1)}) custom-call(s32[64]{0:T(128)} %bitcast.10, s32[64]{0:T(128)} %bitcast.16, bf16[64,16,128]{2,1,0:T(8,128)(2,1)} %bitcast.14, bf16[64,128,128]{2,1,0:T(8,128)(2,1)} %bitcast.12), custom_call_target="tpu_custom_call" | custom-call | flops 33554432 | bytes 3145728 | tf_op jit(solution)/shard_map/forward/pallas_call | solution.py:506
  3.8 10.8 %all-to-all-start = ((bf16[64,40,128]{2,1,0:T(8,128)(2,1)}), bf16[64,40,128]{2,1,0:T(8,128)(2,1)S(1)}, u32[]{:S(2)}, u32[]{:S(2)}) async-start(bf16[64,40,128]{2,1,0:T(8,128)(2,1)} %get-tuple-element.36), calls=%async_computation | async-start | bytes 1310720 | tf_op jit(solution)/shard_map/all_to_all | solution.py:519
  14.6 0.0 copy-done.2
  14.6 0.0 copy-done.1
  14.6 0.0 copy-done
  14.6 0.9 %rows.1 = (bf16[2,176,128]{2,1,0:T(8,128)(2,1)S(1)}, bf16[2,176,128]{2,1,0:T(8,128)(2,1)S(1)}, f32[8,8,128]{2,1,0:T(8,128)S(1)}, f32[2,8,128]{2,1,0:T(8,128)S(1)}) custom-call(f32[160,8,128]{2,1,0:T(8,128)S(1)} %bitcast.6, s32[8,128]{1,0:T(8,128)S(1)} %copy-done.2, f32[80,80]{1,0:T(8,128)S(1)} %copy-done.1), custom_call_target="tpu_custom_call" | custom-call | bytes 1048576 | tf_op jit(solution)/shard_map/rows/pallas_call | solution.py:523
  15.6 5.2 %collective-permute-start = (bf16[2,176,128]{2,1,0:T(8,128)(2,1)S(1)}, bf16[2,176,128]{2,1,0:T(8,128)(2,1)S(1)}, u32[]{:S(2)}, u32[]{:S(2)}) collective-permute-start(bf16[2,176,128]{2,1,0:T(8,128)(2,1)S(1)} %get-tuple-element.29), channel_id=1, source_target_pairs={{0,64},{64,128},{128,192},{192,256},{256,320},{320,384},{384,448},... | collective-permute-start | bytes 270344 | tf_op jit(solution)/shard_map/ppermute | solution.py:528
  20.8 1.9 %collective-permute-start.1 = (bf16[2,176,128]{2,1,0:T(8,128)(2,1)S(1)}, bf16[2,176,128]{2,1,0:T(8,128)(2,1)S(1)}, u32[]{:S(2)}, u32[]{:S(2)}) collective-permute-start(bf16[2,176,128]{2,1,0:T(8,128)(2,1)S(1)} %get-tuple-element.30), channel_id=1, source_target_pairs={{64,0},{128,64},{192,128},{256,192},{320,256},{384,320},{448,384},... | collective-permute-start | bytes 270344 | tf_op jit(solution)/shard_map/ppermute | solution.py:527
  22.7 0.0 collective-permute-done.before_ref
  22.7 4.8 %collective-permute-done.1.after_ref = bf16[2,176,128]{2,1,0:T(8,128)(2,1)S(1)} collective-permute-done((bf16[2,176,128]{2,1,0:T(8,128)(2,1)S(1)}, bf16[2,176,128]{2,1,0:T(8,128)(2,1)S(1)}, u32[]{:S(2)}, u32[]{:S(2)}) %collective-permute-start.1) | collective-permute-done | bytes 90144 | tf_op jit(solution)/shard_map/ppermute | solution.py:527
  27.6 0.0 copy-done.3
  27.6 0.8 %columns.1 = (f32[56,128]{1,0:T(8,128)S(1)}, f32[56,128]{1,0:T(8,128)S(1)}, f32[56,128]{1,0:T(8,128)S(1)}, f32[56,128]{1,0:T(8,128)S(1)}, f32[12,16,128]{2,1,0:T(8,128)S(1)}) custom-call(f32[160,8,128]{2,1,0:T(8,128)S(1)} %bitcast.7, s32[8,128]{1,0:T(8,128)S(1)} %copy-done.2, f32[8,128]{1,0:T(8,128)S(1)} %copy-done.3, ...), custom_call_target="tpu_custom_call" | custom-call | bytes 2097152 | tf_op jit(solution)/shard_map/columns/pallas_call | solution.py:530
  28.4 0.0 copy-start.4
  28.4 3.5 %collective-permute-start.2 = (f32[56,128]{1,0:T(8,128)S(1)}, f32[56,128]{1,0:T(8,128)S(1)}, u32[]{:S(2)}, u32[]{:S(2)}) collective-permute-start(f32[56,128]{1,0:T(8,128)S(1)} %get-tuple-element.34), channel_id=1, source_target_pairs={{0,1},{2,3},{4,5},{6,7},{8,9},{10,11},{12,13},{14,15},{16,17},{18,... | collective-permute-start | bytes 86024 | tf_op jit(solution)/shard_map/ppermute | solution.py:534
  31.9 3.1 %collective-permute-start.3 = (f32[56,128]{1,0:T(8,128)S(1)}, f32[56,128]{1,0:T(8,128)S(1)}, u32[]{:S(2)}, u32[]{:S(2)}) collective-permute-start(f32[56,128]{1,0:T(8,128)S(1)} %get-tuple-element.35), channel_id=1, source_target_pairs={{1,2},{3,4},{5,6},{7,8},{9,10},{11,12},{13,14},{15,16},{17,18},{19... | collective-permute-start | bytes 86024 | tf_op jit(solution)/shard_map/ppermute | solution.py:535
  35.0 0.0 all-to-all-done.received_ref
  35.0 0.8 %drive.1 = (f32[2,8,128]{2,1,0:T(8,128)S(1)}, f32[2,8,128]{2,1,0:T(8,128)S(1)}, f32[2,8,128]{2,1,0:T(8,128)S(1)}, f32[8,128]{1,0:T(8,128)S(1)}) custom-call(bf16[64,40,128]{2,1,0:T(8,128)(2,1)S(1)} %all-to-all-done.received_ref, f32[160,8,128]{2,1,0:T(8,128)S(1)} %bitcast.8, s32[8,128]{1,0:T(8,128)S(1)} %copy-done.2, f32[8,128]{1,0:T(8,128)S(1)} %copy-done.3), custom_call_target="tpu_custom_call" | custom-call | bytes 1048576 | tf_op jit(solution)/shard_map/drive/pallas_call | solution.py:541
  35.8 1.9 %collective-permute-start.5 = (f32[2,8,128]{2,1,0:T(8,128)S(1)}, f32[2,8,128]{2,1,0:T(8,128)S(1)}, u32[]{:S(2)}, u32[]{:S(2)}) collective-permute-start(f32[2,8,128]{2,1,0:T(8,128)S(1)} %get-tuple-element.39.first_ref), channel_id=1, source_target_pairs={{64,0},{128,64},{192,128},{256,192},{320,256},{384,320},{448,384},... | collective-permute-start | bytes 24584 | tf_op jit(solution)/shard_map/ppermute | solution.py:544
  37.7 5.0 %collective-permute-start.4 = (f32[2,8,128]{2,1,0:T(8,128)S(1)}, f32[2,8,128]{2,1,0:T(8,128)S(1)}, u32[]{:S(2)}, u32[]{:S(2)}) collective-permute-start(f32[2,8,128]{2,1,0:T(8,128)S(1)} %get-tuple-element.39.first_ref), channel_id=1, source_target_pairs={{0,64},{64,128},{128,192},{192,256},{256,320},{320,384},{384,448},... | collective-permute-start | bytes 24584 | tf_op jit(solution)/shard_map/ppermute | solution.py:545
  42.7 0.0 collective-permute-done.2.near_ref
  42.7 0.0 collective-permute-done.3.far_ref
  42.7 0.3 light.1
  43.0 0.0 collective-permute-done.5.after_ref
  43.0 0.5 collective-permute-done.4.before_ref
  43.5 1.2 %surface.1 = (f32[2,8,128]{2,1,0:T(8,128)S(1)}, f32[2,8,128]{2,1,0:T(8,128)S(1)}, bf16[64,4,128]{2,1,0:T(4,128)(2,1)}) custom-call(bf16[64,40,128]{2,1,0:T(8,128)(2,1)S(1)} %all-to-all-done.received_ref, s32[8,128]{1,0:T(8,128)S(1)} %copy-done.2, f32[2,8,128]{2,1,0:T(8,128)S(1)} %get-tuple-element.37.sum_ref, f32[2,8,128]{2,1,0:T(8,128)S(1)} %get-tuple-element.38.rate_ref, ...), custom_call_target="tpu_custom_call" | custom-call | bytes 1048576 | tf_op jit(solution)/shard_map/surface/pallas_call | solution.py:546
  44.6 10.1 %all-to-all-start.1 = ((bf16[64,4,128]{2,1,0:T(4,128)(2,1)}), bf16[64,4,128]{2,1,0:T(4,128)(2,1)S(1)}, u32[]{:S(2)}, u32[]{:S(2)}) async-start(bf16[64,4,128]{2,1,0:T(4,128)(2,1)} %get-tuple-element.51), calls=%async_computation.1 | async-start | bytes 131072 | tf_op jit(solution)/shard_map/all_to_all | solution.py:553
  54.7 1.8 %stencil.1.twice_ref = f32[2,8,80,128]{3,2,1,0:T(8,128)S(1)} custom-call(f32[160,8,128]{2,1,0:T(8,128)S(1)} %bitcast.9, s32[8,128]{1,0:T(8,128)S(1)} %copy-done.2, bf16[2,176,128]{2,1,0:T(8,128)(2,1)S(1)} %collective-permute-done.before_ref, bf16[2,176,128]{2,1,0:T(8,128)(2,1)S(1)} %collective-permute-done.1.after_ref, ...), custom_call_target="tpu_custom_call" | custom-call | flops 20971520 | bytes 3145728 | tf_op jit(solution)/shard_map/stencil/pallas_call | solution.py:554
  56.5 0.0 copy-done.4
  56.5 3.8 %ocean.1 = (f32[2,80,8,128]{3,2,1,0:T(8,128)}, f32[128,128]{1,0:T(8,128)S(1)}, bf16[128,512]{1,0:T(8,128)(2,1)S(1)}, bf16[64,128,128]{2,1,0:T(8,128)(2,1)S(1)}) custom-call(s32[64]{0:T(128)S(1)} %bitcast.11, s32[64]{0:T(128)S(1)} %get-tuple-element.28.slot_ref, f32[80,80]{1,0:T(8,128)S(1)} %copy-done.1, f32[2,8,80,128]{3,2,1,0:T(8,128)S(1)} %stencil.1.twice_ref, ...), custom_call_target="tpu_custom_call" | custom-call | flops 157286400 | bytes 2097152 | tf_op jit(solution)/shard_map/ocean/pallas_call | solution.py:561
  60.3 4.2 %all-to-all-done.1.returned_ref = bf16[64,4,128]{2,1,0:T(4,128)(2,1)S(1)} async-done(((bf16[64,4,128]{2,1,0:T(4,128)(2,1)}), bf16[64,4,128]{2,1,0:T(4,128)(2,1)S(1)}, u32[]{:S(2)}, u32[]{:S(2)}) %all-to-all-start.1) | async-done | bytes 65568 | tf_op jit(solution)/shard_map/all_to_all | solution.py:553
  64.5 1.6 %backward.1 = f32[128,128]{1,0:T(8,128)} custom-call(bf16[128,512]{1,0:T(8,128)(2,1)S(1)} %get-tuple-element.50.picks_ref, bf16[64,4,128]{2,1,0:T(4,128)(2,1)S(1)} %all-to-all-done.1.returned_ref, bf16[64,128,128]{2,1,0:T(8,128)(2,1)S(1)} %get-tuple-element.52.weight_ref, f32[128,128]{1,0:T(8,128)S(1)} %get-tuple-element.53.total_ref), custom_call_target="tpu_custom_call" | custom-call | flops 16777216 | bytes 3145728 | tf_op jit(solution)/shard_map/backward/pallas_call | solution.py:570
Async XLA Ops:
  0.6 14.0 %copy-start.2 = (s32[8,128]{1,0:T(8,128)S(1)}, s32[8,128]{1,0:T(8,128)}, u32[]{:S(2)}) copy-start(s32[8,128]{1,0:T(8,128)} %mask_ref.9) | copy-start | bytes 12292
  0.6 14.0 %copy-start.1 = (f32[80,80]{1,0:T(8,128)S(1)}, f32[80,80]{1,0:T(8,128)}, u32[]{:S(2)}) copy-start(f32[80,80]{1,0:T(8,128)} %mixing_ref.3) | copy-start | bytes 76804
  0.7 14.0 %copy-start = (f32[2,80,8,128]{3,2,1,0:T(8,128)S(1)}, f32[2,80,8,128]{3,2,1,0:T(8,128)}, u32[]{:S(2)}) copy-start(f32[2,80,8,128]{3,2,1,0:T(8,128)} %param.12) | copy-start | bytes 1966084
  0.7 26.9 %copy-start.3 = (f32[8,128]{1,0:T(8,128)S(1)}, f32[8,128]{1,0:T(8,128)}, u32[]{:S(2)}) copy-start(f32[8,128]{1,0:T(8,128)} %wet_ref.3) | copy-start | bytes 12292
  3.8 31.2 %all-to-all-start = ((bf16[64,40,128]{2,1,0:T(8,128)(2,1)}), bf16[64,40,128]{2,1,0:T(8,128)(2,1)S(1)}, u32[]{:S(2)}, u32[]{:S(2)}) async-start(bf16[64,40,128]{2,1,0:T(8,128)(2,1)} %get-tuple-element.36), calls=%async_computation | async-start | bytes 1310720 | tf_op jit(solution)/shard_map/all_to_all | solution.py:519
  15.6 7.2 %collective-permute-start = (bf16[2,176,128]{2,1,0:T(8,128)(2,1)S(1)}, bf16[2,176,128]{2,1,0:T(8,128)(2,1)S(1)}, u32[]{:S(2)}, u32[]{:S(2)}) collective-permute-start(bf16[2,176,128]{2,1,0:T(8,128)(2,1)S(1)} %get-tuple-element.29), channel_id=1, source_target_pairs={{0,64},{64,128},{128,192},{192,256},{256,320},{320,384},{384,448},... | collective-permute-start | bytes 270344 | tf_op jit(solution)/shard_map/ppermute | solution.py:528
  20.8 6.8 %collective-permute-start.1 = (bf16[2,176,128]{2,1,0:T(8,128)(2,1)S(1)}, bf16[2,176,128]{2,1,0:T(8,128)(2,1)S(1)}, u32[]{:S(2)}, u32[]{:S(2)}) collective-permute-start(bf16[2,176,128]{2,1,0:T(8,128)(2,1)S(1)} %get-tuple-element.30), channel_id=1, source_target_pairs={{64,0},{128,64},{192,128},{256,192},{320,256},{384,320},{448,384},... | collective-permute-start | bytes 270344 | tf_op jit(solution)/shard_map/ppermute | solution.py:527
  28.4 28.1 %copy-start.4 = (s32[1,64,1]{1,2,0:T(1,128)S(1)}, s32[1,64,1]{1,2,0:T(1,128)}, u32[]{:S(2)}) copy-start(s32[1,64,1]{1,2,0:T(1,128)} %param.10) | copy-start | bytes 772
  28.4 14.3 %collective-permute-start.2 = (f32[56,128]{1,0:T(8,128)S(1)}, f32[56,128]{1,0:T(8,128)S(1)}, u32[]{:S(2)}, u32[]{:S(2)}) collective-permute-start(f32[56,128]{1,0:T(8,128)S(1)} %get-tuple-element.34), channel_id=1, source_target_pairs={{0,1},{2,3},{4,5},{6,7},{8,9},{10,11},{12,13},{14,15},{16,17},{18,... | collective-permute-start | bytes 86024 | tf_op jit(solution)/shard_map/ppermute | solution.py:534
  31.9 10.8 %collective-permute-start.3 = (f32[56,128]{1,0:T(8,128)S(1)}, f32[56,128]{1,0:T(8,128)S(1)}, u32[]{:S(2)}, u32[]{:S(2)}) collective-permute-start(f32[56,128]{1,0:T(8,128)S(1)} %get-tuple-element.35), channel_id=1, source_target_pairs={{1,2},{3,4},{5,6},{7,8},{9,10},{11,12},{13,14},{15,16},{17,18},{19... | collective-permute-start | bytes 86024 | tf_op jit(solution)/shard_map/ppermute | solution.py:535
  35.8 7.2 %collective-permute-start.5 = (f32[2,8,128]{2,1,0:T(8,128)S(1)}, f32[2,8,128]{2,1,0:T(8,128)S(1)}, u32[]{:S(2)}, u32[]{:S(2)}) collective-permute-start(f32[2,8,128]{2,1,0:T(8,128)S(1)} %get-tuple-element.39.first_ref), channel_id=1, source_target_pairs={{64,0},{128,64},{192,128},{256,192},{320,256},{384,320},{448,384},... | collective-permute-start | bytes 24584 | tf_op jit(solution)/shard_map/ppermute | solution.py:544
  37.7 5.7 %collective-permute-start.4 = (f32[2,8,128]{2,1,0:T(8,128)S(1)}, f32[2,8,128]{2,1,0:T(8,128)S(1)}, u32[]{:S(2)}, u32[]{:S(2)}) collective-permute-start(f32[2,8,128]{2,1,0:T(8,128)S(1)} %get-tuple-element.39.first_ref), channel_id=1, source_target_pairs={{0,64},{64,128},{128,192},{192,256},{256,320},{320,384},{384,448},... | collective-permute-start | bytes 24584 | tf_op jit(solution)/shard_map/ppermute | solution.py:545
  44.6 19.9 %all-to-all-start.1 = ((bf16[64,4,128]{2,1,0:T(4,128)(2,1)}), bf16[64,4,128]{2,1,0:T(4,128)(2,1)S(1)}, u32[]{:S(2)}, u32[]{:S(2)}) async-start(bf16[64,4,128]{2,1,0:T(4,128)(2,1)} %get-tuple-element.51), calls=%async_computation.1 | async-start | bytes 131072 | tf_op jit(solution)/shard_map/all_to_all | solution.py:553
